TPU v7x, 32 devices: a whole 2x2x4 slice. The times are simulated.
32 devices in a mesh: dp: 2 (over core), far: 4 (over y, x), near: 4 (over z).
Axes of the slice: x: 2, y: 2, z: 4, core: 2. Of those that a mesh axis runs over, the one named last changes fastest.
Arguments:
- grad_out: bfloat16 [1024, 4096], P(('dp', 'far', 'near')), may hold values from -6 to 6
- hidden: bfloat16 [1024, 8, 768], P(('dp', 'far', 'near')), may hold values from -6 to 6
- gates: float32 [1024, 8], P(('dp', 'far', 'near')), may hold values from 0.05 to 1
- expert_ids: int32 [1024, 8], P(('dp', 'far', 'near')), may hold values from 0 to 15, all different within a row; in each aligned block of 32 rows (0 to 31, 32 to 63, ...) at most 16 rows name the same one
- w_down: bfloat16 [16, 768, 4096], P(('far', 'near')), may hold values from -0.09375 to 0.09375
Outputs:
- grad_hidden: bfloat16 [1024, 8, 768], P(('dp', 'far', 'near'))
- grad_gates: float32 [1024, 8], P(('dp', 'far', 'near'))
- grad_down: bfloat16 [16, 768, 4096], P(('far', 'near'), 'dp')
Inputs may be any that keep to these rules, and one draw needn't show every extreme that they name: `expert_ids`: each token names 8 different experts; among the tokens of one device no expert is named by more than 16 tokens, a bound that some block reaches.
All inputs are finite; a program needn't handle non-finite values.
Results may differ from a plain program's by a relative error of at most 0.008.
Values may be sent and summed in bfloat16 or wider, within the bound.
No kernel may reach another device: no remote copies, remote signals or barrier semaphores. Data moves between devices by JAX's collectives and lax.ppermute only.
A program may use at most 64 MiB of HBM per device.

v0:
```python
import jax
import jax.numpy as jnp
from jax import lax
from jax.sharding import PartitionSpec as P


def partner(array, axis, apart):
    return lax.ppermute(array, axis, [(i, i ^ 1 << apart) for i in range(lax.axis_size(axis))])


def local(grad_out, hidden, gates, expert_ids, w_down):
    tok_local, top_count = expert_ids.shape
    far_count = lax.axis_size("far")
    near_count = lax.axis_size("near")
    experts = far_count * near_count
    capacity = max(4, (tok_local * top_count + experts - 1) // experts)
    width = grad_out.shape[1]
    hidden_width = hidden.shape[2]
    row_total = tok_local * top_count
    flat_ids = expert_ids.reshape(-1)
    one_hot = (flat_ids[:, None] == jnp.arange(experts, dtype=jnp.int32)[None, :]).astype(jnp.int32)
    ranks = jnp.sum(jnp.cumsum(one_hot, axis=0) * one_hot, axis=1) - 1
    slots = flat_ids * capacity + ranks
    out_rows = jnp.broadcast_to(grad_out[:, None, :], (tok_local, top_count, width)).reshape(
        row_total, width
    )
    scaled = (
        (gates[:, :, None] * hidden.astype(jnp.float32))
        .astype(jnp.bfloat16)
        .reshape(row_total, hidden_width)
    )
    send_out = jnp.zeros((experts * capacity, width), jnp.bfloat16).at[slots].set(out_rows)
    send_hid = jnp.zeros((experts * capacity, hidden_width), jnp.bfloat16).at[slots].set(scaled)
    recv_out, recv_hid = (
        lax.all_to_all(
            send_out.reshape(experts, capacity, width),
            ("far", "near"),
            split_axis=0,
            concat_axis=0,
            tiled=True,
        ),
        lax.all_to_all(
            send_hid.reshape(experts, capacity, hidden_width),
            ("far", "near"),
            split_axis=0,
            concat_axis=0,
            tiled=True,
        ),
    )
    recv_out = recv_out.reshape(experts * capacity, width)
    recv_hid = recv_hid.reshape(experts * capacity, hidden_width)
    weight = w_down[0]
    returned = lax.dot_general(
        recv_out, weight, (((1,), (1,)), ((), ())), preferred_element_type=jnp.float32
    ).astype(jnp.bfloat16)
    share = hidden_width // lax.axis_size("dp")
    replica = lax.axis_index("dp")
    own_start = replica * share
    peer_start = (1 - replica) * share
    peer_cols = lax.dynamic_slice_in_dim(recv_hid, peer_start, share, 1)
    peer_out, peer_hid = partner((recv_out, peer_cols), "dp", 0)
    own_cols = lax.dynamic_slice_in_dim(recv_hid, own_start, share, 1)
    own_part = lax.dot_general(
        own_cols, recv_out, (((0,), (0,)), ((), ())), preferred_element_type=jnp.float32
    ).astype(jnp.bfloat16)
    peer_part = lax.dot_general(
        peer_hid, peer_out, (((0,), (0,)), ((), ())), preferred_element_type=jnp.float32
    ).astype(jnp.bfloat16)
    summed = own_part.astype(jnp.float32) + peer_part.astype(jnp.float32)
    grad_down = summed.astype(jnp.bfloat16)[None]
    came_back = lax.all_to_all(
        returned.reshape(experts, capacity, hidden_width),
        ("far", "near"),
        split_axis=0,
        concat_axis=0,
        tiled=True,
    )
    back_rows = came_back.reshape(experts * capacity, hidden_width)[slots]
    back_rows = back_rows.reshape(tok_local, top_count, hidden_width).astype(jnp.float32)
    grad_hidden = (gates[:, :, None] * back_rows).astype(jnp.bfloat16)
    grad_gates = jnp.sum(back_rows * hidden.astype(jnp.float32), axis=-1)
    return (grad_hidden, grad_gates, grad_down)


def solution(mesh):
    placed = (
        P(("dp", "far", "near"), None),
        P(("dp", "far", "near"), None, None),
        P(("dp", "far", "near"), None),
        P(("dp", "far", "near"), None),
        P(("far", "near"), None, None),
    )
    return jax.shard_map(
        local,
        mesh=mesh,
        in_specs=placed,
        out_specs=(
            P(("dp", "far", "near"), None, None),
            P(("dp", "far", "near"), None),
            P(("far", "near"), "dp", None),
        ),
        check_vma=False,
    )
```

profile of v0, /device:TPU:0, one launch (start us, length us, event | category | flops | bytes accessed | tf_op | source)
XLA Modules:
  0.0 110.5 jit_solution(17011288619909106684)
XLA Ops:
  0.6 0.0 copy-start
  0.6 0.8 copy.16
  1.5 0.1 eq.29
  1.5 0.1 eq.25
  1.6 0.7 broadcast_multiply_fusion
  2.3 0.6 reduce-window.6
  2.9 0.2 slice_reduce_fusion
  3.1 0.1 fusion.20
  3.2 0.1 copy.15
  3.3 0.1 mul.45
  3.4 0.0 copy-start.3
  3.4 0.0 copy-done
  3.4 4.0 %scatter_custom_fusion = bf16[256,4096]{1,0:T(8,128)(2,1)S(1)} fusion(s32[256]{0:T(256)S(1)} %bitcast.49, bf16[32,4096]{1,0:T(8,128)(2,1)S(1)} %copy-done, bf16[]{:T(256)} %constant.11.clone.1), kind=kCustom, calls=%fused_computation.9 | custom fusion | bytes 2359298 | tf_op jit(solution)/shard_map/scatter | solution.py:32
  7.5 0.0 copy-start.2
  7.5 0.0 copy-start.1
  7.5 58.2 %all_to_all.15 = bf16[16,16,4096]{2,1,0:T(8,128)(2,1)} all-to-all(bf16[16,16,4096]{2,1,0:T(8,128)(2,1)S(1)} %bitcast.45), channel_id=1, replica_groups=mesh['dp'=2,'far'=4,'near'=4] {'far','near'}, dimensions={0} | all-to-all | bytes 4194304 | tf_op jit(solution)/shard_map/all_to_all | solution.py:35
  65.7 0.0 collective-permute-start.1
  65.7 0.0 copy-done.2
  65.7 0.1 copy.14
  65.8 0.0 copy-done.1
  65.8 2.4 %scatter_custom_fusion.1 = bf16[256,768]{1,0:T(8,128)(2,1)} fusion(s32[256]{0:T(256)S(1)} %bitcast.50, bf16[32,8,768]{2,1,0:T(8,128)(2,1)S(1)} %copy-done.1, f32[32,8]{1,0:T(8,128)S(1)} %copy.14, bf16[]{:T(256)} %constant.11.clone.1), kind=kCustom, calls=%fused_computation.21 | custom fusion | flops 589824 | bytes 802818 | tf_op jit(solution)/shard_map/scatter | solution.py:33
  68.3 0.0 copy-done.3
  68.3 3.6 %all-to-all-start.2 = ((bf16[16,16,768]{2,1,0:T(8,128)(2,1)}), bf16[16,16,768]{2,1,0:T(8,128)(2,1)S(1)}, u32[]{:S(2)}, u32[]{:S(2)}) async-start(bf16[16,16,768]{2,1,0:T(8,128)(2,1)} %bitcast.12), calls=%async_computation.2 | async-start | bytes 786432 | tf_op jit(solution)/shard_map/all_to_all | solution.py:42
  71.8 6.0 %fusion.5 = bf16[256,768]{1,0:T(8,128)(2,1)} fusion(bf16[256,4096]{1,0:T(8,128)(2,1)} %bitcast.5, bf16[1,768,4096]{2,1,0:T(8,128)(2,1)} %param.9), kind=kOutput, calls=%fused_computation.11 | convolution fusion | flops 1610809344 | bytes 8781824 | tf_op jit(solution)/shard_map/dot_general | solution.py:53
  77.8 8.3 %all-to-all-done.2 = bf16[16,16,768]{2,1,0:T(8,128)(2,1)S(1)} async-done(((bf16[16,16,768]{2,1,0:T(8,128)(2,1)}), bf16[16,16,768]{2,1,0:T(8,128)(2,1)S(1)}, u32[]{:S(2)}, u32[]{:S(2)}) %all-to-all-start.2) | async-done | bytes 393248 | tf_op jit(solution)/shard_map/all_to_all | solution.py:42
  86.1 3.6 %all-to-all-start.1 = ((bf16[16,16,768]{2,1,0:T(8,128)(2,1)}), bf16[16,16,768]{2,1,0:T(8,128)(2,1)S(1)}, u32[]{:S(2)}, u32[]{:S(2)}) async-start(bf16[16,16,768]{2,1,0:T(8,128)(2,1)} %bitcast.48), calls=%async_computation.1 | async-start | bytes 786432 | tf_op jit(solution)/shard_map/all_to_all | solution.py:71
  89.7 1.3 %pad_clamp_fusion = s32[1024]{0:T(1024)} fusion(s32[256]{0:T(256)} %bitcast.51), kind=kLoop, calls=%fused_computation.34 | loop fusion | flops 1024 | bytes 5120 | tf_op jit(solution)/shard_map/gather | solution.py:78
  91.0 0.7 constant_dynamic-slice_fusion
  91.7 0.0 collective-permute-start
  91.7 4.3 %convolution_convert_fusion.1 = bf16[384,4096]{1,0:T(8,128)(2,1)} fusion(bf16[256,4096]{1,0:T(8,128)(2,1)} %bitcast.5, bf16[256,768]{1,0:T(8,128)(2,1)S(1)} %bitcast.47, s32[]{:T(128)S(6)} %select_n.19), kind=kOutput, calls=%fused_computation.7 | convolution fusion | flops 806879232 | bytes 5439492 | tf_op jit(solution)/shard_map/dot_general | solution.py:63
  95.9 7.0 %all-to-all-done.1 = bf16[16,16,768]{2,1,0:T(8,128)(2,1)S(1)} async-done(((bf16[16,16,768]{2,1,0:T(8,128)(2,1)}), bf16[16,16,768]{2,1,0:T(8,128)(2,1)S(1)}, u32[]{:S(2)}, u32[]{:S(2)}) %all-to-all-start.1) | async-done | bytes 393248 | tf_op jit(solution)/shard_map/all_to_all | solution.py:71
  102.9 1.3 %gather_fusion = bf16[256,768]{1,0:T(8,128)(2,1)S(1)} fusion(bf16[256,768]{1,0:T(8,128)(2,1)S(1)} %bitcast.44, s32[1024]{0:T(1024)} %pad_clamp_fusion), kind=kCustom, calls=%fused_computation | custom fusion | bytes 787456 | tf_op jit(solution)/shard_map/gather | solution.py:78
  104.2 0.9 fusion.12
  105.2 0.7 copy.19
  105.8 0.0 collective-permute-done
  105.8 0.0 collective-permute-done.1
  105.8 4.7 %fusion.2 = bf16[1,384,4096]{2,1,0:T(8,128)(2,1)} fusion(bf16[256,384]{1,0:T(8,128)(2,1)} %collective-permute-done, bf16[256,4096]{1,0:T(8,128)(2,1)S(1)} %collective-permute-done.1, bf16[384,4096]{1,0:T(8,128)(2,1)} %convolution_convert_fusion.1), kind=kOutput, calls=%fused_computation.8 | convolution fusion | flops 813170688 | bytes 8585216 | tf_op jit(solution)/shard_map/dot_general | solution.py:66
  (5 shorter events, 0.1 us)
Async XLA Ops:
  0.6 2.8 %copy-start = (bf16[32,4096]{1,0:T(8,128)(2,1)S(1)}, bf16[32,4096]{1,0:T(8,128)(2,1)}, u32[]{:S(2)}) copy-start(bf16[32,4096]{1,0:T(8,128)(2,1)} %param.5) | copy-start | bytes 786436
  3.4 64.8 %copy-start.3 = (s32[256,1]{0,1:T(1,128)}, s32[256,1]{0,1:T(1,128)S(1)}, u32[]{:S(2)}) copy-start(s32[256,1]{0,1:T(1,128)S(1)} %compare_select_fusion) | copy-start | bytes 3076
  7.5 58.3 %copy-start.2 = (f32[32,8]{0,1:T(8,128)S(1)}, f32[32,8]{0,1:T(8,128)}, u32[]{:S(2)}) copy-start(f32[32,8]{0,1:T(8,128)} %param.7) | copy-start | bytes 3076
  7.5 58.3 %copy-start.1 = (bf16[32,8,768]{2,1,0:T(8,128)(2,1)S(1)}, bf16[32,8,768]{2,1,0:T(8,128)(2,1)}, u32[]{:S(2)}) copy-start(bf16[32,8,768]{2,1,0:T(8,128)(2,1)} %param.6) | copy-start | bytes 1179652
  65.7 40.1 %collective-permute-start.1 = (bf16[256,4096]{1,0:T(8,128)(2,1)}, bf16[256,4096]{1,0:T(8,128)(2,1)S(1)}, u32[]{:S(2)}, u32[]{:S(2)}) collective-permute-start(bf16[256,4096]{1,0:T(8,128)(2,1)} %bitcast.5), channel_id=1, source_target_pairs={{0,16},{16,0},{1,17},{17,1},{2,18},{18,2},{3,19},{19,3},{4,20},{20... | collective-permute-start | bytes 6291464 | tf_op jit(solution)/shard_map/ppermute | solution.py:8
  68.3 17.9 %all-to-all-start.2 = ((bf16[16,16,768]{2,1,0:T(8,128)(2,1)}), bf16[16,16,768]{2,1,0:T(8,128)(2,1)S(1)}, u32[]{:S(2)}, u32[]{:S(2)}) async-start(bf16[16,16,768]{2,1,0:T(8,128)(2,1)} %bitcast.12), calls=%async_computation.2 | async-start | bytes 786432 | tf_op jit(solution)/shard_map/all_to_all | solution.py:42
  86.1 16.8 %all-to-all-start.1 = ((bf16[16,16,768]{2,1,0:T(8,128)(2,1)}), bf16[16,16,768]{2,1,0:T(8,128)(2,1)S(1)}, u32[]{:S(2)}, u32[]{:S(2)}) async-start(bf16[16,16,768]{2,1,0:T(8,128)(2,1)} %bitcast.48), calls=%async_computation.1 | async-start | bytes 786432 | tf_op jit(solution)/shard_map/all_to_all | solution.py:71
  91.7 14.2 %collective-permute-start = (bf16[256,384]{1,0:T(8,128)(2,1)}, bf16[256,384]{1,0:T(8,128)(2,1)}, u32[]{:S(2)}, u32[]{:S(2)}) collective-permute-start(bf16[256,384]{1,0:T(8,128)(2,1)} %constant_dynamic-slice_fusion), channel_id=1, source_target_pairs={{0,16},{16,0},{1,17},{17,1},{2,18},{18,2},{3,19},{19,3},{4,20},{20... | collective-permute-start | bytes 589832 | tf_op jit(solution)/shard_map/ppermute | solution.py:8
where the time goes:
time: 111 us
  blocking collectives  58.2 us (52%)
  waiting for transfers between devices  15.3 us (14%)
  matrix products  15 us (14%)
  local copies, waits for them, and re-layouts  8.13 us (7%)
  starting transfers between devices  7.11 us (6%)
  other arithmetic  6.08 us (5%)
    all_to_all x1, blocking collectives, local(): lax.all_to_all(send_out.reshape(experts, capacity, width), ('far', 'near'...  58.2 us
    all_to_all x1, waiting for transfers between devices, local(): lax.all_to_all(send_hid.reshape(experts, capacity, hidden_width), ('far',...  8.29 us
    all_to_all x1, waiting for transfers between devices, local(): lax.all_to_all(returned.reshape(experts, capacity, hidden_width), ('far',...  6.97 us
    dot_general x1, matrix products, local(): lax.dot_general(recv_out, weight, (((1,), (1,)), ((), ())), preferred_ele...  6 us
    dot_general x1, matrix products, local(): lax.dot_general(peer_hid, peer_out, (((0,), (0,)), ((), ())), preferred_e...  4.69 us
    dot_general x1, matrix products, local(): lax.dot_general(own_cols, recv_out, (((0,), (0,)), ((), ())), preferred_e...  4.27 us
    scatter x1, local copies, waits for them, and re-layouts, local(): jnp.zeros((experts * capacity, width), jnp.bfloat16).at[slots].set(out_rows)  4.01 us
    all_to_all x1, starting transfers between devices, local(): lax.all_to_all(send_hid.reshape(experts, capacity, hidden_width), ('far',...  3.55 us
  transfers between devices with their start and end apart: 4, of which 2 were waited for; matrix products, arithmetic and copies ran while one was open for 16% of the time, Pallas kernels for 0%

commit v1 on v0

--- a/solution.py
+++ b/solution.py
@@ -17,38 +17,39 @@
     width = grad_out.shape[1]
     hidden_width = hidden.shape[2]
     row_total = tok_local * top_count
+    slot_total = experts * capacity
+    me = lax.axis_index("far") * near_count + lax.axis_index("near")
+
+    all_ids = lax.all_gather(expert_ids, ("far", "near"), axis=0, tiled=True)
+    all_out = lax.all_gather(grad_out, ("far", "near"), axis=0, tiled=True)
+
     flat_ids = expert_ids.reshape(-1)
     one_hot = (flat_ids[:, None] == jnp.arange(experts, dtype=jnp.int32)[None, :]).astype(jnp.int32)
     ranks = jnp.sum(jnp.cumsum(one_hot, axis=0) * one_hot, axis=1) - 1
     slots = flat_ids * capacity + ranks
-    out_rows = jnp.broadcast_to(grad_out[:, None, :], (tok_local, top_count, width)).reshape(
-        row_total, width
-    )
+    place = (jnp.arange(slot_total, dtype=jnp.int32)[:, None] == slots[None, :]).astype(jnp.bfloat16)
     scaled = (
         (gates[:, :, None] * hidden.astype(jnp.float32))
         .astype(jnp.bfloat16)
         .reshape(row_total, hidden_width)
     )
-    send_out = jnp.zeros((experts * capacity, width), jnp.bfloat16).at[slots].set(out_rows)
-    send_hid = jnp.zeros((experts * capacity, hidden_width), jnp.bfloat16).at[slots].set(scaled)
-    recv_out, recv_hid = (
-        lax.all_to_all(
-            send_out.reshape(experts, capacity, width),
-            ("far", "near"),
-            split_axis=0,
-            concat_axis=0,
-            tiled=True,
-        ),
-        lax.all_to_all(
-            send_hid.reshape(experts, capacity, hidden_width),
-            ("far", "near"),
-            split_axis=0,
-            concat_axis=0,
-            tiled=True,
-        ),
-    )
-    recv_out = recv_out.reshape(experts * capacity, width)
-    recv_hid = recv_hid.reshape(experts * capacity, hidden_width)
+    send_hid = jnp.dot(place, scaled, preferred_element_type=jnp.float32).astype(jnp.bfloat16)
+    recv_hid = lax.all_to_all(
+        send_hid.reshape(experts, capacity, hidden_width),
+        ("far", "near"),
+        split_axis=0,
+        concat_axis=0,
+        tiled=True,
+    ).reshape(slot_total, hidden_width)
+
+    named = jnp.any(all_ids == me, axis=1).reshape(experts, tok_local)
+    rank = jnp.cumsum(named.astype(jnp.int32), axis=1) - 1
+    slot = jnp.where(
+        named, jnp.arange(experts, dtype=jnp.int32)[:, None] * capacity + rank, -1
+    ).reshape(-1)
+    pick = (jnp.arange(slot_total, dtype=jnp.int32)[:, None] == slot[None, :]).astype(jnp.bfloat16)
+    recv_out = jnp.dot(pick, all_out, preferred_element_type=jnp.float32).astype(jnp.bfloat16)
+
     weight = w_down[0]
     returned = lax.dot_general(
         recv_out, weight, (((1,), (1,)), ((), ())), preferred_element_type=jnp.float32
@@ -75,8 +76,12 @@
         concat_axis=0,
         tiled=True,
     )
-    back_rows = came_back.reshape(experts * capacity, hidden_width)[slots]
-    back_rows = back_rows.reshape(tok_local, top_count, hidden_width).astype(jnp.float32)
+    back_rows = lax.dot_general(
+        place,
+        came_back.reshape(slot_total, hidden_width),
+        (((0,), (0,)), ((), ())),
+        preferred_element_type=jnp.float32,
+    ).reshape(tok_local, top_count, hidden_width)
     grad_hidden = (gates[:, :, None] * back_rows).astype(jnp.bfloat16)
     grad_gates = jnp.sum(back_rows * hidden.astype(jnp.float32), axis=-1)
     return (grad_hidden, grad_gates, grad_down)

time: 111 us -> 146 us (1.32)
  waiting for transfers between devices: 15.3 us -> 53.4 us
  blocking collectives: 58.2 us -> 43.6 us
  between operations: 0.73 us -> 14.1 us
  matrix products: 15 us -> 21.1 us
  other arithmetic: 6.08 us -> 1.02 us
  local copies, waits for them, and re-layouts: 8.13 us -> 3.35 us
    all_to_all x1 -> x0, blocking collectives: 58.2 us -> none  [local(): lax.all_to_all(send_out.reshape(experts, capacity, width), ('far', 'near'...]
    all_gather x0 -> x1, blocking collectives: none -> 43.6 us  [local(): all_ids = lax.all_gather(expert_ids, ('far', 'near'), axis=0, tiled=True)]
    all_gather x0 -> x1, waiting for transfers between devices: none -> 35 us  [local(): all_out = lax.all_gather(grad_out, ('far', 'near'), axis=0, tiled=True)]
    dot_general x0 -> x3, matrix products: none -> 8.09 us  [the longest x1 4.77 us: local(): jnp.dot(pick, all_out, preferred_element_type=jnp.float32)]
    scatter x1 -> x0, local copies, waits for them, and re-layouts: 4.01 us -> none  [local(): jnp.zeros((experts * capacity, width), jnp.bfloat16).at[slots].set(out_rows)]
    all_to_all x1, waiting for transfers between devices: 6.97 us -> 9.62 us  [local(): lax.all_to_all(returned.reshape(experts, capacity, hidden_width), ('far',...]
    scatter x1 -> x0, other arithmetic: 2.44 us -> none  [local(): jnp.zeros((experts * capacity, hidden_width), jnp.bfloat16).at[slots]]
    dot_general x1, matrix products: 4.27 us -> 2.6 us  [local(): lax.dot_general(own_cols, recv_out, (((0,), (0,)), ((), ())), preferred_e...]
  transfers between devices with their start and end apart: 4 -> 5, of which waited for: 2 -> 3; matrix products, arithmetic and copies ran while one was open for 16% -> 11% of each run, Pallas kernels for 0% -> 0%
where the time goes in v1:
time: 146 us; the launch traced here: 145 us
  waiting for transfers between devices  53.4 us (37%)
  blocking collectives  43.6 us (30%)
  matrix products  21.1 us (14%)
  between operations  14.1 us (10%)
  starting transfers between devices  8.46 us (6%)
  local copies, waits for them, and re-layouts  3.35 us (2%)
    all_gather x1, blocking collectives, local(): all_ids = lax.all_gather(expert_ids, ('far', 'near'), axis=0, tiled=True)  43.6 us
    all_gather x1, waiting for transfers between devices, local(): all_out = lax.all_gather(grad_out, ('far', 'near'), axis=0, tiled=True)  35 us
    all_to_all x1, waiting for transfers between devices, local(): lax.all_to_all(returned.reshape(experts, capacity, hidden_width), ('far',...  9.62 us
    all_to_all x1, waiting for transfers between devices, local(): lax.all_to_all(send_hid.reshape(experts, capacity, hidden_width), ('far',...  8.04 us
    dot_general x1, matrix products, local(): lax.dot_general(recv_out, weight, (((1,), (1,)), ((), ())), preferred_ele...  6 us
    dot_general x1, matrix products, local(): jnp.dot(pick, all_out, preferred_element_type=jnp.float32)  4.77 us
    dot_general x1, matrix products, local(): lax.dot_general(peer_hid, peer_out, (((0,), (0,)), ((), ())), preferred_e...  4.39 us
    all_to_all x1, starting transfers between devices, local(): lax.all_to_all(send_hid.reshape(experts, capacity, hidden_width), ('far',...  4.21 us
  transfers between devices with their start and end apart: 5, of which 3 were waited for; matrix products, arithmetic and copies ran while one was open for 11% of the time, Pallas kernels for 0%

profile of v1, /device:TPU:0, one launch (start us, length us, event | category | flops | bytes accessed | tf_op | source)
XLA Modules:
  0.0 145.0 jit_solution(9419773077919774368)
XLA Ops:
  7.2 0.0 all-gather.3.cloned.1.call-start
  7.2 0.7 all-gather.3.cloned.1.call-update
  7.9 0.8 copy.14
  8.7 0.1 eq.74
  8.8 0.1 reshape.103
  8.9 43.6 %all-gather = s32[16,32,8]{1,2,0:T(8,128)S(1)} all-gather(s32[1,32,8]{1,2,0:T(8,128)} %bitcast.45), channel_id=1, replica_groups=mesh['dp'=2,'far'=4,'near'=4] {'far','near'}, dimensions={0}, use_global_device_ids=true | all-gather | bytes 17408 | tf_op jit(solution)/shard_map/all_gather | solution.py:23
  52.5 0.2 reduce_window_sum.28
  52.7 0.1 add_select_fusion
  52.8 0.1 reshape.117
  52.9 0.6 reduce-window.6
  53.5 0.2 slice_reduce_fusion
  53.7 0.8 copy.13
  54.4 0.1 fusion.19
  54.5 0.0 copy-start
  54.5 35.0 %all-gather.3.cloned.1.call-done = bf16[512,4096]{1,0:T(8,128)(2,1)} async-done(((bf16[32,4096]{1,0:T(8,128)(2,1)}), bf16[512,4096]{1,0:T(8,128)(2,1)}) %all-gather.3.cloned.1.call-update) | async-done | bytes 4194320 | tf_op jit(solution)/shard_map/all_gather | solution.py:24
  89.6 4.8 %convolution_convert_fusion.2 = bf16[256,4096]{1,0:T(8,128)(2,1)} fusion(bf16[512,4096]{1,0:T(8,128)(2,1)} %all-gather.3.cloned.1.call-done, s32[512]{0:T(512)S(1)} %reshape.117), kind=kOutput, calls=%fused_computation.5 | convolution fusion | flops 1074921472 | bytes 6293504 | tf_op jit(solution)/shard_map/dot_general | solution.py:51
  94.3 0.0 collective-permute-start.1
  94.3 0.0 copy-done
  94.3 0.0 copy-start.1
  94.3 1.1 convolution_convert_fusion.3
  95.5 0.0 copy-done.1
  95.5 4.2 %all-to-all-start.1 = ((bf16[16,16,768]{2,1,0:T(8,128)(2,1)}), bf16[16,16,768]{2,1,0:T(8,128)(2,1)S(1)}, u32[]{:S(2)}, u32[]{:S(2)}) async-start(bf16[16,16,768]{2,1,0:T(8,128)(2,1)} %bitcast.8), calls=%async_computation.1 | async-start | bytes 786432 | tf_op jit(solution)/shard_map/all_to_all | solution.py:37
  99.7 6.0 %fusion.3 = bf16[256,768]{1,0:T(8,128)(2,1)} fusion(bf16[256,4096]{1,0:T(8,128)(2,1)} %convolution_convert_fusion.2, bf16[1,768,4096]{2,1,0:T(8,128)(2,1)} %param.9), kind=kOutput, calls=%fused_computation.8 | convolution fusion | flops 1610809344 | bytes 8781824 | tf_op jit(solution)/shard_map/dot_general | solution.py:54
  105.7 8.0 %all-to-all-done.1 = bf16[16,16,768]{2,1,0:T(8,128)(2,1)S(1)} async-done(((bf16[16,16,768]{2,1,0:T(8,128)(2,1)}), bf16[16,16,768]{2,1,0:T(8,128)(2,1)S(1)}, u32[]{:S(2)}, u32[]{:S(2)}) %all-to-all-start.1) | async-done | bytes 393248 | tf_op jit(solution)/shard_map/all_to_all | solution.py:37
  113.7 4.2 %all-to-all-start = ((bf16[16,16,768]{2,1,0:T(8,128)(2,1)}), bf16[16,16,768]{2,1,0:T(8,128)(2,1)}, u32[]{:S(2)}, u32[]{:S(2)}) async-start(bf16[16,16,768]{2,1,0:T(8,128)(2,1)} %bitcast.4), calls=%async_computation | async-start | bytes 786432 | tf_op jit(solution)/shard_map/all_to_all | solution.py:72
  118.0 0.7 constant_dynamic-slice_fusion
  118.7 0.0 collective-permute-start
  118.7 2.6 %convolution_convert_fusion.1 = bf16[384,4096]{1,0:T(8,128)(2,1)S(1)} fusion(bf16[256,4096]{1,0:T(8,128)(2,1)} %convolution_convert_fusion.2, bf16[256,768]{1,0:T(8,128)(2,1)S(1)} %bitcast.44, s32[]{:T(128)S(6)} %select_n.15), kind=kOutput, calls=%fused_computation.4 | convolution fusion | flops 806879232 | bytes 5439492 | tf_op jit(solution)/shard_map/dot_general | solution.py:64
  121.3 9.6 %all-to-all-done = bf16[16,16,768]{2,1,0:T(8,128)(2,1)} async-done(((bf16[16,16,768]{2,1,0:T(8,128)(2,1)}), bf16[16,16,768]{2,1,0:T(8,128)(2,1)}, u32[]{:S(2)}, u32[]{:S(2)}) %all-to-all-start) | async-done | bytes 393248 | tf_op jit(solution)/shard_map/all_to_all | solution.py:72
  130.9 2.2 %fusion.6 = (f32[32,8]{1,0:T(8,128)S(1)}, bf16[32,8,768]{2,1,0:T(8,128)(2,1)}) fusion(bf16[32,8,768]{2,1,0:T(8,128)(2,1)} %param.6, f32[32,8]{1,0:T(8,128)S(1)} %copy.13, bf16[256,768,1]{1,0,2:T(8,128)(2,1)} %bitcast.6, s32[256]{0:T(256)} %copy-done.1), kind=kOutput, calls=%fused_computation.11 | convolution fusion | flops 101711616 | bytes 1182720 | tf_op jit(solution)/shard_map/dot_general | solution.py:79
  133.1 0.7 copy.17
  133.8 0.0 collective-permute-done
  133.8 0.0 collective-permute-done.1
  133.8 4.4 %fusion.2 = bf16[1,384,4096]{2,1,0:T(8,128)(2,1)} fusion(bf16[256,384]{1,0:T(8,128)(2,1)} %collective-permute-done, bf16[256,4096]{1,0:T(8,128)(2,1)} %collective-permute-done.1, bf16[384,4096]{1,0:T(8,128)(2,1)S(1)} %convolution_convert_fusion.1), kind=kOutput, calls=%fused_computation.6 | convolution fusion | flops 813170688 | bytes 8585216 | tf_op jit(solution)/shard_map/dot_general | solution.py:67
  (7 shorter events, 0.1 us)
Async XLA Ops:
  7.2 82.4 %all-gather.3.cloned.1.call-start = ((), (), s32[]{:S(2)}) async-start(), calls=%async_computation.2 | async-start | bytes 4456448 | tf_op jit(solution)/shard_map/all_gather | solution.py:24
  54.5 39.8 %copy-start = (bf16[32,8,768]{2,1,0:T(8,128)(2,1)S(1)}, bf16[32,8,768]{2,1,0:T(8,128)(2,1)}, u32[]{:S(2)}) copy-start(bf16[32,8,768]{2,1,0:T(8,128)(2,1)} %param.6) | copy-start | bytes 1179652
  94.3 39.4 %collective-permute-start.1 = (bf16[256,4096]{1,0:T(8,128)(2,1)}, bf16[256,4096]{1,0:T(8,128)(2,1)}, u32[]{:S(2)}, u32[]{:S(2)}) collective-permute-start(bf16[256,4096]{1,0:T(8,128)(2,1)} %convolution_convert_fusion.2), channel_id=1, source_target_pairs={{0,16},{16,0},{1,17},{17,1},{2,18},{18,2},{3,19},{19,3},{4,20},{20... | collective-permute-start | bytes 6291464 | tf_op jit(solution)/shard_map/ppermute | solution.py:8
  94.3 1.1 copy-start.1
  95.5 18.3 %all-to-all-start.1 = ((bf16[16,16,768]{2,1,0:T(8,128)(2,1)}), bf16[16,16,768]{2,1,0:T(8,128)(2,1)S(1)}, u32[]{:S(2)}, u32[]{:S(2)}) async-start(bf16[16,16,768]{2,1,0:T(8,128)(2,1)} %bitcast.8), calls=%async_computation.1 | async-start | bytes 786432 | tf_op jit(solution)/shard_map/all_to_all | solution.py:37
  113.7 17.2 %all-to-all-start = ((bf16[16,16,768]{2,1,0:T(8,128)(2,1)}), bf16[16,16,768]{2,1,0:T(8,128)(2,1)}, u32[]{:S(2)}, u32[]{:S(2)}) async-start(bf16[16,16,768]{2,1,0:T(8,128)(2,1)} %bitcast.4), calls=%async_computation | async-start | bytes 786432 | tf_op jit(solution)/shard_map/all_to_all | solution.py:72
  118.7 15.1 %collective-permute-start = (bf16[256,384]{1,0:T(8,128)(2,1)}, bf16[256,384]{1,0:T(8,128)(2,1)}, u32[]{:S(2)}, u32[]{:S(2)}) collective-permute-start(bf16[256,384]{1,0:T(8,128)(2,1)} %constant_dynamic-slice_fusion), channel_id=1, source_target_pairs={{0,16},{16,0},{1,17},{17,1},{2,18},{18,2},{3,19},{19,3},{4,20},{20... | collective-permute-start | bytes 589832 | tf_op jit(solution)/shard_map/ppermute | solution.py:8
Sparse Core Ops, SparseCore 0:
  10.7 78.7 all-gather.2

commit v2 on v1

v2 whole, which is shorter than its diff:
```python
import jax
import jax.numpy as jnp
from jax import lax
from jax.sharding import PartitionSpec as P


def local(grad_out, hidden, gates, expert_ids, w_down):
    tok_local, top_count = expert_ids.shape
    far_count = lax.axis_size("far")
    near_count = lax.axis_size("near")
    experts = far_count * near_count
    capacity = max(4, (tok_local * top_count + experts - 1) // experts)
    width = grad_out.shape[1]
    hidden_width = hidden.shape[2]
    row_total = tok_local * top_count
    slot_total = experts * capacity
    far = lax.axis_index("far")
    near = lax.axis_index("near")

    def shift(array, steps):
        return lax.ppermute(
            array, "near", [(i, (i + steps) % near_count) for i in range(near_count)]
        )

    def across(array, apart):
        if apart == 0:
            return array
        return lax.ppermute(array, "far", [(i, i ^ apart) for i in range(far_count)])

    def direct(array, apart, steps):
        if apart == 0 and steps % near_count == 0:
            return array
        return lax.ppermute(
            array,
            ("far", "near"),
            [
                (f * near_count + n, (f ^ apart) * near_count + (n + steps) % near_count)
                for f in range(far_count)
                for n in range(near_count)
            ],
        )

    blocks = [grad_out]
    ids = [expert_ids]
    for step in range(1, near_count):
        ids.append(shift(expert_ids, step))
    for step in range(1, near_count):
        blocks.append(shift(blocks[-1], 1))

    flat_ids = expert_ids.reshape(-1)
    one_hot = (flat_ids[:, None] == jnp.arange(experts, dtype=jnp.int32)[None, :]).astype(jnp.int32)
    ranks = jnp.sum(jnp.cumsum(one_hot, axis=0) * one_hot, axis=1) - 1
    apart_of = (flat_ids // near_count) ^ far
    steps_of = (flat_ids % near_count - near + near_count) % near_count
    slots = (steps_of * far_count + apart_of) * capacity + ranks
    place = (jnp.arange(slot_total, dtype=jnp.int32)[:, None] == slots[None, :]).astype(jnp.bfloat16)
    scaled = (
        (gates[:, :, None] * hidden.astype(jnp.float32))
        .astype(jnp.bfloat16)
        .reshape(row_total, hidden_width)
    )
    send_hid = (
        jnp.dot(place, scaled, preferred_element_type=jnp.float32)
        .astype(jnp.bfloat16)
        .reshape(near_count, far_count, capacity, hidden_width)
    )

    weight = w_down[0]
    plane = (jnp.arange(far_count, dtype=jnp.int32) ^ far) * near_count + near
    recv_out = []
    recv_hid = []
    back = []
    for step in range(near_count):
        named = jnp.any(ids[step][None] == plane[:, None, None], axis=2)
        rank = jnp.cumsum(named.astype(jnp.int32), axis=1) - 1
        pick = (
            named[:, None, :]
            & (rank[:, None, :] == jnp.arange(capacity, dtype=jnp.int32)[None, :, None])
        ).astype(jnp.bfloat16)
        picked = (
            jnp.dot(
                pick.reshape(far_count * capacity, tok_local),
                blocks[step],
                preferred_element_type=jnp.float32,
            )
            .astype(jnp.bfloat16)
            .reshape(far_count, capacity, width)
        )
        rows = jnp.concatenate([across(picked[apart], apart) for apart in range(far_count)], axis=0)
        recv_out.append(rows)
        recv_hid.extend(direct(send_hid[step, apart], apart, step) for apart in range(far_count))
        returned = (
            lax.dot_general(rows, weight, (((1,), (1,)), ((), ())), preferred_element_type=jnp.float32)
            .astype(jnp.bfloat16)
            .reshape(far_count, capacity, hidden_width)
        )
        back.extend(direct(returned[apart], apart, -step) for apart in range(far_count))
    recv_out = jnp.concatenate(recv_out, axis=0)
    recv_hid = jnp.concatenate(recv_hid, axis=0)

    share = hidden_width // lax.axis_size("dp")
    replica = lax.axis_index("dp")
    swap = [(i, i ^ 1) for i in range(lax.axis_size("dp"))]
    peer_cols = lax.dynamic_slice_in_dim(recv_hid, (1 - replica) * share, share, 1)
    peer_out = lax.ppermute(recv_out, "dp", swap)
    peer_hid = lax.ppermute(peer_cols, "dp", swap)
    own_cols = lax.dynamic_slice_in_dim(recv_hid, replica * share, share, 1)
    own_part = lax.dot_general(
        own_cols, recv_out, (((0,), (0,)), ((), ())), preferred_element_type=jnp.float32
    ).astype(jnp.bfloat16)
    peer_part = lax.dot_general(
        peer_hid, peer_out, (((0,), (0,)), ((), ())), preferred_element_type=jnp.float32
    ).astype(jnp.bfloat16)
    summed = own_part.astype(jnp.float32) + peer_part.astype(jnp.float32)
    grad_down = summed.astype(jnp.bfloat16)[None]

    back_rows = lax.dot_general(
        place,
        jnp.concatenate(back, axis=0),
        (((0,), (0,)), ((), ())),
        preferred_element_type=jnp.float32,
    ).reshape(tok_local, top_count, hidden_width)
    grad_hidden = (gates[:, :, None] * back_rows).astype(jnp.bfloat16)
    grad_gates = jnp.sum(back_rows * hidden.astype(jnp.float32), axis=-1)
    return (grad_hidden, grad_gates, grad_down)


def solution(mesh):
    placed = (
        P(("dp", "far", "near"), None),
        P(("dp", "far", "near"), None, None),
        P(("dp", "far", "near"), None),
        P(("dp", "far", "near"), None),
        P(("far", "near"), None, None),
    )
    return jax.shard_map(
        local,
        mesh=mesh,
        in_specs=placed,
        out_specs=(
            P(("dp", "far", "near"), None, None),
            P(("dp", "far", "near"), None),
            P(("far", "near"), "dp", None),
        ),
        check_vma=False,
    )
```

time: 146 us -> 188 us (1.29)
  starting transfers between devices: 8.46 us -> 62.9 us
  blocking collectives: 43.6 us -> 0 us
  waiting for transfers between devices: 53.4 us -> 86 us
  between operations: 14.1 us -> 0.97 us
  local copies, waits for them, and re-layouts: 3.35 us -> 14.3 us
    ppermute x2 -> x50, waiting for transfers between devices: 0.01 us -> 86 us  [the longest x30 68.8 us: direct(): lax.ppermute(array, ('far', 'near'), [(f * near_count + n, (f ^ apart) *...]
    ppermute x2 -> x50, starting transfers between devices: 0.01 us -> 62.9 us  [the longest x30 39 us: direct(): lax.ppermute(array, ('far', 'near'), [(f * near_count + n, (f ^ apart) *...]
    all_gather x1 -> x0, blocking collectives: 43.6 us -> none  [local(): all_ids = lax.all_gather(expert_ids, ('far', 'near'), axis=0, tiled=True)]
    all_gather x1 -> x0, waiting for transfers between devices: 35 us -> none  [local(): all_out = lax.all_gather(grad_out, ('far', 'near'), axis=0, tiled=True)]
    all_to_all x2 -> x0, waiting for transfers between devices: 17.7 us -> none  [the longest x1 9.62 us: local(): lax.all_to_all(returned.reshape(experts, capacity, hidden_width), ('far',...]
    unnamed x7 -> x59, local copies, waits for them, and re-layouts: 2.2 us -> 12.4 us
    all_to_all x2 -> x0, starting transfers between devices: 8.42 us -> none  [the longest x1 4.21 us: local(): lax.all_to_all(send_hid.reshape(experts, capacity, hidden_width), ('far',...]
    dot_general x3 -> x9, matrix products: 13 us -> 13.2 us  [the longest x4 11 us: local(): lax.dot_general(rows, weight, (((1,), (1,)), ((), ())), preferred_element...]
  transfers between devices with their start and end apart: 5 -> 50, of which waited for: 3 -> 27; matrix products, arithmetic and copies ran while one was open for 11% -> 18% of each run, Pallas kernels for 0% -> 0%
where the time goes in v2:
time: 188 us
  waiting for transfers between devices  86 us (46%)
  starting transfers between devices  62.9 us (33%)
  matrix products  21.5 us (11%)
  local copies, waits for them, and re-layouts  14.3 us (8%)
  other arithmetic  2.49 us (1%)
    ppermute x30, waiting for transfers between devices, direct(): lax.ppermute(array, ('far', 'near'), [(f * near_count + n, (f ^ apart) *...  68.8 us
    ppermute x30, starting transfers between devices, direct(): lax.ppermute(array, ('far', 'near'), [(f * near_count + n, (f ^ apart) *...  39 us
    ppermute x12, waiting for transfers between devices, across(): lax.ppermute(array, 'far', [(i, i ^ apart) for i in range(far_count)])  16.7 us
    ppermute x12, starting transfers between devices, across(): lax.ppermute(array, 'far', [(i, i ^ apart) for i in range(far_count)])  14.4 us
    unnamed x59, local copies, waits for them, and re-layouts  12.4 us
    dot_general x4, matrix products, local(): lax.dot_general(rows, weight, (((1,), (1,)), ((), ())), preferred_element...  11 us
    ppermute x6, starting transfers between devices, shift(): lax.ppermute(array, 'near', [(i, (i + steps) % near_count) for i in range...  9.52 us
    dot_general x1, matrix products, local(): lax.dot_general(peer_hid, peer_out, (((0,), (0,)), ((), ())), preferred_e...  4.39 us
  transfers between devices with their start and end apart: 50, of which 27 were waited for; matrix products, arithmetic and copies ran while one was open for 18% of the time, Pallas kernels for 0%

profile of v2, /device:TPU:0, one launch (start us, length us, event | category | flops | bytes accessed | tf_op | source)
XLA Modules:
  0.0 188.2 jit_solution(765755546887386581)
XLA Ops:
  0.6 3.1 %collective-permute-start.6 = (s32[32,8]{0,1:T(8,128)}, s32[32,8]{0,1:T(8,128)S(1)}, u32[]{:S(2)}, u32[]{:S(2)}) collective-permute-start(s32[32,8]{0,1:T(8,128)} %param.8), channel_id=1, source_target_pairs={{0,1},{1,2},{2,3},{3,0},{4,5},{5,6},{6,7},{7,4},{8,9},{9,10},{10,1... | collective-permute-start | bytes 3080 | tf_op jit(solution)/shard_map/ppermute | solution.py:21
  3.7 2.1 %collective-permute-start.24 = (s32[32,8]{0,1:T(8,128)}, s32[32,8]{0,1:T(8,128)S(1)}, u32[]{:S(2)}, u32[]{:S(2)}) collective-permute-start(s32[32,8]{0,1:T(8,128)} %param.8), channel_id=1, source_target_pairs={{0,3},{1,0},{2,1},{3,2},{4,7},{5,4},{6,5},{7,6},{8,11},{9,8},{10,9... | collective-permute-start | bytes 3080 | tf_op jit(solution)/shard_map/ppermute | solution.py:21
  6.8 1.6 collective-permute-start.7
  12.4 4.2 %collective-permute-start.47 = (bf16[16,768]{1,0:T(8,128)(2,1)S(1)}, bf16[16,768]{1,0:T(8,128)(2,1)S(1)}, u32[]{:S(2)}, u32[]{:S(2)}) collective-permute-start(bf16[16,768]{1,0:T(8,128)(2,1)S(1)} %get-tuple-element.35), channel_id=1, source_target_pairs={{0,15},{1,12},{2,13},{3,14},{4,11},{5,8},{6,9},{7,10},{8,7},{9,4},... | collective-permute-start | bytes 73736 | tf_op jit(solution)/shard_map/ppermute | solution.py:33
  16.7 1.5 collective-permute-start.45
  18.3 1.6 collective-permute-start.33
  22.7 1.5 collective-permute-start.34
  24.2 2.3 %collective-permute-done.34 = bf16[16,768]{1,0:T(8,128)(2,1)S(1)} collective-permute-done((bf16[16,768]{1,0:T(8,128)(2,1)S(1)}, bf16[16,768]{1,0:T(8,128)(2,1)S(1)}, u32[]{:S(2)}, u32[]{:S(2)}) %collective-permute-start.34) | collective-permute-done | bytes 24608 | tf_op jit(solution)/shard_map/ppermute | solution.py:33
  26.5 2.3 %collective-permute-start.35 = (bf16[16,768]{1,0:T(8,128)(2,1)S(1)}, bf16[16,768]{1,0:T(8,128)(2,1)S(1)}, u32[]{:S(2)}, u32[]{:S(2)}) collective-permute-start(bf16[16,768]{1,0:T(8,128)(2,1)S(1)} %get-tuple-element.47), channel_id=1, source_target_pairs={{0,12},{1,13},{2,14},{3,15},{4,8},{5,9},{6,10},{7,11},{8,4},{9,5},... | collective-permute-start | bytes 73736 | tf_op jit(solution)/shard_map/ppermute | solution.py:33
  28.8 2.5 %collective-permute-done.35 = bf16[16,768]{1,0:T(8,128)(2,1)S(1)} collective-permute-done((bf16[16,768]{1,0:T(8,128)(2,1)S(1)}, bf16[16,768]{1,0:T(8,128)(2,1)S(1)}, u32[]{:S(2)}, u32[]{:S(2)}) %collective-permute-start.35) | collective-permute-done | bytes 24608 | tf_op jit(solution)/shard_map/ppermute | solution.py:33
  31.6 5.3 %collective-permute-done.36 = bf16[16,768]{1,0:T(8,128)(2,1)S(1)} collective-permute-done((bf16[16,768]{1,0:T(8,128)(2,1)S(1)}, bf16[16,768]{1,0:T(8,128)(2,1)S(1)}, u32[]{:S(2)}, u32[]{:S(2)}) %collective-permute-start.36) | collective-permute-done | bytes 24608 | tf_op jit(solution)/shard_map/ppermute | solution.py:33
  36.9 6.5 %collective-permute-done.37 = bf16[16,768]{1,0:T(8,128)(2,1)S(1)} collective-permute-done((bf16[16,768]{1,0:T(8,128)(2,1)S(1)}, bf16[16,768]{1,0:T(8,128)(2,1)S(1)}, u32[]{:S(2)}, u32[]{:S(2)}) %collective-permute-start.37) | collective-permute-done | bytes 24608 | tf_op jit(solution)/shard_map/ppermute | solution.py:33
  43.4 6.5 %collective-permute-done.38 = bf16[16,768]{1,0:T(8,128)(2,1)S(1)} collective-permute-done((bf16[16,768]{1,0:T(8,128)(2,1)S(1)}, bf16[16,768]{1,0:T(8,128)(2,1)S(1)}, u32[]{:S(2)}, u32[]{:S(2)}) %collective-permute-start.38) | collective-permute-done | bytes 24608 | tf_op jit(solution)/shard_map/ppermute | solution.py:33
  49.9 7.4 %collective-permute-done.39 = bf16[16,768]{1,0:T(8,128)(2,1)S(1)} collective-permute-done((bf16[16,768]{1,0:T(8,128)(2,1)S(1)}, bf16[16,768]{1,0:T(8,128)(2,1)S(1)}, u32[]{:S(2)}, u32[]{:S(2)}) %collective-permute-start.39) | collective-permute-done | bytes 24608 | tf_op jit(solution)/shard_map/ppermute | solution.py:33
  57.4 4.7 %collective-permute-done.40 = bf16[16,768]{1,0:T(8,128)(2,1)S(1)} collective-permute-done((bf16[16,768]{1,0:T(8,128)(2,1)S(1)}, bf16[16,768]{1,0:T(8,128)(2,1)S(1)}, u32[]{:S(2)}, u32[]{:S(2)}) %collective-permute-start.40) | collective-permute-done | bytes 24608 | tf_op jit(solution)/shard_map/ppermute | solution.py:33
  62.8 4.9 %collective-permute-done.41 = bf16[16,768]{1,0:T(8,128)(2,1)S(1)} collective-permute-done((bf16[16,768]{1,0:T(8,128)(2,1)S(1)}, bf16[16,768]{1,0:T(8,128)(2,1)S(1)}, u32[]{:S(2)}, u32[]{:S(2)}) %collective-permute-start.41) | collective-permute-done | bytes 24608 | tf_op jit(solution)/shard_map/ppermute | solution.py:33
  68.7 4.9 %collective-permute-done.42 = bf16[16,768]{1,0:T(8,128)(2,1)S(1)} collective-permute-done((bf16[16,768]{1,0:T(8,128)(2,1)S(1)}, bf16[16,768]{1,0:T(8,128)(2,1)S(1)}, u32[]{:S(2)}, u32[]{:S(2)}) %collective-permute-start.42) | collective-permute-done | bytes 24608 | tf_op jit(solution)/shard_map/ppermute | solution.py:33
  73.7 1.9 %collective-permute-start.43 = (bf16[16,768]{1,0:T(8,128)(2,1)S(1)}, bf16[16,768]{1,0:T(8,128)(2,1)S(1)}, u32[]{:S(2)}, u32[]{:S(2)}) collective-permute-start(bf16[16,768]{1,0:T(8,128)(2,1)S(1)} %get-tuple-element.39), channel_id=1, source_target_pairs={{0,14},{1,15},{2,12},{3,13},{4,10},{5,11},{6,8},{7,9},{8,6},{9,7},... | collective-permute-start | bytes 73736 | tf_op jit(solution)/shard_map/ppermute | solution.py:33
  75.6 4.6 %collective-permute-done.43 = bf16[16,768]{1,0:T(8,128)(2,1)S(1)} collective-permute-done((bf16[16,768]{1,0:T(8,128)(2,1)S(1)}, bf16[16,768]{1,0:T(8,128)(2,1)S(1)}, u32[]{:S(2)}, u32[]{:S(2)}) %collective-permute-start.43) | collective-permute-done | bytes 24608 | tf_op jit(solution)/shard_map/ppermute | solution.py:33
  80.2 3.8 %collective-permute-done.44 = bf16[16,768]{1,0:T(8,128)(2,1)S(1)} collective-permute-done((bf16[16,768]{1,0:T(8,128)(2,1)S(1)}, bf16[16,768]{1,0:T(8,128)(2,1)S(1)}, u32[]{:S(2)}, u32[]{:S(2)}) %collective-permute-start.44) | collective-permute-done | bytes 24608 | tf_op jit(solution)/shard_map/ppermute | solution.py:33
  84.0 2.3 %collective-permute-start.2 = (bf16[16,4096]{1,0:T(8,128)(2,1)S(1)}, bf16[16,4096]{1,0:T(8,128)(2,1)S(1)}, u32[]{:S(2)}, u32[]{:S(2)}) collective-permute-start(bf16[16,4096]{1,0:T(8,128)(2,1)S(1)} %get-tuple-element.31), channel_id=1, source_target_pairs={{0,12},{4,8},{8,4},{12,0},{1,13},{5,9},{9,5},{13,1},{2,14},{6,10},... | collective-permute-start | bytes 393224 | tf_op jit(solution)/shard_map/ppermute | solution.py:28
  88.3 1.6 collective-permute-done.2
  91.8 5.0 %fusion.9 = bf16[64,768]{1,0:T(8,128)(2,1)S(1)} fusion(bf16[1,768,4096]{2,1,0:T(8,128)(2,1)} %param.9, bf16[16,4096]{1,0:T(8,128)(2,1)S(1)} %collective-permute-done.2, bf16[16,4096]{1,0:T(8,128)(2,1)S(1)} %collective-permute-done.1, bf16[16,4096]{1,0:T(8,128)(2,1)S(1)} %collective-permute-done, bf16[16,4096]{1,0:T(8,128)(2,1)S(1)} %get-tuple-element.34), kind=kOutput, calls=%fused_computation.18 | convolution fusion | flops 404799488 | bytes 6914048 | tf_op jit(solution)/shard_map/dot_general | solution.py:93
  96.8 1.7 collective-permute-start.5
  104.1 2.2 %collective-permute-start.10 = (bf16[16,4096]{1,0:T(8,128)(2,1)S(1)}, bf16[16,4096]{1,0:T(8,128)(2,1)S(1)}, u32[]{:S(2)}, u32[]{:S(2)}) collective-permute-start(bf16[16,4096]{1,0:T(8,128)(2,1)S(1)} %get-tuple-element.26), channel_id=1, source_target_pairs={{0,12},{4,8},{8,4},{12,0},{1,13},{5,9},{9,5},{13,1},{2,14},{6,10},... | collective-permute-start | bytes 393224 | tf_op jit(solution)/shard_map/ppermute | solution.py:28
  107.7 2.3 %collective-permute-done.10 = bf16[16,4096]{1,0:T(8,128)(2,1)S(1)} collective-permute-done((bf16[16,4096]{1,0:T(8,128)(2,1)S(1)}, bf16[16,4096]{1,0:T(8,128)(2,1)S(1)}, u32[]{:S(2)}, u32[]{:S(2)}) %collective-permute-start.10) | collective-permute-done | bytes 131104 | tf_op jit(solution)/shard_map/ppermute | solution.py:28
  111.6 2.0 %fusion.12 = bf16[64,768]{1,0:T(8,128)(2,1)S(1)} fusion(bf16[1,768,4096]{2,1,0:T(8,128)(2,1)S(1)} %bitcast.111, bf16[16,4096]{1,0:T(8,128)(2,1)S(1)} %collective-permute-done.10, bf16[16,4096]{1,0:T(8,128)(2,1)S(1)} %collective-permute-done.9, bf16[16,4096]{1,0:T(8,128)(2,1)S(1)} %collective-permute-done.8, bf16[16,4096]{1,0:T(8,128)(2,1)S(1)} %get-tuple-element.29), kind=kOutput, calls=%fused_computation.19 | convolution fusion | flops 404799488 | bytes 6914048 | tf_op jit(solution)/shard_map/dot_general | solution.py:93
  113.6 3.2 %collective-permute-start.14 = (bf16[16,768]{1,0:T(8,128)(2,1)S(1)}, bf16[16,768]{1,0:T(8,128)(2,1)S(1)}, u32[]{:S(2)}, u32[]{:S(2)}) collective-permute-start(bf16[16,768]{1,0:T(8,128)(2,1)S(1)} %get-tuple-element.58), channel_id=1, source_target_pairs={{0,15},{1,12},{2,13},{3,14},{4,11},{5,8},{6,9},{7,10},{8,7},{9,4},... | collective-permute-start | bytes 73736 | tf_op jit(solution)/shard_map/ppermute | solution.py:33
  121.1 2.6 %collective-permute-start.12 = (bf16[16,768]{1,0:T(8,128)(2,1)S(1)}, bf16[16,768]{1,0:T(8,128)(2,1)S(1)}, u32[]{:S(2)}, u32[]{:S(2)}) collective-permute-start(bf16[16,768]{1,0:T(8,128)(2,1)S(1)} %get-tuple-element.60), channel_id=1, source_target_pairs={{0,7},{1,4},{2,5},{3,6},{4,3},{5,0},{6,1},{7,2},{8,15},{9,12},{10,... | collective-permute-start | bytes 73736 | tf_op jit(solution)/shard_map/ppermute | solution.py:33
  123.8 2.2 %collective-permute-done.12 = bf16[16,768]{1,0:T(8,128)(2,1)S(1)} collective-permute-done((bf16[16,768]{1,0:T(8,128)(2,1)S(1)}, bf16[16,768]{1,0:T(8,128)(2,1)S(1)}, u32[]{:S(2)}, u32[]{:S(2)}) %collective-permute-start.12) | collective-permute-done | bytes 24608 | tf_op jit(solution)/shard_map/ppermute | solution.py:33
  127.8 2.2 %collective-permute-start.19 = (bf16[16,4096]{1,0:T(8,128)(2,1)S(1)}, bf16[16,4096]{1,0:T(8,128)(2,1)S(1)}, u32[]{:S(2)}, u32[]{:S(2)}) collective-permute-start(bf16[16,4096]{1,0:T(8,128)(2,1)S(1)} %get-tuple-element.21), channel_id=1, source_target_pairs={{0,12},{4,8},{8,4},{12,0},{1,13},{5,9},{9,5},{13,1},{2,14},{6,10},... | collective-permute-start | bytes 393224 | tf_op jit(solution)/shard_map/ppermute | solution.py:28
  130.5 1.8 collective-permute-start.25
  133.0 2.7 %collective-permute-done.18 = bf16[16,4096]{1,0:T(8,128)(2,1)S(1)} collective-permute-done((bf16[16,4096]{1,0:T(8,128)(2,1)S(1)}, bf16[16,4096]{1,0:T(8,128)(2,1)S(1)}, u32[]{:S(2)}, u32[]{:S(2)}) %collective-permute-start.18) | collective-permute-done | bytes 131104 | tf_op jit(solution)/shard_map/ppermute | solution.py:28
  137.0 2.0 %fusion.15 = bf16[64,768]{1,0:T(8,128)(2,1)S(1)} fusion(bf16[1,768,4096]{2,1,0:T(8,128)(2,1)S(1)} %bitcast.111, bf16[16,4096]{1,0:T(8,128)(2,1)S(1)} %collective-permute-done.19, bf16[16,4096]{1,0:T(8,128)(2,1)S(1)} %collective-permute-done.18, bf16[16,4096]{1,0:T(8,128)(2,1)S(1)} %collective-permute-done.17, bf16[16,4096]{1,0:T(8,128)(2,1)S(1)} %get-tuple-element.24), kind=kOutput, calls=%fused_computation.20 | convolution fusion | flops 404799488 | bytes 6914048 | tf_op jit(solution)/shard_map/dot_general | solution.py:93
  141.4 2.1 %collective-permute-start.23 = (bf16[16,768]{1,0:T(8,128)(2,1)S(1)}, bf16[16,768]{1,0:T(8,128)(2,1)S(1)}, u32[]{:S(2)}, u32[]{:S(2)}) collective-permute-start(bf16[16,768]{1,0:T(8,128)(2,1)S(1)} %get-tuple-element.54), channel_id=1, source_target_pairs={{0,14},{1,15},{2,12},{3,13},{4,10},{5,11},{6,8},{7,9},{8,6},{9,7},... | collective-permute-start | bytes 73736 | tf_op jit(solution)/shard_map/ppermute | solution.py:33
  143.6 2.3 %collective-permute-start.22 = (bf16[16,768]{1,0:T(8,128)(2,1)S(1)}, bf16[16,768]{1,0:T(8,128)(2,1)S(1)}, u32[]{:S(2)}, u32[]{:S(2)}) collective-permute-start(bf16[16,768]{1,0:T(8,128)(2,1)S(1)} %get-tuple-element.55), channel_id=1, source_target_pairs={{0,10},{1,11},{2,8},{3,9},{4,14},{5,15},{6,12},{7,13},{8,2},{9,3},... | collective-permute-start | bytes 73736 | tf_op jit(solution)/shard_map/ppermute | solution.py:33
  145.9 1.6 collective-permute-start.21
  149.2 3.3 %collective-permute-done.27 = bf16[16,4096]{1,0:T(8,128)(2,1)S(1)} collective-permute-done((bf16[16,4096]{1,0:T(8,128)(2,1)S(1)}, bf16[16,4096]{1,0:T(8,128)(2,1)S(1)}, u32[]{:S(2)}, u32[]{:S(2)}) %collective-permute-start.27) | collective-permute-done | bytes 131104 | tf_op jit(solution)/shard_map/ppermute | solution.py:28
  152.5 1.9 %collective-permute-start.28 = (bf16[16,4096]{1,0:T(8,128)(2,1)S(1)}, bf16[16,4096]{1,0:T(8,128)(2,1)S(1)}, u32[]{:S(2)}, u32[]{:S(2)}) collective-permute-start(bf16[16,4096]{1,0:T(8,128)(2,1)S(1)} %get-tuple-element.16), channel_id=1, source_target_pairs={{0,12},{4,8},{8,4},{12,0},{1,13},{5,9},{9,5},{13,1},{2,14},{6,10},... | collective-permute-start | bytes 393224 | tf_op jit(solution)/shard_map/ppermute | solution.py:28
  155.1 3.3 %collective-permute-done.28 = bf16[16,4096]{1,0:T(8,128)(2,1)S(1)} collective-permute-done((bf16[16,4096]{1,0:T(8,128)(2,1)S(1)}, bf16[16,4096]{1,0:T(8,128)(2,1)S(1)}, u32[]{:S(2)}, u32[]{:S(2)}) %collective-permute-start.28) | collective-permute-done | bytes 131104 | tf_op jit(solution)/shard_map/ppermute | solution.py:28
  158.3 1.9 %collective-permute-start.20 = (bf16[16,768]{1,0:T(8,128)(2,1)S(1)}, bf16[16,768]{1,0:T(8,128)(2,1)S(1)}, u32[]{:S(2)}, u32[]{:S(2)}) collective-permute-start(bf16[16,768]{1,0:T(8,128)(2,1)S(1)} %get-tuple-element.57), channel_id=1, source_target_pairs={{0,2},{1,3},{2,0},{3,1},{4,6},{5,7},{6,4},{7,5},{8,10},{9,11},{10,... | collective-permute-start | bytes 73736 | tf_op jit(solution)/shard_map/ppermute | solution.py:33
  160.9 2.2 %collective-permute-done.20 = bf16[16,768]{1,0:T(8,128)(2,1)S(1)} collective-permute-done((bf16[16,768]{1,0:T(8,128)(2,1)S(1)}, bf16[16,768]{1,0:T(8,128)(2,1)S(1)}, u32[]{:S(2)}, u32[]{:S(2)}) %collective-permute-start.20) | collective-permute-done | bytes 24608 | tf_op jit(solution)/shard_map/ppermute | solution.py:33
  163.1 2.0 %fusion.18 = bf16[64,768]{1,0:T(8,128)(2,1)S(1)} fusion(bf16[1,768,4096]{2,1,0:T(8,128)(2,1)S(1)} %bitcast.111, bf16[16,4096]{1,0:T(8,128)(2,1)S(1)} %collective-permute-done.28, bf16[16,4096]{1,0:T(8,128)(2,1)S(1)} %collective-permute-done.27, bf16[16,4096]{1,0:T(8,128)(2,1)S(1)} %collective-permute-done.26, bf16[16,4096]{1,0:T(8,128)(2,1)S(1)} %get-tuple-element.19), kind=kOutput, calls=%fused_computation.21 | convolution fusion | flops 404799488 | bytes 6914048 | tf_op jit(solution)/shard_map/dot_general | solution.py:93
  165.2 4.3 %collective-permute-start.32 = (bf16[16,768]{1,0:T(8,128)(2,1)S(1)}, bf16[16,768]{1,0:T(8,128)(2,1)S(1)}, u32[]{:S(2)}, u32[]{:S(2)}) collective-permute-start(bf16[16,768]{1,0:T(8,128)(2,1)S(1)} %get-tuple-element.50), channel_id=1, source_target_pairs={{0,13},{1,14},{2,15},{3,12},{4,9},{5,10},{6,11},{7,8},{8,5},{9,6},... | collective-permute-start | bytes 73736 | tf_op jit(solution)/shard_map/ppermute | solution.py:33
  170.6 2.6 %convolution_convert_fusion.1 = bf16[384,4096]{1,0:T(8,128)(2,1)S(1)} fusion(bf16[256,4096]{1,0:T(8,128)(2,1)} %constant_dynamic-update-slice_fusion.32, bf16[256,768]{1,0:T(8,128)(2,1)S(1)} %constant_dynamic-update-slice_fusion.16, s32[]{:T(128)S(6)} %select_n.37), kind=kOutput, calls=%fused_computation.10 | convolution fusion | flops 806879232 | bytes 5439492 | tf_op jit(solution)/shard_map/dot_general | solution.py:108
  173.2 2.3 %collective-permute-done.29 = bf16[16,768]{1,0:T(8,128)(2,1)S(1)} collective-permute-done((bf16[16,768]{1,0:T(8,128)(2,1)S(1)}, bf16[16,768]{1,0:T(8,128)(2,1)S(1)}, u32[]{:S(2)}, u32[]{:S(2)}) %collective-permute-start.29) | collective-permute-done | bytes 24608 | tf_op jit(solution)/shard_map/ppermute | solution.py:33
  175.5 6.5 %collective-permute-done.30 = bf16[16,768]{1,0:T(8,128)(2,1)S(1)} collective-permute-done((bf16[16,768]{1,0:T(8,128)(2,1)S(1)}, bf16[16,768]{1,0:T(8,128)(2,1)S(1)}, u32[]{:S(2)}, u32[]{:S(2)}) %collective-permute-start.30) | collective-permute-done | bytes 24608 | tf_op jit(solution)/shard_map/ppermute | solution.py:33
  183.8 4.4 %fusion.8 = bf16[1,384,4096]{2,1,0:T(8,128)(2,1)} fusion(bf16[256,384]{1,0:T(8,128)(2,1)} %collective-permute-done.48, bf16[256,4096]{1,0:T(8,128)(2,1)} %collective-permute-done.49, bf16[384,4096]{1,0:T(8,128)(2,1)S(1)} %convolution_convert_fusion.1), kind=kOutput, calls=%fused_computation.11 | convolution fusion | flops 813170688 | bytes 8585216 | tf_op jit(solution)/shard_map/dot_general | solution.py:111
  (157 shorter events, 39.3 us)
Async XLA Ops:
  0.6 16.1 %collective-permute-start.6 = (s32[32,8]{0,1:T(8,128)}, s32[32,8]{0,1:T(8,128)S(1)}, u32[]{:S(2)}, u32[]{:S(2)}) collective-permute-start(s32[32,8]{0,1:T(8,128)} %param.8), channel_id=1, source_target_pairs={{0,1},{1,2},{2,3},{3,0},{4,5},{5,6},{6,7},{7,4},{8,9},{9,10},{10,1... | collective-permute-start | bytes 3080 | tf_op jit(solution)/shard_map/ppermute | solution.py:21
  3.7 13.0 %collective-permute-start.24 = (s32[32,8]{0,1:T(8,128)}, s32[32,8]{0,1:T(8,128)S(1)}, u32[]{:S(2)}, u32[]{:S(2)}) collective-permute-start(s32[32,8]{0,1:T(8,128)} %param.8), channel_id=1, source_target_pairs={{0,3},{1,0},{2,1},{3,2},{4,7},{5,4},{6,5},{7,6},{8,11},{9,8},{10,9... | collective-permute-start | bytes 3080 | tf_op jit(solution)/shard_map/ppermute | solution.py:21
  5.8 12.4 %collective-permute-start.15 = (s32[32,8]{0,1:T(8,128)}, s32[32,8]{0,1:T(8,128)S(1)}, u32[]{:S(2)}, u32[]{:S(2)}) collective-permute-start(s32[32,8]{0,1:T(8,128)} %param.8), channel_id=1, source_target_pairs={{0,2},{1,3},{2,0},{3,1},{4,6},{5,7},{6,4},{7,5},{8,10},{9,11},{10,... | collective-permute-start | bytes 3080 | tf_op jit(solution)/shard_map/ppermute | solution.py:21
  6.8 96.4 %collective-permute-start.7 = (bf16[32,4096]{1,0:T(8,128)(2,1)}, bf16[32,4096]{1,0:T(8,128)(2,1)S(1)}, u32[]{:S(2)}, u32[]{:S(2)}) collective-permute-start(bf16[32,4096]{1,0:T(8,128)(2,1)} %param.5), channel_id=1, source_target_pairs={{0,1},{1,2},{2,3},{3,0},{4,5},{5,6},{6,7},{7,4},{8,9},{9,10},{10,1... | collective-permute-start | bytes 786440 | tf_op jit(solution)/shard_map/ppermute | solution.py:21
  12.4 75.1 %collective-permute-start.47 = (bf16[16,768]{1,0:T(8,128)(2,1)S(1)}, bf16[16,768]{1,0:T(8,128)(2,1)S(1)}, u32[]{:S(2)}, u32[]{:S(2)}) collective-permute-start(bf16[16,768]{1,0:T(8,128)(2,1)S(1)} %get-tuple-element.35), channel_id=1, source_target_pairs={{0,15},{1,12},{2,13},{3,14},{4,11},{5,8},{6,9},{7,10},{8,7},{9,4},... | collective-permute-start | bytes 73736 | tf_op jit(solution)/shard_map/ppermute | solution.py:33
  16.7 70.1 %collective-permute-start.46 = (bf16[16,768]{1,0:T(8,128)(2,1)S(1)}, bf16[16,768]{1,0:T(8,128)(2,1)S(1)}, u32[]{:S(2)}, u32[]{:S(2)}) collective-permute-start(bf16[16,768]{1,0:T(8,128)(2,1)S(1)} %get-tuple-element.36), channel_id=1, source_target_pairs={{0,11},{1,8},{2,9},{3,10},{4,15},{5,12},{6,13},{7,14},{8,3},{9,0},... | collective-permute-start | bytes 73736 | tf_op jit(solution)/shard_map/ppermute | solution.py:33
  16.7 69.7 %collective-permute-start.45 = (bf16[16,768]{1,0:T(8,128)(2,1)S(1)}, bf16[16,768]{1,0:T(8,128)(2,1)S(1)}, u32[]{:S(2)}, u32[]{:S(2)}) collective-permute-start(bf16[16,768]{1,0:T(8,128)(2,1)S(1)} %get-tuple-element.37), channel_id=1, source_target_pairs={{0,7},{1,4},{2,5},{3,6},{4,3},{5,0},{6,1},{7,2},{8,15},{9,12},{10,... | collective-permute-start | bytes 73736 | tf_op jit(solution)/shard_map/ppermute | solution.py:33
  18.3 4.4 %collective-permute-start.33 = (bf16[16,768]{1,0:T(8,128)(2,1)S(1)}, bf16[16,768]{1,0:T(8,128)(2,1)S(1)}, u32[]{:S(2)}, u32[]{:S(2)}) collective-permute-start(bf16[16,768]{1,0:T(8,128)(2,1)S(1)} %get-tuple-element.49), channel_id=1, source_target_pairs={{0,4},{1,5},{2,6},{3,7},{4,0},{5,1},{6,2},{7,3},{8,12},{9,13},{10,... | collective-permute-start | bytes 73736 | tf_op jit(solution)/shard_map/ppermute | solution.py:33
  22.7 3.8 %collective-permute-start.34 = (bf16[16,768]{1,0:T(8,128)(2,1)S(1)}, bf16[16,768]{1,0:T(8,128)(2,1)S(1)}, u32[]{:S(2)}, u32[]{:S(2)}) collective-permute-start(bf16[16,768]{1,0:T(8,128)(2,1)S(1)} %get-tuple-element.48), channel_id=1, source_target_pairs={{0,8},{1,9},{2,10},{3,11},{4,12},{5,13},{6,14},{7,15},{8,0},{9,1},... | collective-permute-start | bytes 73736 | tf_op jit(solution)/shard_map/ppermute | solution.py:33
  26.5 4.7 %collective-permute-start.35 = (bf16[16,768]{1,0:T(8,128)(2,1)S(1)}, bf16[16,768]{1,0:T(8,128)(2,1)S(1)}, u32[]{:S(2)}, u32[]{:S(2)}) collective-permute-start(bf16[16,768]{1,0:T(8,128)(2,1)S(1)} %get-tuple-element.47), channel_id=1, source_target_pairs={{0,12},{1,13},{2,14},{3,15},{4,8},{5,9},{6,10},{7,11},{8,4},{9,5},... | collective-permute-start | bytes 73736 | tf_op jit(solution)/shard_map/ppermute | solution.py:33
  31.2 5.6 %collective-permute-start.36 = (bf16[16,768]{1,0:T(8,128)(2,1)S(1)}, bf16[16,768]{1,0:T(8,128)(2,1)S(1)}, u32[]{:S(2)}, u32[]{:S(2)}) collective-permute-start(bf16[16,768]{1,0:T(8,128)(2,1)S(1)} %get-tuple-element.46), channel_id=1, source_target_pairs={{0,1},{1,2},{2,3},{3,0},{4,5},{5,6},{6,7},{7,4},{8,9},{9,10},{10,1... | collective-permute-start | bytes 73736 | tf_op jit(solution)/shard_map/ppermute | solution.py:33
  36.9 6.5 %collective-permute-start.37 = (bf16[16,768]{1,0:T(8,128)(2,1)S(1)}, bf16[16,768]{1,0:T(8,128)(2,1)S(1)}, u32[]{:S(2)}, u32[]{:S(2)}) collective-permute-start(bf16[16,768]{1,0:T(8,128)(2,1)S(1)} %get-tuple-element.45), channel_id=1, source_target_pairs={{0,5},{1,6},{2,7},{3,4},{4,1},{5,2},{6,3},{7,0},{8,13},{9,14},{10,... | collective-permute-start | bytes 73736 | tf_op jit(solution)/shard_map/ppermute | solution.py:33
  43.4 6.5 %collective-permute-start.38 = (bf16[16,768]{1,0:T(8,128)(2,1)S(1)}, bf16[16,768]{1,0:T(8,128)(2,1)S(1)}, u32[]{:S(2)}, u32[]{:S(2)}) collective-permute-start(bf16[16,768]{1,0:T(8,128)(2,1)S(1)} %get-tuple-element.44), channel_id=1, source_target_pairs={{0,9},{1,10},{2,11},{3,8},{4,13},{5,14},{6,15},{7,12},{8,1},{9,2},... | collective-permute-start | bytes 73736 | tf_op jit(solution)/shard_map/ppermute | solution.py:33
  49.9 7.5 %collective-permute-start.39 = (bf16[16,768]{1,0:T(8,128)(2,1)S(1)}, bf16[16,768]{1,0:T(8,128)(2,1)S(1)}, u32[]{:S(2)}, u32[]{:S(2)}) collective-permute-start(bf16[16,768]{1,0:T(8,128)(2,1)S(1)} %get-tuple-element.43), channel_id=1, source_target_pairs={{0,13},{1,14},{2,15},{3,12},{4,9},{5,10},{6,11},{7,8},{8,5},{9,6},... | collective-permute-start | bytes 73736 | tf_op jit(solution)/shard_map/ppermute | solution.py:33
  57.4 4.7 %collective-permute-start.40 = (bf16[16,768]{1,0:T(8,128)(2,1)S(1)}, bf16[16,768]{1,0:T(8,128)(2,1)S(1)}, u32[]{:S(2)}, u32[]{:S(2)}) collective-permute-start(bf16[16,768]{1,0:T(8,128)(2,1)S(1)} %get-tuple-element.42), channel_id=1, source_target_pairs={{0,2},{1,3},{2,0},{3,1},{4,6},{5,7},{6,4},{7,5},{8,10},{9,11},{10,... | collective-permute-start | bytes 73736 | tf_op jit(solution)/shard_map/ppermute | solution.py:33
  62.1 5.6 %collective-permute-start.41 = (bf16[16,768]{1,0:T(8,128)(2,1)S(1)}, bf16[16,768]{1,0:T(8,128)(2,1)S(1)}, u32[]{:S(2)}, u32[]{:S(2)}) collective-permute-start(bf16[16,768]{1,0:T(8,128)(2,1)S(1)} %get-tuple-element.41), channel_id=1, source_target_pairs={{0,6},{1,7},{2,4},{3,5},{4,2},{5,3},{6,0},{7,1},{8,14},{9,15},{10,... | collective-permute-start | bytes 73736 | tf_op jit(solution)/shard_map/ppermute | solution.py:33
  67.7 6.0 %collective-permute-start.42 = (bf16[16,768]{1,0:T(8,128)(2,1)S(1)}, bf16[16,768]{1,0:T(8,128)(2,1)S(1)}, u32[]{:S(2)}, u32[]{:S(2)}) collective-permute-start(bf16[16,768]{1,0:T(8,128)(2,1)S(1)} %get-tuple-element.40), channel_id=1, source_target_pairs={{0,10},{1,11},{2,8},{3,9},{4,14},{5,15},{6,12},{7,13},{8,2},{9,3},... | collective-permute-start | bytes 73736 | tf_op jit(solution)/shard_map/ppermute | solution.py:33
  73.7 6.5 %collective-permute-start.43 = (bf16[16,768]{1,0:T(8,128)(2,1)S(1)}, bf16[16,768]{1,0:T(8,128)(2,1)S(1)}, u32[]{:S(2)}, u32[]{:S(2)}) collective-permute-start(bf16[16,768]{1,0:T(8,128)(2,1)S(1)} %get-tuple-element.39), channel_id=1, source_target_pairs={{0,14},{1,15},{2,12},{3,13},{4,10},{5,11},{6,8},{7,9},{8,6},{9,7},... | collective-permute-start | bytes 73736 | tf_op jit(solution)/shard_map/ppermute | solution.py:33
  84.0 5.9 %collective-permute-start.2 = (bf16[16,4096]{1,0:T(8,128)(2,1)S(1)}, bf16[16,4096]{1,0:T(8,128)(2,1)S(1)}, u32[]{:S(2)}, u32[]{:S(2)}) collective-permute-start(bf16[16,4096]{1,0:T(8,128)(2,1)S(1)} %get-tuple-element.31), channel_id=1, source_target_pairs={{0,12},{4,8},{8,4},{12,0},{1,13},{5,9},{9,5},{13,1},{2,14},{6,10},... | collective-permute-start | bytes 393224 | tf_op jit(solution)/shard_map/ppermute | solution.py:28
  86.4 5.0 %collective-permute-start.1 = (bf16[16,4096]{1,0:T(8,128)(2,1)S(1)}, bf16[16,4096]{1,0:T(8,128)(2,1)S(1)}, u32[]{:S(2)}, u32[]{:S(2)}) collective-permute-start(bf16[16,4096]{1,0:T(8,128)(2,1)S(1)} %get-tuple-element.32), channel_id=1, source_target_pairs={{0,8},{4,12},{8,0},{12,4},{1,9},{5,13},{9,1},{13,5},{2,10},{6,14},... | collective-permute-start | bytes 393224 | tf_op jit(solution)/shard_map/ppermute | solution.py:28
  86.8 5.0 %collective-permute-start = (bf16[16,4096]{1,0:T(8,128)(2,1)S(1)}, bf16[16,4096]{1,0:T(8,128)(2,1)S(1)}, u32[]{:S(2)}, u32[]{:S(2)}) collective-permute-start(bf16[16,4096]{1,0:T(8,128)(2,1)S(1)} %get-tuple-element.33), channel_id=1, source_target_pairs={{0,4},{4,0},{8,12},{12,8},{1,5},{5,1},{9,13},{13,9},{2,6},{6,2},{1... | collective-permute-start | bytes 393224 | tf_op jit(solution)/shard_map/ppermute | solution.py:28
  88.2 95.5 %collective-permute-start.48 = (bf16[256,384]{1,0:T(8,128)(2,1)}, bf16[256,384]{1,0:T(8,128)(2,1)}, u32[]{:S(2)}, u32[]{:S(2)}) collective-permute-start(bf16[256,384]{1,0:T(8,128)(2,1)} %constant_dynamic-slice_fusion), channel_id=1, source_target_pairs={{0,16},{16,0},{1,17},{17,1},{2,18},{18,2},{3,19},{19,3},{4,20},{20... | collective-permute-start | bytes 589832 | tf_op jit(solution)/shard_map/ppermute | solution.py:106
  96.8 10.9 %collective-permute-start.5 = (bf16[16,768]{1,0:T(8,128)(2,1)S(1)}, bf16[16,768]{1,0:T(8,128)(2,1)S(1)}, u32[]{:S(2)}, u32[]{:S(2)}) collective-permute-start(bf16[16,768]{1,0:T(8,128)(2,1)S(1)} %get-tuple-element.62), channel_id=1, source_target_pairs={{0,12},{1,13},{2,14},{3,15},{4,8},{5,9},{6,10},{7,11},{8,4},{9,5},... | collective-permute-start | bytes 73736 | tf_op jit(solution)/shard_map/ppermute | solution.py:33
  98.5 8.1 %collective-permute-start.4 = (bf16[16,768]{1,0:T(8,128)(2,1)S(1)}, bf16[16,768]{1,0:T(8,128)(2,1)S(1)}, u32[]{:S(2)}, u32[]{:S(2)}) collective-permute-start(bf16[16,768]{1,0:T(8,128)(2,1)S(1)} %get-tuple-element.63), channel_id=1, source_target_pairs={{0,8},{1,9},{2,10},{3,11},{4,12},{5,13},{6,14},{7,15},{8,0},{9,1},... | collective-permute-start | bytes 73736 | tf_op jit(solution)/shard_map/ppermute | solution.py:33
  104.1 5.9 %collective-permute-start.10 = (bf16[16,4096]{1,0:T(8,128)(2,1)S(1)}, bf16[16,4096]{1,0:T(8,128)(2,1)S(1)}, u32[]{:S(2)}, u32[]{:S(2)}) collective-permute-start(bf16[16,4096]{1,0:T(8,128)(2,1)S(1)} %get-tuple-element.26), channel_id=1, source_target_pairs={{0,12},{4,8},{8,4},{12,0},{1,13},{5,9},{9,5},{13,1},{2,14},{6,10},... | collective-permute-start | bytes 393224 | tf_op jit(solution)/shard_map/ppermute | solution.py:28
  106.4 5.0 %collective-permute-start.9 = (bf16[16,4096]{1,0:T(8,128)(2,1)S(1)}, bf16[16,4096]{1,0:T(8,128)(2,1)S(1)}, u32[]{:S(2)}, u32[]{:S(2)}) collective-permute-start(bf16[16,4096]{1,0:T(8,128)(2,1)S(1)} %get-tuple-element.27), channel_id=1, source_target_pairs={{0,8},{4,12},{8,0},{12,4},{1,9},{5,13},{9,1},{13,5},{2,10},{6,14},... | collective-permute-start | bytes 393224 | tf_op jit(solution)/shard_map/ppermute | solution.py:28
  106.6 5.0 %collective-permute-start.8 = (bf16[16,4096]{1,0:T(8,128)(2,1)S(1)}, bf16[16,4096]{1,0:T(8,128)(2,1)S(1)}, u32[]{:S(2)}, u32[]{:S(2)}) collective-permute-start(bf16[16,4096]{1,0:T(8,128)(2,1)S(1)} %get-tuple-element.28), channel_id=1, source_target_pairs={{0,4},{4,0},{8,12},{12,8},{1,5},{5,1},{9,13},{13,9},{2,6},{6,2},{1... | collective-permute-start | bytes 393224 | tf_op jit(solution)/shard_map/ppermute | solution.py:28
  107.6 18.3 %collective-permute-start.16 = (bf16[32,4096]{1,0:T(8,128)(2,1)S(1)}, bf16[32,4096]{1,0:T(8,128)(2,1)S(1)}, u32[]{:S(2)}, u32[]{:S(2)}) collective-permute-start(bf16[32,4096]{1,0:T(8,128)(2,1)S(1)} %collective-permute-done.7), channel_id=1, source_target_pairs={{0,1},{1,2},{2,3},{3,0},{4,5},{5,6},{6,7},{7,4},{8,9},{9,10},{10,1... | collective-permute-start | bytes 786440 | tf_op jit(solution)/shard_map/ppermute | solution.py:21
  113.6 14.1 %collective-permute-start.14 = (bf16[16,768]{1,0:T(8,128)(2,1)S(1)}, bf16[16,768]{1,0:T(8,128)(2,1)S(1)}, u32[]{:S(2)}, u32[]{:S(2)}) collective-permute-start(bf16[16,768]{1,0:T(8,128)(2,1)S(1)} %get-tuple-element.58), channel_id=1, source_target_pairs={{0,15},{1,12},{2,13},{3,14},{4,11},{5,8},{6,9},{7,10},{8,7},{9,4},... | collective-permute-start | bytes 73736 | tf_op jit(solution)/shard_map/ppermute | solution.py:33
  116.8 10.9 %collective-permute-start.13 = (bf16[16,768]{1,0:T(8,128)(2,1)S(1)}, bf16[16,768]{1,0:T(8,128)(2,1)S(1)}, u32[]{:S(2)}, u32[]{:S(2)}) collective-permute-start(bf16[16,768]{1,0:T(8,128)(2,1)S(1)} %get-tuple-element.59), channel_id=1, source_target_pairs={{0,11},{1,8},{2,9},{3,10},{4,15},{5,12},{6,13},{7,14},{8,3},{9,0},... | collective-permute-start | bytes 73736 | tf_op jit(solution)/shard_map/ppermute | solution.py:33
  116.9 4.3 %collective-permute-start.11 = (bf16[16,768]{1,0:T(8,128)(2,1)S(1)}, bf16[16,768]{1,0:T(8,128)(2,1)S(1)}, u32[]{:S(2)}, u32[]{:S(2)}) collective-permute-start(bf16[16,768]{1,0:T(8,128)(2,1)S(1)} %get-tuple-element.61), channel_id=1, source_target_pairs={{0,3},{1,0},{2,1},{3,2},{4,7},{5,4},{6,5},{7,6},{8,11},{9,8},{10,9... | collective-permute-start | bytes 73736 | tf_op jit(solution)/shard_map/ppermute | solution.py:33
  121.1 4.8 %collective-permute-start.12 = (bf16[16,768]{1,0:T(8,128)(2,1)S(1)}, bf16[16,768]{1,0:T(8,128)(2,1)S(1)}, u32[]{:S(2)}, u32[]{:S(2)}) collective-permute-start(bf16[16,768]{1,0:T(8,128)(2,1)S(1)} %get-tuple-element.60), channel_id=1, source_target_pairs={{0,7},{1,4},{2,5},{3,6},{4,3},{5,0},{6,1},{7,2},{8,15},{9,12},{10,... | collective-permute-start | bytes 73736 | tf_op jit(solution)/shard_map/ppermute | solution.py:33
  127.0 5.4 %collective-permute-start.17 = (bf16[16,4096]{1,0:T(8,128)(2,1)S(1)}, bf16[16,4096]{1,0:T(8,128)(2,1)S(1)}, u32[]{:S(2)}, u32[]{:S(2)}) collective-permute-start(bf16[16,4096]{1,0:T(8,128)(2,1)S(1)} %get-tuple-element.23), channel_id=1, source_target_pairs={{0,4},{4,0},{8,12},{12,8},{1,5},{5,1},{9,13},{13,9},{2,6},{6,2},{1... | collective-permute-start | bytes 393224 | tf_op jit(solution)/shard_map/ppermute | solution.py:28
  127.8 8.5 %collective-permute-start.19 = (bf16[16,4096]{1,0:T(8,128)(2,1)S(1)}, bf16[16,4096]{1,0:T(8,128)(2,1)S(1)}, u32[]{:S(2)}, u32[]{:S(2)}) collective-permute-start(bf16[16,4096]{1,0:T(8,128)(2,1)S(1)} %get-tuple-element.21), channel_id=1, source_target_pairs={{0,12},{4,8},{8,4},{12,0},{1,13},{5,9},{9,5},{13,1},{2,14},{6,10},... | collective-permute-start | bytes 393224 | tf_op jit(solution)/shard_map/ppermute | solution.py:28
  130.0 5.7 %collective-permute-start.18 = (bf16[16,4096]{1,0:T(8,128)(2,1)S(1)}, bf16[16,4096]{1,0:T(8,128)(2,1)S(1)}, u32[]{:S(2)}, u32[]{:S(2)}) collective-permute-start(bf16[16,4096]{1,0:T(8,128)(2,1)S(1)} %get-tuple-element.22), channel_id=1, source_target_pairs={{0,8},{4,12},{8,0},{12,4},{1,9},{5,13},{9,1},{13,5},{2,10},{6,14},... | collective-permute-start | bytes 393224 | tf_op jit(solution)/shard_map/ppermute | solution.py:28
  130.5 9.0 %collective-permute-start.25 = (bf16[32,4096]{1,0:T(8,128)(2,1)S(1)}, bf16[32,4096]{1,0:T(8,128)(2,1)S(1)}, u32[]{:S(2)}, u32[]{:S(2)}) collective-permute-start(bf16[32,4096]{1,0:T(8,128)(2,1)S(1)} %collective-permute-done.16), channel_id=1, source_target_pairs={{0,1},{1,2},{2,3},{3,0},{4,5},{5,6},{6,7},{7,4},{8,9},{9,10},{10,1... | collective-permute-start | bytes 786440 | tf_op jit(solution)/shard_map/ppermute | solution.py:21
  140.5 7.0 %collective-permute-start.26 = (bf16[16,4096]{1,0:T(8,128)(2,1)S(1)}, bf16[16,4096]{1,0:T(8,128)(2,1)S(1)}, u32[]{:S(2)}, u32[]{:S(2)}) collective-permute-start(bf16[16,4096]{1,0:T(8,128)(2,1)S(1)} %get-tuple-element.18), channel_id=1, source_target_pairs={{0,4},{4,0},{8,12},{12,8},{1,5},{5,1},{9,13},{13,9},{2,6},{6,2},{1... | collective-permute-start | bytes 393224 | tf_op jit(solution)/shard_map/ppermute | solution.py:28
  141.4 21.7 %collective-permute-start.23 = (bf16[16,768]{1,0:T(8,128)(2,1)S(1)}, bf16[16,768]{1,0:T(8,128)(2,1)S(1)}, u32[]{:S(2)}, u32[]{:S(2)}) collective-permute-start(bf16[16,768]{1,0:T(8,128)(2,1)S(1)} %get-tuple-element.54), channel_id=1, source_target_pairs={{0,14},{1,15},{2,12},{3,13},{4,10},{5,11},{6,8},{7,9},{8,6},{9,7},... | collective-permute-start | bytes 73736 | tf_op jit(solution)/shard_map/ppermute | solution.py:33
  143.6 19.5 %collective-permute-start.22 = (bf16[16,768]{1,0:T(8,128)(2,1)S(1)}, bf16[16,768]{1,0:T(8,128)(2,1)S(1)}, u32[]{:S(2)}, u32[]{:S(2)}) collective-permute-start(bf16[16,768]{1,0:T(8,128)(2,1)S(1)} %get-tuple-element.55), channel_id=1, source_target_pairs={{0,10},{1,11},{2,8},{3,9},{4,14},{5,15},{6,12},{7,13},{8,2},{9,3},... | collective-permute-start | bytes 73736 | tf_op jit(solution)/shard_map/ppermute | solution.py:33
  145.9 17.2 %collective-permute-start.21 = (bf16[16,768]{1,0:T(8,128)(2,1)S(1)}, bf16[16,768]{1,0:T(8,128)(2,1)S(1)}, u32[]{:S(2)}, u32[]{:S(2)}) collective-permute-start(bf16[16,768]{1,0:T(8,128)(2,1)S(1)} %get-tuple-element.56), channel_id=1, source_target_pairs={{0,6},{1,7},{2,4},{3,5},{4,2},{5,3},{6,0},{7,1},{8,14},{9,15},{10,... | collective-permute-start | bytes 73736 | tf_op jit(solution)/shard_map/ppermute | solution.py:33
  147.5 5.0 %collective-permute-start.27 = (bf16[16,4096]{1,0:T(8,128)(2,1)S(1)}, bf16[16,4096]{1,0:T(8,128)(2,1)S(1)}, u32[]{:S(2)}, u32[]{:S(2)}) collective-permute-start(bf16[16,4096]{1,0:T(8,128)(2,1)S(1)} %get-tuple-element.17), channel_id=1, source_target_pairs={{0,8},{4,12},{8,0},{12,4},{1,9},{5,13},{9,1},{13,5},{2,10},{6,14},... | collective-permute-start | bytes 393224 | tf_op jit(solution)/shard_map/ppermute | solution.py:28
  152.5 5.9 %collective-permute-start.28 = (bf16[16,4096]{1,0:T(8,128)(2,1)S(1)}, bf16[16,4096]{1,0:T(8,128)(2,1)S(1)}, u32[]{:S(2)}, u32[]{:S(2)}) collective-permute-start(bf16[16,4096]{1,0:T(8,128)(2,1)S(1)} %get-tuple-element.16), channel_id=1, source_target_pairs={{0,12},{4,8},{8,4},{12,0},{1,13},{5,9},{9,5},{13,1},{2,14},{6,10},... | collective-permute-start | bytes 393224 | tf_op jit(solution)/shard_map/ppermute | solution.py:28
  158.3 4.7 %collective-permute-start.20 = (bf16[16,768]{1,0:T(8,128)(2,1)S(1)}, bf16[16,768]{1,0:T(8,128)(2,1)S(1)}, u32[]{:S(2)}, u32[]{:S(2)}) collective-permute-start(bf16[16,768]{1,0:T(8,128)(2,1)S(1)} %get-tuple-element.57), channel_id=1, source_target_pairs={{0,2},{1,3},{2,0},{3,1},{4,6},{5,7},{6,4},{7,5},{8,10},{9,11},{10,... | collective-permute-start | bytes 73736 | tf_op jit(solution)/shard_map/ppermute | solution.py:33
  163.1 20.7 %collective-permute-start.49 = (bf16[256,4096]{1,0:T(8,128)(2,1)}, bf16[256,4096]{1,0:T(8,128)(2,1)}, u32[]{:S(2)}, u32[]{:S(2)}) collective-permute-start(bf16[256,4096]{1,0:T(8,128)(2,1)} %constant_dynamic-update-slice_fusion.32), channel_id=1, source_target_pairs={{0,16},{16,0},{1,17},{17,1},{2,18},{18,2},{3,19},{19,3},{4,20},{20... | collective-permute-start | bytes 6291464 | tf_op jit(solution)/shard_map/ppermute | solution.py:105
  165.2 16.8 %collective-permute-start.32 = (bf16[16,768]{1,0:T(8,128)(2,1)S(1)}, bf16[16,768]{1,0:T(8,128)(2,1)S(1)}, u32[]{:S(2)}, u32[]{:S(2)}) collective-permute-start(bf16[16,768]{1,0:T(8,128)(2,1)S(1)} %get-tuple-element.50), channel_id=1, source_target_pairs={{0,13},{1,14},{2,15},{3,12},{4,9},{5,10},{6,11},{7,8},{8,5},{9,6},... | collective-permute-start | bytes 73736 | tf_op jit(solution)/shard_map/ppermute | solution.py:33
  169.4 12.6 %collective-permute-start.31 = (bf16[16,768]{1,0:T(8,128)(2,1)S(1)}, bf16[16,768]{1,0:T(8,128)(2,1)S(1)}, u32[]{:S(2)}, u32[]{:S(2)}) collective-permute-start(bf16[16,768]{1,0:T(8,128)(2,1)S(1)} %get-tuple-element.51), channel_id=1, source_target_pairs={{0,9},{1,10},{2,11},{3,8},{4,13},{5,14},{6,15},{7,12},{8,1},{9,2},... | collective-permute-start | bytes 73736 | tf_op jit(solution)/shard_map/ppermute | solution.py:33
  169.4 6.0 %collective-permute-start.29 = (bf16[16,768]{1,0:T(8,128)(2,1)S(1)}, bf16[16,768]{1,0:T(8,128)(2,1)S(1)}, u32[]{:S(2)}, u32[]{:S(2)}) collective-permute-start(bf16[16,768]{1,0:T(8,128)(2,1)S(1)} %get-tuple-element.53), channel_id=1, source_target_pairs={{0,1},{1,2},{2,3},{3,0},{4,5},{5,6},{6,7},{7,4},{8,9},{9,10},{10,1... | collective-permute-start | bytes 73736 | tf_op jit(solution)/shard_map/ppermute | solution.py:33
  175.5 6.5 %collective-permute-start.30 = (bf16[16,768]{1,0:T(8,128)(2,1)S(1)}, bf16[16,768]{1,0:T(8,128)(2,1)S(1)}, u32[]{:S(2)}, u32[]{:S(2)}) collective-permute-start(bf16[16,768]{1,0:T(8,128)(2,1)S(1)} %get-tuple-element.52), channel_id=1, source_target_pairs={{0,5},{1,6},{2,7},{3,4},{4,1},{5,2},{6,3},{7,0},{8,13},{9,14},{10,... | collective-permute-start | bytes 73736 | tf_op jit(solution)/shard_map/ppermute | solution.py:33
  (8 other events, 164.7 us)

commit v3 on v1

v3 whole, which is shorter than its diff:
```python
import jax
import jax.numpy as jnp
from jax import lax
from jax.sharding import PartitionSpec as P

PARTS = 2
ID_COLS = 128


def swap(array):
    return lax.ppermute(array, "dp", [(i, i ^ 1) for i in range(lax.axis_size("dp"))])


def local(grad_out, hidden, gates, expert_ids, w_down):
    tok_local, top_count = expert_ids.shape
    far_count = lax.axis_size("far")
    near_count = lax.axis_size("near")
    experts = far_count * near_count
    capacity = max(4, (tok_local * top_count + experts - 1) // experts)
    width = grad_out.shape[1]
    part = width // PARTS
    hidden_width = hidden.shape[2]
    row_total = tok_local * top_count
    slot_total = experts * capacity
    near = lax.axis_index("near")

    id_cols = jnp.pad(expert_ids.astype(jnp.bfloat16), ((0, 0), (0, ID_COLS - top_count)))
    pieces = [grad_out[:, i * part : (i + 1) * part] for i in range(PARTS)]
    pieces[0] = jnp.concatenate([pieces[0], id_cols], axis=1)
    lines = [lax.all_gather(piece, "near", axis=0, tiled=True) for piece in pieces]

    flat_ids = expert_ids.reshape(-1)
    one_hot = (flat_ids[:, None] == jnp.arange(experts, dtype=jnp.int32)[None, :]).astype(jnp.int32)
    ranks = jnp.sum(jnp.cumsum(one_hot, axis=0) * one_hot, axis=1) - 1
    slots = flat_ids * capacity + ranks
    place = (jnp.arange(slot_total, dtype=jnp.int32)[:, None] == slots[None, :]).astype(jnp.bfloat16)
    scaled = (
        (gates[:, :, None] * hidden.astype(jnp.float32))
        .astype(jnp.bfloat16)
        .reshape(row_total, hidden_width)
    )
    send_hid = jnp.dot(place, scaled, preferred_element_type=jnp.float32).astype(jnp.bfloat16)

    line_ids = lines[0][:, part : part + top_count].astype(jnp.int32)
    plane = jnp.arange(far_count, dtype=jnp.int32) * near_count + near
    named = jnp.any(line_ids[None] == plane[:, None, None], axis=2).reshape(
        far_count, near_count, tok_local
    )
    rank = jnp.cumsum(named.astype(jnp.int32), axis=2) - 1
    slot = jnp.where(
        named, rank + jnp.arange(near_count, dtype=jnp.int32)[None, :, None] * capacity, -1
    ).reshape(far_count, 1, near_count * tok_local)
    pick = (
        (jnp.arange(near_count * capacity, dtype=jnp.int32)[None, :, None] == slot)
        .astype(jnp.bfloat16)
        .reshape(slot_total, near_count * tok_local)
    )

    weight = w_down[0]
    recv_out = []
    returned = jnp.zeros((slot_total, hidden_width), jnp.float32)
    for i, line in enumerate(lines):
        picked = jnp.dot(pick, line[:, :part], preferred_element_type=jnp.float32).astype(jnp.bfloat16)
        if i == PARTS - 1:
            picked, send_hid = lax.optimization_barrier((picked, send_hid))
        rows = lax.all_to_all(
            picked.reshape(far_count, near_count * capacity, part),
            "far",
            split_axis=0,
            concat_axis=0,
            tiled=True,
        ).reshape(slot_total, part)
        recv_out.append(rows)
        returned = returned + lax.dot_general(
            rows,
            weight[:, i * part : (i + 1) * part],
            (((1,), (1,)), ((), ())),
            preferred_element_type=jnp.float32,
        )
    recv_hid = lax.all_to_all(
        send_hid.reshape(experts, capacity, hidden_width),
        ("far", "near"),
        split_axis=0,
        concat_axis=0,
        tiled=True,
    ).reshape(slot_total, hidden_width)
    came_back = lax.all_to_all(
        returned.astype(jnp.bfloat16).reshape(experts, capacity, hidden_width),
        ("far", "near"),
        split_axis=0,
        concat_axis=0,
        tiled=True,
    )

    share = hidden_width // lax.axis_size("dp")
    replica = lax.axis_index("dp")
    peer_hid = swap(lax.dynamic_slice_in_dim(recv_hid, (1 - replica) * share, share, 1))
    own_hid = lax.dynamic_slice_in_dim(recv_hid, replica * share, share, 1)
    grad_down = []
    for rows in recv_out:
        peer_rows = swap(rows)
        own_part = lax.dot_general(
            own_hid, rows, (((0,), (0,)), ((), ())), preferred_element_type=jnp.float32
        ).astype(jnp.bfloat16)
        peer_part = lax.dot_general(
            peer_hid, peer_rows, (((0,), (0,)), ((), ())), preferred_element_type=jnp.float32
        ).astype(jnp.bfloat16)
        summed = own_part.astype(jnp.float32) + peer_part.astype(jnp.float32)
        grad_down.append(summed.astype(jnp.bfloat16))
    grad_down = jnp.concatenate(grad_down, axis=1)[None]

    back_rows = lax.dot_general(
        place,
        came_back.reshape(slot_total, hidden_width),
        (((0,), (0,)), ((), ())),
        preferred_element_type=jnp.float32,
    ).reshape(tok_local, top_count, hidden_width)
    grad_hidden = (gates[:, :, None] * back_rows).astype(jnp.bfloat16)
    grad_gates = jnp.sum(back_rows * hidden.astype(jnp.float32), axis=-1)
    return (grad_hidden, grad_gates, grad_down)


def solution(mesh):
    placed = (
        P(("dp", "far", "near"), None),
        P(("dp", "far", "near"), None, None),
        P(("dp", "far", "near"), None),
        P(("dp", "far", "near"), None),
        P(("far", "near"), None, None),
    )
    return jax.shard_map(
        local,
        mesh=mesh,
        in_specs=placed,
        out_specs=(
            P(("dp", "far", "near"), None, None),
            P(("dp", "far", "near"), None),
            P(("far", "near"), "dp", None),
        ),
        check_vma=False,
    )
```

time: 146 us -> 110 us (0.75)
  waiting for transfers between devices: 53.4 us -> 26.9 us
  between operations: 14.1 us -> 0.81 us
  starting transfers between devices: 8.46 us -> 18.7 us
  blocking collectives: 43.6 us -> 33.8 us
  other arithmetic: 1.02 us -> 3.8 us
    all_gather x1 -> x0, waiting for transfers between devices: 35 us -> none  [local(): all_out = lax.all_gather(grad_out, ('far', 'near'), axis=0, tiled=True)]
    all_to_all x1 -> x3, waiting for transfers between devices: 9.62 us -> 23.2 us  [the longest x2 17.5 us: local(): lax.all_to_all(picked.reshape(far_count, near_count * capacity, part), 'f...]
    all_gather x1 -> x2, blocking collectives: 43.6 us -> 33.8 us  [local(): lax.all_gather(piece, 'near', axis=0, tiled=True)]
    all_to_all x1 -> x3, starting transfers between devices: 4.2 us -> 12.7 us  [the longest x2 8.5 us: local(): lax.all_to_all(picked.reshape(far_count, near_count * capacity, part), 'f...]
    all_to_all x1, waiting for transfers between devices: 8.04 us -> 3.65 us  [local(): lax.all_to_all(send_hid.reshape(experts, capacity, hidden_width), ('far',...]
    broadcast_in_dim x0 -> x1, other arithmetic: none -> 2.02 us  [local(): grad_down = jnp.concatenate(grad_down, axis=1)[None]]
    dot_general x4 -> x8, matrix products: 17.8 us -> 17.6 us  [the longest x2 7.23 us: local(): lax.dot_general(rows, weight[:, i * part:(i + 1) * part], (((1,), (1,)),...]
  transfers between devices with their start and end apart: 5 -> 7, of which waited for: 3 -> 4; matrix products, arithmetic and copies ran while one was open for 11% -> 16% of each run, Pallas kernels for 0% -> 0%
where the time goes in v3:
time: 110 us
  blocking collectives  33.8 us (31%)
  waiting for transfers between devices  26.9 us (24%)
  matrix products  20.9 us (19%)
  starting transfers between devices  18.7 us (17%)
  local copies, waits for them, and re-layouts  4.77 us (4%)
  other arithmetic  3.8 us (3%)
    all_gather x2, blocking collectives, local(): lax.all_gather(piece, 'near', axis=0, tiled=True)  33.8 us
    all_to_all x2, waiting for transfers between devices, local(): lax.all_to_all(picked.reshape(far_count, near_count * capacity, part), 'f...  17.5 us
    all_to_all x2, starting transfers between devices, local(): lax.all_to_all(picked.reshape(far_count, near_count * capacity, part), 'f...  8.5 us
    dot_general x2, matrix products, local(): lax.dot_general(rows, weight[:, i * part:(i + 1) * part], (((1,), (1,)),...  7.23 us
    all_to_all x1, waiting for transfers between devices, local(): lax.all_to_all(returned.astype(jnp.bfloat16).reshape(experts, capacity, h...  5.71 us
    all_to_all x1, starting transfers between devices, local(): lax.all_to_all(send_hid.reshape(experts, capacity, hidden_width), ('far',...  5.38 us
    all_to_all x1, starting transfers between devices, local(): lax.all_to_all(returned.astype(jnp.bfloat16).reshape(experts, capacity, h...  4.2 us
    dot_general x2, matrix products, local(): lax.dot_general(peer_hid, peer_rows, (((0,), (0,)), ((), ())), preferred_...  3.88 us
  transfers between devices with their start and end apart: 7, of which 4 were waited for; matrix products, arithmetic and copies ran while one was open for 16% of the time, Pallas kernels for 0%

profile of v3, /device:TPU:0, one launch (start us, length us, event | category | flops | bytes accessed | tf_op | source)
XLA Modules:
  0.0 109.6 jit_solution(16949269580500030388)
XLA Ops:
  0.6 0.0 copy-start
  0.7 0.8 copy.35
  1.5 0.1 reshape.125
  1.6 0.1 eq.88
  1.6 0.8 copy.34
  2.4 1.0 fusion.30
  3.4 17.7 %all_gather.6 = bf16[128,2176]{1,0:T(8,128)(2,1)S(1)} all-gather(bf16[32,2176]{1,0:T(8,128)(2,1)S(1)} %fusion.22), channel_id=1, replica_groups=mesh['dp'=2,'far'=4,'near'=4] {'near'}, dimensions={0}, use_global_device_ids=true | all-gather | bytes 696320 | tf_op jit(solution)/shard_map/all_gather | solution.py:30
  21.2 0.1 copy.41
  21.3 0.1 compare_reduce_fusion
  21.4 0.1 reshape.136
  21.5 0.8 reduce_window_sum.28
  22.3 0.1 sub.15
  22.4 0.1 add.64
  22.4 0.1 add.65
  22.5 0.1 eq.96
  22.6 16.1 %all_gather.7 = bf16[128,2048]{1,0:T(8,128)(2,1)S(1)} all-gather(bf16[32,2048]{1,0:T(8,128)(2,1)S(1)} %get-tuple-element.21), channel_id=1, replica_groups=mesh['dp'=2,'far'=4,'near'=4] {'near'}, dimensions={0}, use_global_device_ids=true | all-gather | bytes 655360 | tf_op jit(solution)/shard_map/all_gather | solution.py:30
  38.7 0.6 reduce-window.6
  39.3 0.2 slice_reduce_fusion
  39.5 0.1 fusion.26
  39.6 0.1 bitcast_compare_fusion
  39.7 1.4 %convolution_convert_fusion.4 = bf16[256,2048]{1,0:T(8,128)(2,1)} fusion(pred[256,128]{1,0:T(32,128)(4,1)S(1)} %bitcast_compare_fusion, bf16[128,2048]{1,0:T(8,128)(2,1)S(1)} %all_gather.7), kind=kOutput, calls=%fused_computation.11 | convolution fusion | flops 134742016 | bytes 1605632 | tf_op jit(solution)/shard_map/dot_general | solution.py:63
  41.1 0.0 copy-done
  41.1 1.1 %convolution_convert_fusion.6 = bf16[256,768]{1,0:T(8,128)(2,1)} fusion(bf16[32,8,768]{2,1,0:T(8,128)(2,1)S(1)} %copy-done, f32[32,8]{1,0:T(8,128)S(1)} %copy.34, s32[256]{0:T(256)S(1)} %add_add_fusion), kind=kOutput, calls=%fused_computation.15 | convolution fusion | flops 101515264 | bytes 788480 | tf_op jit(solution)/shard_map/dot_general | solution.py:42
  42.3 4.3 %all-to-all-start.1 = ((bf16[4,64,2048]{2,1,0:T(8,128)(2,1)}), bf16[4,64,2048]{2,1,0:T(8,128)(2,1)}, u32[]{:S(2)}, u32[]{:S(2)}) async-start(bf16[4,64,2048]{2,1,0:T(8,128)(2,1)} %bitcast.7), calls=%async_computation.1 | async-start | bytes 2097152 | tf_op jit(solution)/shard_map/all_to_all | solution.py:66
  46.5 1.4 %convolution_convert_fusion.5 = bf16[256,2048]{1,0:T(8,128)(2,1)} fusion(pred[256,128]{1,0:T(32,128)(4,1)S(1)} %bitcast_compare_fusion, bf16[128,2176]{1,0:T(8,128)(2,1)S(1)} %all_gather.6), kind=kOutput, calls=%fused_computation.12 | convolution fusion | flops 134742016 | bytes 1605632 | tf_op jit(solution)/shard_map/dot_general | solution.py:63
  47.9 8.1 %all-to-all-done.1 = bf16[4,64,2048]{2,1,0:T(8,128)(2,1)} async-done(((bf16[4,64,2048]{2,1,0:T(8,128)(2,1)}), bf16[4,64,2048]{2,1,0:T(8,128)(2,1)}, u32[]{:S(2)}, u32[]{:S(2)}) %all-to-all-start.1) | async-done | bytes 1048608 | tf_op jit(solution)/shard_map/all_to_all | solution.py:66
  56.0 4.2 %all-to-all-start = ((bf16[4,64,2048]{2,1,0:T(8,128)(2,1)}), bf16[4,64,2048]{2,1,0:T(8,128)(2,1)}, u32[]{:S(2)}, u32[]{:S(2)}) async-start(bf16[4,64,2048]{2,1,0:T(8,128)(2,1)} %bitcast.3), calls=%async_computation | async-start | bytes 2097152 | tf_op jit(solution)/shard_map/all_to_all | solution.py:66
  60.3 0.1 collective-permute-start.2
  60.3 9.4 %all-to-all-done = bf16[4,64,2048]{2,1,0:T(8,128)(2,1)} async-done(((bf16[4,64,2048]{2,1,0:T(8,128)(2,1)}), bf16[4,64,2048]{2,1,0:T(8,128)(2,1)}, u32[]{:S(2)}, u32[]{:S(2)}) %all-to-all-start) | async-done | bytes 1048608 | tf_op jit(solution)/shard_map/all_to_all | solution.py:66
  69.8 5.4 %all-to-all-start.3 = ((bf16[16,16,768]{2,1,0:T(8,128)(2,1)}), bf16[16,16,768]{2,1,0:T(8,128)(2,1)S(1)}, u32[]{:S(2)}, u32[]{:S(2)}) async-start(bf16[16,16,768]{2,1,0:T(8,128)(2,1)} %bitcast.12), calls=%async_computation.3 | async-start | bytes 786432 | tf_op jit(solution)/shard_map/all_to_all | solution.py:80
  75.1 3.2 %fusion = f32[256,768]{1,0:T(8,128)S(1)} fusion(bf16[256,2048]{1,0:T(8,128)(2,1)} %bitcast.8, bf16[768,4096]{1,0:T(8,128)(2,1)} %bitcast.53), kind=kOutput, calls=%fused_computation | convolution fusion | flops 805306368 | bytes 4980736 | tf_op jit(solution)/shard_map/dot_general | solution.py:74
  78.4 4.0 %fusion.7 = bf16[256,768]{1,0:T(8,128)(2,1)} fusion(f32[256,768]{1,0:T(8,128)S(1)} %fusion, bf16[256,2048]{1,0:T(8,128)(2,1)} %bitcast.4, bf16[768,4096]{1,0:T(8,128)(2,1)} %bitcast.54), kind=kOutput, calls=%fused_computation.14 | convolution fusion | flops 805699584 | bytes 5373952 | tf_op jit(solution)/shard_map/dot_general | solution.py:74
  82.4 3.6 %all-to-all-done.3 = bf16[16,16,768]{2,1,0:T(8,128)(2,1)S(1)} async-done(((bf16[16,16,768]{2,1,0:T(8,128)(2,1)}), bf16[16,16,768]{2,1,0:T(8,128)(2,1)S(1)}, u32[]{:S(2)}, u32[]{:S(2)}) %all-to-all-start.3) | async-done | bytes 393248 | tf_op jit(solution)/shard_map/all_to_all | solution.py:80
  86.0 4.2 %all-to-all-start.2 = ((bf16[16,16,768]{2,1,0:T(8,128)(2,1)}), bf16[16,16,768]{2,1,0:T(8,128)(2,1)}, u32[]{:S(2)}, u32[]{:S(2)}) async-start(bf16[16,16,768]{2,1,0:T(8,128)(2,1)} %bitcast.9), calls=%async_computation.2 | async-start | bytes 786432 | tf_op jit(solution)/shard_map/all_to_all | solution.py:87
  90.2 0.7 constant_dynamic-slice_fusion
  90.9 0.0 collective-permute-start
  91.0 0.5 collective-permute-start.1
  91.5 1.8 %convolution_convert_fusion.1 = bf16[384,2048]{1,0:T(8,128)(2,1)S(1)} fusion(bf16[256,2048]{1,0:T(8,128)(2,1)} %bitcast.8, bf16[256,768]{1,0:T(8,128)(2,1)S(1)} %bitcast.51, s32[]{:T(128)S(6)} %select_n.15), kind=kOutput, calls=%fused_computation.8 | convolution fusion | flops 403439616 | bytes 2818052 | tf_op jit(solution)/shard_map/dot_general | solution.py:102
  93.3 1.8 %convolution_convert_fusion.3 = bf16[384,2048]{1,0:T(8,128)(2,1)S(1)} fusion(bf16[256,2048]{1,0:T(8,128)(2,1)} %bitcast.4, bf16[256,768]{1,0:T(8,128)(2,1)S(1)} %bitcast.52, s32[]{:T(128)S(6)} %select_n.15), kind=kOutput, calls=%fused_computation.10 | convolution fusion | flops 403439616 | bytes 2818052 | tf_op jit(solution)/shard_map/dot_general | solution.py:102
  95.1 5.7 %all-to-all-done.2 = bf16[16,16,768]{2,1,0:T(8,128)(2,1)} async-done(((bf16[16,16,768]{2,1,0:T(8,128)(2,1)}), bf16[16,16,768]{2,1,0:T(8,128)(2,1)}, u32[]{:S(2)}, u32[]{:S(2)}) %all-to-all-start.2) | async-done | bytes 393248 | tf_op jit(solution)/shard_map/all_to_all | solution.py:87
  100.8 2.2 %fusion.11 = (f32[32,8]{1,0:T(8,128)S(1)}, bf16[32,8,768]{2,1,0:T(8,128)(2,1)}) fusion(bf16[32,8,768]{2,1,0:T(8,128)(2,1)} %param.6, f32[32,8]{1,0:T(8,128)S(1)} %copy.34, bf16[256,768,1]{1,0,2:T(8,128)(2,1)} %bitcast.11, s32[256]{0:T(256)} %copy-done.1), kind=kOutput, calls=%fused_computation.19 | convolution fusion | flops 101711616 | bytes 1182720 | tf_op jit(solution)/shard_map/dot_general | solution.py:112
  103.0 0.7 copy.40
  103.7 0.0 collective-permute-done
  103.7 0.0 collective-permute-done.2
  103.7 1.9 %add_convert_fusion = bf16[384,2048]{1,0:T(8,128)(2,1)S(1)} fusion(bf16[384,2048]{1,0:T(8,128)(2,1)S(1)} %convolution_convert_fusion.1, bf16[256,384]{1,0:T(8,128)(2,1)} %collective-permute-done, bf16[256,2048]{1,0:T(8,128)(2,1)} %collective-permute-done.2), kind=kOutput, calls=%fused_computation.5 | convolution fusion | flops 406585344 | bytes 4390912 | tf_op jit(solution)/shard_map/dot_general | solution.py:105
  105.6 0.0 collective-permute-done.1
  105.7 1.9 %add_convert_fusion.1 = bf16[384,2048]{1,0:T(8,128)(2,1)S(1)} fusion(bf16[384,2048]{1,0:T(8,128)(2,1)S(1)} %convolution_convert_fusion.3, bf16[256,384]{1,0:T(8,128)(2,1)} %collective-permute-done, bf16[256,2048]{1,0:T(8,128)(2,1)} %collective-permute-done.1), kind=kOutput, calls=%fused_computation.6 | convolution fusion | flops 406585344 | bytes 4390912 | tf_op jit(solution)/shard_map/dot_general | solution.py:105
  107.6 2.0 %maximum_bitcast_fusion = bf16[1,384,4096]{2,1,0:T(8,128)(2,1)} fusion(bf16[384,2048]{1,0:T(8,128)(2,1)S(1)} %add_convert_fusion, bf16[384,2048]{1,0:T(8,128)(2,1)S(1)} %add_convert_fusion.1), kind=kLoop, calls=%fused_computation.4 | loop fusion | flops 6291456 | bytes 6291456 | tf_op jit(solution)/shard_map/broadcast_in_dim | solution.py:110
  (16 shorter events, 0.1 us)
Async XLA Ops:
  0.6 40.5 %copy-start = (bf16[32,8,768]{2,1,0:T(8,128)(2,1)S(1)}, bf16[32,8,768]{2,1,0:T(8,128)(2,1)}, u32[]{:S(2)}) copy-start(bf16[32,8,768]{2,1,0:T(8,128)(2,1)} %param.6) | copy-start | bytes 1179652
  39.6 16.4 %copy-start.1 = (s32[256]{0:T(256)}, s32[256]{0:T(256)S(1)}, u32[]{:S(2)}) copy-start(s32[256]{0:T(256)S(1)} %add_add_fusion) | copy-start | bytes 3076
  42.3 13.8 %all-to-all-start.1 = ((bf16[4,64,2048]{2,1,0:T(8,128)(2,1)}), bf16[4,64,2048]{2,1,0:T(8,128)(2,1)}, u32[]{:S(2)}, u32[]{:S(2)}) async-start(bf16[4,64,2048]{2,1,0:T(8,128)(2,1)} %bitcast.7), calls=%async_computation.1 | async-start | bytes 2097152 | tf_op jit(solution)/shard_map/all_to_all | solution.py:66
  56.0 13.7 %all-to-all-start = ((bf16[4,64,2048]{2,1,0:T(8,128)(2,1)}), bf16[4,64,2048]{2,1,0:T(8,128)(2,1)}, u32[]{:S(2)}, u32[]{:S(2)}) async-start(bf16[4,64,2048]{2,1,0:T(8,128)(2,1)} %bitcast.3), calls=%async_computation | async-start | bytes 2097152 | tf_op jit(solution)/shard_map/all_to_all | solution.py:66
  60.3 43.4 %collective-permute-start.2 = (bf16[256,2048]{1,0:T(8,128)(2,1)}, bf16[256,2048]{1,0:T(8,128)(2,1)}, u32[]{:S(2)}, u32[]{:S(2)}) collective-permute-start(bf16[256,2048]{1,0:T(8,128)(2,1)} %bitcast.8), channel_id=1, source_target_pairs={{0,16},{16,0},{1,17},{17,1},{2,18},{18,2},{3,19},{19,3},{4,20},{20... | collective-permute-start | bytes 3145736 | tf_op jit(solution)/shard_map/ppermute | solution.py:11
  69.8 16.3 %all-to-all-start.3 = ((bf16[16,16,768]{2,1,0:T(8,128)(2,1)}), bf16[16,16,768]{2,1,0:T(8,128)(2,1)S(1)}, u32[]{:S(2)}, u32[]{:S(2)}) async-start(bf16[16,16,768]{2,1,0:T(8,128)(2,1)} %bitcast.12), calls=%async_computation.3 | async-start | bytes 786432 | tf_op jit(solution)/shard_map/all_to_all | solution.py:80
  86.0 14.8 %all-to-all-start.2 = ((bf16[16,16,768]{2,1,0:T(8,128)(2,1)}), bf16[16,16,768]{2,1,0:T(8,128)(2,1)}, u32[]{:S(2)}, u32[]{:S(2)}) async-start(bf16[16,16,768]{2,1,0:T(8,128)(2,1)} %bitcast.9), calls=%async_computation.2 | async-start | bytes 786432 | tf_op jit(solution)/shard_map/all_to_all | solution.py:87
  90.9 12.7 %collective-permute-start = (bf16[256,384]{1,0:T(8,128)(2,1)}, bf16[256,384]{1,0:T(8,128)(2,1)}, u32[]{:S(2)}, u32[]{:S(2)}) collective-permute-start(bf16[256,384]{1,0:T(8,128)(2,1)} %constant_dynamic-slice_fusion), channel_id=1, source_target_pairs={{0,16},{16,0},{1,17},{17,1},{2,18},{18,2},{3,19},{19,3},{4,20},{20... | collective-permute-start | bytes 589832 | tf_op jit(solution)/shard_map/ppermute | solution.py:11
  91.0 14.7 %collective-permute-start.1 = (bf16[256,2048]{1,0:T(8,128)(2,1)}, bf16[256,2048]{1,0:T(8,128)(2,1)}, u32[]{:S(2)}, u32[]{:S(2)}) collective-permute-start(bf16[256,2048]{1,0:T(8,128)(2,1)} %bitcast.4), channel_id=1, source_target_pairs={{0,16},{16,0},{1,17},{17,1},{2,18},{18,2},{3,19},{19,3},{4,20},{20... | collective-permute-start | bytes 3145736 | tf_op jit(solution)/shard_map/ppermute | solution.py:11

commit v4 on v1

v4 whole, which is shorter than its diff:
```python
import functools

import jax
import jax.numpy as jnp
from jax import lax
from jax.experimental import pallas as pl
from jax.experimental.pallas import tpu as pltpu
from jax.sharding import PartitionSpec as P

ID_COLS = 128
ROUNDS = 2
VMEM_LIMIT = 48 * 1024 * 1024


def iota(shape, dim):
    return lax.broadcasted_iota(jnp.int32, shape, dim)


def exact_dot(one_hot, values):
    return jnp.dot(one_hot, values, preferred_element_type=jnp.float32)


def pick_kernel(far_count, near_count, capacity, near_ref, *refs):
    out_ref = refs[-1]
    count = (len(refs) - 1) // 2
    blocks, hids = refs[:count], refs[count:-1]
    tok_local = blocks[0].shape[0]
    width = blocks[0].shape[1] - ID_COLS
    near = near_ref[0]
    cols = count * tok_local
    slots = far_count * count * capacity
    ids = jnp.concatenate([block[:, width:] for block in blocks], axis=0).astype(jnp.float32)
    lead = max(8, far_count)
    ones = jnp.ones((lead, ID_COLS), jnp.bfloat16)
    named = jnp.zeros((lead, cols), jnp.float32)
    for j in range(far_count):
        expert = (j * near_count + near).astype(jnp.float32)
        hit = jnp.where(ids == expert, 1.0, 0.0).astype(jnp.bfloat16)
        line = lax.dot_general(ones, hit, (((1,), (1,)), ((), ())), preferred_element_type=jnp.float32)
        named = jnp.where(iota((lead, cols), 0) == j, line, named)
    row, col = iota((cols, cols), 0), iota((cols, cols), 1)
    before = jnp.where((row < col) & (row // tok_local == col // tok_local), 1.0, 0.0).astype(jnp.bfloat16)
    named = named.astype(jnp.bfloat16)
    rank = exact_dot(named, before).astype(jnp.bfloat16)
    per_far = count * capacity
    spread = jnp.where(iota((slots, lead), 0) // per_far == iota((slots, lead), 1), 1.0, 0.0).astype(jnp.bfloat16)
    slot = iota((slots, cols), 0) % per_far
    pick = (
        (exact_dot(spread, named) > 0.5)
        & (iota((slots, cols), 1) // tok_local == slot // capacity)
        & (exact_dot(spread, rank).astype(jnp.int32) == slot % capacity)
    )
    pick = jnp.where(pick, 1.0, 0.0).astype(jnp.bfloat16)
    step = min(width, 512)
    for start in range(0, width, step):
        tokens = jnp.concatenate([block[:, start : start + step] for block in blocks], axis=0)
        out_ref[:, start : start + step] = exact_dot(pick, tokens).astype(jnp.bfloat16)
    out_row, in_row = iota((slots, slots), 0), iota((slots, slots), 1)
    per_block = far_count * capacity
    source = (
        (out_row % per_far // capacity) * per_block + (out_row // per_far) * capacity + out_row % capacity
    )
    order = jnp.where(in_row == source, 1.0, 0.0).astype(jnp.bfloat16)
    hid = jnp.concatenate([hid[...] for hid in hids], axis=0)
    out_ref[:, width:] = exact_dot(order, hid).astype(jnp.bfloat16)


def returned_kernel(far_count, near_count, capacity, near_ref, rows_ref, weight_ref, *refs):
    earlier, (out_ref, total_ref) = refs[:-2], refs[-2:]
    step = pl.program_id(0)
    tile = weight_ref.shape[1]

    @pl.when(step == 0)
    def _():
        total_ref[...] = jnp.zeros_like(total_ref)

    cols = pl.ds(pl.multiple_of(step * tile, 128), tile)
    total_ref[...] += lax.dot_general(
        rows_ref[:, cols], weight_ref[...], (((1,), (1,)), ((), ())), preferred_element_type=jnp.float32
    )

    @pl.when(step == pl.num_programs(0) - 1)
    def _():
        own = total_ref[...].astype(jnp.bfloat16)
        if not earlier:
            out_ref[...] = own
            return
        rows = jnp.concatenate([ref[...] for ref in earlier] + [own], axis=0)
        total = rows.shape[0]
        near = near_ref[0]
        count = near_count // ROUNDS
        out_row, in_row = iota((total, total), 0), iota((total, total), 1)
        back = lax.rem(near - out_row // capacity % near_count + near_count, near_count)
        source = (
            (back // count) * (far_count * count * capacity)
            + (out_row // (near_count * capacity)) * (count * capacity)
            + (back % count) * capacity
            + out_row % capacity
        )
        order = jnp.where(in_row == source, 1.0, 0.0).astype(jnp.bfloat16)
        out_ref[...] = exact_dot(order, rows).astype(jnp.bfloat16)


def down_kernel(width, replica_ref, *refs):
    rows, (out_ref, turned_ref) = refs[:-2], refs[-2:]
    step = pl.program_id(0)
    share, tile = out_ref.shape
    lines = rows[0].shape[0]

    @pl.when(step == 0)
    def _():
        start = pl.multiple_of(width + replica_ref[0] * share, 128)
        for i, ref in enumerate(rows):
            hid = ref[:, pl.ds(start, share)].astype(jnp.float32)
            turned_ref[:, i * lines : (i + 1) * lines] = hid.T.astype(jnp.bfloat16)

    cols = pl.ds(pl.multiple_of(step * tile, 128), tile)
    tokens = jnp.concatenate([ref[:, cols] for ref in rows], axis=0)
    out_ref[...] = exact_dot(turned_ref[...], tokens).astype(jnp.bfloat16)


def scalar_spec():
    return pl.BlockSpec(memory_space=pltpu.SMEM)


def params():
    return pltpu.CompilerParams(vmem_limit_bytes=VMEM_LIMIT)


def pick_rows(far_count, near_count, capacity, near, blocks, hids):
    width = blocks[0].shape[1] - ID_COLS
    slots = far_count * capacity * len(blocks)
    shape = (slots, width + hids[0].shape[1])
    return pl.pallas_call(
        functools.partial(pick_kernel, far_count, near_count, capacity),
        out_shape=jax.ShapeDtypeStruct(shape, jnp.bfloat16),
        in_specs=[scalar_spec()] + [pl.BlockSpec(memory_space=pltpu.VMEM)] * (2 * len(blocks)),
        out_specs=pl.BlockSpec(memory_space=pltpu.VMEM),
        compiler_params=params(),
        cost_estimate=pl.CostEstimate(flops=2 * slots * 64 * shape[1], bytes_accessed=4 * slots * shape[1], transcendentals=0),
        name="pick_rows",
    )(near, *blocks, *hids)


def returned_rows(far_count, near_count, capacity, near, rows, weight, earlier):
    lines = rows.shape[0]
    hidden_width, width = weight.shape
    tile = min(width, 512)
    total = lines * ROUNDS if earlier else lines
    whole = lambda array: pl.BlockSpec(array.shape, lambda i: (0, 0))
    return pl.pallas_call(
        functools.partial(returned_kernel, far_count, near_count, capacity),
        grid=(width // tile,),
        out_shape=jax.ShapeDtypeStruct((total, hidden_width), jnp.bfloat16),
        in_specs=[scalar_spec(), whole(rows), pl.BlockSpec((hidden_width, tile), lambda i: (0, i))]
        + [whole(array) for array in earlier],
        out_specs=pl.BlockSpec((total, hidden_width), lambda i: (0, 0)),
        scratch_shapes=[pltpu.VMEM((lines, hidden_width), jnp.float32)],
        compiler_params=params(),
        cost_estimate=pl.CostEstimate(
            flops=2 * lines * width * hidden_width, bytes_accessed=2 * width * hidden_width, transcendentals=0
        ),
        name="returned_rows",
    )(near, rows, weight, *earlier)


def down_rows(replica, rows, width, share):
    tile = min(width, 512)
    lines = sum(array.shape[0] for array in rows)
    whole = lambda array: pl.BlockSpec(array.shape, lambda i: (0, 0))
    return pl.pallas_call(
        functools.partial(down_kernel, width),
        grid=(width // tile,),
        out_shape=jax.ShapeDtypeStruct((share, width), jnp.bfloat16),
        in_specs=[scalar_spec()] + [whole(array) for array in rows],
        out_specs=pl.BlockSpec((share, tile), lambda i: (0, i)),
        scratch_shapes=[pltpu.VMEM((share, lines), jnp.bfloat16)],
        compiler_params=params(),
        cost_estimate=pl.CostEstimate(
            flops=2 * lines * width * share, bytes_accessed=2 * width * (lines + share), transcendentals=0
        ),
        name="down_rows",
    )(replica, *rows)


def local(grad_out, hidden, gates, expert_ids, w_down):
    tok_local, top_count = expert_ids.shape
    far_count = lax.axis_size("far")
    near_count = lax.axis_size("near")
    experts = far_count * near_count
    capacity = max(4, (tok_local * top_count + experts - 1) // experts)
    width = grad_out.shape[1]
    hidden_width = hidden.shape[2]
    row_total = tok_local * top_count
    slot_total = experts * capacity
    near = lax.axis_index("near")
    near_ref = near.astype(jnp.int32).reshape(1)
    count = near_count // ROUNDS
    weight = w_down[0]

    def along(array, steps):
        return lax.ppermute(array, "near", [(i, (i + steps) % near_count) for i in range(near_count)])

    def swap(array):
        return lax.ppermute(array, "dp", [(i, i ^ 1) for i in range(lax.axis_size("dp"))])

    id_cols = jnp.pad(
        expert_ids.astype(jnp.bfloat16), ((0, 0), (0, ID_COLS - top_count)), constant_values=-1
    )
    blocks = [jnp.concatenate([grad_out, id_cols], axis=1)]
    for _ in range(1, near_count):
        blocks.append(along(blocks[-1], 1))

    flat_ids = expert_ids.reshape(-1)
    one_hot = (flat_ids[:, None] == jnp.arange(experts, dtype=jnp.int32)[None, :]).astype(jnp.int32)
    ranks = jnp.sum(jnp.cumsum(one_hot, axis=0) * one_hot, axis=1) - 1
    steps = (flat_ids % near_count - near + near_count) % near_count
    out_slots = (steps * far_count + flat_ids // near_count) * capacity + ranks
    back_slots = flat_ids * capacity + ranks
    slot_range = jnp.arange(slot_total, dtype=jnp.int32)[:, None]
    out_place = (slot_range == out_slots[None, :]).astype(jnp.bfloat16)
    back_place = (slot_range == back_slots[None, :]).astype(jnp.bfloat16)
    scaled = (
        (gates[:, :, None] * hidden.astype(jnp.float32))
        .astype(jnp.bfloat16)
        .reshape(row_total, hidden_width)
    )
    send_hid = exact_dot(out_place, scaled).astype(jnp.bfloat16).reshape(near_count, -1, hidden_width)
    hids = [send_hid[0]] + [along(send_hid[step], step) for step in range(1, near_count)]

    rows, peers, returned = [], [], []
    for turn in range(ROUNDS):
        part = slice(turn * count, (turn + 1) * count)
        picked = pick_rows(far_count, near_count, capacity, near_ref, blocks[part], hids[part])
        got = lax.all_to_all(
            picked.reshape(far_count, -1, picked.shape[1]), "far", split_axis=0, concat_axis=0, tiled=True
        ).reshape(picked.shape)
        rows.append(got)
        peers.append(swap(got))
        returned.append(
            returned_rows(
                far_count, near_count, capacity, near_ref, got, weight, returned if turn == ROUNDS - 1 else []
            )
        )
    came_back = lax.all_to_all(
        returned[-1].reshape(experts, capacity, hidden_width),
        ("far", "near"),
        split_axis=0,
        concat_axis=0,
        tiled=True,
    )

    replica = lax.axis_index("dp").astype(jnp.int32).reshape(1)
    grad_down = down_rows(replica, rows + peers, width, hidden_width // lax.axis_size("dp"))
    came_back, grad_down = lax.optimization_barrier((came_back, grad_down))

    back_rows = lax.dot_general(
        back_place,
        came_back.reshape(slot_total, hidden_width),
        (((0,), (0,)), ((), ())),
        preferred_element_type=jnp.float32,
    ).reshape(tok_local, top_count, hidden_width)
    grad_hidden = (gates[:, :, None] * back_rows).astype(jnp.bfloat16)
    grad_gates = jnp.sum(back_rows * hidden.astype(jnp.float32), axis=-1)
    return (grad_hidden, grad_gates, grad_down[None])


def solution(mesh):
    placed = (
        P(("dp", "far", "near"), None),
        P(("dp", "far", "near"), None, None),
        P(("dp", "far", "near"), None),
        P(("dp", "far", "near"), None),
        P(("far", "near"), None, None),
    )
    return jax.shard_map(
        local,
        mesh=mesh,
        in_specs=placed,
        out_specs=(
            P(("dp", "far", "near"), None, None),
            P(("dp", "far", "near"), None),
            P(("far", "near"), "dp", None),
        ),
        check_vma=False,
    )
```

time: 146 us -> 99 us (0.68)
  blocking collectives: 43.6 us -> 0 us
  Pallas kernels: 0 us -> 24.1 us
  matrix products: 21.1 us -> 2.43 us
  between operations: 14.1 us -> 0.75 us
  starting transfers between devices: 8.46 us -> 20.4 us
  waiting for transfers between devices: 53.4 us -> 44.4 us
    all_gather x1 -> x0, blocking collectives: 43.6 us -> none  [local(): all_ids = lax.all_gather(expert_ids, ('far', 'near'), axis=0, tiled=True)]
    all_gather x1 -> x0, waiting for transfers between devices: 35 us -> none  [local(): all_out = lax.all_gather(grad_out, ('far', 'near'), axis=0, tiled=True)]
    pallas_call x0 -> x5, Pallas kernels: none -> 24.1 us  [the longest x2 14.6 us: returned_rows(): pl.pallas_call(functools.partial(returned_kernel, far_count, near_count,...]
    ppermute x2 -> x8, waiting for transfers between devices: 0.01 us -> 22.9 us  [the longest x6 22.9 us: along(): lax.ppermute(array, 'near', [(i, (i + steps) % near_count) for i in range...]
    dot_general x6 -> x2, matrix products: 21.1 us -> 2.43 us  [the longest x1 1.35 us: exact_dot(): return jnp.dot(one_hot, values, preferred_element_type=jnp.float32)]
    ppermute x2 -> x8, starting transfers between devices: 0.01 us -> 8.61 us  [the longest x6 8.53 us: along(): lax.ppermute(array, 'near', [(i, (i + steps) % near_count) for i in range...]
    all_to_all x2 -> x3, waiting for transfers between devices: 17.7 us -> 21.5 us  [the longest x2 14.2 us: local(): lax.all_to_all(picked.reshape(far_count, -1, picked.shape[1]), 'far', spl...]
    all_to_all x2 -> x3, starting transfers between devices: 8.42 us -> 11.7 us  [the longest x2 7.25 us: local(): lax.all_to_all(picked.reshape(far_count, -1, picked.shape[1]), 'far', spl...]
  transfers between devices with their start and end apart: 5 -> 11, of which waited for: 3 -> 5; matrix products, arithmetic and copies ran while one was open for 11% -> 4% of each run, Pallas kernels for 0% -> 23%
where the time goes in v4:
time: 99 us; the launch traced here: 98.2 us
  waiting for transfers between devices  44.4 us (45%)
  Pallas kernels  24.1 us (24%)
  starting transfers between devices  20.4 us (21%)
  local copies, waits for them, and re-layouts  3.71 us (4%)
  matrix products  2.43 us (2%)
  other arithmetic  2.41 us (2%)
    ppermute x6, waiting for transfers between devices, along(): lax.ppermute(array, 'near', [(i, (i + steps) % near_count) for i in range...  22.9 us
    pallas_call x2, Pallas kernels, returned_rows(): pl.pallas_call(functools.partial(returned_kernel, far_count, near_count,...  14.6 us
    all_to_all x2, waiting for transfers between devices, local(): lax.all_to_all(picked.reshape(far_count, -1, picked.shape[1]), 'far', spl...  14.2 us
    ppermute x6, starting transfers between devices, along(): lax.ppermute(array, 'near', [(i, (i + steps) % near_count) for i in range...  8.53 us
    all_to_all x2, starting transfers between devices, local(): lax.all_to_all(picked.reshape(far_count, -1, picked.shape[1]), 'far', spl...  7.25 us
    all_to_all x1, waiting for transfers between devices, local(): lax.all_to_all(returned[-1].reshape(experts, capacity, hidden_width), ('f...  7.24 us
    pallas_call x1, Pallas kernels, down_rows(): pl.pallas_call(functools.partial(down_kernel, width), grid=(width // tile...  6.77 us
    all_to_all x1, starting transfers between devices, local(): lax.all_to_all(returned[-1].reshape(experts, capacity, hidden_width), ('f...  4.49 us
  transfers between devices with their start and end apart: 11, of which 5 were waited for; matrix products, arithmetic and copies ran while one was open for 4% of the time, Pallas kernels for 23%

profile of v4, /device:TPU:0, one launch (start us, length us, event | category | flops | bytes accessed | tf_op | source)
XLA Modules:
  0.0 98.2 jit_solution(9569300091468154084)
XLA Ops:
  0.6 0.7 convert_element_type.26
  1.3 0.1 copy.25
  1.4 1.0 fusion.6.refs_0_
  2.4 3.1 %collective-permute-start = (bf16[32,4224]{1,0:T(8,128)(2,1)S(1)}, bf16[32,4224]{1,0:T(8,128)(2,1)S(1)}, u32[]{:S(2)}, u32[]{:S(2)}) collective-permute-start(bf16[32,4224]{1,0:T(8,128)(2,1)S(1)} %fusion.6.refs_0_), channel_id=1, source_target_pairs={{0,1},{1,2},{2,3},{3,0},{4,5},{5,6},{6,7},{7,4},{8,9},{9,10},{10,1... | collective-permute-start | bytes 811016 | tf_op jit(solution)/shard_map/ppermute | solution.py:202
  5.5 0.8 copy.22
  6.2 0.1 eq.65
  6.3 0.1 reshape.165
  6.4 0.6 reduce-window.6
  7.0 0.2 slice_reduce_fusion
  7.2 0.8 copy.21
  8.0 0.1 fusion.13
  8.1 1.4 %convolution_convert_fusion = bf16[256,768]{1,0:T(8,128)(2,1)S(1)} fusion(bf16[32,8,768]{2,1,0:T(8,128)(2,1)} %param.6, f32[32,8]{1,0:T(8,128)S(1)} %copy.21, s32[256]{0:T(256)S(1)} %get-tuple-element.20), kind=kOutput, calls=%fused_computation | convolution fusion | flops 101515264 | bytes 788480 | tf_op jit(solution)/shard_map/dot_general | solution.py:20
  9.5 1.6 %collective-permute-start.5 = (bf16[64,768]{1,0:T(8,128)(2,1)S(1)}, bf16[64,768]{1,0:T(8,128)(2,1)S(1)}, u32[]{:S(2)}, u32[]{:S(2)}) collective-permute-start(bf16[64,768]{1,0:T(8,128)(2,1)S(1)} %get-tuple-element.15), channel_id=1, source_target_pairs={{0,1},{1,2},{2,3},{3,0},{4,5},{5,6},{6,7},{7,4},{8,9},{9,10},{10,1... | collective-permute-start | bytes 294920 | tf_op jit(solution)/shard_map/ppermute | solution.py:202
  11.1 4.9 %collective-permute-done.5.refs_3_ = bf16[64,768]{1,0:T(8,128)(2,1)S(1)} collective-permute-done((bf16[64,768]{1,0:T(8,128)(2,1)S(1)}, bf16[64,768]{1,0:T(8,128)(2,1)S(1)}, u32[]{:S(2)}, u32[]{:S(2)}) %collective-permute-start.5) | collective-permute-done | bytes 98336 | tf_op jit(solution)/shard_map/ppermute | solution.py:202
  16.1 0.0 collective-permute-done.refs_1_
  16.1 1.9 %pick_rows.3 = bf16[128,4864]{1,0:T(8,128)(2,1)} custom-call(s32[1]{0:T(128)} %bitcast.2.near_ref, bf16[32,4224]{1,0:T(8,128)(2,1)S(1)} %fusion.6.refs_0_, bf16[32,4224]{1,0:T(8,128)(2,1)S(1)} %collective-permute-done.refs_1_, bf16[64,768]{1,0:T(8,128)(2,1)S(1)} %get-tuple-element.16.refs_2_, bf16[64,768]{1,0:T(8,128)(2,1)S(1)} %collective-permute-done.5.refs_3_), custom_call_target="tpu_custom_call" | custom-call | flops 79691776 | bytes 2490368 | tf_op jit(solution)/shard_map/pick_rows/pallas_call | solution.py:134
  18.0 3.7 %all-to-all-start.1 = ((bf16[4,32,4864]{2,1,0:T(8,128)(2,1)}), bf16[4,32,4864]{2,1,0:T(8,128)(2,1)S(1)}, u32[]{:S(2)}, u32[]{:S(2)}) async-start(bf16[4,32,4864]{2,1,0:T(8,128)(2,1)} %bitcast.7), calls=%async_computation.1 | async-start | bytes 2490368 | tf_op jit(solution)/shard_map/all_to_all | solution.py:235
  21.7 0.0 collective-permute-start.1
  21.7 9.2 %collective-permute-done.1.refs_0_ = bf16[32,4224]{1,0:T(8,128)(2,1)S(1)} collective-permute-done((bf16[32,4224]{1,0:T(8,128)(2,1)S(1)}, bf16[32,4224]{1,0:T(8,128)(2,1)S(1)}, u32[]{:S(2)}, u32[]{:S(2)}) %collective-permute-start.1) | collective-permute-done | bytes 270368 | tf_op jit(solution)/shard_map/ppermute | solution.py:202
  30.9 0.0 collective-permute-start.2
  30.9 0.4 collective-permute-start.3
  31.2 3.5 %collective-permute-start.4 = (bf16[64,768]{1,0:T(8,128)(2,1)S(1)}, bf16[64,768]{1,0:T(8,128)(2,1)S(1)}, u32[]{:S(2)}, u32[]{:S(2)}) collective-permute-start(bf16[64,768]{1,0:T(8,128)(2,1)S(1)} %get-tuple-element.17), channel_id=1, source_target_pairs={{0,3},{1,0},{2,1},{3,2},{4,7},{5,4},{6,5},{7,6},{8,11},{9,8},{10,9... | collective-permute-start | bytes 294920 | tf_op jit(solution)/shard_map/ppermute | solution.py:202
  34.7 8.8 %collective-permute-done.3.refs_2_ = bf16[64,768]{1,0:T(8,128)(2,1)S(1)} collective-permute-done((bf16[64,768]{1,0:T(8,128)(2,1)S(1)}, bf16[64,768]{1,0:T(8,128)(2,1)S(1)}, u32[]{:S(2)}, u32[]{:S(2)}) %collective-permute-start.3) | collective-permute-done | bytes 98336 | tf_op jit(solution)/shard_map/ppermute | solution.py:202
  43.5 0.0 collective-permute-done.4.refs_3_
  43.5 0.0 collective-permute-done.2.refs_1_
  43.5 0.9 pick_rows.2
  44.4 0.0 copy-start
  44.4 1.0 %copy-done = bf16[128,4864]{1,0:T(8,128)(2,1)} copy-done((bf16[128,4864]{1,0:T(8,128)(2,1)}, bf16[128,4864]{1,0:T(8,128)(2,1)S(1)}, u32[]{:S(2)}) %copy-start) | copy-done | bytes 1245208
  45.4 0.0 all-to-all-done.1
  45.4 3.5 %all-to-all-start = ((bf16[4,32,4864]{2,1,0:T(8,128)(2,1)}), bf16[4,32,4864]{2,1,0:T(8,128)(2,1)S(1)}, u32[]{:S(2)}, u32[]{:S(2)}) async-start(bf16[4,32,4864]{2,1,0:T(8,128)(2,1)} %bitcast.42), calls=%async_computation | async-start | bytes 2490368 | tf_op jit(solution)/shard_map/all_to_all | solution.py:235
  49.0 0.1 collective-permute-start.6
  49.1 14.2 %all-to-all-done = bf16[4,32,4864]{2,1,0:T(8,128)(2,1)S(1)} async-done(((bf16[4,32,4864]{2,1,0:T(8,128)(2,1)}), bf16[4,32,4864]{2,1,0:T(8,128)(2,1)S(1)}, u32[]{:S(2)}, u32[]{:S(2)}) %all-to-all-start) | async-done | bytes 1245216 | tf_op jit(solution)/shard_map/all_to_all | solution.py:235
  63.3 0.0 collective-permute-start.7
  63.3 6.7 %returned_rows.2.refs_0_ = bf16[128,768]{1,0:T(8,128)(2,1)S(1)} custom-call(s32[1]{0:T(128)} %bitcast.2.near_ref, bf16[128,4864]{1,0:T(8,128)(2,1)S(1)} %bitcast.40, bf16[768,4096]{1,0:T(8,128)(2,1)} %bitcast.43), custom_call_target="tpu_custom_call" | custom-call | flops 805306368 | bytes 6291456 | tf_op jit(solution)/shard_map/returned_rows/pallas_call | solution.py:151
  70.0 7.9 %returned_rows.3 = bf16[256,768]{1,0:T(8,128)(2,1)} custom-call(s32[1]{0:T(128)} %bitcast.2.near_ref, bf16[128,4864]{1,0:T(8,128)(2,1)S(1)} %bitcast.37, bf16[768,4096]{1,0:T(8,128)(2,1)} %bitcast.44, bf16[128,768]{1,0:T(8,128)(2,1)S(1)} %returned_rows.2.refs_0_), custom_call_target="tpu_custom_call" | custom-call | flops 805306368 | bytes 6291456 | tf_op jit(solution)/shard_map/returned_rows/pallas_call | solution.py:151
  77.9 4.5 %all-to-all-start.2 = ((bf16[16,16,768]{2,1,0:T(8,128)(2,1)}), bf16[16,16,768]{2,1,0:T(8,128)(2,1)S(1)}, u32[]{:S(2)}, u32[]{:S(2)}) async-start(bf16[16,16,768]{2,1,0:T(8,128)(2,1)} %bitcast.9), calls=%async_computation.2 | async-start | bytes 786432 | tf_op jit(solution)/shard_map/all_to_all | solution.py:245
  82.4 0.0 collective-permute-done.6.refs_2_
  82.4 0.0 collective-permute-done.7.refs_3_
  82.4 0.0 copy-start.1
  82.5 6.8 %down_rows.1 = bf16[384,4096]{1,0:T(8,128)(2,1)} custom-call(s32[1]{0:T(128)} %bitcast.10.replica_ref, bf16[128,4864]{1,0:T(8,128)(2,1)S(1)} %bitcast.41, bf16[128,4864]{1,0:T(8,128)(2,1)S(1)} %bitcast.38, bf16[128,4864]{1,0:T(8,128)(2,1)} %collective-permute-done.6.refs_2_, bf16[128,4864]{1,0:T(8,128)(2,1)} %collective-permute-done.7.refs_3_), custom_call_target="tpu_custom_call" | custom-call | flops 1610612736 | bytes 7340032 | tf_op jit(solution)/shard_map/down_rows/pallas_call | solution.py:171
  89.2 7.2 %all-to-all-done.2 = bf16[16,16,768]{2,1,0:T(8,128)(2,1)S(1)} async-done(((bf16[16,16,768]{2,1,0:T(8,128)(2,1)}), bf16[16,16,768]{2,1,0:T(8,128)(2,1)S(1)}, u32[]{:S(2)}, u32[]{:S(2)}) %all-to-all-start.2) | async-done | bytes 393248 | tf_op jit(solution)/shard_map/all_to_all | solution.py:245
  96.5 0.0 copy-done.1
  96.5 1.1 %fusion.1 = (f32[32,8]{1,0:T(8,128)S(1)}, bf16[32,8,768]{2,1,0:T(8,128)(2,1)}) fusion(bf16[32,8,768]{2,1,0:T(8,128)(2,1)S(1)} %copy-done.1, f32[32,8]{1,0:T(8,128)S(1)} %copy.21, bf16[256,768,1]{1,0,2:T(8,128)(2,1)S(1)} %bitcast.46, s32[256]{0:T(256)S(1)} %get-tuple-element.19), kind=kOutput, calls=%fused_computation.4 | convolution fusion | flops 101711616 | bytes 1182720 | tf_op jit(solution)/shard_map/dot_general | solution.py:257
  97.6 0.7 copy.26
  (5 shorter events, 0.1 us)
Async XLA Ops:
  2.4 13.7 %collective-permute-start = (bf16[32,4224]{1,0:T(8,128)(2,1)S(1)}, bf16[32,4224]{1,0:T(8,128)(2,1)S(1)}, u32[]{:S(2)}, u32[]{:S(2)}) collective-permute-start(bf16[32,4224]{1,0:T(8,128)(2,1)S(1)} %fusion.6.refs_0_), channel_id=1, source_target_pairs={{0,1},{1,2},{2,3},{3,0},{4,5},{5,6},{6,7},{7,4},{8,9},{9,10},{10,1... | collective-permute-start | bytes 811016 | tf_op jit(solution)/shard_map/ppermute | solution.py:202
  9.5 6.6 %collective-permute-start.5 = (bf16[64,768]{1,0:T(8,128)(2,1)S(1)}, bf16[64,768]{1,0:T(8,128)(2,1)S(1)}, u32[]{:S(2)}, u32[]{:S(2)}) collective-permute-start(bf16[64,768]{1,0:T(8,128)(2,1)S(1)} %get-tuple-element.15), channel_id=1, source_target_pairs={{0,1},{1,2},{2,3},{3,0},{4,5},{5,6},{6,7},{7,4},{8,9},{9,10},{10,1... | collective-permute-start | bytes 294920 | tf_op jit(solution)/shard_map/ppermute | solution.py:202
  18.0 27.4 %all-to-all-start.1 = ((bf16[4,32,4864]{2,1,0:T(8,128)(2,1)}), bf16[4,32,4864]{2,1,0:T(8,128)(2,1)S(1)}, u32[]{:S(2)}, u32[]{:S(2)}) async-start(bf16[4,32,4864]{2,1,0:T(8,128)(2,1)} %bitcast.7), calls=%async_computation.1 | async-start | bytes 2490368 | tf_op jit(solution)/shard_map/all_to_all | solution.py:235
  21.7 9.2 %collective-permute-start.1 = (bf16[32,4224]{1,0:T(8,128)(2,1)S(1)}, bf16[32,4224]{1,0:T(8,128)(2,1)S(1)}, u32[]{:S(2)}, u32[]{:S(2)}) collective-permute-start(bf16[32,4224]{1,0:T(8,128)(2,1)S(1)} %collective-permute-done.refs_1_), channel_id=1, source_target_pairs={{0,1},{1,2},{2,3},{3,0},{4,5},{5,6},{6,7},{7,4},{8,9},{9,10},{10,1... | collective-permute-start | bytes 811016 | tf_op jit(solution)/shard_map/ppermute | solution.py:202
  30.9 12.7 %collective-permute-start.2 = (bf16[32,4224]{1,0:T(8,128)(2,1)S(1)}, bf16[32,4224]{1,0:T(8,128)(2,1)S(1)}, u32[]{:S(2)}, u32[]{:S(2)}) collective-permute-start(bf16[32,4224]{1,0:T(8,128)(2,1)S(1)} %collective-permute-done.1.refs_0_), channel_id=1, source_target_pairs={{0,1},{1,2},{2,3},{3,0},{4,5},{5,6},{6,7},{7,4},{8,9},{9,10},{10,1... | collective-permute-start | bytes 811016 | tf_op jit(solution)/shard_map/ppermute | solution.py:202
  30.9 12.7 %collective-permute-start.3 = (bf16[64,768]{1,0:T(8,128)(2,1)S(1)}, bf16[64,768]{1,0:T(8,128)(2,1)S(1)}, u32[]{:S(2)}, u32[]{:S(2)}) collective-permute-start(bf16[64,768]{1,0:T(8,128)(2,1)S(1)} %get-tuple-element.18), channel_id=1, source_target_pairs={{0,2},{1,3},{2,0},{3,1},{4,6},{5,7},{6,4},{7,5},{8,10},{9,11},{10,... | collective-permute-start | bytes 294920 | tf_op jit(solution)/shard_map/ppermute | solution.py:202
  31.2 12.3 %collective-permute-start.4 = (bf16[64,768]{1,0:T(8,128)(2,1)S(1)}, bf16[64,768]{1,0:T(8,128)(2,1)S(1)}, u32[]{:S(2)}, u32[]{:S(2)}) collective-permute-start(bf16[64,768]{1,0:T(8,128)(2,1)S(1)} %get-tuple-element.17), channel_id=1, source_target_pairs={{0,3},{1,0},{2,1},{3,2},{4,7},{5,4},{6,5},{7,6},{8,11},{9,8},{10,9... | collective-permute-start | bytes 294920 | tf_op jit(solution)/shard_map/ppermute | solution.py:202
  44.4 1.0 %copy-start = (bf16[128,4864]{1,0:T(8,128)(2,1)}, bf16[128,4864]{1,0:T(8,128)(2,1)S(1)}, u32[]{:S(2)}) copy-start(bf16[128,4864]{1,0:T(8,128)(2,1)S(1)} %pick_rows.2) | copy-start | bytes 3735556
  45.4 17.9 %all-to-all-start = ((bf16[4,32,4864]{2,1,0:T(8,128)(2,1)}), bf16[4,32,4864]{2,1,0:T(8,128)(2,1)S(1)}, u32[]{:S(2)}, u32[]{:S(2)}) async-start(bf16[4,32,4864]{2,1,0:T(8,128)(2,1)} %bitcast.42), calls=%async_computation | async-start | bytes 2490368 | tf_op jit(solution)/shard_map/all_to_all | solution.py:235
  49.0 33.5 %collective-permute-start.6 = (bf16[128,4864]{1,0:T(8,128)(2,1)S(1)}, bf16[128,4864]{1,0:T(8,128)(2,1)}, u32[]{:S(2)}, u32[]{:S(2)}) collective-permute-start(bf16[128,4864]{1,0:T(8,128)(2,1)S(1)} %bitcast.39), channel_id=1, source_target_pairs={{0,16},{16,0},{1,17},{17,1},{2,18},{18,2},{3,19},{19,3},{4,20},{20... | collective-permute-start | bytes 3735560 | tf_op jit(solution)/shard_map/ppermute | solution.py:205
  63.3 19.1 %collective-permute-start.7 = (bf16[128,4864]{1,0:T(8,128)(2,1)S(1)}, bf16[128,4864]{1,0:T(8,128)(2,1)}, u32[]{:S(2)}, u32[]{:S(2)}) collective-permute-start(bf16[128,4864]{1,0:T(8,128)(2,1)S(1)} %bitcast.36), channel_id=1, source_target_pairs={{0,16},{16,0},{1,17},{17,1},{2,18},{18,2},{3,19},{19,3},{4,20},{20... | collective-permute-start | bytes 3735560 | tf_op jit(solution)/shard_map/ppermute | solution.py:205
  77.9 18.6 %all-to-all-start.2 = ((bf16[16,16,768]{2,1,0:T(8,128)(2,1)}), bf16[16,16,768]{2,1,0:T(8,128)(2,1)S(1)}, u32[]{:S(2)}, u32[]{:S(2)}) async-start(bf16[16,16,768]{2,1,0:T(8,128)(2,1)} %bitcast.9), calls=%async_computation.2 | async-start | bytes 786432 | tf_op jit(solution)/shard_map/all_to_all | solution.py:245
  82.4 14.0 %copy-start.1 = (bf16[32,8,768]{2,1,0:T(8,128)(2,1)S(1)}, bf16[32,8,768]{2,1,0:T(8,128)(2,1)}, u32[]{:S(2)}) copy-start(bf16[32,8,768]{2,1,0:T(8,128)(2,1)} %param.6) | copy-start | bytes 1179652

commit v5 on v4

--- a/solution.py
+++ b/solution.py
@@ -20,49 +20,70 @@
     return jnp.dot(one_hot, values, preferred_element_type=jnp.float32)
 
 
-def pick_kernel(far_count, near_count, capacity, near_ref, *refs):
+def send_kernel(far_count, near_count, capacity, near_ref, ids_ref, gates_ref, hidden_ref, *refs):
+    sends, back_ref = refs[:-1], refs[-1]
+    tok_local, top_count = ids_ref.shape
+    hidden_width = hidden_ref.shape[1]
+    rows = tok_local * top_count
+    experts = far_count * near_count
+    slots = experts * capacity
+    near = near_ref[0]
+    wide = jnp.where(iota((top_count, rows), 1) % top_count == iota((top_count, rows), 0), 1.0, 0.0).astype(jnp.bfloat16)
+    mine = iota((tok_local, rows), 1) // top_count == iota((tok_local, rows), 0)
+
+    def line(values):
+        spread = jnp.zeros((tok_local, rows), jnp.float32)
+        for _ in range(3):
+            piece = values.astype(jnp.bfloat16)
+            values = values - piece.astype(jnp.float32)
+            spread = spread + exact_dot(piece, wide)
+        return jnp.sum(jnp.where(mine, spread, 0.0), axis=0, keepdims=True)
+
+    ids = line(ids_ref[...].astype(jnp.float32)).astype(jnp.int32)
+    gates = line(gates_ref[...])
+    named = iota((experts, rows), 0) == ids
+    before = jnp.where(iota((rows, rows), 0) < iota((rows, rows), 1), 1.0, 0.0).astype(jnp.bfloat16)
+    counts = exact_dot(jnp.where(named, 1.0, 0.0).astype(jnp.bfloat16), before)
+    ranks = jnp.sum(jnp.where(named, counts, 0.0), axis=0, keepdims=True).astype(jnp.int32)
+    steps = (ids % near_count - near + near_count) % near_count
+    out_slots = (steps * far_count + ids // near_count) * capacity + ranks
+    back_slots = ids * capacity + ranks
+    back_ref[...] = jnp.where(iota((slots, rows), 0) == back_slots, 1.0, 0.0).astype(jnp.bfloat16)
+    lines = far_count * capacity
+    tokens = (iota((lines, rows), 1) // top_count + 1).astype(jnp.float32)
+    for step, ref in enumerate(sends):
+        place = iota((lines, rows), 0) + step * lines == out_slots
+        gate = jnp.sum(jnp.where(place, gates, 0.0), axis=1, keepdims=True)
+        token = jnp.sum(jnp.where(place, tokens, 0.0), axis=1, keepdims=True) - 1.0
+        picked = exact_dot(jnp.where(place, 1.0, 0.0).astype(jnp.bfloat16), hidden_ref[...])
+        ref[:, :hidden_width] = (picked * gate).astype(jnp.bfloat16)
+        ref[:, hidden_width:] = jnp.broadcast_to(token, (lines, ID_COLS)).astype(jnp.bfloat16)
+
+
+def pick_kernel(far_count, capacity, *refs):
     out_ref = refs[-1]
     count = (len(refs) - 1) // 2
     blocks, hids = refs[:count], refs[count:-1]
-    tok_local = blocks[0].shape[0]
-    width = blocks[0].shape[1] - ID_COLS
-    near = near_ref[0]
+    tok_local, width = blocks[0].shape
+    hidden_width = hids[0].shape[1] - ID_COLS
     cols = count * tok_local
     slots = far_count * count * capacity
-    ids = jnp.concatenate([block[:, width:] for block in blocks], axis=0).astype(jnp.float32)
-    lead = max(8, far_count)
-    ones = jnp.ones((lead, ID_COLS), jnp.bfloat16)
-    named = jnp.zeros((lead, cols), jnp.float32)
-    for j in range(far_count):
-        expert = (j * near_count + near).astype(jnp.float32)
-        hit = jnp.where(ids == expert, 1.0, 0.0).astype(jnp.bfloat16)
-        line = lax.dot_general(ones, hit, (((1,), (1,)), ((), ())), preferred_element_type=jnp.float32)
-        named = jnp.where(iota((lead, cols), 0) == j, line, named)
-    row, col = iota((cols, cols), 0), iota((cols, cols), 1)
-    before = jnp.where((row < col) & (row // tok_local == col // tok_local), 1.0, 0.0).astype(jnp.bfloat16)
-    named = named.astype(jnp.bfloat16)
-    rank = exact_dot(named, before).astype(jnp.bfloat16)
-    per_far = count * capacity
-    spread = jnp.where(iota((slots, lead), 0) // per_far == iota((slots, lead), 1), 1.0, 0.0).astype(jnp.bfloat16)
-    slot = iota((slots, cols), 0) % per_far
-    pick = (
-        (exact_dot(spread, named) > 0.5)
-        & (iota((slots, cols), 1) // tok_local == slot // capacity)
-        & (exact_dot(spread, rank).astype(jnp.int32) == slot % capacity)
-    )
+    per_far, per_block = count * capacity, far_count * capacity
+    out_row, in_row = iota((slots, slots), 0), iota((slots, slots), 1)
+    source = (
+        (out_row % per_far // capacity) * per_block + (out_row // per_far) * capacity + out_row % capacity
+    )
+    order = jnp.where(in_row == source, 1.0, 0.0).astype(jnp.bfloat16)
+    hid = exact_dot(order, jnp.concatenate([hid[...] for hid in hids], axis=0))
+    out_ref[:, width:] = hid[:, :hidden_width].astype(jnp.bfloat16)
+    token = hid[:, hidden_width : hidden_width + cols].astype(jnp.int32)
+    row, col = iota((slots, cols), 0), iota((slots, cols), 1)
+    pick = (token == col % tok_local) & (col // tok_local == row % per_far // capacity)
     pick = jnp.where(pick, 1.0, 0.0).astype(jnp.bfloat16)
     step = min(width, 512)
     for start in range(0, width, step):
         tokens = jnp.concatenate([block[:, start : start + step] for block in blocks], axis=0)
         out_ref[:, start : start + step] = exact_dot(pick, tokens).astype(jnp.bfloat16)
-    out_row, in_row = iota((slots, slots), 0), iota((slots, slots), 1)
-    per_block = far_count * capacity
-    source = (
-        (out_row % per_far // capacity) * per_block + (out_row // per_far) * capacity + out_row % capacity
-    )
-    order = jnp.where(in_row == source, 1.0, 0.0).astype(jnp.bfloat16)
-    hid = jnp.concatenate([hid[...] for hid in hids], axis=0)
-    out_ref[:, width:] = exact_dot(order, hid).astype(jnp.bfloat16)
 
 
 def returned_kernel(far_count, near_count, capacity, near_ref, rows_ref, weight_ref, *refs):
@@ -76,12 +97,12 @@
 
     cols = pl.ds(pl.multiple_of(step * tile, 128), tile)
     total_ref[...] += lax.dot_general(
-        rows_ref[:, cols], weight_ref[...], (((1,), (1,)), ((), ())), preferred_element_type=jnp.float32
+        weight_ref[...], rows_ref[:, cols], (((1,), (1,)), ((), ())), preferred_element_type=jnp.float32
     )
 
     @pl.when(step == pl.num_programs(0) - 1)
     def _():
-        own = total_ref[...].astype(jnp.bfloat16)
+        own = total_ref[...].T.astype(jnp.bfloat16)
         if not earlier:
             out_ref[...] = own
             return
@@ -127,19 +148,36 @@
     return pltpu.CompilerParams(vmem_limit_bytes=VMEM_LIMIT)
 
 
-def pick_rows(far_count, near_count, capacity, near, blocks, hids):
-    width = blocks[0].shape[1] - ID_COLS
+def send_rows(far_count, near_count, capacity, near, ids, gates, hidden):
+    lines = far_count * capacity
+    wide = hidden.shape[1] + ID_COLS
+    rows = hidden.shape[0]
+    vmem = pl.BlockSpec(memory_space=pltpu.VMEM)
+    return pl.pallas_call(
+        functools.partial(send_kernel, far_count, near_count, capacity),
+        out_shape=[jax.ShapeDtypeStruct((lines, wide), jnp.bfloat16)] * near_count
+        + [jax.ShapeDtypeStruct((near_count * lines, rows), jnp.bfloat16)],
+        in_specs=[scalar_spec()] + [vmem] * 3,
+        out_specs=[vmem] * (near_count + 1),
+        compiler_params=params(),
+        cost_estimate=pl.CostEstimate(flops=2 * rows * rows * wide, bytes_accessed=4 * rows * wide, transcendentals=0),
+        name="send_rows",
+    )(near, ids, gates, hidden)
+
+
+def pick_rows(far_count, capacity, blocks, hids):
+    width = blocks[0].shape[1]
     slots = far_count * capacity * len(blocks)
-    shape = (slots, width + hids[0].shape[1])
+    shape = (slots, width + hids[0].shape[1] - ID_COLS)
     return pl.pallas_call(
-        functools.partial(pick_kernel, far_count, near_count, capacity),
+        functools.partial(pick_kernel, far_count, capacity),
         out_shape=jax.ShapeDtypeStruct(shape, jnp.bfloat16),
-        in_specs=[scalar_spec()] + [pl.BlockSpec(memory_space=pltpu.VMEM)] * (2 * len(blocks)),
+        in_specs=[pl.BlockSpec(memory_space=pltpu.VMEM)] * (2 * len(blocks)),
         out_specs=pl.BlockSpec(memory_space=pltpu.VMEM),
         compiler_params=params(),
         cost_estimate=pl.CostEstimate(flops=2 * slots * 64 * shape[1], bytes_accessed=4 * slots * shape[1], transcendentals=0),
         name="pick_rows",
-    )(near, *blocks, *hids)
+    )(*blocks, *hids)
 
 
 def returned_rows(far_count, near_count, capacity, near, rows, weight, earlier):
@@ -155,7 +193,7 @@
         in_specs=[scalar_spec(), whole(rows), pl.BlockSpec((hidden_width, tile), lambda i: (0, i))]
         + [whole(array) for array in earlier],
         out_specs=pl.BlockSpec((total, hidden_width), lambda i: (0, 0)),
-        scratch_shapes=[pltpu.VMEM((lines, hidden_width), jnp.float32)],
+        scratch_shapes=[pltpu.VMEM((hidden_width, lines), jnp.float32)],
         compiler_params=params(),
         cost_estimate=pl.CostEstimate(
             flops=2 * lines * width * hidden_width, bytes_accessed=2 * width * hidden_width, transcendentals=0
@@ -204,38 +242,28 @@
     def swap(array):
         return lax.ppermute(array, "dp", [(i, i ^ 1) for i in range(lax.axis_size("dp"))])
 
-    id_cols = jnp.pad(
-        expert_ids.astype(jnp.bfloat16), ((0, 0), (0, ID_COLS - top_count)), constant_values=-1
-    )
-    blocks = [jnp.concatenate([grad_out, id_cols], axis=1)]
-    for _ in range(1, near_count):
-        blocks.append(along(blocks[-1], 1))
-
-    flat_ids = expert_ids.reshape(-1)
-    one_hot = (flat_ids[:, None] == jnp.arange(experts, dtype=jnp.int32)[None, :]).astype(jnp.int32)
-    ranks = jnp.sum(jnp.cumsum(one_hot, axis=0) * one_hot, axis=1) - 1
-    steps = (flat_ids % near_count - near + near_count) % near_count
-    out_slots = (steps * far_count + flat_ids // near_count) * capacity + ranks
-    back_slots = flat_ids * capacity + ranks
-    slot_range = jnp.arange(slot_total, dtype=jnp.int32)[:, None]
-    out_place = (slot_range == out_slots[None, :]).astype(jnp.bfloat16)
-    back_place = (slot_range == back_slots[None, :]).astype(jnp.bfloat16)
-    scaled = (
-        (gates[:, :, None] * hidden.astype(jnp.float32))
-        .astype(jnp.bfloat16)
-        .reshape(row_total, hidden_width)
-    )
-    send_hid = exact_dot(out_place, scaled).astype(jnp.bfloat16).reshape(near_count, -1, hidden_width)
-    hids = [send_hid[0]] + [along(send_hid[step], step) for step in range(1, near_count)]
+    blocks = [grad_out, along(grad_out, 1)]
+    *sends, back_place = send_rows(
+        far_count, near_count, capacity, near_ref, expert_ids, gates, hidden.reshape(row_total, hidden_width)
+    )
+    later, sends[1] = lax.optimization_barrier((grad_out, sends[1]))
+    hids = [sends[0]] + [along(sends[step], step) for step in range(1, near_count)]
+    blocks += [along(later, step) for step in range(2, near_count)]
 
     rows, peers, returned = [], [], []
     for turn in range(ROUNDS):
         part = slice(turn * count, (turn + 1) * count)
-        picked = pick_rows(far_count, near_count, capacity, near_ref, blocks[part], hids[part])
+        picked = pick_rows(far_count, capacity, blocks[part], hids[part])
+        if rows:
+            picked, rows[-1] = lax.optimization_barrier((picked, rows[-1]))
         got = lax.all_to_all(
             picked.reshape(far_count, -1, picked.shape[1]), "far", split_axis=0, concat_axis=0, tiled=True
         ).reshape(picked.shape)
         rows.append(got)
+    for turn in range(ROUNDS):
+        if returned:
+            rows[turn], returned[-1] = lax.optimization_barrier((rows[turn], returned[-1]))
+        got = rows[turn]
         peers.append(swap(got))
         returned.append(
             returned_rows(

time: 99 us -> 97.4 us (0.984)
  starting transfers between devices: 20.4 us -> 24.7 us
  waiting for transfers between devices: 44.4 us -> 40.6 us
  other arithmetic: 2.41 us -> 0 us
  local copies, waits for them, and re-layouts: 3.71 us -> 5.27 us
  matrix products: 2.43 us -> 1.03 us
    all_to_all x2, waiting for transfers between devices: 14.2 us -> 9.03 us  [local(): lax.all_to_all(picked.reshape(far_count, -1, picked.shape[1]), 'far', spl...]
    all_to_all x1, starting transfers between devices: 4.49 us -> 7.19 us  [local(): lax.all_to_all(returned[-1].reshape(experts, capacity, hidden_width), ('f...]
    unnamed x7 -> x13, local copies, waits for them, and re-layouts: 3.23 us -> 5.17 us
    ppermute x6, waiting for transfers between devices: 22.9 us -> 24.5 us  [along(): lax.ppermute(array, 'near', [(i, (i + steps) % near_count) for i in range...]
    dot_general x1 -> x0, matrix products: 1.35 us -> none  [exact_dot(): return jnp.dot(one_hot, values, preferred_element_type=jnp.float32)]
    ppermute x6, starting transfers between devices: 8.53 us -> 9.81 us  [along(): lax.ppermute(array, 'near', [(i, (i + steps) % near_count) for i in range...]
    pallas_call x2 -> x3, Pallas kernels: 2.76 us -> 2.95 us  [the longest x2 2.25 us: pick_rows(): pl.pallas_call(functools.partial(pick_kernel, far_count, capacity), out_s...]
  transfers between devices with their start and end apart: 11 -> 11, of which waited for: 5 -> 4; matrix products, arithmetic and copies ran while one was open for 4% -> 2% of each run, Pallas kernels for 23% -> 23%
where the time goes in v5:
time: 97.4 us; the launch traced here: 96.6 us
  waiting for transfers between devices  40.6 us (42%)
  starting transfers between devices  24.7 us (25%)
  Pallas kernels  24.3 us (25%)
  local copies, waits for them, and re-layouts  5.27 us (5%)
  matrix products  1.03 us (1%)
    ppermute x6, waiting for transfers between devices, along(): lax.ppermute(array, 'near', [(i, (i + steps) % near_count) for i in range...  24.5 us
    pallas_call x2, Pallas kernels, returned_rows(): pl.pallas_call(functools.partial(returned_kernel, far_count, near_count,...  14.6 us
    ppermute x6, starting transfers between devices, along(): lax.ppermute(array, 'near', [(i, (i + steps) % near_count) for i in range...  9.81 us
    all_to_all x2, waiting for transfers between devices, local(): lax.all_to_all(picked.reshape(far_count, -1, picked.shape[1]), 'far', spl...  9.03 us
    all_to_all x2, starting transfers between devices, local(): lax.all_to_all(picked.reshape(far_count, -1, picked.shape[1]), 'far', spl...  7.68 us
    all_to_all x1, starting transfers between devices, local(): lax.all_to_all(returned[-1].reshape(experts, capacity, hidden_width), ('f...  7.19 us
    all_to_all x1, waiting for transfers between devices, local(): lax.all_to_all(returned[-1].reshape(experts, capacity, hidden_width), ('f...  7.14 us
    pallas_call x1, Pallas kernels, down_rows(): pl.pallas_call(functools.partial(down_kernel, width), grid=(width // tile...  6.77 us
  transfers between devices with their start and end apart: 11, of which 4 were waited for; matrix products, arithmetic and copies ran while one was open for 2% of the time, Pallas kernels for 23%

profile of v5, /device:TPU:0, one launch (start us, length us, event | category | flops | bytes accessed | tf_op | source)
XLA Modules:
  0.0 96.6 jit_solution(1982316930029772586)
XLA Ops:
  0.6 3.1 %collective-permute-start.4 = (bf16[32,4096]{1,0:T(8,128)(2,1)}, bf16[32,4096]{1,0:T(8,128)(2,1)S(1)}, u32[]{:S(2)}, u32[]{:S(2)}) collective-permute-start(bf16[32,4096]{1,0:T(8,128)(2,1)} %refs_0_.1), channel_id=1, source_target_pairs={{0,1},{1,2},{2,3},{3,0},{4,5},{5,6},{6,7},{7,4},{8,9},{9,10},{10,1... | collective-permute-start | bytes 786440 | tf_op jit(solution)/shard_map/ppermute | solution.py:240
  3.7 0.8 copy.16.gates_ref
  4.5 0.8 copy.17.ids_ref
  5.2 0.0 copy-start.1
  5.2 1.0 %copy-done.1 = bf16[32,8,768]{2,1,0:T(8,128)(2,1)S(1)} copy-done((bf16[32,8,768]{2,1,0:T(8,128)(2,1)S(1)}, bf16[32,8,768]{2,1,0:T(8,128)(2,1)}, u32[]{:S(2)}) %copy-start.1) | copy-done | bytes 393240
  6.2 0.7 send_rows.1
  6.9 1.6 %collective-permute-start.5 = (bf16[64,896]{1,0:T(8,128)(2,1)S(1)}, bf16[64,896]{1,0:T(8,128)(2,1)S(1)}, u32[]{:S(2)}, u32[]{:S(2)}) collective-permute-start(bf16[64,896]{1,0:T(8,128)(2,1)S(1)} %get-tuple-element.22), channel_id=1, source_target_pairs={{0,1},{1,2},{2,3},{3,0},{4,5},{5,6},{6,7},{7,4},{8,9},{9,10},{10,1... | collective-permute-start | bytes 344072 | tf_op jit(solution)/shard_map/ppermute | solution.py:240
  8.6 6.2 %collective-permute-done.5.refs_3_ = bf16[64,896]{1,0:T(8,128)(2,1)S(1)} collective-permute-done((bf16[64,896]{1,0:T(8,128)(2,1)S(1)}, bf16[64,896]{1,0:T(8,128)(2,1)S(1)}, u32[]{:S(2)}, u32[]{:S(2)}) %collective-permute-start.5) | collective-permute-done | bytes 114720 | tf_op jit(solution)/shard_map/ppermute | solution.py:240
  14.7 0.0 collective-permute-done.4.refs_1_
  14.7 0.0 copy-start.3
  14.7 0.9 copy-done.3
  15.7 1.7 %pick_rows.3 = bf16[128,4864]{1,0:T(8,128)(2,1)} custom-call(bf16[32,4096]{1,0:T(8,128)(2,1)S(1)} %copy-done.3, bf16[32,4096]{1,0:T(8,128)(2,1)S(1)} %collective-permute-done.4.refs_1_, bf16[64,896]{1,0:T(8,128)(2,1)S(1)} %get-tuple-element.21.refs_2_, bf16[64,896]{1,0:T(8,128)(2,1)S(1)} %collective-permute-done.5.refs_3_), custom_call_target="tpu_custom_call" | custom-call | flops 79691776 | bytes 2490368 | tf_op jit(solution)/shard_map/pick_rows/pallas_call | solution.py:172
  17.3 0.0 copy-start.4
  17.3 3.8 %all-to-all-start = ((bf16[4,32,4864]{2,1,0:T(8,128)(2,1)}), bf16[4,32,4864]{2,1,0:T(8,128)(2,1)S(1)}, u32[]{:S(2)}, u32[]{:S(2)}) async-start(bf16[4,32,4864]{2,1,0:T(8,128)(2,1)} %bitcast.4), calls=%async_computation | async-start | bytes 2490368 | tf_op jit(solution)/shard_map/all_to_all | solution.py:259
  21.2 0.0 copy-done.4
  21.2 0.7 collective-permute-start
  21.9 1.3 %collective-permute-start.1 = (bf16[32,4096]{1,0:T(8,128)(2,1)S(1)}, bf16[32,4096]{1,0:T(8,128)(2,1)S(1)}, u32[]{:S(2)}, u32[]{:S(2)}) collective-permute-start(bf16[32,4096]{1,0:T(8,128)(2,1)S(1)} %copy-done.4), channel_id=1, source_target_pairs={{0,3},{1,0},{2,1},{3,2},{4,7},{5,4},{6,5},{7,6},{8,11},{9,8},{10,9... | collective-permute-start | bytes 786440 | tf_op jit(solution)/shard_map/ppermute | solution.py:240
  23.2 1.7 %collective-permute-start.2 = (bf16[64,896]{1,0:T(8,128)(2,1)S(1)}, bf16[64,896]{1,0:T(8,128)(2,1)S(1)}, u32[]{:S(2)}, u32[]{:S(2)}) collective-permute-start(bf16[64,896]{1,0:T(8,128)(2,1)S(1)} %get-tuple-element.19), channel_id=1, source_target_pairs={{0,2},{1,3},{2,0},{3,1},{4,6},{5,7},{6,4},{7,5},{8,10},{9,11},{10,... | collective-permute-start | bytes 344072 | tf_op jit(solution)/shard_map/ppermute | solution.py:240
  24.9 1.3 %collective-permute-start.3 = (bf16[64,896]{1,0:T(8,128)(2,1)S(1)}, bf16[64,896]{1,0:T(8,128)(2,1)S(1)}, u32[]{:S(2)}, u32[]{:S(2)}) collective-permute-start(bf16[64,896]{1,0:T(8,128)(2,1)S(1)} %get-tuple-element.20), channel_id=1, source_target_pairs={{0,3},{1,0},{2,1},{3,2},{4,7},{5,4},{6,5},{7,6},{8,11},{9,8},{10,9... | collective-permute-start | bytes 344072 | tf_op jit(solution)/shard_map/ppermute | solution.py:240
  26.3 18.3 %collective-permute-done.2.refs_2_ = bf16[64,896]{1,0:T(8,128)(2,1)S(1)} collective-permute-done((bf16[64,896]{1,0:T(8,128)(2,1)S(1)}, bf16[64,896]{1,0:T(8,128)(2,1)S(1)}, u32[]{:S(2)}, u32[]{:S(2)}) %collective-permute-start.2) | collective-permute-done | bytes 114720 | tf_op jit(solution)/shard_map/ppermute | solution.py:240
  44.6 0.0 collective-permute-done.3.refs_3_
  44.6 0.0 collective-permute-done.refs_0_
  44.6 0.0 collective-permute-done.1.refs_1_
  44.6 0.6 pick_rows.2
  45.2 0.0 copy-start
  45.2 1.0 %copy-done = bf16[128,4864]{1,0:T(8,128)(2,1)} copy-done((bf16[128,4864]{1,0:T(8,128)(2,1)}, bf16[128,4864]{1,0:T(8,128)(2,1)S(1)}, u32[]{:S(2)}) %copy-start) | copy-done | bytes 1245208
  46.2 0.0 all-to-all-done
  46.2 3.8 %all-to-all-start.1 = ((bf16[4,32,4864]{2,1,0:T(8,128)(2,1)}), bf16[4,32,4864]{2,1,0:T(8,128)(2,1)S(1)}, u32[]{:S(2)}, u32[]{:S(2)}) async-start(bf16[4,32,4864]{2,1,0:T(8,128)(2,1)} %bitcast.26), calls=%async_computation.1 | async-start | bytes 2490368 | tf_op jit(solution)/shard_map/all_to_all | solution.py:259
  50.1 0.0 collective-permute-start.6
  50.1 6.8 %returned_rows.2.refs_0_ = bf16[128,768]{1,0:T(8,128)(2,1)S(1)} custom-call(s32[1]{0:T(128)} %bitcast.near_ref, bf16[128,4864]{1,0:T(8,128)(2,1)S(1)} %bitcast.24, bf16[768,4096]{1,0:T(8,128)(2,1)} %bitcast.29), custom_call_target="tpu_custom_call" | custom-call | flops 805306368 | bytes 6291456 | tf_op jit(solution)/shard_map/returned_rows/pallas_call | solution.py:189
  56.8 9.0 %all-to-all-done.1 = bf16[4,32,4864]{2,1,0:T(8,128)(2,1)S(1)} async-done(((bf16[4,32,4864]{2,1,0:T(8,128)(2,1)}), bf16[4,32,4864]{2,1,0:T(8,128)(2,1)S(1)}, u32[]{:S(2)}, u32[]{:S(2)}) %all-to-all-start.1) | async-done | bytes 1245216 | tf_op jit(solution)/shard_map/all_to_all | solution.py:259
  65.9 0.0 collective-permute-start.7
  65.9 7.8 %returned_rows.3 = bf16[256,768]{1,0:T(8,128)(2,1)} custom-call(s32[1]{0:T(128)} %bitcast.near_ref, bf16[128,4864]{1,0:T(8,128)(2,1)S(1)} %bitcast.21, bf16[768,4096]{1,0:T(8,128)(2,1)} %bitcast.30, bf16[128,768]{1,0:T(8,128)(2,1)S(1)} %returned_rows.2.refs_0_), custom_call_target="tpu_custom_call" | custom-call | flops 805306368 | bytes 6291456 | tf_op jit(solution)/shard_map/returned_rows/pallas_call | solution.py:189
  73.7 7.2 %all-to-all-start.2 = ((bf16[16,16,768]{2,1,0:T(8,128)(2,1)}), bf16[16,16,768]{2,1,0:T(8,128)(2,1)S(1)}, u32[]{:S(2)}, u32[]{:S(2)}) async-start(bf16[16,16,768]{2,1,0:T(8,128)(2,1)} %bitcast.9), calls=%async_computation.2 | async-start | bytes 786432 | tf_op jit(solution)/shard_map/all_to_all | solution.py:273
  80.9 0.1 copy.19
  81.0 0.0 collective-permute-done.6.refs_2_
  81.0 0.0 collective-permute-done.7.refs_3_
  81.0 0.0 copy-start.2
  81.0 6.8 %down_rows.1 = bf16[384,4096]{1,0:T(8,128)(2,1)} custom-call(s32[1]{0:T(128)} %bitcast.10.replica_ref, bf16[128,4864]{1,0:T(8,128)(2,1)S(1)} %bitcast.25, bf16[128,4864]{1,0:T(8,128)(2,1)S(1)} %bitcast.22, bf16[128,4864]{1,0:T(8,128)(2,1)} %collective-permute-done.6.refs_2_, bf16[128,4864]{1,0:T(8,128)(2,1)} %collective-permute-done.7.refs_3_), custom_call_target="tpu_custom_call" | custom-call | flops 1610612736 | bytes 7340032 | tf_op jit(solution)/shard_map/down_rows/pallas_call | solution.py:209
  87.8 7.1 %all-to-all-done.2 = bf16[16,16,768]{2,1,0:T(8,128)(2,1)S(1)} async-done(((bf16[16,16,768]{2,1,0:T(8,128)(2,1)}), bf16[16,16,768]{2,1,0:T(8,128)(2,1)S(1)}, u32[]{:S(2)}, u32[]{:S(2)}) %all-to-all-start.2) | async-done | bytes 393248 | tf_op jit(solution)/shard_map/all_to_all | solution.py:273
  94.9 0.0 copy-done.2
  94.9 1.0 %multiply_reduce_fusion = (f32[32,8]{1,0:T(8,128)S(1)}, bf16[32,8,768]{2,1,0:T(8,128)(2,1)}) fusion(bf16[32,8,768]{2,1,0:T(8,128)(2,1)S(1)} %copy-done.2, f32[32,8]{1,0:T(8,128)S(1)} %copy.16.gates_ref, bf16[256,768,1]{1,0,2:T(8,128)(2,1)S(1)} %bitcast.32, bf16[256,256]{1,0:T(8,128)(2,1)S(1)} %copy.19), kind=kOutput, calls=%fused_computation | convolution fusion | flops 101646080 | bytes 1312768 | tf_op jit(solution)/shard_map/dot_general | solution.py:285
  96.0 0.7 copy.20
Async XLA Ops:
  0.6 14.1 %collective-permute-start.4 = (bf16[32,4096]{1,0:T(8,128)(2,1)}, bf16[32,4096]{1,0:T(8,128)(2,1)S(1)}, u32[]{:S(2)}, u32[]{:S(2)}) collective-permute-start(bf16[32,4096]{1,0:T(8,128)(2,1)} %refs_0_.1), channel_id=1, source_target_pairs={{0,1},{1,2},{2,3},{3,0},{4,5},{5,6},{6,7},{7,4},{8,9},{9,10},{10,1... | collective-permute-start | bytes 786440 | tf_op jit(solution)/shard_map/ppermute | solution.py:240
  5.2 1.0 %copy-start.1 = (bf16[32,8,768]{2,1,0:T(8,128)(2,1)S(1)}, bf16[32,8,768]{2,1,0:T(8,128)(2,1)}, u32[]{:S(2)}) copy-start(bf16[32,8,768]{2,1,0:T(8,128)(2,1)} %param.6) | copy-start | bytes 1179652
  6.9 7.8 %collective-permute-start.5 = (bf16[64,896]{1,0:T(8,128)(2,1)S(1)}, bf16[64,896]{1,0:T(8,128)(2,1)S(1)}, u32[]{:S(2)}, u32[]{:S(2)}) collective-permute-start(bf16[64,896]{1,0:T(8,128)(2,1)S(1)} %get-tuple-element.22), channel_id=1, source_target_pairs={{0,1},{1,2},{2,3},{3,0},{4,5},{5,6},{6,7},{7,4},{8,9},{9,10},{10,1... | collective-permute-start | bytes 344072 | tf_op jit(solution)/shard_map/ppermute | solution.py:240
  14.7 1.0 copy-start.3
  17.3 3.9 %copy-start.4 = (bf16[32,4096]{1,0:T(8,128)(2,1)S(1)}, bf16[32,4096]{1,0:T(8,128)(2,1)}, u32[]{:S(2)}) copy-start(bf16[32,4096]{1,0:T(8,128)(2,1)} %refs_0_.1) | copy-start | bytes 786436
  17.3 28.9 %all-to-all-start = ((bf16[4,32,4864]{2,1,0:T(8,128)(2,1)}), bf16[4,32,4864]{2,1,0:T(8,128)(2,1)S(1)}, u32[]{:S(2)}, u32[]{:S(2)}) async-start(bf16[4,32,4864]{2,1,0:T(8,128)(2,1)} %bitcast.4), calls=%async_computation | async-start | bytes 2490368 | tf_op jit(solution)/shard_map/all_to_all | solution.py:259
  21.2 23.4 %collective-permute-start = (bf16[32,4096]{1,0:T(8,128)(2,1)S(1)}, bf16[32,4096]{1,0:T(8,128)(2,1)S(1)}, u32[]{:S(2)}, u32[]{:S(2)}) collective-permute-start(bf16[32,4096]{1,0:T(8,128)(2,1)S(1)} %copy-done.4), channel_id=1, source_target_pairs={{0,2},{1,3},{2,0},{3,1},{4,6},{5,7},{6,4},{7,5},{8,10},{9,11},{10,... | collective-permute-start | bytes 786440 | tf_op jit(solution)/shard_map/ppermute | solution.py:240
  21.9 22.7 %collective-permute-start.1 = (bf16[32,4096]{1,0:T(8,128)(2,1)S(1)}, bf16[32,4096]{1,0:T(8,128)(2,1)S(1)}, u32[]{:S(2)}, u32[]{:S(2)}) collective-permute-start(bf16[32,4096]{1,0:T(8,128)(2,1)S(1)} %copy-done.4), channel_id=1, source_target_pairs={{0,3},{1,0},{2,1},{3,2},{4,7},{5,4},{6,5},{7,6},{8,11},{9,8},{10,9... | collective-permute-start | bytes 786440 | tf_op jit(solution)/shard_map/ppermute | solution.py:240
  23.2 21.3 %collective-permute-start.2 = (bf16[64,896]{1,0:T(8,128)(2,1)S(1)}, bf16[64,896]{1,0:T(8,128)(2,1)S(1)}, u32[]{:S(2)}, u32[]{:S(2)}) collective-permute-start(bf16[64,896]{1,0:T(8,128)(2,1)S(1)} %get-tuple-element.19), channel_id=1, source_target_pairs={{0,2},{1,3},{2,0},{3,1},{4,6},{5,7},{6,4},{7,5},{8,10},{9,11},{10,... | collective-permute-start | bytes 344072 | tf_op jit(solution)/shard_map/ppermute | solution.py:240
  24.9 19.6 %collective-permute-start.3 = (bf16[64,896]{1,0:T(8,128)(2,1)S(1)}, bf16[64,896]{1,0:T(8,128)(2,1)S(1)}, u32[]{:S(2)}, u32[]{:S(2)}) collective-permute-start(bf16[64,896]{1,0:T(8,128)(2,1)S(1)} %get-tuple-element.20), channel_id=1, source_target_pairs={{0,3},{1,0},{2,1},{3,2},{4,7},{5,4},{6,5},{7,6},{8,11},{9,8},{10,9... | collective-permute-start | bytes 344072 | tf_op jit(solution)/shard_map/ppermute | solution.py:240
  45.2 1.0 %copy-start = (bf16[128,4864]{1,0:T(8,128)(2,1)}, bf16[128,4864]{1,0:T(8,128)(2,1)S(1)}, u32[]{:S(2)}) copy-start(bf16[128,4864]{1,0:T(8,128)(2,1)S(1)} %pick_rows.2) | copy-start | bytes 3735556
  46.2 19.6 %all-to-all-start.1 = ((bf16[4,32,4864]{2,1,0:T(8,128)(2,1)}), bf16[4,32,4864]{2,1,0:T(8,128)(2,1)S(1)}, u32[]{:S(2)}, u32[]{:S(2)}) async-start(bf16[4,32,4864]{2,1,0:T(8,128)(2,1)} %bitcast.26), calls=%async_computation.1 | async-start | bytes 2490368 | tf_op jit(solution)/shard_map/all_to_all | solution.py:259
  50.1 30.9 %collective-permute-start.6 = (bf16[128,4864]{1,0:T(8,128)(2,1)S(1)}, bf16[128,4864]{1,0:T(8,128)(2,1)}, u32[]{:S(2)}, u32[]{:S(2)}) collective-permute-start(bf16[128,4864]{1,0:T(8,128)(2,1)S(1)} %bitcast.23), channel_id=1, source_target_pairs={{0,16},{16,0},{1,17},{17,1},{2,18},{18,2},{3,19},{19,3},{4,20},{20... | collective-permute-start | bytes 3735560 | tf_op jit(solution)/shard_map/ppermute | solution.py:243
  65.9 15.1 %collective-permute-start.7 = (bf16[128,4864]{1,0:T(8,128)(2,1)S(1)}, bf16[128,4864]{1,0:T(8,128)(2,1)}, u32[]{:S(2)}, u32[]{:S(2)}) collective-permute-start(bf16[128,4864]{1,0:T(8,128)(2,1)S(1)} %bitcast.20), channel_id=1, source_target_pairs={{0,16},{16,0},{1,17},{17,1},{2,18},{18,2},{3,19},{19,3},{4,20},{20... | collective-permute-start | bytes 3735560 | tf_op jit(solution)/shard_map/ppermute | solution.py:243
  73.7 21.3 %all-to-all-start.2 = ((bf16[16,16,768]{2,1,0:T(8,128)(2,1)}), bf16[16,16,768]{2,1,0:T(8,128)(2,1)S(1)}, u32[]{:S(2)}, u32[]{:S(2)}) async-start(bf16[16,16,768]{2,1,0:T(8,128)(2,1)} %bitcast.9), calls=%async_computation.2 | async-start | bytes 786432 | tf_op jit(solution)/shard_map/all_to_all | solution.py:273
  81.0 13.9 %copy-start.2 = (bf16[32,8,768]{2,1,0:T(8,128)(2,1)S(1)}, bf16[32,8,768]{2,1,0:T(8,128)(2,1)}, u32[]{:S(2)}) copy-start(bf16[32,8,768]{2,1,0:T(8,128)(2,1)} %param.6) | copy-start | bytes 1179652

commit v6 on v5

--- a/solution.py
+++ b/solution.py
@@ -8,7 +8,6 @@
 from jax.sharding import PartitionSpec as P
 
 ID_COLS = 128
-ROUNDS = 2
 VMEM_LIMIT = 48 * 1024 * 1024
 
 
@@ -22,17 +21,17 @@
 
 def send_kernel(far_count, near_count, capacity, near_ref, ids_ref, gates_ref, hidden_ref, *refs):
     sends, back_ref = refs[:-1], refs[-1]
-    tok_local, top_count = ids_ref.shape
+    top_count, tok_local = ids_ref.shape
     hidden_width = hidden_ref.shape[1]
     rows = tok_local * top_count
     experts = far_count * near_count
     slots = experts * capacity
     near = near_ref[0]
-    wide = jnp.where(iota((top_count, rows), 1) % top_count == iota((top_count, rows), 0), 1.0, 0.0).astype(jnp.bfloat16)
-    mine = iota((tok_local, rows), 1) // top_count == iota((tok_local, rows), 0)
+    wide = jnp.where(iota((tok_local, rows), 1) // top_count == iota((tok_local, rows), 0), 1.0, 0.0).astype(jnp.bfloat16)
+    mine = iota((top_count, rows), 1) % top_count == iota((top_count, rows), 0)
 
     def line(values):
-        spread = jnp.zeros((tok_local, rows), jnp.float32)
+        spread = jnp.zeros((top_count, rows), jnp.float32)
         for _ in range(3):
             piece = values.astype(jnp.bfloat16)
             values = values - piece.astype(jnp.float32)
@@ -76,7 +75,7 @@
     order = jnp.where(in_row == source, 1.0, 0.0).astype(jnp.bfloat16)
     hid = exact_dot(order, jnp.concatenate([hid[...] for hid in hids], axis=0))
     out_ref[:, width:] = hid[:, :hidden_width].astype(jnp.bfloat16)
-    token = hid[:, hidden_width : hidden_width + cols].astype(jnp.int32)
+    token = hid[:, hidden_width : hidden_width + 1].astype(jnp.int32)
     row, col = iota((slots, cols), 0), iota((slots, cols), 1)
     pick = (token == col % tok_local) & (col // tok_local == row % per_far // capacity)
     pick = jnp.where(pick, 1.0, 0.0).astype(jnp.bfloat16)
@@ -86,54 +85,16 @@
         out_ref[:, start : start + step] = exact_dot(pick, tokens).astype(jnp.bfloat16)
 
 
-def returned_kernel(far_count, near_count, capacity, near_ref, rows_ref, weight_ref, *refs):
-    earlier, (out_ref, total_ref) = refs[:-2], refs[-2:]
-    step = pl.program_id(0)
-    tile = weight_ref.shape[1]
-
-    @pl.when(step == 0)
-    def _():
-        total_ref[...] = jnp.zeros_like(total_ref)
-
-    cols = pl.ds(pl.multiple_of(step * tile, 128), tile)
-    total_ref[...] += lax.dot_general(
-        weight_ref[...], rows_ref[:, cols], (((1,), (1,)), ((), ())), preferred_element_type=jnp.float32
-    )
-
-    @pl.when(step == pl.num_programs(0) - 1)
-    def _():
-        own = total_ref[...].T.astype(jnp.bfloat16)
-        if not earlier:
-            out_ref[...] = own
-            return
-        rows = jnp.concatenate([ref[...] for ref in earlier] + [own], axis=0)
-        total = rows.shape[0]
-        near = near_ref[0]
-        count = near_count // ROUNDS
-        out_row, in_row = iota((total, total), 0), iota((total, total), 1)
-        back = lax.rem(near - out_row // capacity % near_count + near_count, near_count)
-        source = (
-            (back // count) * (far_count * count * capacity)
-            + (out_row // (near_count * capacity)) * (count * capacity)
-            + (back % count) * capacity
-            + out_row % capacity
-        )
-        order = jnp.where(in_row == source, 1.0, 0.0).astype(jnp.bfloat16)
-        out_ref[...] = exact_dot(order, rows).astype(jnp.bfloat16)
-
-
 def down_kernel(width, replica_ref, *refs):
     rows, (out_ref, turned_ref) = refs[:-2], refs[-2:]
     step = pl.program_id(0)
     share, tile = out_ref.shape
-    lines = rows[0].shape[0]
 
     @pl.when(step == 0)
     def _():
         start = pl.multiple_of(width + replica_ref[0] * share, 128)
-        for i, ref in enumerate(rows):
-            hid = ref[:, pl.ds(start, share)].astype(jnp.float32)
-            turned_ref[:, i * lines : (i + 1) * lines] = hid.T.astype(jnp.bfloat16)
+        hid = jnp.concatenate([ref[:, pl.ds(start, share)] for ref in rows], axis=0)
+        turned_ref[...] = hid.astype(jnp.float32).T.astype(jnp.bfloat16)
 
     cols = pl.ds(pl.multiple_of(step * tile, 128), tile)
     tokens = jnp.concatenate([ref[:, cols] for ref in rows], axis=0)
@@ -180,26 +141,19 @@
     )(*blocks, *hids)
 
 
-def returned_rows(far_count, near_count, capacity, near, rows, weight, earlier):
-    lines = rows.shape[0]
-    hidden_width, width = weight.shape
-    tile = min(width, 512)
-    total = lines * ROUNDS if earlier else lines
-    whole = lambda array: pl.BlockSpec(array.shape, lambda i: (0, 0))
-    return pl.pallas_call(
-        functools.partial(returned_kernel, far_count, near_count, capacity),
-        grid=(width // tile,),
-        out_shape=jax.ShapeDtypeStruct((total, hidden_width), jnp.bfloat16),
-        in_specs=[scalar_spec(), whole(rows), pl.BlockSpec((hidden_width, tile), lambda i: (0, i))]
-        + [whole(array) for array in earlier],
-        out_specs=pl.BlockSpec((total, hidden_width), lambda i: (0, 0)),
-        scratch_shapes=[pltpu.VMEM((hidden_width, lines), jnp.float32)],
-        compiler_params=params(),
-        cost_estimate=pl.CostEstimate(
-            flops=2 * lines * width * hidden_width, bytes_accessed=2 * width * hidden_width, transcendentals=0
-        ),
-        name="returned_rows",
-    )(near, rows, weight, *earlier)
+def back_order(far_count, near_count, capacity, near, groups):
+    slots = far_count * near_count * capacity
+    row = jnp.arange(slots, dtype=jnp.int32)
+    far, rank = row // (near_count * capacity), row % capacity
+    step = (near - row // capacity % near_count + near_count) % near_count
+    source = jnp.zeros_like(row)
+    start = 0
+    for group in groups:
+        count = len(group)
+        place = start + (far * count + step - group[0]) * capacity + rank
+        source = jnp.where((step >= group[0]) & (step <= group[-1]), place, source)
+        start += far_count * count * capacity
+    return (source[:, None] == row[None, :]).astype(jnp.bfloat16)
 
 
 def down_rows(replica, rows, width, share):
@@ -233,7 +187,7 @@
     slot_total = experts * capacity
     near = lax.axis_index("near")
     near_ref = near.astype(jnp.int32).reshape(1)
-    count = near_count // ROUNDS
+    groups = [list(range(near_count - 1)), [near_count - 1]]
     weight = w_down[0]
 
     def along(array, steps):
@@ -244,34 +198,36 @@
 
     blocks = [grad_out, along(grad_out, 1)]
     *sends, back_place = send_rows(
-        far_count, near_count, capacity, near_ref, expert_ids, gates, hidden.reshape(row_total, hidden_width)
-    )
-    later, sends[1] = lax.optimization_barrier((grad_out, sends[1]))
+        far_count, near_count, capacity, near_ref, expert_ids.T, gates.T, hidden.reshape(row_total, hidden_width)
+    )
+    blocks[1], sends[1] = lax.optimization_barrier((blocks[1], sends[1]))
+    for _ in range(2, near_count):
+        blocks.append(along(blocks[-1], 1))
     hids = [sends[0]] + [along(sends[step], step) for step in range(1, near_count)]
-    blocks += [along(later, step) for step in range(2, near_count)]
 
     rows, peers, returned = [], [], []
-    for turn in range(ROUNDS):
-        part = slice(turn * count, (turn + 1) * count)
-        picked = pick_rows(far_count, capacity, blocks[part], hids[part])
+    for group in groups:
+        picked = pick_rows(far_count, capacity, [blocks[step] for step in group], [hids[step] for step in group])
         if rows:
             picked, rows[-1] = lax.optimization_barrier((picked, rows[-1]))
         got = lax.all_to_all(
             picked.reshape(far_count, -1, picked.shape[1]), "far", split_axis=0, concat_axis=0, tiled=True
         ).reshape(picked.shape)
         rows.append(got)
-    for turn in range(ROUNDS):
+    for turn in range(len(rows)):
         if returned:
             rows[turn], returned[-1] = lax.optimization_barrier((rows[turn], returned[-1]))
         got = rows[turn]
         peers.append(swap(got))
         returned.append(
-            returned_rows(
-                far_count, near_count, capacity, near_ref, got, weight, returned if turn == ROUNDS - 1 else []
-            )
+            lax.dot_general(
+                got[:, :width], weight, (((1,), (1,)), ((), ())), preferred_element_type=jnp.float32
+            ).astype(jnp.bfloat16)
         )
+    order = back_order(far_count, near_count, capacity, near, groups)
+    returned = exact_dot(order, jnp.concatenate(returned, axis=0)).astype(jnp.bfloat16)
     came_back = lax.all_to_all(
-        returned[-1].reshape(experts, capacity, hidden_width),
+        returned.reshape(experts, capacity, hidden_width),
         ("far", "near"),
         split_axis=0,
         concat_axis=0,

time: 97.4 us -> 97.9 us (level)
  Pallas kernels: 24.3 us -> 10.8 us
  matrix products: 1.03 us -> 13 us
  waiting for transfers between devices: 40.6 us -> 45.4 us
  starting transfers between devices: 24.7 us -> 22.6 us
    pallas_call x2 -> x0, Pallas kernels: 14.6 us -> none  [returned_rows(): pl.pallas_call(functools.partial(returned_kernel, far_count, near_count,...]
    dot_general x0 -> x3, matrix products: none -> 10.9 us  [the longest x2 9.81 us: local(): lax.dot_general(got[:, :width], weight, (((1,), (1,)), ((), ())), preferr...]
    all_to_all x2, waiting for transfers between devices: 9.03 us -> 15.1 us  [local(): lax.all_to_all(picked.reshape(far_count, -1, picked.shape[1]), 'far', spl...]
    all_to_all x1, starting transfers between devices: 7.19 us -> 4.21 us  [local(): lax.all_to_all(returned.reshape(experts, capacity, hidden_width), ('far',...]
    ppermute x6, starting transfers between devices: 9.81 us -> 11.3 us  [along(): lax.ppermute(array, 'near', [(i, (i + steps) % near_count) for i in range...]
    pallas_call x2, Pallas kernels: 2.25 us -> 3.47 us  [pick_rows(): pl.pallas_call(functools.partial(pick_kernel, far_count, capacity), out_s...]
    unnamed x13 -> x14, local copies, waits for them, and re-layouts: 5.17 us -> 4.06 us
    ppermute x6, waiting for transfers between devices: 24.5 us -> 23.4 us  [along(): lax.ppermute(array, 'near', [(i, (i + steps) % near_count) for i in range...]
  transfers between devices with their start and end apart: 11 -> 11, of which waited for: 4 -> 7; matrix products, arithmetic and copies ran while one was open for 2% -> 12% of each run, Pallas kernels for 23% -> 9%
where the time goes in v6:
time: 97.9 us; the launch traced here: 97.3 us
  waiting for transfers between devices  45.4 us (46%)
  starting transfers between devices  22.6 us (23%)
  matrix products  13 us (13%)
  Pallas kernels  10.8 us (11%)
  local copies, waits for them, and re-layouts  4.81 us (5%)
    ppermute x6, waiting for transfers between devices, along(): lax.ppermute(array, 'near', [(i, (i + steps) % near_count) for i in range...  23.4 us
    all_to_all x2, waiting for transfers between devices, local(): lax.all_to_all(picked.reshape(far_count, -1, picked.shape[1]), 'far', spl...  15.1 us
    ppermute x6, starting transfers between devices, along(): lax.ppermute(array, 'near', [(i, (i + steps) % near_count) for i in range...  11.3 us
    dot_general x2, matrix products, local(): lax.dot_general(got[:, :width], weight, (((1,), (1,)), ((), ())), preferr...  9.81 us
    all_to_all x2, starting transfers between devices, local(): lax.all_to_all(picked.reshape(far_count, -1, picked.shape[1]), 'far', spl...  7.08 us
    all_to_all x1, waiting for transfers between devices, local(): lax.all_to_all(returned.reshape(experts, capacity, hidden_width), ('far',...  6.88 us
    pallas_call x1, Pallas kernels, down_rows(): pl.pallas_call(functools.partial(down_kernel, width), grid=(width // tile...  6.62 us
    all_to_all x1, starting transfers between devices, local(): lax.all_to_all(returned.reshape(experts, capacity, hidden_width), ('far',...  4.21 us
  transfers between devices with their start and end apart: 11, of which 7 were waited for; matrix products, arithmetic and copies ran while one was open for 12% of the time, Pallas kernels for 9%

profile of v6, /device:TPU:0, one launch (start us, length us, event | category | flops | bytes accessed | tf_op | source)
XLA Modules:
  0.0 97.3 jit_solution(5720924929256688881)
XLA Ops:
  0.6 3.1 %collective-permute-start = (bf16[32,4096]{1,0:T(8,128)(2,1)}, bf16[32,4096]{1,0:T(8,128)(2,1)S(1)}, u32[]{:S(2)}, u32[]{:S(2)}) collective-permute-start(bf16[32,4096]{1,0:T(8,128)(2,1)} %refs_0_.1), channel_id=1, source_target_pairs={{0,1},{1,2},{2,3},{3,0},{4,5},{5,6},{6,7},{7,4},{8,9},{9,10},{10,1... | collective-permute-start | bytes 786440 | tf_op jit(solution)/shard_map/ppermute | solution.py:194
  3.7 0.0 copy-start
  3.7 1.0 %copy-done = bf16[32,8,768]{2,1,0:T(8,128)(2,1)S(1)} copy-done((bf16[32,8,768]{2,1,0:T(8,128)(2,1)S(1)}, bf16[32,8,768]{2,1,0:T(8,128)(2,1)}, u32[]{:S(2)}) %copy-start) | copy-done | bytes 393240
  4.7 0.0 copy-start.3
  4.7 0.7 copy-done.3
  5.4 0.0 copy-start.5
  5.4 0.7 copy-done.5
  6.1 0.7 send_rows.1
  6.8 5.4 %collective-permute-done.refs_1_ = bf16[32,4096]{1,0:T(8,128)(2,1)S(1)} collective-permute-done((bf16[32,4096]{1,0:T(8,128)(2,1)}, bf16[32,4096]{1,0:T(8,128)(2,1)S(1)}, u32[]{:S(2)}, u32[]{:S(2)}) %collective-permute-start) | collective-permute-done | bytes 262176 | tf_op jit(solution)/shard_map/ppermute | solution.py:194
  12.2 0.0 collective-permute-start.1
  12.3 2.3 %collective-permute-start.5 = (bf16[64,896]{1,0:T(8,128)(2,1)S(1)}, bf16[64,896]{1,0:T(8,128)(2,1)S(1)}, u32[]{:S(2)}, u32[]{:S(2)}) collective-permute-start(bf16[64,896]{1,0:T(8,128)(2,1)S(1)} %get-tuple-element.22), channel_id=1, source_target_pairs={{0,2},{1,3},{2,0},{3,1},{4,6},{5,7},{6,4},{7,5},{8,10},{9,11},{10,... | collective-permute-start | bytes 344072 | tf_op jit(solution)/shard_map/ppermute | solution.py:194
  14.6 2.1 %collective-permute-start.4 = (bf16[64,896]{1,0:T(8,128)(2,1)S(1)}, bf16[64,896]{1,0:T(8,128)(2,1)S(1)}, u32[]{:S(2)}, u32[]{:S(2)}) collective-permute-start(bf16[64,896]{1,0:T(8,128)(2,1)S(1)} %get-tuple-element.21), channel_id=1, source_target_pairs={{0,1},{1,2},{2,3},{3,0},{4,5},{5,6},{6,7},{7,4},{8,9},{9,10},{10,1... | collective-permute-start | bytes 344072 | tf_op jit(solution)/shard_map/ppermute | solution.py:194
  16.6 11.4 %collective-permute-done.5.refs_5_ = bf16[64,896]{1,0:T(8,128)(2,1)S(1)} collective-permute-done((bf16[64,896]{1,0:T(8,128)(2,1)S(1)}, bf16[64,896]{1,0:T(8,128)(2,1)S(1)}, u32[]{:S(2)}, u32[]{:S(2)}) %collective-permute-start.5) | collective-permute-done | bytes 114720 | tf_op jit(solution)/shard_map/ppermute | solution.py:194
  28.0 0.0 collective-permute-done.4.refs_4_
  28.0 0.0 collective-permute-done.1.refs_2_
  28.0 0.0 copy-start.2
  28.0 0.9 copy-done.2
  29.0 2.1 %pick_rows.3 = bf16[192,4864]{1,0:T(8,128)(2,1)} custom-call(bf16[32,4096]{1,0:T(8,128)(2,1)S(1)} %copy-done.2, bf16[32,4096]{1,0:T(8,128)(2,1)S(1)} %collective-permute-done.refs_1_, bf16[32,4096]{1,0:T(8,128)(2,1)S(1)} %collective-permute-done.1.refs_2_, bf16[64,896]{1,0:T(8,128)(2,1)S(1)} %get-tuple-element.20.refs_3_, ...), custom_call_target="tpu_custom_call" | custom-call | flops 119537664 | bytes 3735552 | tf_op jit(solution)/shard_map/pick_rows/pallas_call | solution.py:133
  31.1 3.6 %all-to-all-start = ((bf16[4,48,4864]{2,1,0:T(8,128)(2,1)}), bf16[4,48,4864]{2,1,0:T(8,128)(2,1)S(1)}, u32[]{:S(2)}, u32[]{:S(2)}) async-start(bf16[4,48,4864]{2,1,0:T(8,128)(2,1)} %bitcast.6), calls=%async_computation | async-start | bytes 3735552 | tf_op jit(solution)/shard_map/all_to_all | solution.py:213
  34.7 0.1 collective-permute-start.2
  34.8 3.8 %collective-permute-start.3 = (bf16[64,896]{1,0:T(8,128)(2,1)S(1)}, bf16[64,896]{1,0:T(8,128)(2,1)S(1)}, u32[]{:S(2)}, u32[]{:S(2)}) collective-permute-start(bf16[64,896]{1,0:T(8,128)(2,1)S(1)} %get-tuple-element.19), channel_id=1, source_target_pairs={{0,3},{1,0},{2,1},{3,2},{4,7},{5,4},{6,5},{7,6},{8,11},{9,8},{10,9... | collective-permute-start | bytes 344072 | tf_op jit(solution)/shard_map/ppermute | solution.py:194
  38.6 6.0 %collective-permute-done.3.refs_1_ = bf16[64,896]{1,0:T(8,128)(2,1)S(1)} collective-permute-done((bf16[64,896]{1,0:T(8,128)(2,1)S(1)}, bf16[64,896]{1,0:T(8,128)(2,1)S(1)}, u32[]{:S(2)}, u32[]{:S(2)}) %collective-permute-start.3) | collective-permute-done | bytes 114720 | tf_op jit(solution)/shard_map/ppermute | solution.py:194
  44.5 0.6 collective-permute-done.2.refs_0_
  45.2 1.3 %pick_rows.2 = bf16[64,4864]{1,0:T(8,128)(2,1)} custom-call(bf16[32,4096]{1,0:T(8,128)(2,1)S(1)} %collective-permute-done.2.refs_0_, bf16[64,896]{1,0:T(8,128)(2,1)S(1)} %collective-permute-done.3.refs_1_), custom_call_target="tpu_custom_call" | custom-call | flops 39845888 | bytes 1245184 | tf_op jit(solution)/shard_map/pick_rows/pallas_call | solution.py:133
  46.5 10.1 %all-to-all-done = bf16[4,48,4864]{2,1,0:T(8,128)(2,1)S(1)} async-done(((bf16[4,48,4864]{2,1,0:T(8,128)(2,1)}), bf16[4,48,4864]{2,1,0:T(8,128)(2,1)S(1)}, u32[]{:S(2)}, u32[]{:S(2)}) %all-to-all-start) | async-done | bytes 1867808 | tf_op jit(solution)/shard_map/all_to_all | solution.py:213
  56.6 0.0 collective-permute-start.6
  56.6 3.5 %all-to-all-start.1 = ((bf16[4,16,4864]{2,1,0:T(8,128)(2,1)}), bf16[4,16,4864]{2,1,0:T(8,128)(2,1)S(1)}, u32[]{:S(2)}, u32[]{:S(2)}) async-start(bf16[4,16,4864]{2,1,0:T(8,128)(2,1)} %bitcast.8), calls=%async_computation.1 | async-start | bytes 1245184 | tf_op jit(solution)/shard_map/all_to_all | solution.py:213
  60.1 5.0 %fusion.5 = bf16[192,768]{1,0:T(8,128)(2,1)S(1)} fusion(bf16[1,768,4096]{2,1,0:T(8,128)(2,1)} %param.9, bf16[192,4864]{1,0:T(8,128)(2,1)S(1)} %bitcast.31), kind=kOutput, calls=%fused_computation.6 | convolution fusion | flops 1208107008 | bytes 8159232 | tf_op jit(solution)/shard_map/dot_general | solution.py:223
  65.1 5.0 %all-to-all-done.1 = bf16[4,16,4864]{2,1,0:T(8,128)(2,1)S(1)} async-done(((bf16[4,16,4864]{2,1,0:T(8,128)(2,1)}), bf16[4,16,4864]{2,1,0:T(8,128)(2,1)S(1)}, u32[]{:S(2)}, u32[]{:S(2)}) %all-to-all-start.1) | async-done | bytes 622624 | tf_op jit(solution)/shard_map/all_to_all | solution.py:213
  70.1 0.0 copy-start.4
  70.1 0.0 collective-permute-start.7
  70.1 4.8 %fusion.10 = bf16[64,768]{1,0:T(8,128)(2,1)S(1)} fusion(bf16[1,768,4096]{2,1,0:T(8,128)(2,1)} %param.9, bf16[64,4864]{1,0:T(8,128)(2,1)S(1)} %bitcast.34), kind=kOutput, calls=%fused_computation.7 | convolution fusion | flops 402702336 | bytes 6914048 | tf_op jit(solution)/shard_map/dot_general | solution.py:223
  74.9 1.1 %convolution_convert_fusion = bf16[256,768]{1,0:T(8,128)(2,1)} fusion(bf16[64,768]{1,0:T(8,128)(2,1)S(1)} %fusion.10, bf16[192,768]{1,0:T(8,128)(2,1)S(1)} %fusion.5, s32[256]{0:T(256)S(1)} %and_select_fusion.3), kind=kOutput, calls=%fused_computation.5 | convolution fusion | flops 101711872 | bytes 787456 | tf_op jit(solution)/shard_map/dot_general | solution.py:19
  76.0 4.2 %all-to-all-start.2 = ((bf16[16,16,768]{2,1,0:T(8,128)(2,1)}), bf16[16,16,768]{2,1,0:T(8,128)(2,1)}, u32[]{:S(2)}, u32[]{:S(2)}) async-start(bf16[16,16,768]{2,1,0:T(8,128)(2,1)} %bitcast.41), calls=%async_computation.2 | async-start | bytes 786432 | tf_op jit(solution)/shard_map/all_to_all | solution.py:229
  80.2 0.0 copy-done.4
  80.2 0.1 copy.12
  80.3 0.7 copy.13
  81.0 0.0 collective-permute-done.7.refs_3_
  81.0 0.0 collective-permute-done.6.refs_2_
  81.0 0.0 copy-start.1
  81.0 6.6 %down_rows.1 = bf16[384,4096]{1,0:T(8,128)(2,1)} custom-call(s32[1]{0:T(128)} %bitcast.12.replica_ref, bf16[192,4864]{1,0:T(8,128)(2,1)S(1)} %bitcast.32, bf16[64,4864]{1,0:T(8,128)(2,1)S(1)} %bitcast.35, bf16[192,4864]{1,0:T(8,128)(2,1)} %collective-permute-done.6.refs_2_, bf16[64,4864]{1,0:T(8,128)(2,1)S(1)} %collective-permute-done.7.refs_3_), custom_call_target="tpu_custom_call" | custom-call | flops 1610612736 | bytes 7340032 | tf_op jit(solution)/shard_map/down_rows/pallas_call | solution.py:163
  87.7 6.9 %all-to-all-done.2 = bf16[16,16,768]{2,1,0:T(8,128)(2,1)} async-done(((bf16[16,16,768]{2,1,0:T(8,128)(2,1)}), bf16[16,16,768]{2,1,0:T(8,128)(2,1)}, u32[]{:S(2)}, u32[]{:S(2)}) %all-to-all-start.2) | async-done | bytes 393248 | tf_op jit(solution)/shard_map/all_to_all | solution.py:229
  94.5 0.0 copy-done.1
  94.5 2.1 %multiply_reduce_fusion = (f32[32,8]{1,0:T(8,128)S(1)}, bf16[32,8,768]{2,1,0:T(8,128)(2,1)}) fusion(bf16[32,8,768]{2,1,0:T(8,128)(2,1)S(1)} %copy-done.1, f32[32,8]{1,0:T(8,128)S(1)} %copy.12, bf16[256,768,1]{1,0,2:T(8,128)(2,1)} %bitcast.14, bf16[256,256]{1,0:T(8,128)(2,1)} %copy.13), kind=kOutput, calls=%fused_computation.8 | convolution fusion | flops 101646080 | bytes 1312768 | tf_op jit(solution)/shard_map/dot_general | solution.py:241
  96.6 0.7 copy.14
  (1 shorter events, 0.0 us)
Async XLA Ops:
  0.6 11.6 %collective-permute-start = (bf16[32,4096]{1,0:T(8,128)(2,1)}, bf16[32,4096]{1,0:T(8,128)(2,1)S(1)}, u32[]{:S(2)}, u32[]{:S(2)}) collective-permute-start(bf16[32,4096]{1,0:T(8,128)(2,1)} %refs_0_.1), channel_id=1, source_target_pairs={{0,1},{1,2},{2,3},{3,0},{4,5},{5,6},{6,7},{7,4},{8,9},{9,10},{10,1... | collective-permute-start | bytes 786440 | tf_op jit(solution)/shard_map/ppermute | solution.py:194
  3.7 1.0 %copy-start = (bf16[32,8,768]{2,1,0:T(8,128)(2,1)S(1)}, bf16[32,8,768]{2,1,0:T(8,128)(2,1)}, u32[]{:S(2)}) copy-start(bf16[32,8,768]{2,1,0:T(8,128)(2,1)} %param.6) | copy-start | bytes 1179652
  4.7 0.7 copy-start.3
  5.4 0.7 copy-start.5
  12.2 15.8 %collective-permute-start.1 = (bf16[32,4096]{1,0:T(8,128)(2,1)S(1)}, bf16[32,4096]{1,0:T(8,128)(2,1)S(1)}, u32[]{:S(2)}, u32[]{:S(2)}) collective-permute-start(bf16[32,4096]{1,0:T(8,128)(2,1)S(1)} %collective-permute-done.refs_1_), channel_id=1, source_target_pairs={{0,1},{1,2},{2,3},{3,0},{4,5},{5,6},{6,7},{7,4},{8,9},{9,10},{10,1... | collective-permute-start | bytes 786440 | tf_op jit(solution)/shard_map/ppermute | solution.py:194
  12.3 15.8 %collective-permute-start.5 = (bf16[64,896]{1,0:T(8,128)(2,1)S(1)}, bf16[64,896]{1,0:T(8,128)(2,1)S(1)}, u32[]{:S(2)}, u32[]{:S(2)}) collective-permute-start(bf16[64,896]{1,0:T(8,128)(2,1)S(1)} %get-tuple-element.22), channel_id=1, source_target_pairs={{0,2},{1,3},{2,0},{3,1},{4,6},{5,7},{6,4},{7,5},{8,10},{9,11},{10,... | collective-permute-start | bytes 344072 | tf_op jit(solution)/shard_map/ppermute | solution.py:194
  14.6 13.5 %collective-permute-start.4 = (bf16[64,896]{1,0:T(8,128)(2,1)S(1)}, bf16[64,896]{1,0:T(8,128)(2,1)S(1)}, u32[]{:S(2)}, u32[]{:S(2)}) collective-permute-start(bf16[64,896]{1,0:T(8,128)(2,1)S(1)} %get-tuple-element.21), channel_id=1, source_target_pairs={{0,1},{1,2},{2,3},{3,0},{4,5},{5,6},{6,7},{7,4},{8,9},{9,10},{10,1... | collective-permute-start | bytes 344072 | tf_op jit(solution)/shard_map/ppermute | solution.py:194
  28.0 1.0 copy-start.2
  31.1 25.5 %all-to-all-start = ((bf16[4,48,4864]{2,1,0:T(8,128)(2,1)}), bf16[4,48,4864]{2,1,0:T(8,128)(2,1)S(1)}, u32[]{:S(2)}, u32[]{:S(2)}) async-start(bf16[4,48,4864]{2,1,0:T(8,128)(2,1)} %bitcast.6), calls=%async_computation | async-start | bytes 3735552 | tf_op jit(solution)/shard_map/all_to_all | solution.py:213
  34.7 10.4 %collective-permute-start.2 = (bf16[32,4096]{1,0:T(8,128)(2,1)S(1)}, bf16[32,4096]{1,0:T(8,128)(2,1)S(1)}, u32[]{:S(2)}, u32[]{:S(2)}) collective-permute-start(bf16[32,4096]{1,0:T(8,128)(2,1)S(1)} %collective-permute-done.1.refs_2_), channel_id=1, source_target_pairs={{0,1},{1,2},{2,3},{3,0},{4,5},{5,6},{6,7},{7,4},{8,9},{9,10},{10,1... | collective-permute-start | bytes 786440 | tf_op jit(solution)/shard_map/ppermute | solution.py:194
  34.8 9.8 %collective-permute-start.3 = (bf16[64,896]{1,0:T(8,128)(2,1)S(1)}, bf16[64,896]{1,0:T(8,128)(2,1)S(1)}, u32[]{:S(2)}, u32[]{:S(2)}) collective-permute-start(bf16[64,896]{1,0:T(8,128)(2,1)S(1)} %get-tuple-element.19), channel_id=1, source_target_pairs={{0,3},{1,0},{2,1},{3,2},{4,7},{5,4},{6,5},{7,6},{8,11},{9,8},{10,9... | collective-permute-start | bytes 344072 | tf_op jit(solution)/shard_map/ppermute | solution.py:194
  56.6 24.4 %collective-permute-start.6 = (bf16[192,4864]{1,0:T(8,128)(2,1)S(1)}, bf16[192,4864]{1,0:T(8,128)(2,1)}, u32[]{:S(2)}, u32[]{:S(2)}) collective-permute-start(bf16[192,4864]{1,0:T(8,128)(2,1)S(1)} %bitcast.30), channel_id=1, source_target_pairs={{0,16},{16,0},{1,17},{17,1},{2,18},{18,2},{3,19},{19,3},{4,20},{20... | collective-permute-start | bytes 5603336 | tf_op jit(solution)/shard_map/ppermute | solution.py:197
  56.6 13.5 %all-to-all-start.1 = ((bf16[4,16,4864]{2,1,0:T(8,128)(2,1)}), bf16[4,16,4864]{2,1,0:T(8,128)(2,1)S(1)}, u32[]{:S(2)}, u32[]{:S(2)}) async-start(bf16[4,16,4864]{2,1,0:T(8,128)(2,1)} %bitcast.8), calls=%async_computation.1 | async-start | bytes 1245184 | tf_op jit(solution)/shard_map/all_to_all | solution.py:213
  70.1 10.1 %copy-start.4 = (f32[32,8]{0,1:T(8,128)S(1)}, f32[32,8]{0,1:T(8,128)}, u32[]{:S(2)}) copy-start(f32[32,8]{0,1:T(8,128)} %param.7) | copy-start | bytes 3076
  70.1 10.9 %collective-permute-start.7 = (bf16[64,4864]{1,0:T(8,128)(2,1)S(1)}, bf16[64,4864]{1,0:T(8,128)(2,1)S(1)}, u32[]{:S(2)}, u32[]{:S(2)}) collective-permute-start(bf16[64,4864]{1,0:T(8,128)(2,1)S(1)} %bitcast.33), channel_id=1, source_target_pairs={{0,16},{16,0},{1,17},{17,1},{2,18},{18,2},{3,19},{19,3},{4,20},{20... | collective-permute-start | bytes 1867784 | tf_op jit(solution)/shard_map/ppermute | solution.py:197
  76.0 18.6 %all-to-all-start.2 = ((bf16[16,16,768]{2,1,0:T(8,128)(2,1)}), bf16[16,16,768]{2,1,0:T(8,128)(2,1)}, u32[]{:S(2)}, u32[]{:S(2)}) async-start(bf16[16,16,768]{2,1,0:T(8,128)(2,1)} %bitcast.41), calls=%async_computation.2 | async-start | bytes 786432 | tf_op jit(solution)/shard_map/all_to_all | solution.py:229
  81.0 13.5 %copy-start.1 = (bf16[32,8,768]{2,1,0:T(8,128)(2,1)S(1)}, bf16[32,8,768]{2,1,0:T(8,128)(2,1)}, u32[]{:S(2)}) copy-start(bf16[32,8,768]{2,1,0:T(8,128)(2,1)} %param.6) | copy-start | bytes 1179652

commit v7 on v6

--- a/solution.py
+++ b/solution.py
@@ -7,8 +7,7 @@
 from jax.experimental.pallas import tpu as pltpu
 from jax.sharding import PartitionSpec as P
 
-ID_COLS = 128
-VMEM_LIMIT = 48 * 1024 * 1024
+MIB = 1024 * 1024
 
 
 def iota(shape, dim):
@@ -22,7 +21,6 @@
 def send_kernel(far_count, near_count, capacity, near_ref, ids_ref, gates_ref, hidden_ref, *refs):
     sends, back_ref = refs[:-1], refs[-1]
     top_count, tok_local = ids_ref.shape
-    hidden_width = hidden_ref.shape[1]
     rows = tok_local * top_count
     experts = far_count * near_count
     slots = experts * capacity
@@ -49,52 +47,70 @@
     back_slots = ids * capacity + ranks
     back_ref[...] = jnp.where(iota((slots, rows), 0) == back_slots, 1.0, 0.0).astype(jnp.bfloat16)
     lines = far_count * capacity
-    tokens = (iota((lines, rows), 1) // top_count + 1).astype(jnp.float32)
     for step, ref in enumerate(sends):
         place = iota((lines, rows), 0) + step * lines == out_slots
         gate = jnp.sum(jnp.where(place, gates, 0.0), axis=1, keepdims=True)
-        token = jnp.sum(jnp.where(place, tokens, 0.0), axis=1, keepdims=True) - 1.0
         picked = exact_dot(jnp.where(place, 1.0, 0.0).astype(jnp.bfloat16), hidden_ref[...])
-        ref[:, :hidden_width] = (picked * gate).astype(jnp.bfloat16)
-        ref[:, hidden_width:] = jnp.broadcast_to(token, (lines, ID_COLS)).astype(jnp.bfloat16)
-
-
-def pick_kernel(far_count, capacity, *refs):
-    out_ref = refs[-1]
-    count = (len(refs) - 1) // 2
-    blocks, hids = refs[:count], refs[count:-1]
+        ref[...] = (picked * gate).astype(jnp.bfloat16)
+
+
+def pick_kernel(far_count, near_count, capacity, count, near_ref, *refs):
+    ids, blocks, hids, out_ref = refs[:count], refs[count : 2 * count], refs[2 * count : -1], refs[-1]
     tok_local, width = blocks[0].shape
-    hidden_width = hids[0].shape[1] - ID_COLS
     cols = count * tok_local
     slots = far_count * count * capacity
-    per_far, per_block = count * capacity, far_count * capacity
-    out_row, in_row = iota((slots, slots), 0), iota((slots, slots), 1)
-    source = (
-        (out_row % per_far // capacity) * per_block + (out_row // per_far) * capacity + out_row % capacity
-    )
-    order = jnp.where(in_row == source, 1.0, 0.0).astype(jnp.bfloat16)
-    hid = exact_dot(order, jnp.concatenate([hid[...] for hid in hids], axis=0))
-    out_ref[:, width:] = hid[:, :hidden_width].astype(jnp.bfloat16)
-    token = hid[:, hidden_width : hidden_width + 1].astype(jnp.int32)
-    row, col = iota((slots, cols), 0), iota((slots, cols), 1)
-    pick = (token == col % tok_local) & (col // tok_local == row % per_far // capacity)
+    near = near_ref[0]
+    ids = jnp.concatenate([ref[...] for ref in ids], axis=1)
+    lead = max(8, far_count)
+    named = jnp.zeros((lead, cols), jnp.float32)
+    for far in range(far_count):
+        hit = jnp.where(ids == far * near_count + near, 1.0, 0.0)
+        named = jnp.where(iota((lead, cols), 0) == far, jnp.sum(hit, axis=0, keepdims=True), named)
+    row, col = iota((cols, cols), 0), iota((cols, cols), 1)
+    before = jnp.where((row < col) & (row // tok_local == col // tok_local), 1.0, 0.0).astype(jnp.bfloat16)
+    named = named.astype(jnp.bfloat16)
+    rank = exact_dot(named, before)
+    place = jnp.where(named.astype(jnp.float32) > 0.5, rank, float(capacity)).astype(jnp.bfloat16)
+    per_far = count * capacity
+    spread = jnp.where(iota((slots, lead), 0) // per_far == iota((slots, lead), 1), 1.0, 0.0).astype(jnp.bfloat16)
+    slot = iota((slots, cols), 0) % per_far
+    pick = (iota((slots, cols), 1) // tok_local == slot // capacity) & (
+        exact_dot(spread, place).astype(jnp.int32) == slot % capacity
+    )
     pick = jnp.where(pick, 1.0, 0.0).astype(jnp.bfloat16)
     step = min(width, 512)
     for start in range(0, width, step):
         tokens = jnp.concatenate([block[:, start : start + step] for block in blocks], axis=0)
         out_ref[:, start : start + step] = exact_dot(pick, tokens).astype(jnp.bfloat16)
-
-
-def down_kernel(width, replica_ref, *refs):
+    for i, hid in enumerate(hids):
+        start = width + i * hid.shape[1]
+        out_ref[:, start : start + hid.shape[1]] = hid[...]
+
+
+def down_kernel(far_count, capacity, width, replica_ref, *refs):
     rows, (out_ref, turned_ref) = refs[:-2], refs[-2:]
     step = pl.program_id(0)
     share, tile = out_ref.shape
 
     @pl.when(step == 0)
     def _():
-        start = pl.multiple_of(width + replica_ref[0] * share, 128)
-        hid = jnp.concatenate([ref[:, pl.ds(start, share)] for ref in rows], axis=0)
-        turned_ref[...] = hid.astype(jnp.float32).T.astype(jnp.bfloat16)
+        hids = []
+        for early, late in (rows[:2], rows[2:]):
+            lines, last = early.shape[0], late.shape[0]
+            count = lines // last
+            hidden_width = (late.shape[1] - width) // (count + 1)
+            row, col = iota((lines, last), 0), iota((lines, last), 1)
+            match = (row // (count * capacity) == col // capacity) & (row % capacity == col % capacity)
+            total = jnp.zeros((lines, share), jnp.float32)
+            for i in range(count + 1):
+                start = pl.multiple_of(width + i * hidden_width + replica_ref[0] * share, 128)
+                hid = late[:, pl.ds(start, share)]
+                if i < count:
+                    order = jnp.where(match & (row // capacity % count == i), 1.0, 0.0).astype(jnp.bfloat16)
+                    total = total + exact_dot(order, hid)
+                else:
+                    hids += [total, hid.astype(jnp.float32)]
+        turned_ref[...] = jnp.concatenate(hids, axis=0).T.astype(jnp.bfloat16)
 
     cols = pl.ds(pl.multiple_of(step * tile, 128), tile)
     tokens = jnp.concatenate([ref[:, cols] for ref in rows], axis=0)
@@ -105,14 +121,13 @@
     return pl.BlockSpec(memory_space=pltpu.SMEM)
 
 
-def params():
-    return pltpu.CompilerParams(vmem_limit_bytes=VMEM_LIMIT)
+def params(mib):
+    return pltpu.CompilerParams(vmem_limit_bytes=mib * MIB)
 
 
 def send_rows(far_count, near_count, capacity, near, ids, gates, hidden):
     lines = far_count * capacity
-    wide = hidden.shape[1] + ID_COLS
-    rows = hidden.shape[0]
+    rows, wide = hidden.shape
     vmem = pl.BlockSpec(memory_space=pltpu.VMEM)
     return pl.pallas_call(
         functools.partial(send_kernel, far_count, near_count, capacity),
@@ -120,25 +135,26 @@
         + [jax.ShapeDtypeStruct((near_count * lines, rows), jnp.bfloat16)],
         in_specs=[scalar_spec()] + [vmem] * 3,
         out_specs=[vmem] * (near_count + 1),
-        compiler_params=params(),
+        compiler_params=params(12),
         cost_estimate=pl.CostEstimate(flops=2 * rows * rows * wide, bytes_accessed=4 * rows * wide, transcendentals=0),
         name="send_rows",
     )(near, ids, gates, hidden)
 
 
-def pick_rows(far_count, capacity, blocks, hids):
+def pick_rows(far_count, near_count, capacity, near, ids, blocks, hids):
     width = blocks[0].shape[1]
     slots = far_count * capacity * len(blocks)
-    shape = (slots, width + hids[0].shape[1] - ID_COLS)
+    shape = (slots, width + sum(hid.shape[1] for hid in hids))
+    operands = ids + blocks + hids
     return pl.pallas_call(
-        functools.partial(pick_kernel, far_count, capacity),
+        functools.partial(pick_kernel, far_count, near_count, capacity, len(blocks)),
         out_shape=jax.ShapeDtypeStruct(shape, jnp.bfloat16),
-        in_specs=[pl.BlockSpec(memory_space=pltpu.VMEM)] * (2 * len(blocks)),
+        in_specs=[scalar_spec()] + [pl.BlockSpec(memory_space=pltpu.VMEM)] * len(operands),
         out_specs=pl.BlockSpec(memory_space=pltpu.VMEM),
-        compiler_params=params(),
+        compiler_params=params(16),
         cost_estimate=pl.CostEstimate(flops=2 * slots * 64 * shape[1], bytes_accessed=4 * slots * shape[1], transcendentals=0),
         name="pick_rows",
-    )(*blocks, *hids)
+    )(near, *operands)
 
 
 def back_order(far_count, near_count, capacity, near, groups):
@@ -156,18 +172,18 @@
     return (source[:, None] == row[None, :]).astype(jnp.bfloat16)
 
 
-def down_rows(replica, rows, width, share):
+def down_rows(far_count, capacity, replica, rows, width, share):
     tile = min(width, 512)
     lines = sum(array.shape[0] for array in rows)
     whole = lambda array: pl.BlockSpec(array.shape, lambda i: (0, 0))
     return pl.pallas_call(
-        functools.partial(down_kernel, width),
+        functools.partial(down_kernel, far_count, capacity, width),
         grid=(width // tile,),
         out_shape=jax.ShapeDtypeStruct((share, width), jnp.bfloat16),
         in_specs=[scalar_spec()] + [whole(array) for array in rows],
         out_specs=pl.BlockSpec((share, tile), lambda i: (0, i)),
         scratch_shapes=[pltpu.VMEM((share, lines), jnp.bfloat16)],
-        compiler_params=params(),
+        compiler_params=params(32),
         cost_estimate=pl.CostEstimate(
             flops=2 * lines * width * share, bytes_accessed=2 * width * (lines + share), transcendentals=0
         ),
@@ -196,20 +212,31 @@
     def swap(array):
         return lax.ppermute(array, "dp", [(i, i ^ 1) for i in range(lax.axis_size("dp"))])
 
-    blocks = [grad_out, along(grad_out, 1)]
+    blocks = [grad_out]
+    for _ in range(1, near_count):
+        blocks.append(along(blocks[-1], 1))
+    ids = [expert_ids.T] + [along(expert_ids.T, step) for step in range(1, near_count)]
     *sends, back_place = send_rows(
-        far_count, near_count, capacity, near_ref, expert_ids.T, gates.T, hidden.reshape(row_total, hidden_width)
-    )
-    blocks[1], sends[1] = lax.optimization_barrier((blocks[1], sends[1]))
-    for _ in range(2, near_count):
-        blocks.append(along(blocks[-1], 1))
-    hids = [sends[0]] + [along(sends[step], step) for step in range(1, near_count)]
-
+        far_count, near_count, capacity, near_ref, ids[0], gates.T, hidden.reshape(row_total, hidden_width)
+    )
     rows, peers, returned = [], [], []
     for group in groups:
-        picked = pick_rows(far_count, capacity, [blocks[step] for step in group], [hids[step] for step in group])
+        hids = []
+        if rows:
+            hids = [sends[0]] + [along(sends[step], step) for step in range(1, near_count)]
+        picked = pick_rows(
+            far_count,
+            near_count,
+            capacity,
+            near_ref,
+            [ids[step] for step in group],
+            [blocks[step] for step in group],
+            hids,
+        )
         if rows:
             picked, rows[-1] = lax.optimization_barrier((picked, rows[-1]))
+        else:
+            picked, sends = lax.optimization_barrier((picked, sends))
         got = lax.all_to_all(
             picked.reshape(far_count, -1, picked.shape[1]), "far", split_axis=0, concat_axis=0, tiled=True
         ).reshape(picked.shape)
@@ -235,7 +262,9 @@
     )
 
     replica = lax.axis_index("dp").astype(jnp.int32).reshape(1)
-    grad_down = down_rows(replica, rows + peers, width, hidden_width // lax.axis_size("dp"))
+    grad_down = down_rows(
+        far_count, capacity, replica, rows + peers, width, hidden_width // lax.axis_size("dp")
+    )
     came_back, grad_down = lax.optimization_barrier((came_back, grad_down))
 
     back_rows = lax.dot_general(

time: 97.9 us -> 88 us (0.90)
  waiting for transfers between devices: 45.4 us -> 33.7 us
  starting transfers between devices: 22.6 us -> 24.9 us
    all_to_all x2, waiting for transfers between devices: 15.1 us -> 7.48 us  [local(): lax.all_to_all(picked.reshape(far_count, -1, picked.shape[1]), 'far', spl...]
    ppermute x6 -> x9, waiting for transfers between devices: 23.4 us -> 19.5 us  [along(): lax.ppermute(array, 'near', [(i, (i + steps) % near_count) for i in range...]
    ppermute x6 -> x9, starting transfers between devices: 11.3 us -> 13.4 us  [along(): lax.ppermute(array, 'near', [(i, (i + steps) % near_count) for i in range...]
    dot_general x1, matrix products: 2.1 us -> 1.03 us  [local(): lax.dot_general(back_place, came_back.reshape(slot_total, hidden_width),...]
    unnamed x14 -> x16, local copies, waits for them, and re-layouts: 4.06 us -> 4.07 us
  transfers between devices with their start and end apart: 11 -> 14, of which waited for: 7 -> 7; matrix products, arithmetic and copies ran while one was open for 12% -> 14% of each run, Pallas kernels for 9% -> 11%
where the time goes in v7:
time: 88 us; the launch traced here: 87.4 us
  waiting for transfers between devices  33.7 us (38%)
  starting transfers between devices  24.9 us (28%)
  matrix products  12.7 us (14%)
  Pallas kernels  11.3 us (13%)
  local copies, waits for them, and re-layouts  4.17 us (5%)
    ppermute x9, waiting for transfers between devices, along(): lax.ppermute(array, 'near', [(i, (i + steps) % near_count) for i in range...  19.5 us
    ppermute x9, starting transfers between devices, along(): lax.ppermute(array, 'near', [(i, (i + steps) % near_count) for i in range...  13.4 us
    dot_general x2, matrix products, local(): lax.dot_general(got[:, :width], weight, (((1,), (1,)), ((), ())), preferr...  10.6 us
    all_to_all x2, waiting for transfers between devices, local(): lax.all_to_all(picked.reshape(far_count, -1, picked.shape[1]), 'far', spl...  7.48 us
    all_to_all x2, starting transfers between devices, local(): lax.all_to_all(picked.reshape(far_count, -1, picked.shape[1]), 'far', spl...  7.07 us
    pallas_call x1, Pallas kernels, down_rows(): pl.pallas_call(functools.partial(down_kernel, far_count, capacity, width)...  7.06 us
    all_to_all x1, waiting for transfers between devices, local(): lax.all_to_all(returned.reshape(experts, capacity, hidden_width), ('far',...  6.74 us
    all_to_all x1, starting transfers between devices, local(): lax.all_to_all(returned.reshape(experts, capacity, hidden_width), ('far',...  4.39 us
  transfers between devices with their start and end apart: 14, of which 7 were waited for; matrix products, arithmetic and copies ran while one was open for 14% of the time, Pallas kernels for 11%

profile of v7, /device:TPU:0, one launch (start us, length us, event | category | flops | bytes accessed | tf_op | source)
XLA Modules:
  0.0 87.4 jit_solution(12733863300170769145)
XLA Ops:
  0.6 3.1 %collective-permute-start.1 = (bf16[32,4096]{1,0:T(8,128)(2,1)}, bf16[32,4096]{1,0:T(8,128)(2,1)S(1)}, u32[]{:S(2)}, u32[]{:S(2)}) collective-permute-start(bf16[32,4096]{1,0:T(8,128)(2,1)} %refs_3_.1), channel_id=1, source_target_pairs={{0,1},{1,2},{2,3},{3,0},{4,5},{5,6},{6,7},{7,4},{8,9},{9,10},{10,1... | collective-permute-start | bytes 786440 | tf_op jit(solution)/shard_map/ppermute | solution.py:210
  3.7 8.5 %collective-permute-done.1.refs_4_ = bf16[32,4096]{1,0:T(8,128)(2,1)S(1)} collective-permute-done((bf16[32,4096]{1,0:T(8,128)(2,1)}, bf16[32,4096]{1,0:T(8,128)(2,1)S(1)}, u32[]{:S(2)}, u32[]{:S(2)}) %collective-permute-start.1) | collective-permute-done | bytes 262176 | tf_op jit(solution)/shard_map/ppermute | solution.py:210
  12.2 0.0 collective-permute-start.2
  12.3 1.3 %collective-permute-start.4 = (s32[8,32]{1,0:T(8,128)}, s32[8,32]{1,0:T(8,128)S(1)}, u32[]{:S(2)}, u32[]{:S(2)}) collective-permute-start(s32[8,32]{1,0:T(8,128)} %bitcast.39), channel_id=1, source_target_pairs={{0,1},{1,2},{2,3},{3,0},{4,5},{5,6},{6,7},{7,4},{8,9},{9,10},{10,1... | collective-permute-start | bytes 3080 | tf_op jit(solution)/shard_map/ppermute | solution.py:210
  13.5 3.1 %collective-permute-start.5 = (s32[8,32]{1,0:T(8,128)}, s32[8,32]{1,0:T(8,128)S(1)}, u32[]{:S(2)}, u32[]{:S(2)}) collective-permute-start(s32[8,32]{1,0:T(8,128)} %bitcast.40), channel_id=1, source_target_pairs={{0,2},{1,3},{2,0},{3,1},{4,6},{5,7},{6,4},{7,5},{8,10},{9,11},{10,... | collective-permute-start | bytes 3080 | tf_op jit(solution)/shard_map/ppermute | solution.py:210
  16.6 0.0 copy-start
  16.6 1.0 %copy-done = bf16[32,8,768]{2,1,0:T(8,128)(2,1)S(1)} copy-done((bf16[32,8,768]{2,1,0:T(8,128)(2,1)S(1)}, bf16[32,8,768]{2,1,0:T(8,128)(2,1)}, u32[]{:S(2)}) %copy-start) | copy-done | bytes 393240
  17.6 0.7 copy-done.3
  18.3 0.7 copy-done.4
  19.0 0.7 send_rows.1
  19.7 2.0 %collective-permute-done.4.refs_1_ = s32[8,32]{1,0:T(8,128)S(1)} collective-permute-done((s32[8,32]{1,0:T(8,128)}, s32[8,32]{1,0:T(8,128)S(1)}, u32[]{:S(2)}, u32[]{:S(2)}) %collective-permute-start.4) | collective-permute-done | bytes 1056 | tf_op jit(solution)/shard_map/ppermute | solution.py:210
  21.8 0.0 collective-permute-done.5.refs_2_
  21.8 0.0 collective-permute-done.2.refs_5_
  21.8 0.9 %copy-done.2 = bf16[32,4096]{1,0:T(8,128)(2,1)S(1)} copy-done((bf16[32,4096]{1,0:T(8,128)(2,1)S(1)}, bf16[32,4096]{1,0:T(8,128)(2,1)}, u32[]{:S(2)}) %copy-start.2) | copy-done | bytes 262168
  22.7 2.0 %pick_rows.2 = bf16[192,4096]{1,0:T(8,128)(2,1)} custom-call(s32[1]{0:T(128)} %bitcast.near_ref, s32[8,32]{1,0:T(8,128)S(1)} %bitcast.43, s32[8,32]{1,0:T(8,128)S(1)} %collective-permute-done.4.refs_1_, s32[8,32]{1,0:T(8,128)S(1)} %collective-permute-done.5.refs_2_, bf16[32,4096]{1,0:T(8,128)(2,1)S(1)} %copy-done.2, ...), custom_call_target="tpu_custom_call" | custom-call | flops 100663296 | bytes 3145728 | tf_op jit(solution)/shard_map/pick_rows/pallas_call | solution.py:149
  24.7 3.6 %all-to-all-start = ((bf16[4,48,4096]{2,1,0:T(8,128)(2,1)}), bf16[4,48,4096]{2,1,0:T(8,128)(2,1)S(1)}, u32[]{:S(2)}, u32[]{:S(2)}) async-start(bf16[4,48,4096]{2,1,0:T(8,128)(2,1)} %bitcast.6), calls=%async_computation | async-start | bytes 3145728 | tf_op jit(solution)/shard_map/all_to_all | solution.py:240
  28.3 0.7 collective-permute-start.3
  29.0 0.1 collective-permute-start.6
  29.0 3.7 %collective-permute-start.7 = (bf16[64,768]{1,0:T(8,128)(2,1)S(1)}, bf16[64,768]{1,0:T(8,128)(2,1)S(1)}, u32[]{:S(2)}, u32[]{:S(2)}) collective-permute-start(bf16[64,768]{1,0:T(8,128)(2,1)S(1)} %get-tuple-element.26), channel_id=1, source_target_pairs={{0,2},{1,3},{2,0},{3,1},{4,6},{5,7},{6,4},{7,5},{8,10},{9,11},{10,... | collective-permute-start | bytes 294920 | tf_op jit(solution)/shard_map/ppermute | solution.py:210
  32.7 0.0 collective-permute-start.8
  32.8 1.4 %collective-permute-start = (s32[8,32]{1,0:T(8,128)}, s32[8,32]{1,0:T(8,128)S(1)}, u32[]{:S(2)}, u32[]{:S(2)}) collective-permute-start(s32[8,32]{1,0:T(8,128)} %bitcast.41), channel_id=1, source_target_pairs={{0,3},{1,0},{2,1},{3,2},{4,7},{5,4},{6,5},{7,6},{8,11},{9,8},{10,9... | collective-permute-start | bytes 3080 | tf_op jit(solution)/shard_map/ppermute | solution.py:210
  34.2 7.9 %collective-permute-done.refs_0_ = s32[8,32]{1,0:T(8,128)S(1)} collective-permute-done((s32[8,32]{1,0:T(8,128)}, s32[8,32]{1,0:T(8,128)S(1)}, u32[]{:S(2)}, u32[]{:S(2)}) %collective-permute-start) | collective-permute-done | bytes 1056 | tf_op jit(solution)/shard_map/ppermute | solution.py:210
  42.1 0.0 collective-permute-done.6.refs_3_
  42.1 1.0 %collective-permute-done.7.refs_4_ = bf16[64,768]{1,0:T(8,128)(2,1)S(1)} collective-permute-done((bf16[64,768]{1,0:T(8,128)(2,1)S(1)}, bf16[64,768]{1,0:T(8,128)(2,1)S(1)}, u32[]{:S(2)}, u32[]{:S(2)}) %collective-permute-start.7) | collective-permute-done | bytes 98336 | tf_op jit(solution)/shard_map/ppermute | solution.py:210
  43.1 0.0 collective-permute-done.8.refs_5_
  43.1 0.0 collective-permute-done.3.refs_1_
  43.1 1.5 %pick_rows.3 = bf16[64,7168]{1,0:T(8,128)(2,1)} custom-call(s32[1]{0:T(128)} %bitcast.near_ref, s32[8,32]{1,0:T(8,128)S(1)} %collective-permute-done.refs_0_, bf16[32,4096]{1,0:T(8,128)(2,1)S(1)} %collective-permute-done.3.refs_1_, bf16[64,768]{1,0:T(8,128)(2,1)S(1)} %get-tuple-element.24.refs_2_, bf16[64,768]{1,0:T(8,128)(2,1)S(1)} %collective-permute-done.6.refs_3_, ...), custom_call_target="tpu_custom_call" | custom-call | flops 58720256 | bytes 1835008 | tf_op jit(solution)/shard_map/pick_rows/pallas_call | solution.py:149
  44.6 1.7 %all-to-all-done = bf16[4,48,4096]{2,1,0:T(8,128)(2,1)S(1)} async-done(((bf16[4,48,4096]{2,1,0:T(8,128)(2,1)}), bf16[4,48,4096]{2,1,0:T(8,128)(2,1)S(1)}, u32[]{:S(2)}, u32[]{:S(2)}) %all-to-all-start) | async-done | bytes 1572896 | tf_op jit(solution)/shard_map/all_to_all | solution.py:240
  46.2 3.5 %all-to-all-start.1 = ((bf16[4,16,7168]{2,1,0:T(8,128)(2,1)}), bf16[4,16,7168]{2,1,0:T(8,128)(2,1)S(1)}, u32[]{:S(2)}, u32[]{:S(2)}) async-start(bf16[4,16,7168]{2,1,0:T(8,128)(2,1)} %bitcast.8), calls=%async_computation.1 | async-start | bytes 1835008 | tf_op jit(solution)/shard_map/all_to_all | solution.py:240
  49.8 0.1 collective-permute-start.9
  49.8 5.7 %fusion.4 = bf16[192,768]{1,0:T(8,128)(2,1)} fusion(bf16[192,4096]{1,0:T(8,128)(2,1)S(1)} %bitcast.32, bf16[1,768,4096]{2,1,0:T(8,128)(2,1)} %param.9), kind=kOutput, calls=%fused_computation.5 | convolution fusion | flops 1208107008 | bytes 8159232 | tf_op jit(solution)/shard_map/dot_general | solution.py:250
  55.6 5.8 %all-to-all-done.1 = bf16[4,16,7168]{2,1,0:T(8,128)(2,1)S(1)} async-done(((bf16[4,16,7168]{2,1,0:T(8,128)(2,1)}), bf16[4,16,7168]{2,1,0:T(8,128)(2,1)S(1)}, u32[]{:S(2)}, u32[]{:S(2)}) %all-to-all-start.1) | async-done | bytes 917536 | tf_op jit(solution)/shard_map/all_to_all | solution.py:240
  61.4 0.0 collective-permute-start.10
  61.4 4.9 %fusion.7 = bf16[64,768]{1,0:T(8,128)(2,1)S(1)} fusion(bf16[1,768,4096]{2,1,0:T(8,128)(2,1)} %param.9, bf16[64,7168]{1,0:T(8,128)(2,1)S(1)} %bitcast.35), kind=kOutput, calls=%fused_computation.6 | convolution fusion | flops 402702336 | bytes 6914048 | tf_op jit(solution)/shard_map/dot_general | solution.py:250
  66.2 0.0 copy-done.6
  66.2 0.0 copy-start.1
  66.3 1.1 %convolution_convert_fusion = bf16[256,768]{1,0:T(8,128)(2,1)} fusion(bf16[64,768]{1,0:T(8,128)(2,1)S(1)} %fusion.7, bf16[192,768]{1,0:T(8,128)(2,1)S(1)} %copy-done.6, s32[256]{0:T(256)S(1)} %and_select_fusion.3), kind=kOutput, calls=%fused_computation.4 | convolution fusion | flops 101711872 | bytes 787456 | tf_op jit(solution)/shard_map/dot_general | solution.py:18
  67.3 4.4 %all-to-all-start.2 = ((bf16[16,16,768]{2,1,0:T(8,128)(2,1)}), bf16[16,16,768]{2,1,0:T(8,128)(2,1)S(1)}, u32[]{:S(2)}, u32[]{:S(2)}) async-start(bf16[16,16,768]{2,1,0:T(8,128)(2,1)} %bitcast.47), calls=%async_computation.2 | async-start | bytes 786432 | tf_op jit(solution)/shard_map/all_to_all | solution.py:256
  71.7 0.0 copy-done.5
  71.7 0.1 copy.12
  71.8 0.1 copy.13
  71.9 0.0 collective-permute-done.9.refs_2_
  71.9 0.0 collective-permute-done.10.refs_3_
  71.9 7.1 %down_rows.1 = bf16[384,4096]{1,0:T(8,128)(2,1)} custom-call(s32[1]{0:T(128)} %bitcast.12.replica_ref, bf16[192,4096]{1,0:T(8,128)(2,1)S(1)} %bitcast.33, bf16[64,7168]{1,0:T(8,128)(2,1)S(1)} %bitcast.36, bf16[192,4096]{1,0:T(8,128)(2,1)} %collective-permute-done.9.refs_2_, bf16[64,7168]{1,0:T(8,128)(2,1)} %collective-permute-done.10.refs_3_), custom_call_target="tpu_custom_call" | custom-call | flops 1610612736 | bytes 7340032 | tf_op jit(solution)/shard_map/down_rows/pallas_call | solution.py:179
  79.0 6.7 %all-to-all-done.2 = bf16[16,16,768]{2,1,0:T(8,128)(2,1)S(1)} async-done(((bf16[16,16,768]{2,1,0:T(8,128)(2,1)}), bf16[16,16,768]{2,1,0:T(8,128)(2,1)S(1)}, u32[]{:S(2)}, u32[]{:S(2)}) %all-to-all-start.2) | async-done | bytes 393248 | tf_op jit(solution)/shard_map/all_to_all | solution.py:256
  85.7 0.0 copy-done.1
  85.7 1.0 %multiply_reduce_fusion = (f32[32,8]{1,0:T(8,128)S(1)}, bf16[32,8,768]{2,1,0:T(8,128)(2,1)}) fusion(bf16[32,8,768]{2,1,0:T(8,128)(2,1)S(1)} %copy-done.1, f32[32,8]{1,0:T(8,128)S(1)} %copy.12, bf16[256,768,1]{1,0,2:T(8,128)(2,1)S(1)} %bitcast.46, bf16[256,256]{1,0:T(8,128)(2,1)S(1)} %copy.13), kind=kOutput, calls=%fused_computation.7 | convolution fusion | flops 101646080 | bytes 1312768 | tf_op jit(solution)/shard_map/dot_general | solution.py:270
  86.8 0.7 copy.14
  (6 shorter events, 0.0 us)
Async XLA Ops:
  0.6 11.6 %collective-permute-start.1 = (bf16[32,4096]{1,0:T(8,128)(2,1)}, bf16[32,4096]{1,0:T(8,128)(2,1)S(1)}, u32[]{:S(2)}, u32[]{:S(2)}) collective-permute-start(bf16[32,4096]{1,0:T(8,128)(2,1)} %refs_3_.1), channel_id=1, source_target_pairs={{0,1},{1,2},{2,3},{3,0},{4,5},{5,6},{6,7},{7,4},{8,9},{9,10},{10,1... | collective-permute-start | bytes 786440 | tf_op jit(solution)/shard_map/ppermute | solution.py:210
  12.2 9.5 %collective-permute-start.2 = (bf16[32,4096]{1,0:T(8,128)(2,1)S(1)}, bf16[32,4096]{1,0:T(8,128)(2,1)S(1)}, u32[]{:S(2)}, u32[]{:S(2)}) collective-permute-start(bf16[32,4096]{1,0:T(8,128)(2,1)S(1)} %collective-permute-done.1.refs_4_), channel_id=1, source_target_pairs={{0,1},{1,2},{2,3},{3,0},{4,5},{5,6},{6,7},{7,4},{8,9},{9,10},{10,1... | collective-permute-start | bytes 786440 | tf_op jit(solution)/shard_map/ppermute | solution.py:210
  12.3 9.5 %collective-permute-start.4 = (s32[8,32]{1,0:T(8,128)}, s32[8,32]{1,0:T(8,128)S(1)}, u32[]{:S(2)}, u32[]{:S(2)}) collective-permute-start(s32[8,32]{1,0:T(8,128)} %bitcast.39), channel_id=1, source_target_pairs={{0,1},{1,2},{2,3},{3,0},{4,5},{5,6},{6,7},{7,4},{8,9},{9,10},{10,1... | collective-permute-start | bytes 3080 | tf_op jit(solution)/shard_map/ppermute | solution.py:210
  13.5 8.2 %collective-permute-start.5 = (s32[8,32]{1,0:T(8,128)}, s32[8,32]{1,0:T(8,128)S(1)}, u32[]{:S(2)}, u32[]{:S(2)}) collective-permute-start(s32[8,32]{1,0:T(8,128)} %bitcast.40), channel_id=1, source_target_pairs={{0,2},{1,3},{2,0},{3,1},{4,6},{5,7},{6,4},{7,5},{8,10},{9,11},{10,... | collective-permute-start | bytes 3080 | tf_op jit(solution)/shard_map/ppermute | solution.py:210
  16.6 1.0 %copy-start = (bf16[32,8,768]{2,1,0:T(8,128)(2,1)S(1)}, bf16[32,8,768]{2,1,0:T(8,128)(2,1)}, u32[]{:S(2)}) copy-start(bf16[32,8,768]{2,1,0:T(8,128)(2,1)} %param.6) | copy-start | bytes 1179652
  17.6 0.7 copy-start.3
  18.3 0.7 copy-start.4
  21.8 1.0 %copy-start.2 = (bf16[32,4096]{1,0:T(8,128)(2,1)S(1)}, bf16[32,4096]{1,0:T(8,128)(2,1)}, u32[]{:S(2)}) copy-start(bf16[32,4096]{1,0:T(8,128)(2,1)} %refs_3_.1) | copy-start | bytes 786436
  24.7 21.5 %all-to-all-start = ((bf16[4,48,4096]{2,1,0:T(8,128)(2,1)}), bf16[4,48,4096]{2,1,0:T(8,128)(2,1)S(1)}, u32[]{:S(2)}, u32[]{:S(2)}) async-start(bf16[4,48,4096]{2,1,0:T(8,128)(2,1)} %bitcast.6), calls=%async_computation | async-start | bytes 3145728 | tf_op jit(solution)/shard_map/all_to_all | solution.py:240
  28.3 14.8 %collective-permute-start.3 = (bf16[32,4096]{1,0:T(8,128)(2,1)S(1)}, bf16[32,4096]{1,0:T(8,128)(2,1)S(1)}, u32[]{:S(2)}, u32[]{:S(2)}) collective-permute-start(bf16[32,4096]{1,0:T(8,128)(2,1)S(1)} %collective-permute-done.2.refs_5_), channel_id=1, source_target_pairs={{0,1},{1,2},{2,3},{3,0},{4,5},{5,6},{6,7},{7,4},{8,9},{9,10},{10,1... | collective-permute-start | bytes 786440 | tf_op jit(solution)/shard_map/ppermute | solution.py:210
  29.0 13.1 %collective-permute-start.6 = (bf16[64,768]{1,0:T(8,128)(2,1)S(1)}, bf16[64,768]{1,0:T(8,128)(2,1)S(1)}, u32[]{:S(2)}, u32[]{:S(2)}) collective-permute-start(bf16[64,768]{1,0:T(8,128)(2,1)S(1)} %get-tuple-element.25), channel_id=1, source_target_pairs={{0,1},{1,2},{2,3},{3,0},{4,5},{5,6},{6,7},{7,4},{8,9},{9,10},{10,1... | collective-permute-start | bytes 294920 | tf_op jit(solution)/shard_map/ppermute | solution.py:210
  29.0 14.1 %collective-permute-start.7 = (bf16[64,768]{1,0:T(8,128)(2,1)S(1)}, bf16[64,768]{1,0:T(8,128)(2,1)S(1)}, u32[]{:S(2)}, u32[]{:S(2)}) collective-permute-start(bf16[64,768]{1,0:T(8,128)(2,1)S(1)} %get-tuple-element.26), channel_id=1, source_target_pairs={{0,2},{1,3},{2,0},{3,1},{4,6},{5,7},{6,4},{7,5},{8,10},{9,11},{10,... | collective-permute-start | bytes 294920 | tf_op jit(solution)/shard_map/ppermute | solution.py:210
  32.7 10.3 %collective-permute-start.8 = (bf16[64,768]{1,0:T(8,128)(2,1)S(1)}, bf16[64,768]{1,0:T(8,128)(2,1)S(1)}, u32[]{:S(2)}, u32[]{:S(2)}) collective-permute-start(bf16[64,768]{1,0:T(8,128)(2,1)S(1)} %get-tuple-element.27), channel_id=1, source_target_pairs={{0,3},{1,0},{2,1},{3,2},{4,7},{5,4},{6,5},{7,6},{8,11},{9,8},{10,9... | collective-permute-start | bytes 294920 | tf_op jit(solution)/shard_map/ppermute | solution.py:210
  32.8 9.3 %collective-permute-start = (s32[8,32]{1,0:T(8,128)}, s32[8,32]{1,0:T(8,128)S(1)}, u32[]{:S(2)}, u32[]{:S(2)}) collective-permute-start(s32[8,32]{1,0:T(8,128)} %bitcast.41), channel_id=1, source_target_pairs={{0,3},{1,0},{2,1},{3,2},{4,7},{5,4},{6,5},{7,6},{8,11},{9,8},{10,9... | collective-permute-start | bytes 3080 | tf_op jit(solution)/shard_map/ppermute | solution.py:210
  46.2 15.2 %all-to-all-start.1 = ((bf16[4,16,7168]{2,1,0:T(8,128)(2,1)}), bf16[4,16,7168]{2,1,0:T(8,128)(2,1)S(1)}, u32[]{:S(2)}, u32[]{:S(2)}) async-start(bf16[4,16,7168]{2,1,0:T(8,128)(2,1)} %bitcast.8), calls=%async_computation.1 | async-start | bytes 1835008 | tf_op jit(solution)/shard_map/all_to_all | solution.py:240
  49.8 22.1 %collective-permute-start.9 = (bf16[192,4096]{1,0:T(8,128)(2,1)S(1)}, bf16[192,4096]{1,0:T(8,128)(2,1)}, u32[]{:S(2)}, u32[]{:S(2)}) collective-permute-start(bf16[192,4096]{1,0:T(8,128)(2,1)S(1)} %bitcast.31), channel_id=1, source_target_pairs={{0,16},{16,0},{1,17},{17,1},{2,18},{18,2},{3,19},{19,3},{4,20},{20... | collective-permute-start | bytes 4718600 | tf_op jit(solution)/shard_map/ppermute | solution.py:213
  55.6 16.2 %copy-start.5 = (f32[32,8]{0,1:T(8,128)S(1)}, f32[32,8]{0,1:T(8,128)}, u32[]{:S(2)}) copy-start(f32[32,8]{0,1:T(8,128)} %param.7) | copy-start | bytes 3076
  61.4 4.9 %copy-start.6 = (bf16[192,768]{1,0:T(8,128)(2,1)S(1)}, bf16[192,768]{1,0:T(8,128)(2,1)}, u32[]{:S(2)}) copy-start(bf16[192,768]{1,0:T(8,128)(2,1)} %fusion.4) | copy-start | bytes 884740
  61.4 10.5 %collective-permute-start.10 = (bf16[64,7168]{1,0:T(8,128)(2,1)S(1)}, bf16[64,7168]{1,0:T(8,128)(2,1)}, u32[]{:S(2)}, u32[]{:S(2)}) collective-permute-start(bf16[64,7168]{1,0:T(8,128)(2,1)S(1)} %bitcast.34), channel_id=1, source_target_pairs={{0,16},{16,0},{1,17},{17,1},{2,18},{18,2},{3,19},{19,3},{4,20},{20... | collective-permute-start | bytes 2752520 | tf_op jit(solution)/shard_map/ppermute | solution.py:213
  66.2 19.5 %copy-start.1 = (bf16[32,8,768]{2,1,0:T(8,128)(2,1)S(1)}, bf16[32,8,768]{2,1,0:T(8,128)(2,1)}, u32[]{:S(2)}) copy-start(bf16[32,8,768]{2,1,0:T(8,128)(2,1)} %param.6) | copy-start | bytes 1179652
  67.3 18.4 %all-to-all-start.2 = ((bf16[16,16,768]{2,1,0:T(8,128)(2,1)}), bf16[16,16,768]{2,1,0:T(8,128)(2,1)S(1)}, u32[]{:S(2)}, u32[]{:S(2)}) async-start(bf16[16,16,768]{2,1,0:T(8,128)(2,1)} %bitcast.47), calls=%async_computation.2 | async-start | bytes 786432 | tf_op jit(solution)/shard_map/all_to_all | solution.py:256

commit v8 on v7

v8 whole, which is shorter than its diff:
```python
import functools

import jax
import jax.numpy as jnp
from jax import lax
from jax.experimental import pallas as pl
from jax.experimental.pallas import tpu as pltpu
from jax.sharding import PartitionSpec as P

MIB = 1024 * 1024


def iota(shape, dim):
    return lax.broadcasted_iota(jnp.int32, shape, dim)


def exact_dot(one_hot, values):
    return jnp.dot(one_hot, values, preferred_element_type=jnp.float32)


def send_kernel(far_count, near_count, capacity, near_ref, ids_ref, gates_ref, hidden_ref, send_ref, back_ref):
    top_count, tok_local = ids_ref.shape
    rows = tok_local * top_count
    experts = far_count * near_count
    slots = experts * capacity
    near = near_ref[0]
    wide = jnp.where(iota((tok_local, rows), 1) // top_count == iota((tok_local, rows), 0), 1.0, 0.0).astype(jnp.bfloat16)
    mine = iota((top_count, rows), 1) % top_count == iota((top_count, rows), 0)

    def line(values):
        spread = jnp.zeros((top_count, rows), jnp.float32)
        for _ in range(3):
            piece = values.astype(jnp.bfloat16)
            values = values - piece.astype(jnp.float32)
            spread = spread + exact_dot(piece, wide)
        return jnp.sum(jnp.where(mine, spread, 0.0), axis=0, keepdims=True)

    ids = line(ids_ref[...].astype(jnp.float32)).astype(jnp.int32)
    gates = line(gates_ref[...])
    named = iota((experts, rows), 0) == ids
    before = jnp.where(iota((rows, rows), 0) < iota((rows, rows), 1), 1.0, 0.0).astype(jnp.bfloat16)
    counts = exact_dot(jnp.where(named, 1.0, 0.0).astype(jnp.bfloat16), before)
    ranks = jnp.sum(jnp.where(named, counts, 0.0), axis=0, keepdims=True).astype(jnp.int32)
    steps = (ids % near_count - near + near_count) % near_count
    out_slots = (ids // near_count * near_count + steps) * capacity + ranks
    back_slots = ids * capacity + ranks
    back_ref[...] = jnp.where(iota((slots, rows), 0) == back_slots, 1.0, 0.0).astype(jnp.bfloat16)
    place = iota((slots, rows), 0) == out_slots
    gate = jnp.sum(jnp.where(place, gates, 0.0), axis=1, keepdims=True)
    picked = exact_dot(jnp.where(place, 1.0, 0.0).astype(jnp.bfloat16), hidden_ref[...])
    send_ref[...] = (picked * gate).astype(jnp.bfloat16)


def plan_kernel(far_count, near_count, capacity, groups, near_ref, *refs):
    all_ids, outs = refs[: -len(groups)], refs[-len(groups) :]
    tok_local = all_ids[0].shape[1]
    near = near_ref[0]
    lead = max(8, far_count)
    for group, out_ref in zip(groups, outs):
        count = len(group)
        slots, cols = out_ref.shape
        ids = jnp.concatenate([all_ids[step][...] for step in group], axis=1)
        named = jnp.zeros((lead, cols), jnp.float32)
        for far in range(far_count):
            hit = jnp.where(ids == far * near_count + near, 1.0, 0.0)
            named = jnp.where(iota((lead, cols), 0) == far, jnp.sum(hit, axis=0, keepdims=True), named)
        row, col = iota((cols, cols), 0), iota((cols, cols), 1)
        before = jnp.where((row < col) & (row // tok_local == col // tok_local), 1.0, 0.0).astype(jnp.bfloat16)
        rank = exact_dot(named.astype(jnp.bfloat16), before)
        place = jnp.where(named > 0.5, rank, float(capacity)).astype(jnp.bfloat16)
        per_far = count * capacity
        spread = jnp.where(iota((slots, lead), 0) // per_far == iota((slots, lead), 1), 1.0, 0.0).astype(jnp.bfloat16)
        slot = iota((slots, cols), 0) % per_far
        pick = (iota((slots, cols), 1) // tok_local == slot // capacity) & (
            exact_dot(spread, place).astype(jnp.int32) == slot % capacity
        )
        out_ref[...] = jnp.where(pick, 1.0, 0.0).astype(jnp.bfloat16)


def pick_kernel(pick_ref, *refs):
    blocks, (out_ref, first_ref, sem) = refs[:-3], refs[-3:]
    copy = pltpu.make_async_copy(blocks[0], first_ref, sem)
    copy.start()
    copy.wait()
    width = first_ref.shape[1]
    step = min(width, 512)
    for start in range(0, width, step):
        tokens = [first_ref[:, start : start + step]] + [block[:, start : start + step] for block in blocks[1:]]
        out_ref[:, start : start + step] = exact_dot(pick_ref[...], jnp.concatenate(tokens, axis=0)).astype(jnp.bfloat16)


def join_kernel(*refs):
    out_ref = refs[-1]
    start = 0
    for ref in refs[:-1]:
        out_ref[:, start : start + ref.shape[1]] = ref[...]
        start += ref.shape[1]


def hold_kernel(weight_ref, out_ref, sem):
    copy = pltpu.make_async_copy(weight_ref, out_ref, sem)
    copy.start()
    copy.wait()


def down_kernel(capacity, replica_ref, *refs):
    rows, (out_ref, turned_ref) = refs[:-2], refs[-2:]
    step = pl.program_id(0)
    share, tile = out_ref.shape

    @pl.when(step == 0)
    def _():
        hids = []
        for early, late in ((rows[0], rows[2]), (rows[3], rows[5])):
            lines, last = early.shape[0], late.shape[0]
            count = lines // last
            hidden_width = late.shape[1] // (count + 1)
            row, col = iota((lines, last), 0), iota((lines, last), 1)
            match = (row // (count * capacity) == col // capacity) & (row % capacity == col % capacity)
            total = jnp.zeros((lines, share), jnp.float32)
            for i in range(count + 1):
                start = pl.multiple_of(i * hidden_width + replica_ref[0] * share, 128)
                hid = late[:, pl.ds(start, share)]
                if i < count:
                    order = jnp.where(match & (row // capacity % count == i), 1.0, 0.0).astype(jnp.bfloat16)
                    total = total + exact_dot(order, hid)
                else:
                    hids += [total, hid.astype(jnp.float32)]
        turned_ref[...] = jnp.concatenate(hids, axis=0).T.astype(jnp.bfloat16)

    cols = pl.ds(pl.multiple_of(step * tile, 128), tile)
    tokens = jnp.concatenate([rows[i][:, cols] for i in (0, 1, 3, 4)], axis=0)
    out_ref[...] = exact_dot(turned_ref[...], tokens).astype(jnp.bfloat16)


def scalar_spec():
    return pl.BlockSpec(memory_space=pltpu.SMEM)


def params(mib):
    return pltpu.CompilerParams(vmem_limit_bytes=mib * MIB)


def send_rows(far_count, near_count, capacity, near, ids, gates, hidden):
    slots = far_count * near_count * capacity
    rows, wide = hidden.shape
    vmem = pl.BlockSpec(memory_space=pltpu.VMEM)
    return pl.pallas_call(
        functools.partial(send_kernel, far_count, near_count, capacity),
        out_shape=[
            jax.ShapeDtypeStruct((slots, wide), jnp.bfloat16),
            jax.ShapeDtypeStruct((slots, rows), jnp.bfloat16),
        ],
        in_specs=[scalar_spec()] + [vmem] * 3,
        out_specs=[vmem] * 2,
        compiler_params=params(12),
        cost_estimate=pl.CostEstimate(flops=2 * rows * rows * wide, bytes_accessed=4 * rows * wide, transcendentals=0),
        name="send_rows",
    )(near, ids, gates, hidden)


def plan_rows(far_count, near_count, capacity, groups, near, ids):
    tok_local = ids[0].shape[1]
    vmem = pl.BlockSpec(memory_space=pltpu.VMEM)
    return pl.pallas_call(
        functools.partial(plan_kernel, far_count, near_count, capacity, groups),
        out_shape=[
            jax.ShapeDtypeStruct((far_count * len(group) * capacity, len(group) * tok_local), jnp.bfloat16)
            for group in groups
        ],
        in_specs=[scalar_spec()] + [vmem] * len(ids),
        out_specs=[vmem] * len(groups),
        compiler_params=params(12),
        name="plan_rows",
    )(near, *ids)


def pick_rows(pick, blocks):
    width = blocks[0].shape[1]
    slots = pick.shape[0]
    vmem = pl.BlockSpec(memory_space=pltpu.VMEM)
    return pl.pallas_call(
        pick_kernel,
        out_shape=jax.ShapeDtypeStruct((slots, width), jnp.bfloat16),
        in_specs=[vmem, pl.BlockSpec(memory_space=pl.ANY)] + [vmem] * (len(blocks) - 1),
        out_specs=vmem,
        scratch_shapes=[pltpu.VMEM(blocks[0].shape, jnp.bfloat16), pltpu.SemaphoreType.DMA],
        compiler_params=params(12),
        cost_estimate=pl.CostEstimate(flops=2 * slots * 64 * width, bytes_accessed=4 * slots * width, transcendentals=0),
        name="pick_rows",
    )(pick, *blocks)


def join_rows(arrays):
    vmem = pl.BlockSpec(memory_space=pltpu.VMEM)
    shape = (arrays[0].shape[0], sum(array.shape[1] for array in arrays))
    return pl.pallas_call(
        join_kernel,
        out_shape=jax.ShapeDtypeStruct(shape, jnp.bfloat16),
        in_specs=[vmem] * len(arrays),
        out_specs=vmem,
        compiler_params=params(8),
        name="join_rows",
    )(*arrays)


def hold(weight):
    return pl.pallas_call(
        hold_kernel,
        out_shape=jax.ShapeDtypeStruct(weight.shape, weight.dtype),
        in_specs=[pl.BlockSpec(memory_space=pl.ANY)],
        out_specs=pl.BlockSpec(memory_space=pltpu.VMEM),
        scratch_shapes=[pltpu.SemaphoreType.DMA],
        compiler_params=params(14),
        cost_estimate=pl.CostEstimate(flops=0, bytes_accessed=2 * weight.size, transcendentals=0),
        name="hold_weight",
    )(weight)


def back_order(far_count, near_count, capacity, near, groups):
    slots = far_count * near_count * capacity
    row = jnp.arange(slots, dtype=jnp.int32)
    far, rank = row // (near_count * capacity), row % capacity
    step = (near - row // capacity % near_count + near_count) % near_count
    source = jnp.zeros_like(row)
    start = 0
    for group in groups:
        count = len(group)
        place = start + (far * count + step - group[0]) * capacity + rank
        source = jnp.where((step >= group[0]) & (step <= group[-1]), place, source)
        start += far_count * count * capacity
    return (source[:, None] == row[None, :]).astype(jnp.bfloat16)


def down_rows(capacity, replica, rows, share):
    width = rows[0].shape[1]
    tile = min(width, 512)
    lines = sum(rows[i].shape[0] for i in (0, 1, 3, 4))
    whole = lambda array: pl.BlockSpec(array.shape, lambda i: (0, 0))
    return pl.pallas_call(
        functools.partial(down_kernel, capacity),
        grid=(width // tile,),
        out_shape=jax.ShapeDtypeStruct((share, width), jnp.bfloat16),
        in_specs=[scalar_spec()] + [whole(array) for array in rows],
        out_specs=pl.BlockSpec((share, tile), lambda i: (0, i)),
        scratch_shapes=[pltpu.VMEM((share, lines), jnp.bfloat16)],
        compiler_params=params(32),
        cost_estimate=pl.CostEstimate(
            flops=2 * lines * width * share, bytes_accessed=2 * width * (lines + share), transcendentals=0
        ),
        name="down_rows",
    )(replica, *rows)


def local(grad_out, hidden, gates, expert_ids, w_down):
    tok_local, top_count = expert_ids.shape
    far_count = lax.axis_size("far")
    near_count = lax.axis_size("near")
    experts = far_count * near_count
    capacity = max(4, (tok_local * top_count + experts - 1) // experts)
    width = grad_out.shape[1]
    hidden_width = hidden.shape[2]
    row_total = tok_local * top_count
    slot_total = experts * capacity
    near = lax.axis_index("near")
    near_ref = near.astype(jnp.int32).reshape(1)
    groups = [list(range(near_count - 1)), [near_count - 1]]
    weight = w_down[0]

    def along(array, steps):
        return lax.ppermute(array, "near", [(i, (i + steps) % near_count) for i in range(near_count)])

    def swap(array):
        return lax.ppermute(array, "dp", [(i, i ^ 1) for i in range(lax.axis_size("dp"))])

    blocks = [grad_out, along(grad_out, 1)]
    ids = [expert_ids.T] + [along(expert_ids.T, step) for step in range(1, near_count)]
    send, back_place = send_rows(
        far_count, near_count, capacity, near_ref, ids[0], gates.T, hidden.reshape(row_total, hidden_width)
    )
    blocks[1], ids, send = lax.optimization_barrier((blocks[1], ids, send))
    for _ in range(2, near_count):
        blocks.append(along(blocks[-1], 1))
    picks = plan_rows(far_count, near_count, capacity, groups, near_ref, ids)
    weight = hold(weight)
    blocks[-2], picks, weight = lax.optimization_barrier((blocks[-2], picks, weight))
    crossed = lax.all_to_all(
        send.reshape(far_count, -1, hidden_width), "far", split_axis=0, concat_axis=0, tiled=True
    ).reshape(far_count, near_count, capacity, hidden_width)

    rows, returned = [], []
    for pick, group in zip(picks, groups):
        picked = pick_rows(pick, [blocks[step] for step in group])
        if rows:
            picked, rows[-1] = lax.optimization_barrier((picked, rows[-1]))
        else:
            picked, crossed = lax.optimization_barrier((picked, crossed))
        got = lax.all_to_all(
            picked.reshape(far_count, -1, width), "far", split_axis=0, concat_axis=0, tiled=True
        ).reshape(picked.shape)
        rows.append(got)
    hids = [crossed[:, step].reshape(-1, hidden_width) for step in range(near_count)]
    hids = join_rows(hids[:1] + [along(hids[step], step) for step in range(1, near_count)])
    for turn in range(len(rows)):
        if returned:
            rows[turn], returned[-1] = lax.optimization_barrier((rows[turn], returned[-1]))
        returned.append(
            lax.dot_general(
                rows[turn], weight, (((1,), (1,)), ((), ())), preferred_element_type=jnp.float32
            ).astype(jnp.bfloat16)
        )
    rows.append(hids)
    peers = [swap(array) for array in rows]
    order = back_order(far_count, near_count, capacity, near, groups)
    returned = exact_dot(order, jnp.concatenate(returned, axis=0)).astype(jnp.bfloat16)
    came_back = lax.all_to_all(
        returned.reshape(experts, capacity, hidden_width),
        ("far", "near"),
        split_axis=0,
        concat_axis=0,
        tiled=True,
    )

    replica = lax.axis_index("dp").astype(jnp.int32).reshape(1)
    grad_down = down_rows(capacity, replica, rows + peers, hidden_width // lax.axis_size("dp"))
    came_back, grad_down = lax.optimization_barrier((came_back, grad_down))

    back_rows = lax.dot_general(
        back_place,
        came_back.reshape(slot_total, hidden_width),
        (((0,), (0,)), ((), ())),
        preferred_element_type=jnp.float32,
    ).reshape(tok_local, top_count, hidden_width)
    grad_hidden = (gates[:, :, None] * back_rows).astype(jnp.bfloat16)
    grad_gates = jnp.sum(back_rows * hidden.astype(jnp.float32), axis=-1)
    return (grad_hidden, grad_gates, grad_down[None])


def solution(mesh):
    placed = (
        P(("dp", "far", "near"), None),
        P(("dp", "far", "near"), None, None),
        P(("dp", "far", "near"), None),
        P(("dp", "far", "near"), None),
        P(("far", "near"), None, None),
    )
    return jax.shard_map(
        local,
        mesh=mesh,
        in_specs=placed,
        out_specs=(
            P(("dp", "far", "near"), None, None),
            P(("dp", "far", "near"), None),
            P(("far", "near"), "dp", None),
        ),
        check_vma=False,
    )
```

time: 88 us -> 101 us (1.15)
  local copies, waits for them, and re-layouts: 4.17 us -> 9.92 us
  starting transfers between devices: 24.9 us -> 30.5 us
    all_to_all x1, waiting for transfers between devices: 6.74 us -> 0.01 us  [local(): lax.all_to_all(returned.reshape(experts, capacity, hidden_width), ('far',...]
    unnamed x16 -> x26, local copies, waits for them, and re-layouts: 4.07 us -> 9.14 us
    ppermute x9, waiting for transfers between devices: 19.5 us -> 23.7 us  [along(): lax.ppermute(array, 'near', [(i, (i + steps) % near_count) for i in range...]
    all_to_all x2 -> x3, starting transfers between devices: 7.07 us -> 11.1 us  [the longest x2 7.32 us: local(): lax.all_to_all(picked.reshape(far_count, -1, width), 'far', split_axis=0,...]
    all_to_all x2 -> x3, waiting for transfers between devices: 7.48 us -> 9.31 us  [the longest x2 9.31 us: local(): lax.all_to_all(picked.reshape(far_count, -1, width), 'far', split_axis=0,...]
    ppermute x9, starting transfers between devices: 13.4 us -> 14.6 us  [along(): lax.ppermute(array, 'near', [(i, (i + steps) % near_count) for i in range...]
    pallas_call x3 -> x6, Pallas kernels: 10.5 us -> 10.6 us  [the longest x1 6.87 us: down_rows(): pl.pallas_call(functools.partial(down_kernel, capacity), grid=(width // t...]
  transfers between devices with their start and end apart: 14 -> 16, of which waited for: 7 -> 7; matrix products, arithmetic and copies ran while one was open for 14% -> 13% of each run, Pallas kernels for 11% -> 12%
where the time goes in v8:
time: 101 us; the launch traced here: 100 us
  waiting for transfers between devices  33.4 us (33%)
  starting transfers between devices  30.5 us (30%)
  matrix products  13.6 us (13%)
  Pallas kernels  11.9 us (12%)
  local copies, waits for them, and re-layouts  9.92 us (10%)
    ppermute x9, waiting for transfers between devices, along(): lax.ppermute(array, 'near', [(i, (i + steps) % near_count) for i in range...  23.7 us
    ppermute x9, starting transfers between devices, along(): lax.ppermute(array, 'near', [(i, (i + steps) % near_count) for i in range...  14.6 us
    dot_general x2, matrix products, local(): lax.dot_general(rows[turn], weight, (((1,), (1,)), ((), ())), preferred_e...  10.6 us
    all_to_all x2, waiting for transfers between devices, local(): lax.all_to_all(picked.reshape(far_count, -1, width), 'far', split_axis=0,...  9.31 us
    unnamed x26, local copies, waits for them, and re-layouts  9.14 us
    all_to_all x2, starting transfers between devices, local(): lax.all_to_all(picked.reshape(far_count, -1, width), 'far', split_axis=0,...  7.32 us
    pallas_call x1, Pallas kernels, down_rows(): pl.pallas_call(functools.partial(down_kernel, capacity), grid=(width // t...  6.87 us
    all_to_all x1, starting transfers between devices, local(): lax.all_to_all(returned.reshape(experts, capacity, hidden_width), ('far',...  4.77 us
  transfers between devices with their start and end apart: 16, of which 7 were waited for; matrix products, arithmetic and copies ran while one was open for 13% of the time, Pallas kernels for 12%

profile of v8, /device:TPU:0, one launch (start us, length us, event | category | flops | bytes accessed | tf_op | source)
XLA Modules:
  0.0 100.2 jit_solution(339761024093458659)
XLA Ops:
  0.6 3.1 %collective-permute-start = (bf16[32,4096]{1,0:T(8,128)(2,1)}, bf16[32,4096]{1,0:T(8,128)(2,1)S(1)}, u32[]{:S(2)}, u32[]{:S(2)}) collective-permute-start(bf16[32,4096]{1,0:T(8,128)(2,1)} %refs_0_.1), channel_id=1, source_target_pairs={{0,1},{1,2},{2,3},{3,0},{4,5},{5,6},{6,7},{7,4},{8,9},{9,10},{10,1... | collective-permute-start | bytes 786440 | tf_op jit(solution)/shard_map/ppermute | solution.py:271
  3.7 1.6 %collective-permute-start.1 = (s32[8,32]{1,0:T(8,128)}, s32[8,32]{1,0:T(8,128)S(1)}, u32[]{:S(2)}, u32[]{:S(2)}) collective-permute-start(s32[8,32]{1,0:T(8,128)} %bitcast.43), channel_id=1, source_target_pairs={{0,1},{1,2},{2,3},{3,0},{4,5},{5,6},{6,7},{7,4},{8,9},{9,10},{10,1... | collective-permute-start | bytes 3080 | tf_op jit(solution)/shard_map/ppermute | solution.py:271
  5.3 1.1 %collective-permute-start.2 = (s32[8,32]{1,0:T(8,128)}, s32[8,32]{1,0:T(8,128)S(1)}, u32[]{:S(2)}, u32[]{:S(2)}) collective-permute-start(s32[8,32]{1,0:T(8,128)} %bitcast.44), channel_id=1, source_target_pairs={{0,2},{1,3},{2,0},{3,1},{4,6},{5,7},{6,4},{7,5},{8,10},{9,11},{10,... | collective-permute-start | bytes 3080 | tf_op jit(solution)/shard_map/ppermute | solution.py:271
  6.4 2.9 %collective-permute-start.3 = (s32[8,32]{1,0:T(8,128)}, s32[8,32]{1,0:T(8,128)S(1)}, u32[]{:S(2)}, u32[]{:S(2)}) collective-permute-start(s32[8,32]{1,0:T(8,128)} %bitcast.45), channel_id=1, source_target_pairs={{0,3},{1,0},{2,1},{3,2},{4,7},{5,4},{6,5},{7,6},{8,11},{9,8},{10,9... | collective-permute-start | bytes 3080 | tf_op jit(solution)/shard_map/ppermute | solution.py:271
  9.2 1.0 copy-done.2
  10.2 0.7 copy-done.5
  10.9 0.7 copy-done.7
  11.6 1.3 %send_rows.1 = (bf16[256,768]{1,0:T(8,128)(2,1)}, bf16[256,256]{1,0:T(8,128)(2,1)S(1)}) custom-call(s32[1]{0:T(128)} %bitcast.near_ref, s32[8,32]{1,0:T(8,128)S(1)} %bitcast.46, f32[8,32]{1,0:T(8,128)S(1)} %bitcast.42, bf16[256,768]{1,0:T(8,128)(2,1)S(1)} %bitcast.39), custom_call_target="tpu_custom_call" | custom-call | flops 100663296 | bytes 786432 | tf_op jit(solution)/shard_map/send_rows/pallas_call | solution.py:148
  12.9 0.0 collective-permute-done.1.refs_1_
  12.9 0.0 collective-permute-done.2.refs_2_
  12.9 0.0 collective-permute-done.3.refs_3_
  12.9 0.0 collective-permute-done.refs_1_
  12.9 3.7 %all-to-all-start = ((bf16[4,64,768]{2,1,0:T(8,128)(2,1)}), bf16[4,64,768]{2,1,0:T(8,128)(2,1)S(1)}, u32[]{:S(2)}, u32[]{:S(2)}) async-start(bf16[4,64,768]{2,1,0:T(8,128)(2,1)} %bitcast.7), calls=%async_computation | async-start | bytes 786432 | tf_op jit(solution)/shard_map/all_to_all | solution.py:287
  16.7 0.2 collective-permute-start.4
  16.9 2.8 %copy-done.1 = bf16[1,768,4096]{2,1,0:T(8,128)(2,1)S(1)} copy-done((bf16[1,768,4096]{2,1,0:T(8,128)(2,1)S(1)}, bf16[1,768,4096]{2,1,0:T(8,128)(2,1)}, u32[]{:S(2)}) %copy-start.1) | copy-done | bytes 6291480
  19.7 0.4 hold_weight.1
  20.1 2.6 %copy-done = bf16[768,4096]{1,0:T(8,128)(2,1)} copy-done((bf16[768,4096]{1,0:T(8,128)(2,1)}, bf16[768,4096]{1,0:T(8,128)(2,1)S(1)}, u32[]{:S(2)}) %copy-start) | copy-done | bytes 6291480
  22.7 0.4 plan_rows.1
  23.1 2.1 %collective-permute-done.4.refs_2_ = bf16[32,4096]{1,0:T(8,128)(2,1)S(1)} collective-permute-done((bf16[32,4096]{1,0:T(8,128)(2,1)S(1)}, bf16[32,4096]{1,0:T(8,128)(2,1)S(1)}, u32[]{:S(2)}, u32[]{:S(2)}) %collective-permute-start.4) | collective-permute-done | bytes 262176 | tf_op jit(solution)/shard_map/ppermute | solution.py:271
  25.2 1.7 %pick_rows.3 = bf16[192,4096]{1,0:T(8,128)(2,1)} custom-call(bf16[192,96]{1,0:T(8,128)(2,1)S(1)} %get-tuple-element.35.pick_ref, bf16[32,4096]{1,0:T(8,128)(2,1)S(1)} %copy-done.4, bf16[32,4096]{1,0:T(8,128)(2,1)S(1)} %collective-permute-done.refs_1_, bf16[32,4096]{1,0:T(8,128)(2,1)S(1)} %collective-permute-done.4.refs_2_), custom_call_target="tpu_custom_call" | custom-call | flops 100663296 | bytes 3145728 | tf_op jit(solution)/shard_map/pick_rows/pallas_call | solution.py:182
  27.0 0.0 all-to-all-done
  27.0 3.8 %all-to-all-start.1 = ((bf16[4,48,4096]{2,1,0:T(8,128)(2,1)}), bf16[4,48,4096]{2,1,0:T(8,128)(2,1)S(1)}, u32[]{:S(2)}, u32[]{:S(2)}) async-start(bf16[4,48,4096]{2,1,0:T(8,128)(2,1)} %bitcast.9), calls=%async_computation.1 | async-start | bytes 3145728 | tf_op jit(solution)/shard_map/all_to_all | solution.py:298
  30.8 0.0 collective-permute-start.5
  30.8 8.1 %collective-permute-done.5.refs_0_ = bf16[32,4096]{1,0:T(8,128)(2,1)S(1)} collective-permute-done((bf16[32,4096]{1,0:T(8,128)(2,1)S(1)}, bf16[32,4096]{1,0:T(8,128)(2,1)S(1)}, u32[]{:S(2)}, u32[]{:S(2)}) %collective-permute-start.5) | collective-permute-done | bytes 262176 | tf_op jit(solution)/shard_map/ppermute | solution.py:271
  39.0 1.2 %pick_rows.2 = bf16[64,4096]{1,0:T(8,128)(2,1)} custom-call(bf16[64,32]{1,0:T(8,128)(2,1)S(1)} %get-tuple-element.34.pick_ref, bf16[32,4096]{1,0:T(8,128)(2,1)S(1)} %collective-permute-done.5.refs_0_), custom_call_target="tpu_custom_call" | custom-call | flops 33554432 | bytes 1048576 | tf_op jit(solution)/shard_map/pick_rows/pallas_call | solution.py:182
  40.1 7.7 %all-to-all-done.1 = bf16[4,48,4096]{2,1,0:T(8,128)(2,1)S(1)} async-done(((bf16[4,48,4096]{2,1,0:T(8,128)(2,1)}), bf16[4,48,4096]{2,1,0:T(8,128)(2,1)S(1)}, u32[]{:S(2)}, u32[]{:S(2)}) %all-to-all-start.1) | async-done | bytes 1572896 | tf_op jit(solution)/shard_map/all_to_all | solution.py:298
  47.8 3.5 %all-to-all-start.2 = ((bf16[4,16,4096]{2,1,0:T(8,128)(2,1)}), bf16[4,16,4096]{2,1,0:T(8,128)(2,1)S(1)}, u32[]{:S(2)}, u32[]{:S(2)}) async-start(bf16[4,16,4096]{2,1,0:T(8,128)(2,1)} %bitcast.11), calls=%async_computation.2 | async-start | bytes 1048576 | tf_op jit(solution)/shard_map/all_to_all | solution.py:298
  51.3 0.1 collective-permute-start.9
  51.4 5.7 %convolution_convert_fusion.1 = bf16[192,768]{1,0:T(8,128)(2,1)} fusion(bf16[192,4096]{1,0:T(8,128)(2,1)S(1)} %bitcast.34, bf16[768,4096]{1,0:T(8,128)(2,1)} %copy-done), kind=kOutput, calls=%fused_computation.1 | convolution fusion | flops 1208107008 | bytes 8159232 | tf_op jit(solution)/shard_map/dot_general | solution.py:308
  57.1 1.6 %all-to-all-done.2 = bf16[4,16,4096]{2,1,0:T(8,128)(2,1)S(1)} async-done(((bf16[4,16,4096]{2,1,0:T(8,128)(2,1)}), bf16[4,16,4096]{2,1,0:T(8,128)(2,1)S(1)}, u32[]{:S(2)}, u32[]{:S(2)}) %all-to-all-start.2) | async-done | bytes 524320 | tf_op jit(solution)/shard_map/all_to_all | solution.py:298
  58.7 4.9 %convolution_convert_fusion.2 = bf16[64,768]{1,0:T(8,128)(2,1)S(1)} fusion(bf16[64,4096]{1,0:T(8,128)(2,1)S(1)} %bitcast.37, bf16[768,4096]{1,0:T(8,128)(2,1)} %copy-done), kind=kOutput, calls=%fused_computation.2 | convolution fusion | flops 402702336 | bytes 6914048 | tf_op jit(solution)/shard_map/dot_general | solution.py:308
  63.6 0.0 copy-start.3
  63.6 1.1 %convolution_convert_fusion = bf16[256,768]{1,0:T(8,128)(2,1)} fusion(bf16[64,768]{1,0:T(8,128)(2,1)S(1)} %convolution_convert_fusion.2, bf16[192,768]{1,0:T(8,128)(2,1)S(1)} %copy-done.11, s32[256]{0:T(256)S(1)} %and_select_fusion.3), kind=kOutput, calls=%fused_computation | convolution fusion | flops 101711872 | bytes 787456 | tf_op jit(solution)/shard_map/dot_general | solution.py:18
  64.7 4.8 %all-to-all-start.3 = ((bf16[16,16,768]{2,1,0:T(8,128)(2,1)}), bf16[16,16,768]{2,1,0:T(8,128)(2,1)}, u32[]{:S(2)}, u32[]{:S(2)}) async-start(bf16[16,16,768]{2,1,0:T(8,128)(2,1)} %bitcast.50), calls=%async_computation.3 | async-start | bytes 786432 | tf_op jit(solution)/shard_map/all_to_all | solution.py:316
  69.5 1.9 %collective-permute-start.6 = (bf16[64,768]{1,0:T(8,128)(2,1)S(1)}, bf16[64,768]{1,0:T(8,128)(2,1)S(1)}, u32[]{:S(2)}, u32[]{:S(2)}) collective-permute-start(bf16[64,768]{1,0:T(8,128)(2,1)S(1)} %bitcast.53), channel_id=1, source_target_pairs={{0,1},{1,2},{2,3},{3,0},{4,5},{5,6},{6,7},{7,4},{8,9},{9,10},{10,1... | collective-permute-start | bytes 294920 | tf_op jit(solution)/shard_map/ppermute | solution.py:271
  71.4 2.4 %collective-permute-start.7 = (bf16[64,768]{1,0:T(8,128)(2,1)S(1)}, bf16[64,768]{1,0:T(8,128)(2,1)S(1)}, u32[]{:S(2)}, u32[]{:S(2)}) collective-permute-start(bf16[64,768]{1,0:T(8,128)(2,1)S(1)} %bitcast.52), channel_id=1, source_target_pairs={{0,2},{1,3},{2,0},{3,1},{4,6},{5,7},{6,4},{7,5},{8,10},{9,11},{10,... | collective-permute-start | bytes 294920 | tf_op jit(solution)/shard_map/ppermute | solution.py:271
  73.8 1.5 %collective-permute-start.8 = (bf16[64,768]{1,0:T(8,128)(2,1)S(1)}, bf16[64,768]{1,0:T(8,128)(2,1)S(1)}, u32[]{:S(2)}, u32[]{:S(2)}) collective-permute-start(bf16[64,768]{1,0:T(8,128)(2,1)S(1)} %bitcast.51), channel_id=1, source_target_pairs={{0,3},{1,0},{2,1},{3,2},{4,7},{5,4},{6,5},{7,6},{8,11},{9,8},{10,9... | collective-permute-start | bytes 294920 | tf_op jit(solution)/shard_map/ppermute | solution.py:271
  75.2 8.1 %collective-permute-done.6.refs_1_ = bf16[64,768]{1,0:T(8,128)(2,1)S(1)} collective-permute-done((bf16[64,768]{1,0:T(8,128)(2,1)S(1)}, bf16[64,768]{1,0:T(8,128)(2,1)S(1)}, u32[]{:S(2)}, u32[]{:S(2)}) %collective-permute-start.6) | collective-permute-done | bytes 98336 | tf_op jit(solution)/shard_map/ppermute | solution.py:271
  83.3 5.4 %collective-permute-done.7.refs_2_ = bf16[64,768]{1,0:T(8,128)(2,1)S(1)} collective-permute-done((bf16[64,768]{1,0:T(8,128)(2,1)S(1)}, bf16[64,768]{1,0:T(8,128)(2,1)S(1)}, u32[]{:S(2)}, u32[]{:S(2)}) %collective-permute-start.7) | collective-permute-done | bytes 98336 | tf_op jit(solution)/shard_map/ppermute | solution.py:271
  88.7 0.1 collective-permute-start.11
  88.8 0.7 copy.12
  89.5 0.8 copy.13
  90.2 0.4 collective-permute-done.11.refs_5_
  90.6 0.0 collective-permute-done.10.refs_4_
  90.6 6.9 %down_rows.1 = bf16[384,4096]{1,0:T(8,128)(2,1)} custom-call(s32[1]{0:T(128)} %bitcast.14.replica_ref, bf16[192,4096]{1,0:T(8,128)(2,1)S(1)} %bitcast.35, bf16[64,4096]{1,0:T(8,128)(2,1)S(1)} %bitcast.38, bf16[64,3072]{1,0:T(8,128)(2,1)S(1)} %join_rows.1.refs_2_, bf16[192,4096]{1,0:T(8,128)(2,1)} %collective-permute-done.9.refs_3_, ...), custom_call_target="tpu_custom_call" | custom-call | flops 1610612736 | bytes 7340032 | tf_op jit(solution)/shard_map/down_rows/pallas_call | solution.py:240
  97.5 0.0 all-to-all-done.3
  97.5 2.0 %multiply_reduce_fusion = (f32[32,8]{1,0:T(8,128)S(1)}, bf16[32,8,768]{2,1,0:T(8,128)(2,1)}) fusion(bf16[32,8,768]{2,1,0:T(8,128)(2,1)S(1)} %copy-done.3, f32[32,8]{1,0:T(8,128)S(1)} %copy-done.10, bf16[256,768,1]{1,0,2:T(8,128)(2,1)} %bitcast.20, bf16[256,256]{1,0:T(8,128)(2,1)S(1)} %copy-done.9), kind=kOutput, calls=%fused_computation.3 | convolution fusion | flops 101646080 | bytes 1312768 | tf_op jit(solution)/shard_map/dot_general | solution.py:328
  99.6 0.7 copy.14
  (24 shorter events, 0.1 us)
Async XLA Ops:
  0.6 12.3 %collective-permute-start = (bf16[32,4096]{1,0:T(8,128)(2,1)}, bf16[32,4096]{1,0:T(8,128)(2,1)S(1)}, u32[]{:S(2)}, u32[]{:S(2)}) collective-permute-start(bf16[32,4096]{1,0:T(8,128)(2,1)} %refs_0_.1), channel_id=1, source_target_pairs={{0,1},{1,2},{2,3},{3,0},{4,5},{5,6},{6,7},{7,4},{8,9},{9,10},{10,1... | collective-permute-start | bytes 786440 | tf_op jit(solution)/shard_map/ppermute | solution.py:271
  3.7 9.2 %collective-permute-start.1 = (s32[8,32]{1,0:T(8,128)}, s32[8,32]{1,0:T(8,128)S(1)}, u32[]{:S(2)}, u32[]{:S(2)}) collective-permute-start(s32[8,32]{1,0:T(8,128)} %bitcast.43), channel_id=1, source_target_pairs={{0,1},{1,2},{2,3},{3,0},{4,5},{5,6},{6,7},{7,4},{8,9},{9,10},{10,1... | collective-permute-start | bytes 3080 | tf_op jit(solution)/shard_map/ppermute | solution.py:271
  5.3 7.6 %collective-permute-start.2 = (s32[8,32]{1,0:T(8,128)}, s32[8,32]{1,0:T(8,128)S(1)}, u32[]{:S(2)}, u32[]{:S(2)}) collective-permute-start(s32[8,32]{1,0:T(8,128)} %bitcast.44), channel_id=1, source_target_pairs={{0,2},{1,3},{2,0},{3,1},{4,6},{5,7},{6,4},{7,5},{8,10},{9,11},{10,... | collective-permute-start | bytes 3080 | tf_op jit(solution)/shard_map/ppermute | solution.py:271
  6.4 6.6 %collective-permute-start.3 = (s32[8,32]{1,0:T(8,128)}, s32[8,32]{1,0:T(8,128)S(1)}, u32[]{:S(2)}, u32[]{:S(2)}) collective-permute-start(s32[8,32]{1,0:T(8,128)} %bitcast.45), channel_id=1, source_target_pairs={{0,3},{1,0},{2,1},{3,2},{4,7},{5,4},{6,5},{7,6},{8,11},{9,8},{10,9... | collective-permute-start | bytes 3080 | tf_op jit(solution)/shard_map/ppermute | solution.py:271
  9.2 1.0 copy-start.2
  10.2 0.7 copy-start.5
  10.9 0.7 copy-start.7
  12.9 14.0 %all-to-all-start = ((bf16[4,64,768]{2,1,0:T(8,128)(2,1)}), bf16[4,64,768]{2,1,0:T(8,128)(2,1)S(1)}, u32[]{:S(2)}, u32[]{:S(2)}) async-start(bf16[4,64,768]{2,1,0:T(8,128)(2,1)} %bitcast.7), calls=%async_computation | async-start | bytes 786432 | tf_op jit(solution)/shard_map/all_to_all | solution.py:287
  16.7 8.5 %collective-permute-start.4 = (bf16[32,4096]{1,0:T(8,128)(2,1)S(1)}, bf16[32,4096]{1,0:T(8,128)(2,1)S(1)}, u32[]{:S(2)}, u32[]{:S(2)}) collective-permute-start(bf16[32,4096]{1,0:T(8,128)(2,1)S(1)} %collective-permute-done.refs_1_), channel_id=1, source_target_pairs={{0,1},{1,2},{2,3},{3,0},{4,5},{5,6},{6,7},{7,4},{8,9},{9,10},{10,1... | collective-permute-start | bytes 786440 | tf_op jit(solution)/shard_map/ppermute | solution.py:271
  16.9 2.8 %copy-start.1 = (bf16[1,768,4096]{2,1,0:T(8,128)(2,1)S(1)}, bf16[1,768,4096]{2,1,0:T(8,128)(2,1)}, u32[]{:S(2)}) copy-start(bf16[1,768,4096]{2,1,0:T(8,128)(2,1)} %param.9) | copy-start | bytes 18874372
  19.7 3.1 %copy-start.8 = (s32[32,8]{0,1:T(8,128)S(1)}, s32[32,8]{0,1:T(8,128)}, u32[]{:S(2)}) copy-start(s32[32,8]{0,1:T(8,128)} %param.8) | copy-start | bytes 3076
  19.7 5.5 %copy-start.4 = (bf16[32,4096]{1,0:T(8,128)(2,1)S(1)}, bf16[32,4096]{1,0:T(8,128)(2,1)}, u32[]{:S(2)}) copy-start(bf16[32,4096]{1,0:T(8,128)(2,1)} %refs_0_.1) | copy-start | bytes 786436
  20.1 2.6 %copy-start = (bf16[768,4096]{1,0:T(8,128)(2,1)}, bf16[768,4096]{1,0:T(8,128)(2,1)S(1)}, u32[]{:S(2)}) copy-start(bf16[768,4096]{1,0:T(8,128)(2,1)S(1)} %hold_weight.1) | copy-start | bytes 18874372
  27.0 20.9 %all-to-all-start.1 = ((bf16[4,48,4096]{2,1,0:T(8,128)(2,1)}), bf16[4,48,4096]{2,1,0:T(8,128)(2,1)S(1)}, u32[]{:S(2)}, u32[]{:S(2)}) async-start(bf16[4,48,4096]{2,1,0:T(8,128)(2,1)} %bitcast.9), calls=%async_computation.1 | async-start | bytes 3145728 | tf_op jit(solution)/shard_map/all_to_all | solution.py:298
  30.8 8.2 %collective-permute-start.5 = (bf16[32,4096]{1,0:T(8,128)(2,1)S(1)}, bf16[32,4096]{1,0:T(8,128)(2,1)S(1)}, u32[]{:S(2)}, u32[]{:S(2)}) collective-permute-start(bf16[32,4096]{1,0:T(8,128)(2,1)S(1)} %collective-permute-done.4.refs_2_), channel_id=1, source_target_pairs={{0,1},{1,2},{2,3},{3,0},{4,5},{5,6},{6,7},{7,4},{8,9},{9,10},{10,1... | collective-permute-start | bytes 786440 | tf_op jit(solution)/shard_map/ppermute | solution.py:271
  47.8 10.9 %all-to-all-start.2 = ((bf16[4,16,4096]{2,1,0:T(8,128)(2,1)}), bf16[4,16,4096]{2,1,0:T(8,128)(2,1)S(1)}, u32[]{:S(2)}, u32[]{:S(2)}) async-start(bf16[4,16,4096]{2,1,0:T(8,128)(2,1)} %bitcast.11), calls=%async_computation.2 | async-start | bytes 1048576 | tf_op jit(solution)/shard_map/all_to_all | solution.py:298
  51.3 39.3 %collective-permute-start.9 = (bf16[192,4096]{1,0:T(8,128)(2,1)S(1)}, bf16[192,4096]{1,0:T(8,128)(2,1)}, u32[]{:S(2)}, u32[]{:S(2)}) collective-permute-start(bf16[192,4096]{1,0:T(8,128)(2,1)S(1)} %bitcast.33), channel_id=1, source_target_pairs={{0,16},{16,0},{1,17},{17,1},{2,18},{18,2},{3,19},{19,3},{4,20},{20... | collective-permute-start | bytes 4718600 | tf_op jit(solution)/shard_map/ppermute | solution.py:274
  57.1 31.7 %copy-start.6 = (f32[32,8]{0,1:T(8,128)S(1)}, f32[32,8]{0,1:T(8,128)}, u32[]{:S(2)}) copy-start(f32[32,8]{0,1:T(8,128)} %param.7) | copy-start | bytes 3076
  58.7 4.9 %copy-start.11 = (bf16[192,768]{1,0:T(8,128)(2,1)S(1)}, bf16[192,768]{1,0:T(8,128)(2,1)}, u32[]{:S(2)}) copy-start(bf16[192,768]{1,0:T(8,128)(2,1)} %convolution_convert_fusion.1) | copy-start | bytes 884740
  58.7 31.9 %collective-permute-start.10 = (bf16[64,4096]{1,0:T(8,128)(2,1)S(1)}, bf16[64,4096]{1,0:T(8,128)(2,1)S(1)}, u32[]{:S(2)}, u32[]{:S(2)}) collective-permute-start(bf16[64,4096]{1,0:T(8,128)(2,1)S(1)} %bitcast.36), channel_id=1, source_target_pairs={{0,16},{16,0},{1,17},{17,1},{2,18},{18,2},{3,19},{19,3},{4,20},{20... | collective-permute-start | bytes 1572872 | tf_op jit(solution)/shard_map/ppermute | solution.py:274
  63.6 33.9 %copy-start.3 = (bf16[32,8,768]{2,1,0:T(8,128)(2,1)S(1)}, bf16[32,8,768]{2,1,0:T(8,128)(2,1)}, u32[]{:S(2)}) copy-start(bf16[32,8,768]{2,1,0:T(8,128)(2,1)} %param.6) | copy-start | bytes 1179652
  64.7 32.8 %all-to-all-start.3 = ((bf16[16,16,768]{2,1,0:T(8,128)(2,1)}), bf16[16,16,768]{2,1,0:T(8,128)(2,1)}, u32[]{:S(2)}, u32[]{:S(2)}) async-start(bf16[16,16,768]{2,1,0:T(8,128)(2,1)} %bitcast.50), calls=%async_computation.3 | async-start | bytes 786432 | tf_op jit(solution)/shard_map/all_to_all | solution.py:316
  69.5 13.8 %collective-permute-start.6 = (bf16[64,768]{1,0:T(8,128)(2,1)S(1)}, bf16[64,768]{1,0:T(8,128)(2,1)S(1)}, u32[]{:S(2)}, u32[]{:S(2)}) collective-permute-start(bf16[64,768]{1,0:T(8,128)(2,1)S(1)} %bitcast.53), channel_id=1, source_target_pairs={{0,1},{1,2},{2,3},{3,0},{4,5},{5,6},{6,7},{7,4},{8,9},{9,10},{10,1... | collective-permute-start | bytes 294920 | tf_op jit(solution)/shard_map/ppermute | solution.py:271
  71.4 17.3 %collective-permute-start.7 = (bf16[64,768]{1,0:T(8,128)(2,1)S(1)}, bf16[64,768]{1,0:T(8,128)(2,1)S(1)}, u32[]{:S(2)}, u32[]{:S(2)}) collective-permute-start(bf16[64,768]{1,0:T(8,128)(2,1)S(1)} %bitcast.52), channel_id=1, source_target_pairs={{0,2},{1,3},{2,0},{3,1},{4,6},{5,7},{6,4},{7,5},{8,10},{9,11},{10,... | collective-permute-start | bytes 294920 | tf_op jit(solution)/shard_map/ppermute | solution.py:271
  73.8 14.9 %collective-permute-start.8 = (bf16[64,768]{1,0:T(8,128)(2,1)S(1)}, bf16[64,768]{1,0:T(8,128)(2,1)S(1)}, u32[]{:S(2)}, u32[]{:S(2)}) collective-permute-start(bf16[64,768]{1,0:T(8,128)(2,1)S(1)} %bitcast.51), channel_id=1, source_target_pairs={{0,3},{1,0},{2,1},{3,2},{4,7},{5,4},{6,5},{7,6},{8,11},{9,8},{10,9... | collective-permute-start | bytes 294920 | tf_op jit(solution)/shard_map/ppermute | solution.py:271
  88.7 1.9 %collective-permute-start.11 = (bf16[64,3072]{1,0:T(8,128)(2,1)S(1)}, bf16[64,3072]{1,0:T(8,128)(2,1)}, u32[]{:S(2)}, u32[]{:S(2)}) collective-permute-start(bf16[64,3072]{1,0:T(8,128)(2,1)S(1)} %join_rows.1.refs_2_), channel_id=1, source_target_pairs={{0,16},{16,0},{1,17},{17,1},{2,18},{18,2},{3,19},{19,3},{4,20},{20... | collective-permute-start | bytes 1179656 | tf_op jit(solution)/shard_map/ppermute | solution.py:274
  89.5 8.0 %copy-start.10 = (f32[32,8]{1,0:T(8,128)S(1)}, f32[32,8]{1,0:T(8,128)}, u32[]{:S(2)}) copy-start(f32[32,8]{1,0:T(8,128)} %copy.12) | copy-start | bytes 3076
  90.2 7.3 %copy-start.9 = (bf16[256,256]{1,0:T(8,128)(2,1)S(1)}, bf16[256,256]{1,0:T(8,128)(2,1)}, u32[]{:S(2)}) copy-start(bf16[256,256]{1,0:T(8,128)(2,1)} %copy.13) | copy-start | bytes 393220

commit v9 on v8

v9 whole, which is shorter than its diff:
```python
import functools

import jax
import jax.numpy as jnp
from jax import lax
from jax.experimental import pallas as pl
from jax.experimental.pallas import tpu as pltpu
from jax.sharding import PartitionSpec as P

ID_COLS = 128
PARTS = 2
MIB = 1024 * 1024


def iota(shape, dim):
    return lax.broadcasted_iota(jnp.int32, shape, dim)


def exact_dot(one_hot, values):
    return jnp.dot(one_hot, values, preferred_element_type=jnp.float32)


def send_kernel(far_count, near_count, capacity, near_ref, ids_ref, gates_ref, hidden_ref, send_ref, back_ref):
    top_count, tok_local = ids_ref.shape
    rows = tok_local * top_count
    experts = far_count * near_count
    slots = experts * capacity
    near = near_ref[0]
    wide = jnp.where(iota((tok_local, rows), 1) // top_count == iota((tok_local, rows), 0), 1.0, 0.0).astype(jnp.bfloat16)
    mine = iota((top_count, rows), 1) % top_count == iota((top_count, rows), 0)

    def line(values):
        spread = jnp.zeros((top_count, rows), jnp.float32)
        for _ in range(3):
            piece = values.astype(jnp.bfloat16)
            values = values - piece.astype(jnp.float32)
            spread = spread + exact_dot(piece, wide)
        return jnp.sum(jnp.where(mine, spread, 0.0), axis=0, keepdims=True)

    ids = line(ids_ref[...].astype(jnp.float32)).astype(jnp.int32)
    gates = line(gates_ref[...])
    named = iota((experts, rows), 0) == ids
    before = jnp.where(iota((rows, rows), 0) < iota((rows, rows), 1), 1.0, 0.0).astype(jnp.bfloat16)
    counts = exact_dot(jnp.where(named, 1.0, 0.0).astype(jnp.bfloat16), before)
    ranks = jnp.sum(jnp.where(named, counts, 0.0), axis=0, keepdims=True).astype(jnp.int32)
    steps = (ids % near_count - near + near_count) % near_count
    out_slots = (ids // near_count * near_count + steps) * capacity + ranks
    back_slots = ids * capacity + ranks
    back_ref[...] = jnp.where(iota((slots, rows), 0) == back_slots, 1.0, 0.0).astype(jnp.bfloat16)
    place = iota((slots, rows), 0) == out_slots
    gate = jnp.sum(jnp.where(place, gates, 0.0), axis=1, keepdims=True)
    picked = exact_dot(jnp.where(place, 1.0, 0.0).astype(jnp.bfloat16), hidden_ref[...])
    send_ref[...] = (picked * gate).astype(jnp.bfloat16)


def split_kernel(ids_ref, tokens_ref, *refs):
    outs, sem = refs[:-1], refs[-1]
    part = outs[1].shape[1]
    copies = [
        pltpu.make_async_copy(tokens_ref.at[:, i * part : (i + 1) * part], out.at[:, :part], sem.at[i])
        for i, out in enumerate(outs)
    ]
    for copy in copies:
        copy.start()
    top_count, tok_local = ids_ref.shape
    same = jnp.where(iota((top_count, ID_COLS), 0) == iota((top_count, ID_COLS), 1), 1.0, 0.0).astype(jnp.bfloat16)
    ids = lax.dot_general(
        ids_ref[...].astype(jnp.float32).astype(jnp.bfloat16),
        same,
        (((0,), (0,)), ((), ())),
        preferred_element_type=jnp.float32,
    )
    ids = jnp.where(iota((tok_local, ID_COLS), 1) < top_count, ids, -1.0)
    outs[0][:, part:] = ids.astype(jnp.bfloat16)
    for copy in copies:
        copy.wait()


def picked_rows(pick, blocks, out_ref):
    width = out_ref.shape[1]
    step = min(width, 512)
    for start in range(0, width, step):
        tokens = jnp.concatenate([block[:, start : start + step] for block in blocks], axis=0)
        out_ref[:, start : start + step] = exact_dot(pick, tokens).astype(jnp.bfloat16)


def first_pick_kernel(far_count, near_count, capacity, near_ref, *refs):
    blocks, (out_ref, pick_ref) = refs[:-2], refs[-2:]
    tok_local = blocks[0].shape[0]
    width = out_ref.shape[1]
    near = near_ref[0]
    cols = near_count * tok_local
    slots = far_count * near_count * capacity
    lead = max(8, far_count)
    ids = jnp.concatenate([block[:, width:] for block in blocks], axis=0).astype(jnp.float32)
    ones = jnp.ones((lead, ID_COLS), jnp.bfloat16)
    named = jnp.zeros((lead, cols), jnp.float32)
    for far in range(far_count):
        expert = (far * near_count + near).astype(jnp.float32)
        hit = jnp.where(ids == expert, 1.0, 0.0).astype(jnp.bfloat16)
        line = lax.dot_general(ones, hit, (((1,), (1,)), ((), ())), preferred_element_type=jnp.float32)
        named = jnp.where(iota((lead, cols), 0) == far, line, named)
    row, col = iota((cols, cols), 0), iota((cols, cols), 1)
    before = jnp.where((row < col) & (row // tok_local == col // tok_local), 1.0, 0.0).astype(jnp.bfloat16)
    rank = exact_dot(named.astype(jnp.bfloat16), before)
    place = jnp.where(named > 0.5, rank, float(capacity)).astype(jnp.bfloat16)
    per_far = near_count * capacity
    spread = jnp.where(iota((slots, lead), 0) // per_far == iota((slots, lead), 1), 1.0, 0.0).astype(jnp.bfloat16)
    slot = iota((slots, cols), 0) % per_far
    block = (near - slot // capacity + near_count) % near_count
    pick = (iota((slots, cols), 1) // tok_local == block) & (
        exact_dot(spread, place).astype(jnp.int32) == slot % capacity
    )
    pick = jnp.where(pick, 1.0, 0.0).astype(jnp.bfloat16)
    pick_ref[...] = pick
    picked_rows(pick, blocks, out_ref)


def pick_kernel(pick_ref, *refs):
    picked_rows(pick_ref[...], refs[:-1], refs[-1])


def join_kernel(*refs):
    out_ref = refs[-1]
    start = 0
    for ref in refs[:-1]:
        out_ref[:, start : start + ref.shape[1]] = ref[...]
        start += ref.shape[1]


def down_kernel(near_count, capacity, scalars_ref, *refs):
    rows, hids, (out_ref, turned_ref) = refs[: 2 * PARTS], refs[2 * PARTS : -2], refs[-2:]
    step = pl.program_id(0)
    share, tile = out_ref.shape
    near, replica = scalars_ref[0], scalars_ref[1]

    @pl.when(step == 0)
    def _():
        slots, lines = rows[0].shape[0], hids[0].shape[0]
        hidden_width = hids[0].shape[1] // near_count
        row, col = iota((slots, lines), 0), iota((slots, lines), 1)
        match = (row // (near_count * capacity) == col // capacity) & (row % capacity == col % capacity)
        block = (near - row // capacity % near_count + near_count) % near_count
        for i, ref in enumerate(hids):
            total = jnp.zeros((slots, share), jnp.float32)
            for j in range(near_count):
                start = pl.multiple_of(j * hidden_width + replica * share, 128)
                order = jnp.where(match & (block == j), 1.0, 0.0).astype(jnp.bfloat16)
                total = total + exact_dot(order, ref[:, pl.ds(start, share)])
            turned_ref[:, i * slots : (i + 1) * slots] = total.T.astype(jnp.bfloat16)

    steps = rows[0].shape[1] // tile
    for part in range(PARTS):

        @pl.when(step // steps == part)
        def _(part=part):
            cols = pl.ds(pl.multiple_of(step % steps * tile, 128), tile)
            tokens = jnp.concatenate([ref[:, cols] for ref in rows[part::PARTS]], axis=0)
            out_ref[...] = exact_dot(turned_ref[...], tokens).astype(jnp.bfloat16)


def scalar_spec():
    return pl.BlockSpec(memory_space=pltpu.SMEM)


def params(mib):
    return pltpu.CompilerParams(vmem_limit_bytes=mib * MIB)


def send_rows(far_count, near_count, capacity, near, ids, gates, hidden):
    slots = far_count * near_count * capacity
    rows, wide = hidden.shape
    vmem = pl.BlockSpec(memory_space=pltpu.VMEM)
    return pl.pallas_call(
        functools.partial(send_kernel, far_count, near_count, capacity),
        out_shape=[
            jax.ShapeDtypeStruct((slots, wide), jnp.bfloat16),
            jax.ShapeDtypeStruct((slots, rows), jnp.bfloat16),
        ],
        in_specs=[scalar_spec()] + [vmem] * 3,
        out_specs=[vmem] * 2,
        compiler_params=params(12),
        cost_estimate=pl.CostEstimate(flops=2 * rows * rows * wide, bytes_accessed=4 * rows * wide, transcendentals=0),
        name="send_rows",
    )(near, ids, gates, hidden)


def split_rows(ids, tokens):
    tok_local, width = tokens.shape
    part = width // PARTS
    vmem = pl.BlockSpec(memory_space=pltpu.VMEM)
    return pl.pallas_call(
        split_kernel,
        out_shape=[
            jax.ShapeDtypeStruct((tok_local, part + (ID_COLS if i == 0 else 0)), jnp.bfloat16) for i in range(PARTS)
        ],
        in_specs=[vmem, pl.BlockSpec(memory_space=pl.ANY)],
        out_specs=[vmem] * PARTS,
        scratch_shapes=[pltpu.SemaphoreType.DMA((PARTS,))],
        compiler_params=params(8),
        name="split_rows",
    )(ids, tokens)


def first_pick(far_count, near_count, capacity, near, blocks):
    tok_local, wide = blocks[0].shape
    slots = far_count * near_count * capacity
    vmem = pl.BlockSpec(memory_space=pltpu.VMEM)
    return pl.pallas_call(
        functools.partial(first_pick_kernel, far_count, near_count, capacity),
        out_shape=[
            jax.ShapeDtypeStruct((slots, wide - ID_COLS), jnp.bfloat16),
            jax.ShapeDtypeStruct((slots, near_count * tok_local), jnp.bfloat16),
        ],
        in_specs=[scalar_spec()] + [vmem] * len(blocks),
        out_specs=[vmem] * 2,
        compiler_params=params(16),
        name="first_pick",
    )(near, *blocks)


def pick_rows(pick, blocks):
    vmem = pl.BlockSpec(memory_space=pltpu.VMEM)
    return pl.pallas_call(
        pick_kernel,
        out_shape=jax.ShapeDtypeStruct((pick.shape[0], blocks[0].shape[1]), jnp.bfloat16),
        in_specs=[vmem] * (1 + len(blocks)),
        out_specs=vmem,
        compiler_params=params(16),
        name="pick_rows",
    )(pick, *blocks)


def join_rows(arrays):
    vmem = pl.BlockSpec(memory_space=pltpu.VMEM)
    shape = (arrays[0].shape[0], sum(array.shape[1] for array in arrays))
    return pl.pallas_call(
        join_kernel,
        out_shape=jax.ShapeDtypeStruct(shape, jnp.bfloat16),
        in_specs=[vmem] * len(arrays),
        out_specs=vmem,
        compiler_params=params(8),
        name="join_rows",
    )(*arrays)


def down_rows(near_count, capacity, scalars, rows, hids, share):
    part = rows[0].shape[1]
    tile = min(part, 512)
    lines = 2 * rows[0].shape[0]
    width = part * PARTS
    whole = lambda array: pl.BlockSpec(array.shape, lambda i: (0, 0))
    return pl.pallas_call(
        functools.partial(down_kernel, near_count, capacity),
        grid=(width // tile,),
        out_shape=jax.ShapeDtypeStruct((share, width), jnp.bfloat16),
        in_specs=[scalar_spec()] + [whole(array) for array in rows + hids],
        out_specs=pl.BlockSpec((share, tile), lambda i: (0, i)),
        scratch_shapes=[pltpu.VMEM((share, lines), jnp.bfloat16)],
        compiler_params=params(32),
        cost_estimate=pl.CostEstimate(
            flops=2 * lines * width * share, bytes_accessed=2 * width * (lines + share), transcendentals=0
        ),
        name="down_rows",
    )(scalars, *rows, *hids)


def local(grad_out, hidden, gates, expert_ids, w_down):
    tok_local, top_count = expert_ids.shape
    far_count = lax.axis_size("far")
    near_count = lax.axis_size("near")
    experts = far_count * near_count
    capacity = max(4, (tok_local * top_count + experts - 1) // experts)
    width = grad_out.shape[1]
    hidden_width = hidden.shape[2]
    row_total = tok_local * top_count
    slot_total = experts * capacity
    near = lax.axis_index("near")
    near_ref = near.astype(jnp.int32).reshape(1)
    part = width // PARTS
    weight = w_down[0]

    def along(array, steps):
        return lax.ppermute(array, "near", [(i, (i + steps) % near_count) for i in range(near_count)])

    def swap(array):
        return lax.ppermute(array, "dp", [(i, i ^ 1) for i in range(lax.axis_size("dp"))])

    def line(array):
        return [array] + [along(array, step) for step in range(1, near_count)]

    ids = expert_ids.T
    parts = list(split_rows(ids, grad_out))
    blocks = line(parts[0])
    send, back_place = send_rows(
        far_count, near_count, capacity, near_ref, ids, gates.T, hidden.reshape(row_total, hidden_width)
    )
    crossed = lax.all_to_all(
        send.reshape(far_count, -1, hidden_width), "far", split_axis=0, concat_axis=0, tiled=True
    ).reshape(far_count, near_count, capacity, hidden_width)

    rows, total = [], None
    for i in range(PARTS):
        if i == 0:
            picked, pick = first_pick(far_count, near_count, capacity, near_ref, blocks)
            picked, crossed, parts[1] = lax.optimization_barrier((picked, crossed, parts[1]))
        else:
            picked = pick_rows(pick, line(parts[i]))
            picked, rows[-1] = lax.optimization_barrier((picked, rows[-1]))
        got = lax.all_to_all(
            picked.reshape(far_count, -1, part), "far", split_axis=0, concat_axis=0, tiled=True
        ).reshape(slot_total, part)
        rows.append(got)
    rows[0], crossed = lax.optimization_barrier((rows[0], crossed))
    hids = [crossed[:, step].reshape(-1, hidden_width) for step in range(near_count)]
    hids = join_rows(hids[:1] + [along(hids[step], step) for step in range(1, near_count)])
    for i in range(PARTS):
        if i:
            rows[i], total, hids = lax.optimization_barrier((rows[i], total, hids))
        product = lax.dot_general(
            rows[i],
            weight[:, i * part : (i + 1) * part],
            (((1,), (1,)), ((), ())),
            preferred_element_type=jnp.float32,
        )
        total = product if total is None else total + product
    came_back = lax.all_to_all(
        total.astype(jnp.bfloat16).reshape(experts, capacity, hidden_width),
        ("far", "near"),
        split_axis=0,
        concat_axis=0,
        tiled=True,
    )

    scalars = jnp.stack([near, lax.axis_index("dp")]).astype(jnp.int32)
    grad_down = down_rows(
        near_count,
        capacity,
        scalars,
        rows + [swap(array) for array in rows],
        [hids, swap(hids)],
        hidden_width // lax.axis_size("dp"),
    )
    came_back, grad_down = lax.optimization_barrier((came_back, grad_down))

    back_rows = lax.dot_general(
        back_place,
        came_back.reshape(slot_total, hidden_width),
        (((0,), (0,)), ((), ())),
        preferred_element_type=jnp.float32,
    ).reshape(tok_local, top_count, hidden_width)
    grad_hidden = (gates[:, :, None] * back_rows).astype(jnp.bfloat16)
    grad_gates = jnp.sum(back_rows * hidden.astype(jnp.float32), axis=-1)
    return (grad_hidden, grad_gates, grad_down[None])


def solution(mesh):
    placed = (
        P(("dp", "far", "near"), None),
        P(("dp", "far", "near"), None, None),
        P(("dp", "far", "near"), None),
        P(("dp", "far", "near"), None),
        P(("far", "near"), None, None),
    )
    return jax.shard_map(
        local,
        mesh=mesh,
        in_specs=placed,
        out_specs=(
            P(("dp", "far", "near"), None, None),
            P(("dp", "far", "near"), None),
            P(("far", "near"), "dp", None),
        ),
        check_vma=False,
    )
```

time: 101 us -> 89.8 us (0.89)
  local copies, waits for them, and re-layouts: 9.92 us -> 4.87 us
  matrix products: 13.6 us -> 8.79 us
  waiting for transfers between devices: 33.4 us -> 29.7 us
  starting transfers between devices: 30.5 us -> 32.1 us
    dot_general x3 -> x2, matrix products: 11.6 us -> 6.77 us  [local(): lax.dot_general(rows[i], weight[:, i * part:(i + 1) * part], (((1,), (1,)...]
    unnamed x26 -> x18, local copies, waits for them, and re-layouts: 9.14 us -> 4.75 us
    all_to_all x3, waiting for transfers between devices: 9.31 us -> 6.9 us  [the longest x1 5.02 us: local(): lax.all_to_all(total.astype(jnp.bfloat16).reshape(experts, capacity, hidd...]
    ppermute x9, waiting for transfers between devices: 23.7 us -> 21.5 us  [along(): lax.ppermute(array, 'near', [(i, (i + steps) % near_count) for i in range...]
    all_to_all x3, starting transfers between devices: 12.1 us -> 14.1 us  [the longest x2 7.98 us: local(): lax.all_to_all(picked.reshape(far_count, -1, part), 'far', split_axis=0,...]
    ppermute x9, starting transfers between devices: 14.6 us -> 12.6 us  [along(): lax.ppermute(array, 'near', [(i, (i + steps) % near_count) for i in range...]
    all_to_all x1, starting transfers between devices: 3.73 us -> 5.16 us  [local(): lax.all_to_all(send.reshape(far_count, -1, hidden_width), 'far', split_ax...]
    pallas_call x5 -> x4, Pallas kernels: 10.5 us -> 10.7 us  [the longest x1 7.23 us: down_rows(): pl.pallas_call(functools.partial(down_kernel, near_count, capacity), grid...]
  transfers between devices with their start and end apart: 16 -> 16, of which waited for: 7 -> 8; matrix products, arithmetic and copies ran while one was open for 13% -> 9% of each run, Pallas kernels for 12% -> 12%
where the time goes in v9:
time: 89.8 us; the launch traced here: 89.1 us
  starting transfers between devices  32.1 us (36%)
  waiting for transfers between devices  29.7 us (33%)
  Pallas kernels  12.1 us (13%)
  matrix products  8.79 us (10%)
  local copies, waits for them, and re-layouts  4.87 us (5%)
  other arithmetic  0.9 us (1%)
    ppermute x9, waiting for transfers between devices, along(): lax.ppermute(array, 'near', [(i, (i + steps) % near_count) for i in range...  21.5 us
    ppermute x9, starting transfers between devices, along(): lax.ppermute(array, 'near', [(i, (i + steps) % near_count) for i in range...  12.6 us
    all_to_all x2, starting transfers between devices, local(): lax.all_to_all(picked.reshape(far_count, -1, part), 'far', split_axis=0,...  7.98 us
    pallas_call x1, Pallas kernels, down_rows(): pl.pallas_call(functools.partial(down_kernel, near_count, capacity), grid...  7.23 us
    dot_general x2, matrix products, local(): lax.dot_general(rows[i], weight[:, i * part:(i + 1) * part], (((1,), (1,)...  6.77 us
    all_to_all x1, starting transfers between devices, local(): lax.all_to_all(total.astype(jnp.bfloat16).reshape(experts, capacity, hidd...  6.1 us
    all_to_all x1, starting transfers between devices, local(): lax.all_to_all(send.reshape(far_count, -1, hidden_width), 'far', split_ax...  5.16 us
    all_to_all x1, waiting for transfers between devices, local(): lax.all_to_all(total.astype(jnp.bfloat16).reshape(experts, capacity, hidd...  5.02 us
  transfers between devices with their start and end apart: 16, of which 8 were waited for; matrix products, arithmetic and copies ran while one was open for 9% of the time, Pallas kernels for 12%

profile of v9, /device:TPU:0, one launch (start us, length us, event | category | flops | bytes accessed | tf_op | source)
XLA Modules:
  0.0 89.1 jit_solution(14644826959928050324)
XLA Ops:
  0.6 0.0 copy-start
  0.6 1.0 %copy-done = bf16[32,8,768]{2,1,0:T(8,128)(2,1)S(1)} copy-done((bf16[32,8,768]{2,1,0:T(8,128)(2,1)S(1)}, bf16[32,8,768]{2,1,0:T(8,128)(2,1)}, u32[]{:S(2)}) %copy-start) | copy-done | bytes 393240
  1.6 0.7 copy-done.3
  2.3 0.7 copy-done.5
  3.0 1.3 %send_rows.1 = (bf16[256,768]{1,0:T(8,128)(2,1)}, bf16[256,256]{1,0:T(8,128)(2,1)S(1)}) custom-call(s32[1]{0:T(128)} %bitcast.near_ref, s32[8,32]{1,0:T(8,128)S(1)} %bitcast.39, f32[8,32]{1,0:T(8,128)S(1)} %bitcast.41, bf16[256,768]{1,0:T(8,128)(2,1)S(1)} %bitcast.36), custom_call_target="tpu_custom_call" | custom-call | flops 100663296 | bytes 786432 | tf_op jit(solution)/shard_map/send_rows/pallas_call | solution.py:174
  4.3 5.2 %all-to-all-start = ((bf16[4,64,768]{2,1,0:T(8,128)(2,1)}), bf16[4,64,768]{2,1,0:T(8,128)(2,1)S(1)}, u32[]{:S(2)}, u32[]{:S(2)}) async-start(bf16[4,64,768]{2,1,0:T(8,128)(2,1)} %bitcast.6), calls=%async_computation | async-start | bytes 786432 | tf_op jit(solution)/shard_map/all_to_all | solution.py:298
  9.5 0.9 %copy-done.2 = bf16[32,4096]{1,0:T(8,128)(2,1)S(1)} copy-done((bf16[32,4096]{1,0:T(8,128)(2,1)S(1)}, bf16[32,4096]{1,0:T(8,128)(2,1)}, u32[]{:S(2)}) %copy-start.2) | copy-done | bytes 262168
  10.4 0.7 copy-done.4
  11.1 0.3 split_rows.1
  11.4 3.7 %collective-permute-start.2 = (bf16[32,2176]{1,0:T(8,128)(2,1)S(1)}, bf16[32,2176]{1,0:T(8,128)(2,1)S(1)}, u32[]{:S(2)}, u32[]{:S(2)}) collective-permute-start(bf16[32,2176]{1,0:T(8,128)(2,1)S(1)} %get-tuple-element.22.refs_0_), channel_id=1, source_target_pairs={{0,3},{1,0},{2,1},{3,2},{4,7},{5,4},{6,5},{7,6},{8,11},{9,8},{10,9... | collective-permute-start | bytes 417800 | tf_op jit(solution)/shard_map/ppermute | solution.py:284
  15.1 0.0 collective-permute-start.1
  15.1 1.0 %collective-permute-start = (bf16[32,2176]{1,0:T(8,128)(2,1)S(1)}, bf16[32,2176]{1,0:T(8,128)(2,1)S(1)}, u32[]{:S(2)}, u32[]{:S(2)}) collective-permute-start(bf16[32,2176]{1,0:T(8,128)(2,1)S(1)} %get-tuple-element.22.refs_0_), channel_id=1, source_target_pairs={{0,1},{1,2},{2,3},{3,0},{4,5},{5,6},{6,7},{7,4},{8,9},{9,10},{10,1... | collective-permute-start | bytes 417800 | tf_op jit(solution)/shard_map/ppermute | solution.py:284
  16.1 3.1 %collective-permute-done.2.refs_3_ = bf16[32,2176]{1,0:T(8,128)(2,1)S(1)} collective-permute-done((bf16[32,2176]{1,0:T(8,128)(2,1)S(1)}, bf16[32,2176]{1,0:T(8,128)(2,1)S(1)}, u32[]{:S(2)}, u32[]{:S(2)}) %collective-permute-start.2) | collective-permute-done | bytes 139296 | tf_op jit(solution)/shard_map/ppermute | solution.py:284
  19.2 7.4 %collective-permute-done.1.refs_2_ = bf16[32,2176]{1,0:T(8,128)(2,1)S(1)} collective-permute-done((bf16[32,2176]{1,0:T(8,128)(2,1)S(1)}, bf16[32,2176]{1,0:T(8,128)(2,1)S(1)}, u32[]{:S(2)}, u32[]{:S(2)}) %collective-permute-start.1) | collective-permute-done | bytes 139296 | tf_op jit(solution)/shard_map/ppermute | solution.py:284
  26.6 0.0 collective-permute-done.refs_1_
  26.6 1.8 %first_pick.1 = (bf16[256,2048]{1,0:T(8,128)(2,1)}, bf16[256,128]{1,0:T(8,128)(2,1)S(1)}) custom-call(s32[1]{0:T(128)} %bitcast.near_ref, bf16[32,2176]{1,0:T(8,128)(2,1)S(1)} %get-tuple-element.22.refs_0_, bf16[32,2176]{1,0:T(8,128)(2,1)S(1)} %collective-permute-done.refs_1_, bf16[32,2176]{1,0:T(8,128)(2,1)S(1)} %collective-permute-done.1.refs_2_, ...), custom_call_target="tpu_custom_call" | custom-call | tf_op jit(solution)/shard_map/first_pick/pallas_call | solution.py:209
  28.4 4.1 %all-to-all-start.1 = ((bf16[4,64,2048]{2,1,0:T(8,128)(2,1)}), bf16[4,64,2048]{2,1,0:T(8,128)(2,1)S(1)}, u32[]{:S(2)}, u32[]{:S(2)}) async-start(bf16[4,64,2048]{2,1,0:T(8,128)(2,1)} %bitcast.8), calls=%async_computation.1 | async-start | bytes 2097152 | tf_op jit(solution)/shard_map/all_to_all | solution.py:310
  32.5 1.4 %collective-permute-start.5 = (bf16[32,2048]{1,0:T(8,128)(2,1)S(1)}, bf16[32,2048]{1,0:T(8,128)(2,1)S(1)}, u32[]{:S(2)}, u32[]{:S(2)}) collective-permute-start(bf16[32,2048]{1,0:T(8,128)(2,1)S(1)} %get-tuple-element.27.refs_0_), channel_id=1, source_target_pairs={{0,3},{1,0},{2,1},{3,2},{4,7},{5,4},{6,5},{7,6},{8,11},{9,8},{10,9... | collective-permute-start | bytes 393224 | tf_op jit(solution)/shard_map/ppermute | solution.py:284
  33.9 1.2 %collective-permute-start.4 = (bf16[32,2048]{1,0:T(8,128)(2,1)S(1)}, bf16[32,2048]{1,0:T(8,128)(2,1)S(1)}, u32[]{:S(2)}, u32[]{:S(2)}) collective-permute-start(bf16[32,2048]{1,0:T(8,128)(2,1)S(1)} %get-tuple-element.27.refs_0_), channel_id=1, source_target_pairs={{0,2},{1,3},{2,0},{3,1},{4,6},{5,7},{6,4},{7,5},{8,10},{9,11},{10,... | collective-permute-start | bytes 393224 | tf_op jit(solution)/shard_map/ppermute | solution.py:284
  35.1 2.0 %collective-permute-start.3 = (bf16[32,2048]{1,0:T(8,128)(2,1)S(1)}, bf16[32,2048]{1,0:T(8,128)(2,1)S(1)}, u32[]{:S(2)}, u32[]{:S(2)}) collective-permute-start(bf16[32,2048]{1,0:T(8,128)(2,1)S(1)} %get-tuple-element.27.refs_0_), channel_id=1, source_target_pairs={{0,1},{1,2},{2,3},{3,0},{4,5},{5,6},{6,7},{7,4},{8,9},{9,10},{10,1... | collective-permute-start | bytes 393224 | tf_op jit(solution)/shard_map/ppermute | solution.py:284
  37.1 1.2 %collective-permute-done.5.refs_3_ = bf16[32,2048]{1,0:T(8,128)(2,1)S(1)} collective-permute-done((bf16[32,2048]{1,0:T(8,128)(2,1)S(1)}, bf16[32,2048]{1,0:T(8,128)(2,1)S(1)}, u32[]{:S(2)}, u32[]{:S(2)}) %collective-permute-start.5) | collective-permute-done | bytes 131104 | tf_op jit(solution)/shard_map/ppermute | solution.py:284
  38.3 7.8 %collective-permute-done.4.refs_2_ = bf16[32,2048]{1,0:T(8,128)(2,1)S(1)} collective-permute-done((bf16[32,2048]{1,0:T(8,128)(2,1)S(1)}, bf16[32,2048]{1,0:T(8,128)(2,1)S(1)}, u32[]{:S(2)}, u32[]{:S(2)}) %collective-permute-start.4) | collective-permute-done | bytes 131104 | tf_op jit(solution)/shard_map/ppermute | solution.py:284
  46.1 0.0 collective-permute-done.3.refs_1_
  46.1 1.4 %pick_rows.1 = bf16[256,2048]{1,0:T(8,128)(2,1)} custom-call(bf16[256,128]{1,0:T(8,128)(2,1)S(1)} %get-tuple-element.23.pick_ref, bf16[32,2048]{1,0:T(8,128)(2,1)S(1)} %get-tuple-element.27.refs_0_, bf16[32,2048]{1,0:T(8,128)(2,1)S(1)} %collective-permute-done.3.refs_1_, bf16[32,2048]{1,0:T(8,128)(2,1)S(1)} %collective-permute-done.4.refs_2_, ...), custom_call_target="tpu_custom_call" | custom-call | tf_op jit(solution)/shard_map/pick_rows/pallas_call | solution.py:224
  47.5 0.0 all-to-all-done.1
  47.5 3.9 %all-to-all-start.2 = ((bf16[4,64,2048]{2,1,0:T(8,128)(2,1)}), bf16[4,64,2048]{2,1,0:T(8,128)(2,1)S(1)}, u32[]{:S(2)}, u32[]{:S(2)}) async-start(bf16[4,64,2048]{2,1,0:T(8,128)(2,1)} %bitcast.10), calls=%async_computation.2 | async-start | bytes 2097152 | tf_op jit(solution)/shard_map/all_to_all | solution.py:310
  51.4 1.3 %collective-permute-start.7 = (bf16[64,768]{1,0:T(8,128)(2,1)S(1)}, bf16[64,768]{1,0:T(8,128)(2,1)S(1)}, u32[]{:S(2)}, u32[]{:S(2)}) collective-permute-start(bf16[64,768]{1,0:T(8,128)(2,1)S(1)} %bitcast.46), channel_id=1, source_target_pairs={{0,2},{1,3},{2,0},{3,1},{4,6},{5,7},{6,4},{7,5},{8,10},{9,11},{10,... | collective-permute-start | bytes 294920 | tf_op jit(solution)/shard_map/ppermute | solution.py:284
  52.7 0.4 collective-permute-start.8
  53.2 1.6 %collective-permute-start.6 = (bf16[64,768]{1,0:T(8,128)(2,1)S(1)}, bf16[64,768]{1,0:T(8,128)(2,1)S(1)}, u32[]{:S(2)}, u32[]{:S(2)}) collective-permute-start(bf16[64,768]{1,0:T(8,128)(2,1)S(1)} %bitcast.44), channel_id=1, source_target_pairs={{0,1},{1,2},{2,3},{3,0},{4,5},{5,6},{6,7},{7,4},{8,9},{9,10},{10,1... | collective-permute-start | bytes 294920 | tf_op jit(solution)/shard_map/ppermute | solution.py:284
  54.8 0.0 collective-permute-start.9
  54.8 3.8 %fusion.2 = f32[256,768]{1,0:T(8,128)} fusion(bf16[256,2048]{1,0:T(8,128)(2,1)S(1)} %bitcast.31, bf16[768,4096]{1,0:T(8,128)(2,1)} %bitcast.47), kind=kOutput, calls=%fused_computation.2 | convolution fusion | flops 805306368 | bytes 4980736 | tf_op jit(solution)/shard_map/dot_general | solution.py:320
  58.6 2.0 %collective-permute-done.7.refs_2_ = bf16[64,768]{1,0:T(8,128)(2,1)S(1)} collective-permute-done((bf16[64,768]{1,0:T(8,128)(2,1)S(1)}, bf16[64,768]{1,0:T(8,128)(2,1)S(1)}, u32[]{:S(2)}, u32[]{:S(2)}) %collective-permute-start.7) | collective-permute-done | bytes 98336 | tf_op jit(solution)/shard_map/ppermute | solution.py:284
  60.5 0.0 collective-permute-done.8.refs_3_
  60.5 0.0 collective-permute-done.6.refs_1_
  60.6 1.9 %all-to-all-done.2 = bf16[4,64,2048]{2,1,0:T(8,128)(2,1)S(1)} async-done(((bf16[4,64,2048]{2,1,0:T(8,128)(2,1)}), bf16[4,64,2048]{2,1,0:T(8,128)(2,1)S(1)}, u32[]{:S(2)}, u32[]{:S(2)}) %all-to-all-start.2) | async-done | bytes 1048608 | tf_op jit(solution)/shard_map/all_to_all | solution.py:310
  62.4 3.0 %fusion = f32[256,768]{1,0:T(8,128)S(1)} fusion(bf16[256,2048]{1,0:T(8,128)(2,1)S(1)} %bitcast.34, bf16[768,4096]{1,0:T(8,128)(2,1)} %bitcast.48), kind=kOutput, calls=%fused_computation | convolution fusion | flops 805306368 | bytes 4980736 | tf_op jit(solution)/shard_map/dot_general | solution.py:320
  65.4 0.0 copy-start.1
  65.5 0.8 add_convert_fusion
  66.3 6.1 %all-to-all-start.3 = ((bf16[16,16,768]{2,1,0:T(8,128)(2,1)}), bf16[16,16,768]{2,1,0:T(8,128)(2,1)}, u32[]{:S(2)}, u32[]{:S(2)}) async-start(bf16[16,16,768]{2,1,0:T(8,128)(2,1)} %bitcast.17), calls=%async_computation.3 | async-start | bytes 786432 | tf_op jit(solution)/shard_map/all_to_all | solution.py:327
  72.4 0.2 collective-permute-start.11
  72.6 0.1 copy.12
  72.7 0.1 copy.13
  72.8 0.1 pad_add_fusion.scalars_ref
  72.9 1.3 %collective-permute-done.11.refs_5_ = bf16[64,3072]{1,0:T(8,128)(2,1)S(1)} collective-permute-done((bf16[64,3072]{1,0:T(8,128)(2,1)S(1)}, bf16[64,3072]{1,0:T(8,128)(2,1)S(1)}, u32[]{:S(2)}, u32[]{:S(2)}) %collective-permute-start.11) | collective-permute-done | bytes 393248 | tf_op jit(solution)/shard_map/ppermute | solution.py:287
  74.2 7.2 %down_rows.1 = bf16[384,4096]{1,0:T(8,128)(2,1)} custom-call(s32[2]{0:T(128)S(1)} %pad_add_fusion.scalars_ref, bf16[256,2048]{1,0:T(8,128)(2,1)S(1)} %bitcast.32, bf16[256,2048]{1,0:T(8,128)(2,1)S(1)} %bitcast.35, bf16[256,2048]{1,0:T(8,128)(2,1)} %collective-permute-done.9.refs_2_, bf16[256,2048]{1,0:T(8,128)(2,1)} %collective-permute-done.10.refs_3_, ...), custom_call_target="tpu_custom_call" | custom-call | flops 1610612736 | bytes 7340032 | tf_op jit(solution)/shard_map/down_rows/pallas_call | solution.py:253
  81.4 5.0 %all-to-all-done.3 = bf16[16,16,768]{2,1,0:T(8,128)(2,1)} async-done(((bf16[16,16,768]{2,1,0:T(8,128)(2,1)}), bf16[16,16,768]{2,1,0:T(8,128)(2,1)}, u32[]{:S(2)}, u32[]{:S(2)}) %all-to-all-start.3) | async-done | bytes 393248 | tf_op jit(solution)/shard_map/all_to_all | solution.py:327
  86.4 2.0 %multiply_reduce_fusion = (f32[32,8]{1,0:T(8,128)S(1)}, bf16[32,8,768]{2,1,0:T(8,128)(2,1)}) fusion(bf16[32,8,768]{2,1,0:T(8,128)(2,1)S(1)} %copy-done.1, f32[32,8]{1,0:T(8,128)S(1)} %copy.12, bf16[256,768,1]{1,0,2:T(8,128)(2,1)} %bitcast.20, bf16[256,256]{1,0:T(8,128)(2,1)S(1)} %copy.13), kind=kOutput, calls=%fused_computation.4 | convolution fusion | flops 101646080 | bytes 1312768 | tf_op jit(solution)/shard_map/dot_general | solution.py:346
  88.4 0.7 copy.14
  (15 shorter events, 0.1 us)
Async XLA Ops:
  0.6 1.0 %copy-start = (bf16[32,8,768]{2,1,0:T(8,128)(2,1)S(1)}, bf16[32,8,768]{2,1,0:T(8,128)(2,1)}, u32[]{:S(2)}) copy-start(bf16[32,8,768]{2,1,0:T(8,128)(2,1)} %param.6) | copy-start | bytes 1179652
  1.6 0.7 copy-start.3
  2.3 0.7 copy-start.5
  4.3 24.1 %all-to-all-start = ((bf16[4,64,768]{2,1,0:T(8,128)(2,1)}), bf16[4,64,768]{2,1,0:T(8,128)(2,1)S(1)}, u32[]{:S(2)}, u32[]{:S(2)}) async-start(bf16[4,64,768]{2,1,0:T(8,128)(2,1)} %bitcast.6), calls=%async_computation | async-start | bytes 786432 | tf_op jit(solution)/shard_map/all_to_all | solution.py:298
  9.5 0.9 %copy-start.2 = (bf16[32,4096]{1,0:T(8,128)(2,1)S(1)}, bf16[32,4096]{1,0:T(8,128)(2,1)}, u32[]{:S(2)}) copy-start(bf16[32,4096]{1,0:T(8,128)(2,1)} %tokens_ref.1) | copy-start | bytes 786436
  10.4 0.7 copy-start.4
  11.4 7.8 %collective-permute-start.2 = (bf16[32,2176]{1,0:T(8,128)(2,1)S(1)}, bf16[32,2176]{1,0:T(8,128)(2,1)S(1)}, u32[]{:S(2)}, u32[]{:S(2)}) collective-permute-start(bf16[32,2176]{1,0:T(8,128)(2,1)S(1)} %get-tuple-element.22.refs_0_), channel_id=1, source_target_pairs={{0,3},{1,0},{2,1},{3,2},{4,7},{5,4},{6,5},{7,6},{8,11},{9,8},{10,9... | collective-permute-start | bytes 417800 | tf_op jit(solution)/shard_map/ppermute | solution.py:284
  15.1 11.5 %collective-permute-start.1 = (bf16[32,2176]{1,0:T(8,128)(2,1)S(1)}, bf16[32,2176]{1,0:T(8,128)(2,1)S(1)}, u32[]{:S(2)}, u32[]{:S(2)}) collective-permute-start(bf16[32,2176]{1,0:T(8,128)(2,1)S(1)} %get-tuple-element.22.refs_0_), channel_id=1, source_target_pairs={{0,2},{1,3},{2,0},{3,1},{4,6},{5,7},{6,4},{7,5},{8,10},{9,11},{10,... | collective-permute-start | bytes 417800 | tf_op jit(solution)/shard_map/ppermute | solution.py:284
  15.1 11.5 %collective-permute-start = (bf16[32,2176]{1,0:T(8,128)(2,1)S(1)}, bf16[32,2176]{1,0:T(8,128)(2,1)S(1)}, u32[]{:S(2)}, u32[]{:S(2)}) collective-permute-start(bf16[32,2176]{1,0:T(8,128)(2,1)S(1)} %get-tuple-element.22.refs_0_), channel_id=1, source_target_pairs={{0,1},{1,2},{2,3},{3,0},{4,5},{5,6},{6,7},{7,4},{8,9},{9,10},{10,1... | collective-permute-start | bytes 417800 | tf_op jit(solution)/shard_map/ppermute | solution.py:284
  28.4 19.1 %all-to-all-start.1 = ((bf16[4,64,2048]{2,1,0:T(8,128)(2,1)}), bf16[4,64,2048]{2,1,0:T(8,128)(2,1)S(1)}, u32[]{:S(2)}, u32[]{:S(2)}) async-start(bf16[4,64,2048]{2,1,0:T(8,128)(2,1)} %bitcast.8), calls=%async_computation.1 | async-start | bytes 2097152 | tf_op jit(solution)/shard_map/all_to_all | solution.py:310
  32.5 5.8 %collective-permute-start.5 = (bf16[32,2048]{1,0:T(8,128)(2,1)S(1)}, bf16[32,2048]{1,0:T(8,128)(2,1)S(1)}, u32[]{:S(2)}, u32[]{:S(2)}) collective-permute-start(bf16[32,2048]{1,0:T(8,128)(2,1)S(1)} %get-tuple-element.27.refs_0_), channel_id=1, source_target_pairs={{0,3},{1,0},{2,1},{3,2},{4,7},{5,4},{6,5},{7,6},{8,11},{9,8},{10,9... | collective-permute-start | bytes 393224 | tf_op jit(solution)/shard_map/ppermute | solution.py:284
  33.9 12.2 %collective-permute-start.4 = (bf16[32,2048]{1,0:T(8,128)(2,1)S(1)}, bf16[32,2048]{1,0:T(8,128)(2,1)S(1)}, u32[]{:S(2)}, u32[]{:S(2)}) collective-permute-start(bf16[32,2048]{1,0:T(8,128)(2,1)S(1)} %get-tuple-element.27.refs_0_), channel_id=1, source_target_pairs={{0,2},{1,3},{2,0},{3,1},{4,6},{5,7},{6,4},{7,5},{8,10},{9,11},{10,... | collective-permute-start | bytes 393224 | tf_op jit(solution)/shard_map/ppermute | solution.py:284
  35.1 11.0 %collective-permute-start.3 = (bf16[32,2048]{1,0:T(8,128)(2,1)S(1)}, bf16[32,2048]{1,0:T(8,128)(2,1)S(1)}, u32[]{:S(2)}, u32[]{:S(2)}) collective-permute-start(bf16[32,2048]{1,0:T(8,128)(2,1)S(1)} %get-tuple-element.27.refs_0_), channel_id=1, source_target_pairs={{0,1},{1,2},{2,3},{3,0},{4,5},{5,6},{6,7},{7,4},{8,9},{9,10},{10,1... | collective-permute-start | bytes 393224 | tf_op jit(solution)/shard_map/ppermute | solution.py:284
  47.5 15.0 %all-to-all-start.2 = ((bf16[4,64,2048]{2,1,0:T(8,128)(2,1)}), bf16[4,64,2048]{2,1,0:T(8,128)(2,1)S(1)}, u32[]{:S(2)}, u32[]{:S(2)}) async-start(bf16[4,64,2048]{2,1,0:T(8,128)(2,1)} %bitcast.10), calls=%async_computation.2 | async-start | bytes 2097152 | tf_op jit(solution)/shard_map/all_to_all | solution.py:310
  51.4 9.1 %collective-permute-start.7 = (bf16[64,768]{1,0:T(8,128)(2,1)S(1)}, bf16[64,768]{1,0:T(8,128)(2,1)S(1)}, u32[]{:S(2)}, u32[]{:S(2)}) collective-permute-start(bf16[64,768]{1,0:T(8,128)(2,1)S(1)} %bitcast.46), channel_id=1, source_target_pairs={{0,2},{1,3},{2,0},{3,1},{4,6},{5,7},{6,4},{7,5},{8,10},{9,11},{10,... | collective-permute-start | bytes 294920 | tf_op jit(solution)/shard_map/ppermute | solution.py:284
  52.7 7.8 %collective-permute-start.8 = (bf16[64,768]{1,0:T(8,128)(2,1)S(1)}, bf16[64,768]{1,0:T(8,128)(2,1)S(1)}, u32[]{:S(2)}, u32[]{:S(2)}) collective-permute-start(bf16[64,768]{1,0:T(8,128)(2,1)S(1)} %bitcast.45), channel_id=1, source_target_pairs={{0,3},{1,0},{2,1},{3,2},{4,7},{5,4},{6,5},{7,6},{8,11},{9,8},{10,9... | collective-permute-start | bytes 294920 | tf_op jit(solution)/shard_map/ppermute | solution.py:284
  53.2 7.3 %collective-permute-start.6 = (bf16[64,768]{1,0:T(8,128)(2,1)S(1)}, bf16[64,768]{1,0:T(8,128)(2,1)S(1)}, u32[]{:S(2)}, u32[]{:S(2)}) collective-permute-start(bf16[64,768]{1,0:T(8,128)(2,1)S(1)} %bitcast.44), channel_id=1, source_target_pairs={{0,1},{1,2},{2,3},{3,0},{4,5},{5,6},{6,7},{7,4},{8,9},{9,10},{10,1... | collective-permute-start | bytes 294920 | tf_op jit(solution)/shard_map/ppermute | solution.py:284
  54.8 18.1 %collective-permute-start.9 = (bf16[256,2048]{1,0:T(8,128)(2,1)S(1)}, bf16[256,2048]{1,0:T(8,128)(2,1)}, u32[]{:S(2)}, u32[]{:S(2)}) collective-permute-start(bf16[256,2048]{1,0:T(8,128)(2,1)S(1)} %bitcast.30), channel_id=1, source_target_pairs={{0,16},{16,0},{1,17},{17,1},{2,18},{18,2},{3,19},{19,3},{4,20},{20... | collective-permute-start | bytes 3145736 | tf_op jit(solution)/shard_map/ppermute | solution.py:287
  58.6 14.0 %copy-start.6 = (f32[32,8]{0,1:T(8,128)S(1)}, f32[32,8]{0,1:T(8,128)}, u32[]{:S(2)}) copy-start(f32[32,8]{0,1:T(8,128)} %param.7) | copy-start | bytes 3076
  62.4 3.0 %copy-start.7 = (f32[256,768]{1,0:T(8,128)S(1)}, f32[256,768]{1,0:T(8,128)}, u32[]{:S(2)}) copy-start(f32[256,768]{1,0:T(8,128)} %fusion.2) | copy-start | bytes 2359300
  62.4 11.7 %collective-permute-start.10 = (bf16[256,2048]{1,0:T(8,128)(2,1)S(1)}, bf16[256,2048]{1,0:T(8,128)(2,1)}, u32[]{:S(2)}, u32[]{:S(2)}) collective-permute-start(bf16[256,2048]{1,0:T(8,128)(2,1)S(1)} %bitcast.33), channel_id=1, source_target_pairs={{0,16},{16,0},{1,17},{17,1},{2,18},{18,2},{3,19},{19,3},{4,20},{20... | collective-permute-start | bytes 3145736 | tf_op jit(solution)/shard_map/ppermute | solution.py:287
  65.4 21.0 %copy-start.1 = (bf16[32,8,768]{2,1,0:T(8,128)(2,1)S(1)}, bf16[32,8,768]{2,1,0:T(8,128)(2,1)}, u32[]{:S(2)}) copy-start(bf16[32,8,768]{2,1,0:T(8,128)(2,1)} %param.6) | copy-start | bytes 1179652
  66.3 20.2 %all-to-all-start.3 = ((bf16[16,16,768]{2,1,0:T(8,128)(2,1)}), bf16[16,16,768]{2,1,0:T(8,128)(2,1)}, u32[]{:S(2)}, u32[]{:S(2)}) async-start(bf16[16,16,768]{2,1,0:T(8,128)(2,1)} %bitcast.17), calls=%async_computation.3 | async-start | bytes 786432 | tf_op jit(solution)/shard_map/all_to_all | solution.py:327
  72.4 1.8 %collective-permute-start.11 = (bf16[64,3072]{1,0:T(8,128)(2,1)S(1)}, bf16[64,3072]{1,0:T(8,128)(2,1)S(1)}, u32[]{:S(2)}, u32[]{:S(2)}) collective-permute-start(bf16[64,3072]{1,0:T(8,128)(2,1)S(1)} %join_rows.1.refs_4_), channel_id=1, source_target_pairs={{0,16},{16,0},{1,17},{17,1},{2,18},{18,2},{3,19},{19,3},{4,20},{20... | collective-permute-start | bytes 1179656 | tf_op jit(solution)/shard_map/ppermute | solution.py:287

commit v10 on v9

--- a/solution.py
+++ b/solution.py
@@ -20,12 +20,28 @@
     return jnp.dot(one_hot, values, preferred_element_type=jnp.float32)
 
 
-def send_kernel(far_count, near_count, capacity, near_ref, ids_ref, gates_ref, hidden_ref, send_ref, back_ref):
+def prepare_kernel(far_count, near_count, capacity, near_ref, ids_ref, gates_ref, hidden_hbm, tokens_hbm, *refs):
+    outs, (send_ref, back_ref, hidden_ref, sem) = refs[:PARTS], refs[PARTS:]
+    part = outs[1].shape[1]
+    copies = [
+        pltpu.make_async_copy(tokens_hbm.at[:, i * part : (i + 1) * part], out.at[:, :part], sem.at[i])
+        for i, out in enumerate(outs)
+    ]
+    copies.append(pltpu.make_async_copy(hidden_hbm, hidden_ref, sem.at[PARTS]))
+    for copy in copies:
+        copy.start()
     top_count, tok_local = ids_ref.shape
     rows = tok_local * top_count
     experts = far_count * near_count
     slots = experts * capacity
     near = near_ref[0]
+    own_ids = ids_ref[...].astype(jnp.float32)
+    same = jnp.where(iota((top_count, ID_COLS), 0) == iota((top_count, ID_COLS), 1), 1.0, 0.0).astype(jnp.bfloat16)
+    id_cols = lax.dot_general(
+        own_ids.astype(jnp.bfloat16), same, (((0,), (0,)), ((), ())), preferred_element_type=jnp.float32
+    )
+    id_cols = jnp.where(iota((tok_local, ID_COLS), 1) < top_count, id_cols, -1.0)
+    outs[0][:, part:] = id_cols.astype(jnp.bfloat16)
     wide = jnp.where(iota((tok_local, rows), 1) // top_count == iota((tok_local, rows), 0), 1.0, 0.0).astype(jnp.bfloat16)
     mine = iota((top_count, rows), 1) % top_count == iota((top_count, rows), 0)
 
@@ -37,7 +53,7 @@
             spread = spread + exact_dot(piece, wide)
         return jnp.sum(jnp.where(mine, spread, 0.0), axis=0, keepdims=True)
 
-    ids = line(ids_ref[...].astype(jnp.float32)).astype(jnp.int32)
+    ids = line(own_ids).astype(jnp.int32)
     gates = line(gates_ref[...])
     named = iota((experts, rows), 0) == ids
     before = jnp.where(iota((rows, rows), 0) < iota((rows, rows), 1), 1.0, 0.0).astype(jnp.bfloat16)
@@ -49,31 +65,28 @@
     back_ref[...] = jnp.where(iota((slots, rows), 0) == back_slots, 1.0, 0.0).astype(jnp.bfloat16)
     place = iota((slots, rows), 0) == out_slots
     gate = jnp.sum(jnp.where(place, gates, 0.0), axis=1, keepdims=True)
-    picked = exact_dot(jnp.where(place, 1.0, 0.0).astype(jnp.bfloat16), hidden_ref[...])
-    send_ref[...] = (picked * gate).astype(jnp.bfloat16)
-
-
-def split_kernel(ids_ref, tokens_ref, *refs):
-    outs, sem = refs[:-1], refs[-1]
-    part = outs[1].shape[1]
-    copies = [
-        pltpu.make_async_copy(tokens_ref.at[:, i * part : (i + 1) * part], out.at[:, :part], sem.at[i])
-        for i, out in enumerate(outs)
-    ]
-    for copy in copies:
-        copy.start()
-    top_count, tok_local = ids_ref.shape
-    same = jnp.where(iota((top_count, ID_COLS), 0) == iota((top_count, ID_COLS), 1), 1.0, 0.0).astype(jnp.bfloat16)
-    ids = lax.dot_general(
-        ids_ref[...].astype(jnp.float32).astype(jnp.bfloat16),
-        same,
-        (((0,), (0,)), ((), ())),
-        preferred_element_type=jnp.float32,
-    )
-    ids = jnp.where(iota((tok_local, ID_COLS), 1) < top_count, ids, -1.0)
-    outs[0][:, part:] = ids.astype(jnp.bfloat16)
+    place = jnp.where(place, 1.0, 0.0).astype(jnp.bfloat16)
     for copy in copies:
         copy.wait()
+    send_ref[...] = (exact_dot(place, hidden_ref[...]) * gate).astype(jnp.bfloat16)
+
+
+def close_kernel(back_ref, came_ref, gates_ref, hidden_hbm, hid_ref, gates_out_ref, hidden_ref, sem):
+    copy = pltpu.make_async_copy(hidden_hbm, hidden_ref, sem)
+    copy.start()
+    top_count, tok_local = gates_ref.shape
+    rows = tok_local * top_count
+    back = lax.dot_general(
+        back_ref[...], came_ref[...], (((0,), (0,)), ((), ())), preferred_element_type=jnp.float32
+    )
+    mine = iota((tok_local, top_count, tok_local), 0) == iota((tok_local, top_count, tok_local), 2)
+    gate = jnp.where(mine, gates_ref[...][None], 0.0).reshape(rows, tok_local)
+    gate = jnp.sum(gate, axis=1, keepdims=True)
+    hid_ref[...] = (gate * back).astype(jnp.bfloat16)
+    copy.wait()
+    sums = jnp.sum(back * hidden_ref[...].astype(jnp.float32), axis=1, keepdims=True)
+    spread = jnp.broadcast_to(sums, (rows, tok_local)).reshape(tok_local, top_count, tok_local)
+    gates_out_ref[...] = jnp.sum(jnp.where(mine, spread, 0.0), axis=0)
 
 
 def picked_rows(pick, blocks, out_ref):
@@ -167,39 +180,39 @@
     return pltpu.CompilerParams(vmem_limit_bytes=mib * MIB)
 
 
-def send_rows(far_count, near_count, capacity, near, ids, gates, hidden):
+def prepare(far_count, near_count, capacity, near, ids, gates, hidden, tokens):
     slots = far_count * near_count * capacity
     rows, wide = hidden.shape
-    vmem = pl.BlockSpec(memory_space=pltpu.VMEM)
-    return pl.pallas_call(
-        functools.partial(send_kernel, far_count, near_count, capacity),
-        out_shape=[
-            jax.ShapeDtypeStruct((slots, wide), jnp.bfloat16),
-            jax.ShapeDtypeStruct((slots, rows), jnp.bfloat16),
-        ],
-        in_specs=[scalar_spec()] + [vmem] * 3,
-        out_specs=[vmem] * 2,
+    tok_local, width = tokens.shape
+    part = width // PARTS
+    vmem, hbm = pl.BlockSpec(memory_space=pltpu.VMEM), pl.BlockSpec(memory_space=pl.ANY)
+    shapes = [(tok_local, part + (ID_COLS if i == 0 else 0)) for i in range(PARTS)] + [(slots, wide), (slots, rows)]
+    return pl.pallas_call(
+        functools.partial(prepare_kernel, far_count, near_count, capacity),
+        out_shape=[jax.ShapeDtypeStruct(shape, jnp.bfloat16) for shape in shapes],
+        in_specs=[scalar_spec(), vmem, vmem, hbm, hbm],
+        out_specs=[vmem] * len(shapes),
+        scratch_shapes=[pltpu.VMEM(hidden.shape, jnp.bfloat16), pltpu.SemaphoreType.DMA((PARTS + 1,))],
         compiler_params=params(12),
         cost_estimate=pl.CostEstimate(flops=2 * rows * rows * wide, bytes_accessed=4 * rows * wide, transcendentals=0),
-        name="send_rows",
-    )(near, ids, gates, hidden)
-
-
-def split_rows(ids, tokens):
-    tok_local, width = tokens.shape
-    part = width // PARTS
+        name="prepare_rows",
+    )(near, ids, gates, hidden, tokens)
+
+
+def close(back_place, came_back, gates, hidden):
     vmem = pl.BlockSpec(memory_space=pltpu.VMEM)
     return pl.pallas_call(
-        split_kernel,
+        close_kernel,
         out_shape=[
-            jax.ShapeDtypeStruct((tok_local, part + (ID_COLS if i == 0 else 0)), jnp.bfloat16) for i in range(PARTS)
+            jax.ShapeDtypeStruct(hidden.shape, jnp.bfloat16),
+            jax.ShapeDtypeStruct(gates.shape, jnp.float32),
         ],
-        in_specs=[vmem, pl.BlockSpec(memory_space=pl.ANY)],
-        out_specs=[vmem] * PARTS,
-        scratch_shapes=[pltpu.SemaphoreType.DMA((PARTS,))],
-        compiler_params=params(8),
-        name="split_rows",
-    )(ids, tokens)
+        in_specs=[vmem, vmem, vmem, pl.BlockSpec(memory_space=pl.ANY)],
+        out_specs=[vmem] * 2,
+        scratch_shapes=[pltpu.VMEM(hidden.shape, jnp.bfloat16), pltpu.SemaphoreType.DMA],
+        compiler_params=params(12),
+        name="close_rows",
+    )(back_place, came_back, gates, hidden)
 
 
 def first_pick(far_count, near_count, capacity, near, blocks):
@@ -289,12 +302,11 @@
     def line(array):
         return [array] + [along(array, step) for step in range(1, near_count)]
 
-    ids = expert_ids.T
-    parts = list(split_rows(ids, grad_out))
+    hidden_rows = hidden.reshape(row_total, hidden_width)
+    *parts, send, back_place = prepare(
+        far_count, near_count, capacity, near_ref, expert_ids.T, gates.T, hidden_rows, grad_out
+    )
     blocks = line(parts[0])
-    send, back_place = send_rows(
-        far_count, near_count, capacity, near_ref, ids, gates.T, hidden.reshape(row_total, hidden_width)
-    )
     crossed = lax.all_to_all(
         send.reshape(far_count, -1, hidden_width), "far", split_axis=0, concat_axis=0, tiled=True
     ).reshape(far_count, near_count, capacity, hidden_width)
@@ -343,15 +355,10 @@
     )
     came_back, grad_down = lax.optimization_barrier((came_back, grad_down))
 
-    back_rows = lax.dot_general(
-        back_place,
-        came_back.reshape(slot_total, hidden_width),
-        (((0,), (0,)), ((), ())),
-        preferred_element_type=jnp.float32,
-    ).reshape(tok_local, top_count, hidden_width)
-    grad_hidden = (gates[:, :, None] * back_rows).astype(jnp.bfloat16)
-    grad_gates = jnp.sum(back_rows * hidden.astype(jnp.float32), axis=-1)
-    return (grad_hidden, grad_gates, grad_down[None])
+    grad_hidden, grad_gates = close(
+        back_place, came_back.reshape(slot_total, hidden_width), gates.T, hidden_rows
+    )
+    return (grad_hidden.reshape(hidden.shape), grad_gates.T, grad_down[None])
 
 
 def solution(mesh):

time: 89.8 us -> 87.7 us (0.977)
  matrix products: 8.79 us -> 6.77 us
  local copies, waits for them, and re-layouts: 4.87 us -> 3.36 us
  Pallas kernels: 12.1 us -> 13.5 us
    dot_general x1 -> x0, matrix products: 2.02 us -> none  [local(): lax.dot_general(back_place, came_back.reshape(slot_total, hidden_width),...]
    unnamed x18 -> x14, local copies, waits for them, and re-layouts: 4.75 us -> 3.33 us
    pallas_call x2, Pallas kernels: 1.59 us -> 3 us  [the longest x1 1.75 us: prepare(): pl.pallas_call(functools.partial(prepare_kernel, far_count, near_count, c...]
where the time goes in v10:
time: 87.7 us; the launch traced here: 87.1 us
  starting transfers between devices  32 us (36%)
  waiting for transfers between devices  29.8 us (34%)
  Pallas kernels  13.5 us (15%)
  matrix products  6.77 us (8%)
  local copies, waits for them, and re-layouts  3.36 us (4%)
  other arithmetic  0.89 us (1%)
    ppermute x9, waiting for transfers between devices, along(): lax.ppermute(array, 'near', [(i, (i + steps) % near_count) for i in range...  21.6 us
    ppermute x9, starting transfers between devices, along(): lax.ppermute(array, 'near', [(i, (i + steps) % near_count) for i in range...  12.5 us
    all_to_all x2, starting transfers between devices, local(): lax.all_to_all(picked.reshape(far_count, -1, part), 'far', split_axis=0,...  7.91 us
    pallas_call x1, Pallas kernels, down_rows(): pl.pallas_call(functools.partial(down_kernel, near_count, capacity), grid...  7.32 us
    dot_general x2, matrix products, local(): lax.dot_general(rows[i], weight[:, i * part:(i + 1) * part], (((1,), (1,)...  6.77 us
    all_to_all x1, starting transfers between devices, local(): lax.all_to_all(total.astype(jnp.bfloat16).reshape(experts, capacity, hidd...  6.13 us
    all_to_all x1, starting transfers between devices, local(): lax.all_to_all(send.reshape(far_count, -1, hidden_width), 'far', split_ax...  5.18 us
    all_to_all x1, waiting for transfers between devices, local(): lax.all_to_all(total.astype(jnp.bfloat16).reshape(experts, capacity, hidd...  4.74 us
  transfers between devices with their start and end apart: 16, of which 8 were waited for; matrix products, arithmetic and copies ran while one was open for 9% of the time, Pallas kernels for 12%

profile of v10, /device:TPU:0, one launch (start us, length us, event | category | flops | bytes accessed | tf_op | source)
XLA Modules:
  0.0 87.1 jit_solution(12208424397083662335)
XLA Ops:
  0.6 0.0 copy-start
  0.6 1.0 %copy-done = bf16[32,8,768]{2,1,0:T(8,128)(2,1)S(1)} copy-done((bf16[32,8,768]{2,1,0:T(8,128)(2,1)S(1)}, bf16[32,8,768]{2,1,0:T(8,128)(2,1)}, u32[]{:S(2)}) %copy-start) | copy-done | bytes 393240
  1.6 0.9 %copy-done.2 = bf16[32,4096]{1,0:T(8,128)(2,1)S(1)} copy-done((bf16[32,4096]{1,0:T(8,128)(2,1)S(1)}, bf16[32,4096]{1,0:T(8,128)(2,1)}, u32[]{:S(2)}) %copy-start.2) | copy-done | bytes 262168
  2.6 0.7 copy-done.3
  3.3 0.7 copy-done.5
  4.0 1.8 %prepare_rows.1 = (bf16[32,2176]{1,0:T(8,128)(2,1)S(1)}, bf16[32,2048]{1,0:T(8,128)(2,1)S(1)}, bf16[256,768]{1,0:T(8,128)(2,1)}, bf16[256,256]{1,0:T(8,128)(2,1)S(1)}) custom-call(s32[1]{0:T(128)} %bitcast.near_ref, s32[8,32]{1,0:T(8,128)S(1)} %bitcast.35, f32[8,32]{1,0:T(8,128)S(1)} %bitcast.33, bf16[256,768]{1,0:T(8,128)(2,1)S(1)} %bitcast.29, ...), custom_call_target="tpu_custom_call" | custom-call | flops 100663296 | bytes 786432 | tf_op jit(solution)/shard_map/prepare_rows/pallas_call | solution.py:190
  5.7 5.2 %all-to-all-start = ((bf16[4,64,768]{2,1,0:T(8,128)(2,1)}), bf16[4,64,768]{2,1,0:T(8,128)(2,1)S(1)}, u32[]{:S(2)}, u32[]{:S(2)}) async-start(bf16[4,64,768]{2,1,0:T(8,128)(2,1)} %bitcast.4), calls=%async_computation | async-start | bytes 786432 | tf_op jit(solution)/shard_map/all_to_all | solution.py:310
  10.9 3.6 %collective-permute-start.2 = (bf16[32,2176]{1,0:T(8,128)(2,1)S(1)}, bf16[32,2176]{1,0:T(8,128)(2,1)S(1)}, u32[]{:S(2)}, u32[]{:S(2)}) collective-permute-start(bf16[32,2176]{1,0:T(8,128)(2,1)S(1)} %get-tuple-element.24.refs_0_), channel_id=1, source_target_pairs={{0,3},{1,0},{2,1},{3,2},{4,7},{5,4},{6,5},{7,6},{8,11},{9,8},{10,9... | collective-permute-start | bytes 417800 | tf_op jit(solution)/shard_map/ppermute | solution.py:297
  14.5 0.0 collective-permute-start.1
  14.5 1.0 %collective-permute-start = (bf16[32,2176]{1,0:T(8,128)(2,1)S(1)}, bf16[32,2176]{1,0:T(8,128)(2,1)S(1)}, u32[]{:S(2)}, u32[]{:S(2)}) collective-permute-start(bf16[32,2176]{1,0:T(8,128)(2,1)S(1)} %get-tuple-element.24.refs_0_), channel_id=1, source_target_pairs={{0,1},{1,2},{2,3},{3,0},{4,5},{5,6},{6,7},{7,4},{8,9},{9,10},{10,1... | collective-permute-start | bytes 417800 | tf_op jit(solution)/shard_map/ppermute | solution.py:297
  15.5 3.1 %collective-permute-done.2.refs_3_ = bf16[32,2176]{1,0:T(8,128)(2,1)S(1)} collective-permute-done((bf16[32,2176]{1,0:T(8,128)(2,1)S(1)}, bf16[32,2176]{1,0:T(8,128)(2,1)S(1)}, u32[]{:S(2)}, u32[]{:S(2)}) %collective-permute-start.2) | collective-permute-done | bytes 139296 | tf_op jit(solution)/shard_map/ppermute | solution.py:297
  18.6 7.5 %collective-permute-done.1.refs_2_ = bf16[32,2176]{1,0:T(8,128)(2,1)S(1)} collective-permute-done((bf16[32,2176]{1,0:T(8,128)(2,1)S(1)}, bf16[32,2176]{1,0:T(8,128)(2,1)S(1)}, u32[]{:S(2)}, u32[]{:S(2)}) %collective-permute-start.1) | collective-permute-done | bytes 139296 | tf_op jit(solution)/shard_map/ppermute | solution.py:297
  26.1 0.0 collective-permute-done.refs_1_
  26.1 1.8 %first_pick.1 = (bf16[256,2048]{1,0:T(8,128)(2,1)}, bf16[256,128]{1,0:T(8,128)(2,1)S(1)}) custom-call(s32[1]{0:T(128)} %bitcast.near_ref, bf16[32,2176]{1,0:T(8,128)(2,1)S(1)} %get-tuple-element.24.refs_0_, bf16[32,2176]{1,0:T(8,128)(2,1)S(1)} %collective-permute-done.refs_1_, bf16[32,2176]{1,0:T(8,128)(2,1)S(1)} %collective-permute-done.1.refs_2_, ...), custom_call_target="tpu_custom_call" | custom-call | tf_op jit(solution)/shard_map/first_pick/pallas_call | solution.py:222
  27.9 0.0 all-to-all-done
  27.9 4.0 %all-to-all-start.1 = ((bf16[4,64,2048]{2,1,0:T(8,128)(2,1)}), bf16[4,64,2048]{2,1,0:T(8,128)(2,1)S(1)}, u32[]{:S(2)}, u32[]{:S(2)}) async-start(bf16[4,64,2048]{2,1,0:T(8,128)(2,1)} %bitcast.6), calls=%async_computation.1 | async-start | bytes 2097152 | tf_op jit(solution)/shard_map/all_to_all | solution.py:322
  31.9 1.4 %collective-permute-start.5 = (bf16[32,2048]{1,0:T(8,128)(2,1)S(1)}, bf16[32,2048]{1,0:T(8,128)(2,1)S(1)}, u32[]{:S(2)}, u32[]{:S(2)}) collective-permute-start(bf16[32,2048]{1,0:T(8,128)(2,1)S(1)} %get-tuple-element.29.refs_0_), channel_id=1, source_target_pairs={{0,3},{1,0},{2,1},{3,2},{4,7},{5,4},{6,5},{7,6},{8,11},{9,8},{10,9... | collective-permute-start | bytes 393224 | tf_op jit(solution)/shard_map/ppermute | solution.py:297
  33.3 1.2 %collective-permute-start.4 = (bf16[32,2048]{1,0:T(8,128)(2,1)S(1)}, bf16[32,2048]{1,0:T(8,128)(2,1)S(1)}, u32[]{:S(2)}, u32[]{:S(2)}) collective-permute-start(bf16[32,2048]{1,0:T(8,128)(2,1)S(1)} %get-tuple-element.29.refs_0_), channel_id=1, source_target_pairs={{0,2},{1,3},{2,0},{3,1},{4,6},{5,7},{6,4},{7,5},{8,10},{9,11},{10,... | collective-permute-start | bytes 393224 | tf_op jit(solution)/shard_map/ppermute | solution.py:297
  34.5 2.0 %collective-permute-start.3 = (bf16[32,2048]{1,0:T(8,128)(2,1)S(1)}, bf16[32,2048]{1,0:T(8,128)(2,1)S(1)}, u32[]{:S(2)}, u32[]{:S(2)}) collective-permute-start(bf16[32,2048]{1,0:T(8,128)(2,1)S(1)} %get-tuple-element.29.refs_0_), channel_id=1, source_target_pairs={{0,1},{1,2},{2,3},{3,0},{4,5},{5,6},{6,7},{7,4},{8,9},{9,10},{10,1... | collective-permute-start | bytes 393224 | tf_op jit(solution)/shard_map/ppermute | solution.py:297
  36.5 1.2 %collective-permute-done.5.refs_3_ = bf16[32,2048]{1,0:T(8,128)(2,1)S(1)} collective-permute-done((bf16[32,2048]{1,0:T(8,128)(2,1)S(1)}, bf16[32,2048]{1,0:T(8,128)(2,1)S(1)}, u32[]{:S(2)}, u32[]{:S(2)}) %collective-permute-start.5) | collective-permute-done | bytes 131104 | tf_op jit(solution)/shard_map/ppermute | solution.py:297
  37.7 7.8 %collective-permute-done.4.refs_2_ = bf16[32,2048]{1,0:T(8,128)(2,1)S(1)} collective-permute-done((bf16[32,2048]{1,0:T(8,128)(2,1)S(1)}, bf16[32,2048]{1,0:T(8,128)(2,1)S(1)}, u32[]{:S(2)}, u32[]{:S(2)}) %collective-permute-start.4) | collective-permute-done | bytes 131104 | tf_op jit(solution)/shard_map/ppermute | solution.py:297
  45.5 0.0 collective-permute-done.3.refs_1_
  45.5 1.4 %pick_rows.1 = bf16[256,2048]{1,0:T(8,128)(2,1)} custom-call(bf16[256,128]{1,0:T(8,128)(2,1)S(1)} %get-tuple-element.25.pick_ref, bf16[32,2048]{1,0:T(8,128)(2,1)S(1)} %get-tuple-element.29.refs_0_, bf16[32,2048]{1,0:T(8,128)(2,1)S(1)} %collective-permute-done.3.refs_1_, bf16[32,2048]{1,0:T(8,128)(2,1)S(1)} %collective-permute-done.4.refs_2_, ...), custom_call_target="tpu_custom_call" | custom-call | tf_op jit(solution)/shard_map/pick_rows/pallas_call | solution.py:237
  46.9 0.0 all-to-all-done.1
  46.9 3.9 %all-to-all-start.2 = ((bf16[4,64,2048]{2,1,0:T(8,128)(2,1)}), bf16[4,64,2048]{2,1,0:T(8,128)(2,1)S(1)}, u32[]{:S(2)}, u32[]{:S(2)}) async-start(bf16[4,64,2048]{2,1,0:T(8,128)(2,1)} %bitcast.8), calls=%async_computation.2 | async-start | bytes 2097152 | tf_op jit(solution)/shard_map/all_to_all | solution.py:322
  50.8 1.3 %collective-permute-start.7 = (bf16[64,768]{1,0:T(8,128)(2,1)S(1)}, bf16[64,768]{1,0:T(8,128)(2,1)S(1)}, u32[]{:S(2)}, u32[]{:S(2)}) collective-permute-start(bf16[64,768]{1,0:T(8,128)(2,1)S(1)} %bitcast.41), channel_id=1, source_target_pairs={{0,2},{1,3},{2,0},{3,1},{4,6},{5,7},{6,4},{7,5},{8,10},{9,11},{10,... | collective-permute-start | bytes 294920 | tf_op jit(solution)/shard_map/ppermute | solution.py:297
  52.2 0.4 collective-permute-start.8
  52.6 1.6 %collective-permute-start.6 = (bf16[64,768]{1,0:T(8,128)(2,1)S(1)}, bf16[64,768]{1,0:T(8,128)(2,1)S(1)}, u32[]{:S(2)}, u32[]{:S(2)}) collective-permute-start(bf16[64,768]{1,0:T(8,128)(2,1)S(1)} %bitcast.39), channel_id=1, source_target_pairs={{0,1},{1,2},{2,3},{3,0},{4,5},{5,6},{6,7},{7,4},{8,9},{9,10},{10,1... | collective-permute-start | bytes 294920 | tf_op jit(solution)/shard_map/ppermute | solution.py:297
  54.2 0.0 collective-permute-start.9
  54.2 3.8 %fusion.2 = f32[256,768]{1,0:T(8,128)} fusion(bf16[256,2048]{1,0:T(8,128)(2,1)S(1)} %bitcast.24, bf16[768,4096]{1,0:T(8,128)(2,1)} %bitcast.42), kind=kOutput, calls=%fused_computation.2 | convolution fusion | flops 805306368 | bytes 4980736 | tf_op jit(solution)/shard_map/dot_general | solution.py:332
  58.0 2.0 %collective-permute-done.7.refs_2_ = bf16[64,768]{1,0:T(8,128)(2,1)S(1)} collective-permute-done((bf16[64,768]{1,0:T(8,128)(2,1)S(1)}, bf16[64,768]{1,0:T(8,128)(2,1)S(1)}, u32[]{:S(2)}, u32[]{:S(2)}) %collective-permute-start.7) | collective-permute-done | bytes 98336 | tf_op jit(solution)/shard_map/ppermute | solution.py:297
  60.0 0.0 collective-permute-done.8.refs_3_
  60.0 0.0 collective-permute-done.6.refs_1_
  60.0 1.8 %all-to-all-done.2 = bf16[4,64,2048]{2,1,0:T(8,128)(2,1)S(1)} async-done(((bf16[4,64,2048]{2,1,0:T(8,128)(2,1)}), bf16[4,64,2048]{2,1,0:T(8,128)(2,1)S(1)}, u32[]{:S(2)}, u32[]{:S(2)}) %all-to-all-start.2) | async-done | bytes 1048608 | tf_op jit(solution)/shard_map/all_to_all | solution.py:322
  61.9 0.0 collective-permute-start.10
  61.9 3.0 %fusion = f32[256,768]{1,0:T(8,128)S(1)} fusion(bf16[256,2048]{1,0:T(8,128)(2,1)S(1)} %bitcast.27, bf16[768,4096]{1,0:T(8,128)(2,1)} %bitcast.43), kind=kOutput, calls=%fused_computation | convolution fusion | flops 805306368 | bytes 4980736 | tf_op jit(solution)/shard_map/dot_general | solution.py:332
  64.9 0.0 copy-start.1
  64.9 0.0 copy-start.4
  64.9 0.8 add_convert_fusion
  65.7 6.1 %all-to-all-start.3 = ((bf16[16,16,768]{2,1,0:T(8,128)(2,1)}), bf16[16,16,768]{2,1,0:T(8,128)(2,1)S(1)}, u32[]{:S(2)}, u32[]{:S(2)}) async-start(bf16[16,16,768]{2,1,0:T(8,128)(2,1)} %bitcast.38), calls=%async_computation.3 | async-start | bytes 786432 | tf_op jit(solution)/shard_map/all_to_all | solution.py:339
  71.9 0.2 collective-permute-start.11
  72.1 0.1 pad_add_fusion.scalars_ref
  72.2 0.0 collective-permute-done.9.refs_2_
  72.2 1.6 %collective-permute-done.11.refs_5_ = bf16[64,3072]{1,0:T(8,128)(2,1)} collective-permute-done((bf16[64,3072]{1,0:T(8,128)(2,1)S(1)}, bf16[64,3072]{1,0:T(8,128)(2,1)}, u32[]{:S(2)}, u32[]{:S(2)}) %collective-permute-start.11) | collective-permute-done | bytes 393248 | tf_op jit(solution)/shard_map/ppermute | solution.py:300
  73.8 0.0 collective-permute-done.10.refs_3_
  73.8 7.3 %down_rows.1 = bf16[384,4096]{1,0:T(8,128)(2,1)} custom-call(s32[2]{0:T(128)S(1)} %pad_add_fusion.scalars_ref, bf16[256,2048]{1,0:T(8,128)(2,1)S(1)} %bitcast.25, bf16[256,2048]{1,0:T(8,128)(2,1)S(1)} %bitcast.28, bf16[256,2048]{1,0:T(8,128)(2,1)} %collective-permute-done.9.refs_2_, bf16[256,2048]{1,0:T(8,128)(2,1)} %collective-permute-done.10.refs_3_, ...), custom_call_target="tpu_custom_call" | custom-call | flops 1610612736 | bytes 7340032 | tf_op jit(solution)/shard_map/down_rows/pallas_call | solution.py:266
  81.1 4.7 %all-to-all-done.3 = bf16[16,16,768]{2,1,0:T(8,128)(2,1)S(1)} async-done(((bf16[16,16,768]{2,1,0:T(8,128)(2,1)}), bf16[16,16,768]{2,1,0:T(8,128)(2,1)S(1)}, u32[]{:S(2)}, u32[]{:S(2)}) %all-to-all-start.3) | async-done | bytes 393248 | tf_op jit(solution)/shard_map/all_to_all | solution.py:339
  85.9 1.2 %close_rows.1 = (bf16[256,768]{1,0:T(8,128)(2,1)}, f32[8,32]{1,0:T(8,128)}) custom-call(bf16[256,256]{1,0:T(8,128)(2,1)S(1)} %get-tuple-element.23.back_ref, bf16[256,768]{1,0:T(8,128)(2,1)S(1)} %bitcast.31, f32[8,32]{1,0:T(8,128)S(1)} %bitcast.34, bf16[256,768]{1,0:T(8,128)(2,1)S(1)} %bitcast.30), custom_call_target="tpu_custom_call" | custom-call | tf_op jit(solution)/shard_map/close_rows/pallas_call | solution.py:204
  (9 shorter events, 0.1 us)
Async XLA Ops:
  0.6 1.0 %copy-start = (bf16[32,8,768]{2,1,0:T(8,128)(2,1)S(1)}, bf16[32,8,768]{2,1,0:T(8,128)(2,1)}, u32[]{:S(2)}) copy-start(bf16[32,8,768]{2,1,0:T(8,128)(2,1)} %param.6) | copy-start | bytes 1179652
  1.6 0.9 %copy-start.2 = (bf16[32,4096]{1,0:T(8,128)(2,1)S(1)}, bf16[32,4096]{1,0:T(8,128)(2,1)}, u32[]{:S(2)}) copy-start(bf16[32,4096]{1,0:T(8,128)(2,1)} %tokens_hbm.1) | copy-start | bytes 786436
  2.6 0.7 copy-start.3
  3.3 0.7 copy-start.5
  5.7 22.2 %all-to-all-start = ((bf16[4,64,768]{2,1,0:T(8,128)(2,1)}), bf16[4,64,768]{2,1,0:T(8,128)(2,1)S(1)}, u32[]{:S(2)}, u32[]{:S(2)}) async-start(bf16[4,64,768]{2,1,0:T(8,128)(2,1)} %bitcast.4), calls=%async_computation | async-start | bytes 786432 | tf_op jit(solution)/shard_map/all_to_all | solution.py:310
  10.9 7.7 %collective-permute-start.2 = (bf16[32,2176]{1,0:T(8,128)(2,1)S(1)}, bf16[32,2176]{1,0:T(8,128)(2,1)S(1)}, u32[]{:S(2)}, u32[]{:S(2)}) collective-permute-start(bf16[32,2176]{1,0:T(8,128)(2,1)S(1)} %get-tuple-element.24.refs_0_), channel_id=1, source_target_pairs={{0,3},{1,0},{2,1},{3,2},{4,7},{5,4},{6,5},{7,6},{8,11},{9,8},{10,9... | collective-permute-start | bytes 417800 | tf_op jit(solution)/shard_map/ppermute | solution.py:297
  14.5 11.6 %collective-permute-start.1 = (bf16[32,2176]{1,0:T(8,128)(2,1)S(1)}, bf16[32,2176]{1,0:T(8,128)(2,1)S(1)}, u32[]{:S(2)}, u32[]{:S(2)}) collective-permute-start(bf16[32,2176]{1,0:T(8,128)(2,1)S(1)} %get-tuple-element.24.refs_0_), channel_id=1, source_target_pairs={{0,2},{1,3},{2,0},{3,1},{4,6},{5,7},{6,4},{7,5},{8,10},{9,11},{10,... | collective-permute-start | bytes 417800 | tf_op jit(solution)/shard_map/ppermute | solution.py:297
  14.5 11.6 %collective-permute-start = (bf16[32,2176]{1,0:T(8,128)(2,1)S(1)}, bf16[32,2176]{1,0:T(8,128)(2,1)S(1)}, u32[]{:S(2)}, u32[]{:S(2)}) collective-permute-start(bf16[32,2176]{1,0:T(8,128)(2,1)S(1)} %get-tuple-element.24.refs_0_), channel_id=1, source_target_pairs={{0,1},{1,2},{2,3},{3,0},{4,5},{5,6},{6,7},{7,4},{8,9},{9,10},{10,1... | collective-permute-start | bytes 417800 | tf_op jit(solution)/shard_map/ppermute | solution.py:297
  27.9 19.0 %all-to-all-start.1 = ((bf16[4,64,2048]{2,1,0:T(8,128)(2,1)}), bf16[4,64,2048]{2,1,0:T(8,128)(2,1)S(1)}, u32[]{:S(2)}, u32[]{:S(2)}) async-start(bf16[4,64,2048]{2,1,0:T(8,128)(2,1)} %bitcast.6), calls=%async_computation.1 | async-start | bytes 2097152 | tf_op jit(solution)/shard_map/all_to_all | solution.py:322
  31.9 5.8 %collective-permute-start.5 = (bf16[32,2048]{1,0:T(8,128)(2,1)S(1)}, bf16[32,2048]{1,0:T(8,128)(2,1)S(1)}, u32[]{:S(2)}, u32[]{:S(2)}) collective-permute-start(bf16[32,2048]{1,0:T(8,128)(2,1)S(1)} %get-tuple-element.29.refs_0_), channel_id=1, source_target_pairs={{0,3},{1,0},{2,1},{3,2},{4,7},{5,4},{6,5},{7,6},{8,11},{9,8},{10,9... | collective-permute-start | bytes 393224 | tf_op jit(solution)/shard_map/ppermute | solution.py:297
  33.3 12.2 %collective-permute-start.4 = (bf16[32,2048]{1,0:T(8,128)(2,1)S(1)}, bf16[32,2048]{1,0:T(8,128)(2,1)S(1)}, u32[]{:S(2)}, u32[]{:S(2)}) collective-permute-start(bf16[32,2048]{1,0:T(8,128)(2,1)S(1)} %get-tuple-element.29.refs_0_), channel_id=1, source_target_pairs={{0,2},{1,3},{2,0},{3,1},{4,6},{5,7},{6,4},{7,5},{8,10},{9,11},{10,... | collective-permute-start | bytes 393224 | tf_op jit(solution)/shard_map/ppermute | solution.py:297
  34.5 11.1 %collective-permute-start.3 = (bf16[32,2048]{1,0:T(8,128)(2,1)S(1)}, bf16[32,2048]{1,0:T(8,128)(2,1)S(1)}, u32[]{:S(2)}, u32[]{:S(2)}) collective-permute-start(bf16[32,2048]{1,0:T(8,128)(2,1)S(1)} %get-tuple-element.29.refs_0_), channel_id=1, source_target_pairs={{0,1},{1,2},{2,3},{3,0},{4,5},{5,6},{6,7},{7,4},{8,9},{9,10},{10,1... | collective-permute-start | bytes 393224 | tf_op jit(solution)/shard_map/ppermute | solution.py:297
  46.9 14.9 %all-to-all-start.2 = ((bf16[4,64,2048]{2,1,0:T(8,128)(2,1)}), bf16[4,64,2048]{2,1,0:T(8,128)(2,1)S(1)}, u32[]{:S(2)}, u32[]{:S(2)}) async-start(bf16[4,64,2048]{2,1,0:T(8,128)(2,1)} %bitcast.8), calls=%async_computation.2 | async-start | bytes 2097152 | tf_op jit(solution)/shard_map/all_to_all | solution.py:322
  50.8 9.2 %collective-permute-start.7 = (bf16[64,768]{1,0:T(8,128)(2,1)S(1)}, bf16[64,768]{1,0:T(8,128)(2,1)S(1)}, u32[]{:S(2)}, u32[]{:S(2)}) collective-permute-start(bf16[64,768]{1,0:T(8,128)(2,1)S(1)} %bitcast.41), channel_id=1, source_target_pairs={{0,2},{1,3},{2,0},{3,1},{4,6},{5,7},{6,4},{7,5},{8,10},{9,11},{10,... | collective-permute-start | bytes 294920 | tf_op jit(solution)/shard_map/ppermute | solution.py:297
  52.2 7.8 %collective-permute-start.8 = (bf16[64,768]{1,0:T(8,128)(2,1)S(1)}, bf16[64,768]{1,0:T(8,128)(2,1)S(1)}, u32[]{:S(2)}, u32[]{:S(2)}) collective-permute-start(bf16[64,768]{1,0:T(8,128)(2,1)S(1)} %bitcast.40), channel_id=1, source_target_pairs={{0,3},{1,0},{2,1},{3,2},{4,7},{5,4},{6,5},{7,6},{8,11},{9,8},{10,9... | collective-permute-start | bytes 294920 | tf_op jit(solution)/shard_map/ppermute | solution.py:297
  52.6 7.4 %collective-permute-start.6 = (bf16[64,768]{1,0:T(8,128)(2,1)S(1)}, bf16[64,768]{1,0:T(8,128)(2,1)S(1)}, u32[]{:S(2)}, u32[]{:S(2)}) collective-permute-start(bf16[64,768]{1,0:T(8,128)(2,1)S(1)} %bitcast.39), channel_id=1, source_target_pairs={{0,1},{1,2},{2,3},{3,0},{4,5},{5,6},{6,7},{7,4},{8,9},{9,10},{10,1... | collective-permute-start | bytes 294920 | tf_op jit(solution)/shard_map/ppermute | solution.py:297
  54.2 18.0 %collective-permute-start.9 = (bf16[256,2048]{1,0:T(8,128)(2,1)S(1)}, bf16[256,2048]{1,0:T(8,128)(2,1)}, u32[]{:S(2)}, u32[]{:S(2)}) collective-permute-start(bf16[256,2048]{1,0:T(8,128)(2,1)S(1)} %bitcast.23), channel_id=1, source_target_pairs={{0,16},{16,0},{1,17},{17,1},{2,18},{18,2},{3,19},{19,3},{4,20},{20... | collective-permute-start | bytes 3145736 | tf_op jit(solution)/shard_map/ppermute | solution.py:300
  61.9 3.0 %copy-start.6 = (f32[256,768]{1,0:T(8,128)S(1)}, f32[256,768]{1,0:T(8,128)}, u32[]{:S(2)}) copy-start(f32[256,768]{1,0:T(8,128)} %fusion.2) | copy-start | bytes 2359300
  61.9 11.9 %collective-permute-start.10 = (bf16[256,2048]{1,0:T(8,128)(2,1)S(1)}, bf16[256,2048]{1,0:T(8,128)(2,1)}, u32[]{:S(2)}, u32[]{:S(2)}) collective-permute-start(bf16[256,2048]{1,0:T(8,128)(2,1)S(1)} %bitcast.26), channel_id=1, source_target_pairs={{0,16},{16,0},{1,17},{17,1},{2,18},{18,2},{3,19},{19,3},{4,20},{20... | collective-permute-start | bytes 3145736 | tf_op jit(solution)/shard_map/ppermute | solution.py:300
  64.9 21.0 %copy-start.1 = (bf16[32,8,768]{2,1,0:T(8,128)(2,1)S(1)}, bf16[32,8,768]{2,1,0:T(8,128)(2,1)}, u32[]{:S(2)}) copy-start(bf16[32,8,768]{2,1,0:T(8,128)(2,1)} %param.6) | copy-start | bytes 1179652
  64.9 21.0 %copy-start.4 = (f32[32,8]{0,1:T(8,128)S(1)}, f32[32,8]{0,1:T(8,128)}, u32[]{:S(2)}) copy-start(f32[32,8]{0,1:T(8,128)} %param.7) | copy-start | bytes 3076
  65.7 20.1 %all-to-all-start.3 = ((bf16[16,16,768]{2,1,0:T(8,128)(2,1)}), bf16[16,16,768]{2,1,0:T(8,128)(2,1)S(1)}, u32[]{:S(2)}, u32[]{:S(2)}) async-start(bf16[16,16,768]{2,1,0:T(8,128)(2,1)} %bitcast.38), calls=%async_computation.3 | async-start | bytes 786432 | tf_op jit(solution)/shard_map/all_to_all | solution.py:339
  71.9 1.9 %collective-permute-start.11 = (bf16[64,3072]{1,0:T(8,128)(2,1)S(1)}, bf16[64,3072]{1,0:T(8,128)(2,1)}, u32[]{:S(2)}, u32[]{:S(2)}) collective-permute-start(bf16[64,3072]{1,0:T(8,128)(2,1)S(1)} %join_rows.1.refs_4_), channel_id=1, source_target_pairs={{0,16},{16,0},{1,17},{17,1},{2,18},{18,2},{3,19},{19,3},{4,20},{20... | collective-permute-start | bytes 1179656 | tf_op jit(solution)/shard_map/ppermute | solution.py:300

commit v11 on v10

--- a/solution.py
+++ b/solution.py
@@ -20,21 +20,27 @@
     return jnp.dot(one_hot, values, preferred_element_type=jnp.float32)
 
 
-def prepare_kernel(far_count, near_count, capacity, near_ref, ids_ref, gates_ref, hidden_hbm, tokens_hbm, *refs):
-    outs, (send_ref, back_ref, hidden_ref, sem) = refs[:PARTS], refs[PARTS:]
+def prepare_kernel(far_count, near_count, capacity, scalars_ref, ids_hbm, gates_hbm, hidden_hbm, tokens_hbm, *refs):
+    outs, sends, (back_ref, ids_ref, gates_ref, hidden_ref, sem) = refs[:PARTS], refs[PARTS:-5], refs[-5:]
     part = outs[1].shape[1]
     copies = [
         pltpu.make_async_copy(tokens_hbm.at[:, i * part : (i + 1) * part], out.at[:, :part], sem.at[i])
         for i, out in enumerate(outs)
     ]
     copies.append(pltpu.make_async_copy(hidden_hbm, hidden_ref, sem.at[PARTS]))
-    for copy in copies:
+    small = [
+        pltpu.make_async_copy(ids_hbm, ids_ref, sem.at[PARTS + 1]),
+        pltpu.make_async_copy(gates_hbm, gates_ref, sem.at[PARTS + 2]),
+    ]
+    for copy in small + copies:
         copy.start()
     top_count, tok_local = ids_ref.shape
     rows = tok_local * top_count
     experts = far_count * near_count
     slots = experts * capacity
-    near = near_ref[0]
+    near, own_far = scalars_ref[0], scalars_ref[1]
+    for copy in small:
+        copy.wait()
     own_ids = ids_ref[...].astype(jnp.float32)
     same = jnp.where(iota((top_count, ID_COLS), 0) == iota((top_count, ID_COLS), 1), 1.0, 0.0).astype(jnp.bfloat16)
     id_cols = lax.dot_general(
@@ -60,7 +66,7 @@
     counts = exact_dot(jnp.where(named, 1.0, 0.0).astype(jnp.bfloat16), before)
     ranks = jnp.sum(jnp.where(named, counts, 0.0), axis=0, keepdims=True).astype(jnp.int32)
     steps = (ids % near_count - near + near_count) % near_count
-    out_slots = (ids // near_count * near_count + steps) * capacity + ranks
+    out_slots = ((ids // near_count ^ own_far) * near_count + steps) * capacity + ranks
     back_slots = ids * capacity + ranks
     back_ref[...] = jnp.where(iota((slots, rows), 0) == back_slots, 1.0, 0.0).astype(jnp.bfloat16)
     place = iota((slots, rows), 0) == out_slots
@@ -68,17 +74,32 @@
     place = jnp.where(place, 1.0, 0.0).astype(jnp.bfloat16)
     for copy in copies:
         copy.wait()
-    send_ref[...] = (exact_dot(place, hidden_ref[...]) * gate).astype(jnp.bfloat16)
-
-
-def close_kernel(back_ref, came_ref, gates_ref, hidden_hbm, hid_ref, gates_out_ref, hidden_ref, sem):
-    copy = pltpu.make_async_copy(hidden_hbm, hidden_ref, sem)
+    send = (exact_dot(place, hidden_ref[...]) * gate).astype(jnp.bfloat16)
+    for i, ref in enumerate(sends):
+        ref[...] = send[i * ref.shape[0] : (i + 1) * ref.shape[0]]
+
+
+def regroup_kernel(far_count, near_count, capacity, *refs):
+    ins, outs = refs[:far_count], refs[far_count:]
+    rows = jnp.concatenate([ref[...] for ref in ins], axis=0)
+    for step, ref in enumerate(outs):
+        shape = (ref.shape[0], rows.shape[0])
+        row, col = iota(shape, 0), iota(shape, 1)
+        source = (row // capacity * near_count + step) * capacity + row % capacity
+        ref[...] = exact_dot(jnp.where(col == source, 1.0, 0.0).astype(jnp.bfloat16), rows).astype(jnp.bfloat16)
+
+
+def close_kernel(back_ref, came_ref, gates_hbm, hidden_hbm, hid_ref, gates_out_ref, gates_ref, hidden_ref, sem):
+    copy = pltpu.make_async_copy(hidden_hbm, hidden_ref, sem.at[0])
+    small = pltpu.make_async_copy(gates_hbm, gates_ref, sem.at[1])
+    small.start()
     copy.start()
     top_count, tok_local = gates_ref.shape
     rows = tok_local * top_count
     back = lax.dot_general(
         back_ref[...], came_ref[...], (((0,), (0,)), ((), ())), preferred_element_type=jnp.float32
     )
+    small.wait()
     mine = iota((tok_local, top_count, tok_local), 0) == iota((tok_local, top_count, tok_local), 2)
     gate = jnp.where(mine, gates_ref[...][None], 0.0).reshape(rows, tok_local)
     gate = jnp.sum(gate, axis=1, keepdims=True)
@@ -145,14 +166,14 @@
     rows, hids, (out_ref, turned_ref) = refs[: 2 * PARTS], refs[2 * PARTS : -2], refs[-2:]
     step = pl.program_id(0)
     share, tile = out_ref.shape
-    near, replica = scalars_ref[0], scalars_ref[1]
+    near, far, replica = scalars_ref[0], scalars_ref[1], scalars_ref[2]
 
     @pl.when(step == 0)
     def _():
         slots, lines = rows[0].shape[0], hids[0].shape[0]
         hidden_width = hids[0].shape[1] // near_count
         row, col = iota((slots, lines), 0), iota((slots, lines), 1)
-        match = (row // (near_count * capacity) == col // capacity) & (row % capacity == col % capacity)
+        match = (row // (near_count * capacity) ^ far == col // capacity) & (row % capacity == col % capacity)
         block = (near - row // capacity % near_count + near_count) % near_count
         for i, ref in enumerate(hids):
             total = jnp.zeros((slots, share), jnp.float32)
@@ -180,23 +201,42 @@
     return pltpu.CompilerParams(vmem_limit_bytes=mib * MIB)
 
 
-def prepare(far_count, near_count, capacity, near, ids, gates, hidden, tokens):
+def hbm_spec():
+    return pl.BlockSpec(memory_space=pltpu.HBM)
+
+
+def prepare(far_count, near_count, capacity, scalars, ids, gates, hidden, tokens):
     slots = far_count * near_count * capacity
     rows, wide = hidden.shape
     tok_local, width = tokens.shape
     part = width // PARTS
-    vmem, hbm = pl.BlockSpec(memory_space=pltpu.VMEM), pl.BlockSpec(memory_space=pl.ANY)
-    shapes = [(tok_local, part + (ID_COLS if i == 0 else 0)) for i in range(PARTS)] + [(slots, wide), (slots, rows)]
+    vmem = pl.BlockSpec(memory_space=pltpu.VMEM)
+    shapes = [(tok_local, part + (ID_COLS if i == 0 else 0)) for i in range(PARTS)]
+    shapes += [(slots // far_count, wide)] * far_count + [(slots, rows)]
     return pl.pallas_call(
         functools.partial(prepare_kernel, far_count, near_count, capacity),
         out_shape=[jax.ShapeDtypeStruct(shape, jnp.bfloat16) for shape in shapes],
-        in_specs=[scalar_spec(), vmem, vmem, hbm, hbm],
+        in_specs=[scalar_spec()] + [hbm_spec()] * 4,
         out_specs=[vmem] * len(shapes),
-        scratch_shapes=[pltpu.VMEM(hidden.shape, jnp.bfloat16), pltpu.SemaphoreType.DMA((PARTS + 1,))],
+        scratch_shapes=[pltpu.VMEM(array.shape, array.dtype) for array in (ids, gates, hidden)]
+        + [pltpu.SemaphoreType.DMA((PARTS + 3,))],
         compiler_params=params(12),
         cost_estimate=pl.CostEstimate(flops=2 * rows * rows * wide, bytes_accessed=4 * rows * wide, transcendentals=0),
         name="prepare_rows",
-    )(near, ids, gates, hidden, tokens)
+    )(scalars, ids, gates, hidden, tokens)
+
+
+def regroup(near_count, capacity, arrays):
+    lines = len(arrays) * capacity
+    vmem = pl.BlockSpec(memory_space=pltpu.VMEM)
+    return pl.pallas_call(
+        functools.partial(regroup_kernel, len(arrays), near_count, capacity),
+        out_shape=[jax.ShapeDtypeStruct((lines, arrays[0].shape[1]), jnp.bfloat16)] * near_count,
+        in_specs=[vmem] * len(arrays),
+        out_specs=[vmem] * near_count,
+        compiler_params=params(8),
+        name="regroup_rows",
+    )(*arrays)
 
 
 def close(back_place, came_back, gates, hidden):
@@ -207,9 +247,13 @@
             jax.ShapeDtypeStruct(hidden.shape, jnp.bfloat16),
             jax.ShapeDtypeStruct(gates.shape, jnp.float32),
         ],
-        in_specs=[vmem, vmem, vmem, pl.BlockSpec(memory_space=pl.ANY)],
+        in_specs=[vmem, vmem, hbm_spec(), hbm_spec()],
         out_specs=[vmem] * 2,
-        scratch_shapes=[pltpu.VMEM(hidden.shape, jnp.bfloat16), pltpu.SemaphoreType.DMA],
+        scratch_shapes=[
+            pltpu.VMEM(gates.shape, gates.dtype),
+            pltpu.VMEM(hidden.shape, hidden.dtype),
+            pltpu.SemaphoreType.DMA((2,)),
+        ],
         compiler_params=params(12),
         name="close_rows",
     )(back_place, came_back, gates, hidden)
@@ -296,6 +340,9 @@
     def along(array, steps):
         return lax.ppermute(array, "near", [(i, (i + steps) % near_count) for i in range(near_count)])
 
+    def across(array, apart):
+        return lax.ppermute(array, "far", [(i, i ^ apart) for i in range(far_count)])
+
     def swap(array):
         return lax.ppermute(array, "dp", [(i, i ^ 1) for i in range(lax.axis_size("dp"))])
 
@@ -303,19 +350,17 @@
         return [array] + [along(array, step) for step in range(1, near_count)]
 
     hidden_rows = hidden.reshape(row_total, hidden_width)
-    *parts, send, back_place = prepare(
-        far_count, near_count, capacity, near_ref, expert_ids.T, gates.T, hidden_rows, grad_out
-    )
+    scalars = jnp.stack([near, lax.axis_index("far"), lax.axis_index("dp")]).astype(jnp.int32)
+    prepared = prepare(far_count, near_count, capacity, scalars, expert_ids.T, gates.T, hidden_rows, grad_out)
+    prepared = list(prepared)
+    parts, sends, back_place = prepared[:PARTS], prepared[PARTS:-1], prepared[-1]
     blocks = line(parts[0])
-    crossed = lax.all_to_all(
-        send.reshape(far_count, -1, hidden_width), "far", split_axis=0, concat_axis=0, tiled=True
-    ).reshape(far_count, near_count, capacity, hidden_width)
 
     rows, total = [], None
     for i in range(PARTS):
         if i == 0:
             picked, pick = first_pick(far_count, near_count, capacity, near_ref, blocks)
-            picked, crossed, parts[1] = lax.optimization_barrier((picked, crossed, parts[1]))
+            picked, sends, parts = lax.optimization_barrier((picked, sends, parts))
         else:
             picked = pick_rows(pick, line(parts[i]))
             picked, rows[-1] = lax.optimization_barrier((picked, rows[-1]))
@@ -323,8 +368,9 @@
             picked.reshape(far_count, -1, part), "far", split_axis=0, concat_axis=0, tiled=True
         ).reshape(slot_total, part)
         rows.append(got)
+    crossed = [sends[0]] + [across(sends[apart], apart) for apart in range(1, far_count)]
     rows[0], crossed = lax.optimization_barrier((rows[0], crossed))
-    hids = [crossed[:, step].reshape(-1, hidden_width) for step in range(near_count)]
+    hids = list(regroup(near_count, capacity, crossed))
     hids = join_rows(hids[:1] + [along(hids[step], step) for step in range(1, near_count)])
     for i in range(PARTS):
         if i:
@@ -344,7 +390,6 @@
         tiled=True,
     )
 
-    scalars = jnp.stack([near, lax.axis_index("dp")]).astype(jnp.int32)
     grad_down = down_rows(
         near_count,
         capacity,

time: 87.7 us -> 100 us (1.14)
  waiting for transfers between devices: 29.8 us -> 38.8 us
  starting transfers between devices: 32 us -> 35.1 us
    ppermute x0 -> x3, waiting for transfers between devices: none -> 12.3 us  [across(): lax.ppermute(array, 'far', [(i, i ^ apart) for i in range(far_count)])]
    ppermute x9, starting transfers between devices: 12.5 us -> 18.2 us  [along(): lax.ppermute(array, 'near', [(i, (i + steps) % near_count) for i in range...]
    all_to_all x1 -> x0, starting transfers between devices: 5.18 us -> none  [local(): lax.all_to_all(send.reshape(far_count, -1, hidden_width), 'far', split_ax...]
    ppermute x0 -> x3, starting transfers between devices: none -> 3.52 us  [across(): lax.ppermute(array, 'far', [(i, i ^ apart) for i in range(far_count)])]
    all_to_all x2, waiting for transfers between devices: 1.84 us -> 0.01 us  [local(): lax.all_to_all(picked.reshape(far_count, -1, part), 'far', split_axis=0,...]
    ppermute x9, waiting for transfers between devices: 21.6 us -> 20 us  [along(): lax.ppermute(array, 'near', [(i, (i + steps) % near_count) for i in range...]
    all_to_all x1, starting transfers between devices: 6.13 us -> 5.02 us  [local(): lax.all_to_all(total.astype(jnp.bfloat16).reshape(experts, capacity, hidd...]
  transfers between devices with their start and end apart: 16 -> 18, of which waited for: 8 -> 8; matrix products, arithmetic and copies ran while one was open for 9% -> 8% of each run, Pallas kernels for 12% -> 9%
where the time goes in v11:
time: 100 us; the launch traced here: 99.4 us
  waiting for transfers between devices  38.8 us (39%)
  starting transfers between devices  35.1 us (35%)
  Pallas kernels  13.8 us (14%)
  matrix products  6.71 us (7%)
  local copies, waits for them, and re-layouts  3.34 us (3%)
    ppermute x9, waiting for transfers between devices, along(): lax.ppermute(array, 'near', [(i, (i + steps) % near_count) for i in range...  20 us
    ppermute x9, starting transfers between devices, along(): lax.ppermute(array, 'near', [(i, (i + steps) % near_count) for i in range...  18.2 us
    ppermute x3, waiting for transfers between devices, across(): lax.ppermute(array, 'far', [(i, i ^ apart) for i in range(far_count)])  12.3 us
    all_to_all x2, starting transfers between devices, local(): lax.all_to_all(picked.reshape(far_count, -1, part), 'far', split_axis=0,...  7.54 us
    pallas_call x1, Pallas kernels, down_rows(): pl.pallas_call(functools.partial(down_kernel, near_count, capacity), grid...  7.22 us
    dot_general x2, matrix products, local(): lax.dot_general(rows[i], weight[:, i * part:(i + 1) * part], (((1,), (1,)...  6.71 us
    all_to_all x1, starting transfers between devices, local(): lax.all_to_all(total.astype(jnp.bfloat16).reshape(experts, capacity, hidd...  5.02 us
    all_to_all x1, waiting for transfers between devices, local(): lax.all_to_all(total.astype(jnp.bfloat16).reshape(experts, capacity, hidd...  4.98 us
  transfers between devices with their start and end apart: 18, of which 8 were waited for; matrix products, arithmetic and copies ran while one was open for 8% of the time, Pallas kernels for 9%

profile of v11, /device:TPU:0, one launch (start us, length us, event | category | flops | bytes accessed | tf_op | source)
XLA Modules:
  0.0 99.4 jit_solution(789505024256061745)
XLA Ops:
  0.6 0.1 pad_add_fusion.scalars_ref
  0.7 1.0 %copy-done = bf16[32,8,768]{2,1,0:T(8,128)(2,1)S(1)} copy-done((bf16[32,8,768]{2,1,0:T(8,128)(2,1)S(1)}, bf16[32,8,768]{2,1,0:T(8,128)(2,1)}, u32[]{:S(2)}) %copy-start) | copy-done | bytes 393240
  1.7 0.9 copy-done.2
  2.7 0.7 copy-done.3
  3.4 0.7 copy-done.5
  4.0 1.6 %prepare_rows.1 = (bf16[32,2176]{1,0:T(8,128)(2,1)S(1)}, bf16[32,2048]{1,0:T(8,128)(2,1)S(1)}, bf16[64,768]{1,0:T(8,128)(2,1)S(1)}, bf16[64,768]{1,0:T(8,128)(2,...) custom-call(s32[3]{0:T(128)S(1)} %pad_add_fusion.scalars_ref, ...), custom_call_target="tpu_custom_call" | custom-call | flops 100663296 | bytes 786432 | tf_op jit(solution)/shard_map/prepare_rows/pallas_call | solution.py:216
  5.6 5.1 %collective-permute-start.2 = (bf16[32,2176]{1,0:T(8,128)(2,1)S(1)}, bf16[32,2176]{1,0:T(8,128)(2,1)S(1)}, u32[]{:S(2)}, u32[]{:S(2)}) collective-permute-start(bf16[32,2176]{1,0:T(8,128)(2,1)S(1)} %get-tuple-element.37.refs_0_), channel_id=1, source_target_pairs={{0,3},{1,0},{2,1},{3,2},{4,7},{5,4},{6,5},{7,6},{8,11},{9,8},{10,9... | collective-permute-start | bytes 417800 | tf_op jit(solution)/shard_map/ppermute | solution.py:341
  10.7 0.0 collective-permute-start.1
  10.7 1.0 %collective-permute-start = (bf16[32,2176]{1,0:T(8,128)(2,1)S(1)}, bf16[32,2176]{1,0:T(8,128)(2,1)S(1)}, u32[]{:S(2)}, u32[]{:S(2)}) collective-permute-start(bf16[32,2176]{1,0:T(8,128)(2,1)S(1)} %get-tuple-element.37.refs_0_), channel_id=1, source_target_pairs={{0,1},{1,2},{2,3},{3,0},{4,5},{5,6},{6,7},{7,4},{8,9},{9,10},{10,1... | collective-permute-start | bytes 417800 | tf_op jit(solution)/shard_map/ppermute | solution.py:341
  11.8 3.1 %collective-permute-done.2.refs_3_ = bf16[32,2176]{1,0:T(8,128)(2,1)S(1)} collective-permute-done((bf16[32,2176]{1,0:T(8,128)(2,1)S(1)}, bf16[32,2176]{1,0:T(8,128)(2,1)S(1)}, u32[]{:S(2)}, u32[]{:S(2)}) %collective-permute-start.2) | collective-permute-done | bytes 139296 | tf_op jit(solution)/shard_map/ppermute | solution.py:341
  14.8 7.7 %collective-permute-done.1.refs_2_ = bf16[32,2176]{1,0:T(8,128)(2,1)S(1)} collective-permute-done((bf16[32,2176]{1,0:T(8,128)(2,1)S(1)}, bf16[32,2176]{1,0:T(8,128)(2,1)S(1)}, u32[]{:S(2)}, u32[]{:S(2)}) %collective-permute-start.1) | collective-permute-done | bytes 139296 | tf_op jit(solution)/shard_map/ppermute | solution.py:341
  22.6 0.0 collective-permute-done.refs_1_
  22.6 1.8 %first_pick.1 = (bf16[256,2048]{1,0:T(8,128)(2,1)}, bf16[256,128]{1,0:T(8,128)(2,1)S(1)}) custom-call(s32[1]{0:T(128)} %bitcast.near_ref, bf16[32,2176]{1,0:T(8,128)(2,1)S(1)} %get-tuple-element.37.refs_0_, bf16[32,2176]{1,0:T(8,128)(2,1)S(1)} %collective-permute-done.refs_1_, bf16[32,2176]{1,0:T(8,128)(2,1)S(1)} %collective-permute-done.1.refs_2_, ...), custom_call_target="tpu_custom_call" | custom-call | tf_op jit(solution)/shard_map/first_pick/pallas_call | solution.py:266
  24.4 3.7 %all-to-all-start = ((bf16[4,64,2048]{2,1,0:T(8,128)(2,1)}), bf16[4,64,2048]{2,1,0:T(8,128)(2,1)S(1)}, u32[]{:S(2)}, u32[]{:S(2)}) async-start(bf16[4,64,2048]{2,1,0:T(8,128)(2,1)} %bitcast.6), calls=%async_computation | async-start | bytes 2097152 | tf_op jit(solution)/shard_map/all_to_all | solution.py:367
  28.1 1.5 %collective-permute-start.5 = (bf16[32,2048]{1,0:T(8,128)(2,1)S(1)}, bf16[32,2048]{1,0:T(8,128)(2,1)S(1)}, u32[]{:S(2)}, u32[]{:S(2)}) collective-permute-start(bf16[32,2048]{1,0:T(8,128)(2,1)S(1)} %get-tuple-element.45.refs_0_), channel_id=1, source_target_pairs={{0,3},{1,0},{2,1},{3,2},{4,7},{5,4},{6,5},{7,6},{8,11},{9,8},{10,9... | collective-permute-start | bytes 393224 | tf_op jit(solution)/shard_map/ppermute | solution.py:341
  29.6 1.2 %collective-permute-start.4 = (bf16[32,2048]{1,0:T(8,128)(2,1)S(1)}, bf16[32,2048]{1,0:T(8,128)(2,1)S(1)}, u32[]{:S(2)}, u32[]{:S(2)}) collective-permute-start(bf16[32,2048]{1,0:T(8,128)(2,1)S(1)} %get-tuple-element.45.refs_0_), channel_id=1, source_target_pairs={{0,2},{1,3},{2,0},{3,1},{4,6},{5,7},{6,4},{7,5},{8,10},{9,11},{10,... | collective-permute-start | bytes 393224 | tf_op jit(solution)/shard_map/ppermute | solution.py:341
  30.8 2.0 %collective-permute-start.3 = (bf16[32,2048]{1,0:T(8,128)(2,1)S(1)}, bf16[32,2048]{1,0:T(8,128)(2,1)S(1)}, u32[]{:S(2)}, u32[]{:S(2)}) collective-permute-start(bf16[32,2048]{1,0:T(8,128)(2,1)S(1)} %get-tuple-element.45.refs_0_), channel_id=1, source_target_pairs={{0,1},{1,2},{2,3},{3,0},{4,5},{5,6},{6,7},{7,4},{8,9},{9,10},{10,1... | collective-permute-start | bytes 393224 | tf_op jit(solution)/shard_map/ppermute | solution.py:341
  32.8 1.0 collective-permute-done.5.refs_3_
  33.8 8.2 %collective-permute-done.4.refs_2_ = bf16[32,2048]{1,0:T(8,128)(2,1)S(1)} collective-permute-done((bf16[32,2048]{1,0:T(8,128)(2,1)S(1)}, bf16[32,2048]{1,0:T(8,128)(2,1)S(1)}, u32[]{:S(2)}, u32[]{:S(2)}) %collective-permute-start.4) | collective-permute-done | bytes 131104 | tf_op jit(solution)/shard_map/ppermute | solution.py:341
  42.0 1.4 %pick_rows.1 = bf16[256,2048]{1,0:T(8,128)(2,1)} custom-call(bf16[256,128]{1,0:T(8,128)(2,1)S(1)} %get-tuple-element.38.pick_ref, bf16[32,2048]{1,0:T(8,128)(2,1)S(1)} %get-tuple-element.45.refs_0_, bf16[32,2048]{1,0:T(8,128)(2,1)S(1)} %collective-permute-done.3.refs_1_, bf16[32,2048]{1,0:T(8,128)(2,1)S(1)} %collective-permute-done.4.refs_2_, ...), custom_call_target="tpu_custom_call" | custom-call | tf_op jit(solution)/shard_map/pick_rows/pallas_call | solution.py:281
  43.4 0.0 all-to-all-done
  43.4 3.8 %all-to-all-start.1 = ((bf16[4,64,2048]{2,1,0:T(8,128)(2,1)}), bf16[4,64,2048]{2,1,0:T(8,128)(2,1)S(1)}, u32[]{:S(2)}, u32[]{:S(2)}) async-start(bf16[4,64,2048]{2,1,0:T(8,128)(2,1)} %bitcast.8), calls=%async_computation.1 | async-start | bytes 2097152 | tf_op jit(solution)/shard_map/all_to_all | solution.py:367
  47.2 2.0 %collective-permute-start.6 = (bf16[64,768]{1,0:T(8,128)(2,1)S(1)}, bf16[64,768]{1,0:T(8,128)(2,1)S(1)}, u32[]{:S(2)}, u32[]{:S(2)}) collective-permute-start(bf16[64,768]{1,0:T(8,128)(2,1)S(1)} %get-tuple-element.50), channel_id=1, source_target_pairs={{0,4},{4,0},{8,12},{12,8},{1,5},{5,1},{9,13},{13,9},{2,6},{6,2},{1... | collective-permute-start | bytes 294920 | tf_op jit(solution)/shard_map/ppermute | solution.py:344
  49.2 1.5 %collective-permute-start.7 = (bf16[64,768]{1,0:T(8,128)(2,1)S(1)}, bf16[64,768]{1,0:T(8,128)(2,1)S(1)}, u32[]{:S(2)}, u32[]{:S(2)}) collective-permute-start(bf16[64,768]{1,0:T(8,128)(2,1)S(1)} %get-tuple-element.51), channel_id=1, source_target_pairs={{0,8},{4,12},{8,0},{12,4},{1,9},{5,13},{9,1},{13,5},{2,10},{6,14},... | collective-permute-start | bytes 294920 | tf_op jit(solution)/shard_map/ppermute | solution.py:344
  50.7 0.0 collective-permute-start.8
  50.7 10.3 %collective-permute-done.6.refs_1_ = bf16[64,768]{1,0:T(8,128)(2,1)S(1)} collective-permute-done((bf16[64,768]{1,0:T(8,128)(2,1)S(1)}, bf16[64,768]{1,0:T(8,128)(2,1)S(1)}, u32[]{:S(2)}, u32[]{:S(2)}) %collective-permute-start.6) | collective-permute-done | bytes 98336 | tf_op jit(solution)/shard_map/ppermute | solution.py:344
  61.1 2.0 %collective-permute-done.8.refs_3_ = bf16[64,768]{1,0:T(8,128)(2,1)S(1)} collective-permute-done((bf16[64,768]{1,0:T(8,128)(2,1)S(1)}, bf16[64,768]{1,0:T(8,128)(2,1)S(1)}, u32[]{:S(2)}, u32[]{:S(2)}) %collective-permute-start.8) | collective-permute-done | bytes 98336 | tf_op jit(solution)/shard_map/ppermute | solution.py:344
  63.0 0.4 regroup_rows.1
  63.4 2.5 %collective-permute-start.9 = (bf16[64,768]{1,0:T(8,128)(2,1)S(1)}, bf16[64,768]{1,0:T(8,128)(2,1)S(1)}, u32[]{:S(2)}, u32[]{:S(2)}) collective-permute-start(bf16[64,768]{1,0:T(8,128)(2,1)S(1)} %get-tuple-element.59), channel_id=1, source_target_pairs={{0,1},{1,2},{2,3},{3,0},{4,5},{5,6},{6,7},{7,4},{8,9},{9,10},{10,1... | collective-permute-start | bytes 294920 | tf_op jit(solution)/shard_map/ppermute | solution.py:341
  65.9 2.0 %collective-permute-start.10 = (bf16[64,768]{1,0:T(8,128)(2,1)S(1)}, bf16[64,768]{1,0:T(8,128)(2,1)S(1)}, u32[]{:S(2)}, u32[]{:S(2)}) collective-permute-start(bf16[64,768]{1,0:T(8,128)(2,1)S(1)} %get-tuple-element.60), channel_id=1, source_target_pairs={{0,2},{1,3},{2,0},{3,1},{4,6},{5,7},{6,4},{7,5},{8,10},{9,11},{10,... | collective-permute-start | bytes 294920 | tf_op jit(solution)/shard_map/ppermute | solution.py:341
  67.9 2.8 %collective-permute-start.11 = (bf16[64,768]{1,0:T(8,128)(2,1)S(1)}, bf16[64,768]{1,0:T(8,128)(2,1)S(1)}, u32[]{:S(2)}, u32[]{:S(2)}) collective-permute-start(bf16[64,768]{1,0:T(8,128)(2,1)S(1)} %get-tuple-element.61), channel_id=1, source_target_pairs={{0,3},{1,0},{2,1},{3,2},{4,7},{5,4},{6,5},{7,6},{8,11},{9,8},{10,9... | collective-permute-start | bytes 294920 | tf_op jit(solution)/shard_map/ppermute | solution.py:341
  70.8 3.8 %fusion.2 = f32[256,768]{1,0:T(8,128)} fusion(bf16[256,2048]{1,0:T(8,128)(2,1)S(1)} %bitcast.19, bf16[768,4096]{1,0:T(8,128)(2,1)} %bitcast.32), kind=kOutput, calls=%fused_computation.2 | convolution fusion | flops 805306368 | bytes 4980736 | tf_op jit(solution)/shard_map/dot_general | solution.py:378
  74.6 0.0 collective-permute-done.9.refs_1_
  74.6 0.0 collective-permute-done.10.refs_2_
  74.6 0.0 collective-permute-done.11.refs_3_
  74.6 0.0 all-to-all-done.1
  74.6 0.0 copy-start.6
  74.7 0.6 collective-permute-start.13
  75.2 2.9 %fusion = f32[256,768]{1,0:T(8,128)S(1)} fusion(bf16[256,2048]{1,0:T(8,128)(2,1)S(1)} %bitcast.22, bf16[768,4096]{1,0:T(8,128)(2,1)} %bitcast.33), kind=kOutput, calls=%fused_computation | convolution fusion | flops 805306368 | bytes 4980736 | tf_op jit(solution)/shard_map/dot_general | solution.py:378
  78.1 0.0 copy-start.1
  78.2 0.0 copy-start.4
  78.2 0.8 add_convert_fusion
  79.0 5.0 %all-to-all-start.2 = ((bf16[16,16,768]{2,1,0:T(8,128)(2,1)}), bf16[16,16,768]{2,1,0:T(8,128)(2,1)S(1)}, u32[]{:S(2)}, u32[]{:S(2)}) async-start(bf16[16,16,768]{2,1,0:T(8,128)(2,1)} %bitcast.31), calls=%async_computation.2 | async-start | bytes 786432 | tf_op jit(solution)/shard_map/all_to_all | solution.py:385
  84.0 0.2 collective-permute-start.14
  84.3 1.6 %collective-permute-done.14.refs_5_ = bf16[64,3072]{1,0:T(8,128)(2,1)S(1)} collective-permute-done((bf16[64,3072]{1,0:T(8,128)(2,1)S(1)}, bf16[64,3072]{1,0:T(8,128)(2,1)S(1)}, u32[]{:S(2)}, u32[]{:S(2)}) %collective-permute-start.14) | collective-permute-done | bytes 393248 | tf_op jit(solution)/shard_map/ppermute | solution.py:347
  85.8 7.2 %down_rows.1 = bf16[384,4096]{1,0:T(8,128)(2,1)} custom-call(s32[3]{0:T(128)S(1)} %pad_add_fusion.scalars_ref, bf16[256,2048]{1,0:T(8,128)(2,1)S(1)} %bitcast.20, bf16[256,2048]{1,0:T(8,128)(2,1)S(1)} %bitcast.23, bf16[256,2048]{1,0:T(8,128)(2,1)} %collective-permute-done.12.refs_2_, bf16[256,2048]{1,0:T(8,128)(2,1)} %collective-permute-done.13.refs_3_, ...), custom_call_target="tpu_custom_call" | custom-call | flops 1610612736 | bytes 7340032 | tf_op jit(solution)/shard_map/down_rows/pallas_call | solution.py:310
  93.0 5.0 %all-to-all-done.2 = bf16[16,16,768]{2,1,0:T(8,128)(2,1)S(1)} async-done(((bf16[16,16,768]{2,1,0:T(8,128)(2,1)}), bf16[16,16,768]{2,1,0:T(8,128)(2,1)S(1)}, u32[]{:S(2)}, u32[]{:S(2)}) %all-to-all-start.2) | async-done | bytes 393248 | tf_op jit(solution)/shard_map/all_to_all | solution.py:385
  98.0 1.4 %close_rows.1 = (bf16[256,768]{1,0:T(8,128)(2,1)}, f32[8,32]{1,0:T(8,128)}) custom-call(bf16[256,256]{1,0:T(8,128)(2,1)S(1)} %get-tuple-element.36.back_ref, bf16[256,768]{1,0:T(8,128)(2,1)S(1)} %bitcast.26, f32[8,32]{1,0:T(8,128)S(1)} %bitcast.28, bf16[256,768]{1,0:T(8,128)(2,1)S(1)} %bitcast.25), custom_call_target="tpu_custom_call" | custom-call | tf_op jit(solution)/shard_map/close_rows/pallas_call | solution.py:244
  (13 shorter events, 0.1 us)
Async XLA Ops:
  0.7 1.0 %copy-start = (bf16[32,8,768]{2,1,0:T(8,128)(2,1)S(1)}, bf16[32,8,768]{2,1,0:T(8,128)(2,1)}, u32[]{:S(2)}) copy-start(bf16[32,8,768]{2,1,0:T(8,128)(2,1)} %param.6) | copy-start | bytes 1179652
  1.7 0.9 copy-start.2
  2.7 0.7 copy-start.3
  3.3 0.7 copy-start.5
  5.6 9.2 %collective-permute-start.2 = (bf16[32,2176]{1,0:T(8,128)(2,1)S(1)}, bf16[32,2176]{1,0:T(8,128)(2,1)S(1)}, u32[]{:S(2)}, u32[]{:S(2)}) collective-permute-start(bf16[32,2176]{1,0:T(8,128)(2,1)S(1)} %get-tuple-element.37.refs_0_), channel_id=1, source_target_pairs={{0,3},{1,0},{2,1},{3,2},{4,7},{5,4},{6,5},{7,6},{8,11},{9,8},{10,9... | collective-permute-start | bytes 417800 | tf_op jit(solution)/shard_map/ppermute | solution.py:341
  10.7 11.8 %collective-permute-start.1 = (bf16[32,2176]{1,0:T(8,128)(2,1)S(1)}, bf16[32,2176]{1,0:T(8,128)(2,1)S(1)}, u32[]{:S(2)}, u32[]{:S(2)}) collective-permute-start(bf16[32,2176]{1,0:T(8,128)(2,1)S(1)} %get-tuple-element.37.refs_0_), channel_id=1, source_target_pairs={{0,2},{1,3},{2,0},{3,1},{4,6},{5,7},{6,4},{7,5},{8,10},{9,11},{10,... | collective-permute-start | bytes 417800 | tf_op jit(solution)/shard_map/ppermute | solution.py:341
  10.7 11.8 %collective-permute-start = (bf16[32,2176]{1,0:T(8,128)(2,1)S(1)}, bf16[32,2176]{1,0:T(8,128)(2,1)S(1)}, u32[]{:S(2)}, u32[]{:S(2)}) collective-permute-start(bf16[32,2176]{1,0:T(8,128)(2,1)S(1)} %get-tuple-element.37.refs_0_), channel_id=1, source_target_pairs={{0,1},{1,2},{2,3},{3,0},{4,5},{5,6},{6,7},{7,4},{8,9},{9,10},{10,1... | collective-permute-start | bytes 417800 | tf_op jit(solution)/shard_map/ppermute | solution.py:341
  24.4 19.0 %all-to-all-start = ((bf16[4,64,2048]{2,1,0:T(8,128)(2,1)}), bf16[4,64,2048]{2,1,0:T(8,128)(2,1)S(1)}, u32[]{:S(2)}, u32[]{:S(2)}) async-start(bf16[4,64,2048]{2,1,0:T(8,128)(2,1)} %bitcast.6), calls=%async_computation | async-start | bytes 2097152 | tf_op jit(solution)/shard_map/all_to_all | solution.py:367
  28.1 5.7 %collective-permute-start.5 = (bf16[32,2048]{1,0:T(8,128)(2,1)S(1)}, bf16[32,2048]{1,0:T(8,128)(2,1)S(1)}, u32[]{:S(2)}, u32[]{:S(2)}) collective-permute-start(bf16[32,2048]{1,0:T(8,128)(2,1)S(1)} %get-tuple-element.45.refs_0_), channel_id=1, source_target_pairs={{0,3},{1,0},{2,1},{3,2},{4,7},{5,4},{6,5},{7,6},{8,11},{9,8},{10,9... | collective-permute-start | bytes 393224 | tf_op jit(solution)/shard_map/ppermute | solution.py:341
  29.6 12.4 %collective-permute-start.4 = (bf16[32,2048]{1,0:T(8,128)(2,1)S(1)}, bf16[32,2048]{1,0:T(8,128)(2,1)S(1)}, u32[]{:S(2)}, u32[]{:S(2)}) collective-permute-start(bf16[32,2048]{1,0:T(8,128)(2,1)S(1)} %get-tuple-element.45.refs_0_), channel_id=1, source_target_pairs={{0,2},{1,3},{2,0},{3,1},{4,6},{5,7},{6,4},{7,5},{8,10},{9,11},{10,... | collective-permute-start | bytes 393224 | tf_op jit(solution)/shard_map/ppermute | solution.py:341
  30.8 11.2 %collective-permute-start.3 = (bf16[32,2048]{1,0:T(8,128)(2,1)S(1)}, bf16[32,2048]{1,0:T(8,128)(2,1)S(1)}, u32[]{:S(2)}, u32[]{:S(2)}) collective-permute-start(bf16[32,2048]{1,0:T(8,128)(2,1)S(1)} %get-tuple-element.45.refs_0_), channel_id=1, source_target_pairs={{0,1},{1,2},{2,3},{3,0},{4,5},{5,6},{6,7},{7,4},{8,9},{9,10},{10,1... | collective-permute-start | bytes 393224 | tf_op jit(solution)/shard_map/ppermute | solution.py:341
  43.4 31.2 %all-to-all-start.1 = ((bf16[4,64,2048]{2,1,0:T(8,128)(2,1)}), bf16[4,64,2048]{2,1,0:T(8,128)(2,1)S(1)}, u32[]{:S(2)}, u32[]{:S(2)}) async-start(bf16[4,64,2048]{2,1,0:T(8,128)(2,1)} %bitcast.8), calls=%async_computation.1 | async-start | bytes 2097152 | tf_op jit(solution)/shard_map/all_to_all | solution.py:367
  47.2 13.8 %collective-permute-start.6 = (bf16[64,768]{1,0:T(8,128)(2,1)S(1)}, bf16[64,768]{1,0:T(8,128)(2,1)S(1)}, u32[]{:S(2)}, u32[]{:S(2)}) collective-permute-start(bf16[64,768]{1,0:T(8,128)(2,1)S(1)} %get-tuple-element.50), channel_id=1, source_target_pairs={{0,4},{4,0},{8,12},{12,8},{1,5},{5,1},{9,13},{13,9},{2,6},{6,2},{1... | collective-permute-start | bytes 294920 | tf_op jit(solution)/shard_map/ppermute | solution.py:344
  49.2 11.8 %collective-permute-start.7 = (bf16[64,768]{1,0:T(8,128)(2,1)S(1)}, bf16[64,768]{1,0:T(8,128)(2,1)S(1)}, u32[]{:S(2)}, u32[]{:S(2)}) collective-permute-start(bf16[64,768]{1,0:T(8,128)(2,1)S(1)} %get-tuple-element.51), channel_id=1, source_target_pairs={{0,8},{4,12},{8,0},{12,4},{1,9},{5,13},{9,1},{13,5},{2,10},{6,14},... | collective-permute-start | bytes 294920 | tf_op jit(solution)/shard_map/ppermute | solution.py:344
  50.7 12.3 %collective-permute-start.8 = (bf16[64,768]{1,0:T(8,128)(2,1)S(1)}, bf16[64,768]{1,0:T(8,128)(2,1)S(1)}, u32[]{:S(2)}, u32[]{:S(2)}) collective-permute-start(bf16[64,768]{1,0:T(8,128)(2,1)S(1)} %get-tuple-element.52), channel_id=1, source_target_pairs={{0,12},{4,8},{8,4},{12,0},{1,13},{5,9},{9,5},{13,1},{2,14},{6,10},... | collective-permute-start | bytes 294920 | tf_op jit(solution)/shard_map/ppermute | solution.py:344
  63.4 11.2 %collective-permute-start.9 = (bf16[64,768]{1,0:T(8,128)(2,1)S(1)}, bf16[64,768]{1,0:T(8,128)(2,1)S(1)}, u32[]{:S(2)}, u32[]{:S(2)}) collective-permute-start(bf16[64,768]{1,0:T(8,128)(2,1)S(1)} %get-tuple-element.59), channel_id=1, source_target_pairs={{0,1},{1,2},{2,3},{3,0},{4,5},{5,6},{6,7},{7,4},{8,9},{9,10},{10,1... | collective-permute-start | bytes 294920 | tf_op jit(solution)/shard_map/ppermute | solution.py:341
  65.9 8.6 %collective-permute-start.10 = (bf16[64,768]{1,0:T(8,128)(2,1)S(1)}, bf16[64,768]{1,0:T(8,128)(2,1)S(1)}, u32[]{:S(2)}, u32[]{:S(2)}) collective-permute-start(bf16[64,768]{1,0:T(8,128)(2,1)S(1)} %get-tuple-element.60), channel_id=1, source_target_pairs={{0,2},{1,3},{2,0},{3,1},{4,6},{5,7},{6,4},{7,5},{8,10},{9,11},{10,... | collective-permute-start | bytes 294920 | tf_op jit(solution)/shard_map/ppermute | solution.py:341
  67.9 6.7 %collective-permute-start.11 = (bf16[64,768]{1,0:T(8,128)(2,1)S(1)}, bf16[64,768]{1,0:T(8,128)(2,1)S(1)}, u32[]{:S(2)}, u32[]{:S(2)}) collective-permute-start(bf16[64,768]{1,0:T(8,128)(2,1)S(1)} %get-tuple-element.61), channel_id=1, source_target_pairs={{0,3},{1,0},{2,1},{3,2},{4,7},{5,4},{6,5},{7,6},{8,11},{9,8},{10,9... | collective-permute-start | bytes 294920 | tf_op jit(solution)/shard_map/ppermute | solution.py:341
  70.8 13.5 %collective-permute-start.12 = (bf16[256,2048]{1,0:T(8,128)(2,1)S(1)}, bf16[256,2048]{1,0:T(8,128)(2,1)}, u32[]{:S(2)}, u32[]{:S(2)}) collective-permute-start(bf16[256,2048]{1,0:T(8,128)(2,1)S(1)} %bitcast.18), channel_id=1, source_target_pairs={{0,16},{16,0},{1,17},{17,1},{2,18},{18,2},{3,19},{19,3},{4,20},{20... | collective-permute-start | bytes 3145736 | tf_op jit(solution)/shard_map/ppermute | solution.py:347
  74.6 3.5 %copy-start.6 = (f32[256,768]{1,0:T(8,128)S(1)}, f32[256,768]{1,0:T(8,128)}, u32[]{:S(2)}) copy-start(f32[256,768]{1,0:T(8,128)} %fusion.2) | copy-start | bytes 2359300
  74.7 11.2 %collective-permute-start.13 = (bf16[256,2048]{1,0:T(8,128)(2,1)S(1)}, bf16[256,2048]{1,0:T(8,128)(2,1)}, u32[]{:S(2)}, u32[]{:S(2)}) collective-permute-start(bf16[256,2048]{1,0:T(8,128)(2,1)S(1)} %bitcast.21), channel_id=1, source_target_pairs={{0,16},{16,0},{1,17},{17,1},{2,18},{18,2},{3,19},{19,3},{4,20},{20... | collective-permute-start | bytes 3145736 | tf_op jit(solution)/shard_map/ppermute | solution.py:347
  78.1 19.9 %copy-start.1 = (bf16[32,8,768]{2,1,0:T(8,128)(2,1)S(1)}, bf16[32,8,768]{2,1,0:T(8,128)(2,1)}, u32[]{:S(2)}) copy-start(bf16[32,8,768]{2,1,0:T(8,128)(2,1)} %param.6) | copy-start | bytes 1179652
  78.2 19.9 %copy-start.4 = (f32[32,8]{0,1:T(8,128)S(1)}, f32[32,8]{0,1:T(8,128)}, u32[]{:S(2)}) copy-start(f32[32,8]{0,1:T(8,128)} %param.7) | copy-start | bytes 3076
  79.0 19.0 %all-to-all-start.2 = ((bf16[16,16,768]{2,1,0:T(8,128)(2,1)}), bf16[16,16,768]{2,1,0:T(8,128)(2,1)S(1)}, u32[]{:S(2)}, u32[]{:S(2)}) async-start(bf16[16,16,768]{2,1,0:T(8,128)(2,1)} %bitcast.31), calls=%async_computation.2 | async-start | bytes 786432 | tf_op jit(solution)/shard_map/all_to_all | solution.py:385
  84.0 1.8 %collective-permute-start.14 = (bf16[64,3072]{1,0:T(8,128)(2,1)S(1)}, bf16[64,3072]{1,0:T(8,128)(2,1)S(1)}, u32[]{:S(2)}, u32[]{:S(2)}) collective-permute-start(bf16[64,3072]{1,0:T(8,128)(2,1)S(1)} %join_rows.1.refs_4_), channel_id=1, source_target_pairs={{0,16},{16,0},{1,17},{17,1},{2,18},{18,2},{3,19},{19,3},{4,20},{20... | collective-permute-start | bytes 1179656 | tf_op jit(solution)/shard_map/ppermute | solution.py:347

commit v12 on v11

--- a/solution.py
+++ b/solution.py
@@ -20,34 +20,32 @@
     return jnp.dot(one_hot, values, preferred_element_type=jnp.float32)
 
 
-def prepare_kernel(far_count, near_count, capacity, scalars_ref, ids_hbm, gates_hbm, hidden_hbm, tokens_hbm, *refs):
-    outs, sends, (back_ref, ids_ref, gates_ref, hidden_ref, sem) = refs[:PARTS], refs[PARTS:-5], refs[-5:]
+def split_kernel(ids_ref, tokens_hbm, *refs):
+    outs, sem = refs[:-1], refs[-1]
     part = outs[1].shape[1]
     copies = [
         pltpu.make_async_copy(tokens_hbm.at[:, i * part : (i + 1) * part], out.at[:, :part], sem.at[i])
         for i, out in enumerate(outs)
     ]
-    copies.append(pltpu.make_async_copy(hidden_hbm, hidden_ref, sem.at[PARTS]))
-    small = [
-        pltpu.make_async_copy(ids_hbm, ids_ref, sem.at[PARTS + 1]),
-        pltpu.make_async_copy(gates_hbm, gates_ref, sem.at[PARTS + 2]),
-    ]
-    for copy in small + copies:
+    for copy in copies:
         copy.start()
+    top_count, tok_local = ids_ref.shape
+    same = jnp.where(iota((top_count, ID_COLS), 0) == iota((top_count, ID_COLS), 1), 1.0, 0.0).astype(jnp.bfloat16)
+    ids = ids_ref[...].astype(jnp.float32).astype(jnp.bfloat16)
+    ids = lax.dot_general(ids, same, (((0,), (0,)), ((), ())), preferred_element_type=jnp.float32)
+    ids = jnp.where(iota((tok_local, ID_COLS), 1) < top_count, ids, -1.0)
+    outs[0][:, part:] = ids.astype(jnp.bfloat16)
+    for copy in copies:
+        copy.wait()
+
+
+def send_kernel(far_count, near_count, capacity, scalars_ref, ids_ref, gates_ref, hidden_ref, *refs):
+    sends, back_ref = refs[:-1], refs[-1]
     top_count, tok_local = ids_ref.shape
     rows = tok_local * top_count
     experts = far_count * near_count
     slots = experts * capacity
     near, own_far = scalars_ref[0], scalars_ref[1]
-    for copy in small:
-        copy.wait()
-    own_ids = ids_ref[...].astype(jnp.float32)
-    same = jnp.where(iota((top_count, ID_COLS), 0) == iota((top_count, ID_COLS), 1), 1.0, 0.0).astype(jnp.bfloat16)
-    id_cols = lax.dot_general(
-        own_ids.astype(jnp.bfloat16), same, (((0,), (0,)), ((), ())), preferred_element_type=jnp.float32
-    )
-    id_cols = jnp.where(iota((tok_local, ID_COLS), 1) < top_count, id_cols, -1.0)
-    outs[0][:, part:] = id_cols.astype(jnp.bfloat16)
     wide = jnp.where(iota((tok_local, rows), 1) // top_count == iota((tok_local, rows), 0), 1.0, 0.0).astype(jnp.bfloat16)
     mine = iota((top_count, rows), 1) % top_count == iota((top_count, rows), 0)
 
@@ -59,7 +57,7 @@
             spread = spread + exact_dot(piece, wide)
         return jnp.sum(jnp.where(mine, spread, 0.0), axis=0, keepdims=True)
 
-    ids = line(own_ids).astype(jnp.int32)
+    ids = line(ids_ref[...].astype(jnp.float32)).astype(jnp.int32)
     gates = line(gates_ref[...])
     named = iota((experts, rows), 0) == ids
     before = jnp.where(iota((rows, rows), 0) < iota((rows, rows), 1), 1.0, 0.0).astype(jnp.bfloat16)
@@ -72,8 +70,6 @@
     place = iota((slots, rows), 0) == out_slots
     gate = jnp.sum(jnp.where(place, gates, 0.0), axis=1, keepdims=True)
     place = jnp.where(place, 1.0, 0.0).astype(jnp.bfloat16)
-    for copy in copies:
-        copy.wait()
     send = (exact_dot(place, hidden_ref[...]) * gate).astype(jnp.bfloat16)
     for i, ref in enumerate(sends):
         ref[...] = send[i * ref.shape[0] : (i + 1) * ref.shape[0]]
@@ -205,25 +201,37 @@
     return pl.BlockSpec(memory_space=pltpu.HBM)
 
 
-def prepare(far_count, near_count, capacity, scalars, ids, gates, hidden, tokens):
+def split_rows(ids, tokens):
+    tok_local, width = tokens.shape
+    part = width // PARTS
+    vmem = pl.BlockSpec(memory_space=pltpu.VMEM)
+    return pl.pallas_call(
+        split_kernel,
+        out_shape=[
+            jax.ShapeDtypeStruct((tok_local, part + (ID_COLS if i == 0 else 0)), jnp.bfloat16) for i in range(PARTS)
+        ],
+        in_specs=[vmem, hbm_spec()],
+        out_specs=[vmem] * PARTS,
+        scratch_shapes=[pltpu.SemaphoreType.DMA((PARTS,))],
+        compiler_params=params(8),
+        name="split_rows",
+    )(ids, tokens)
+
+
+def send_rows(far_count, near_count, capacity, scalars, ids, gates, hidden):
     slots = far_count * near_count * capacity
     rows, wide = hidden.shape
-    tok_local, width = tokens.shape
-    part = width // PARTS
-    vmem = pl.BlockSpec(memory_space=pltpu.VMEM)
-    shapes = [(tok_local, part + (ID_COLS if i == 0 else 0)) for i in range(PARTS)]
-    shapes += [(slots // far_count, wide)] * far_count + [(slots, rows)]
-    return pl.pallas_call(
-        functools.partial(prepare_kernel, far_count, near_count, capacity),
+    vmem = pl.BlockSpec(memory_space=pltpu.VMEM)
+    shapes = [(slots // far_count, wide)] * far_count + [(slots, rows)]
+    return pl.pallas_call(
+        functools.partial(send_kernel, far_count, near_count, capacity),
         out_shape=[jax.ShapeDtypeStruct(shape, jnp.bfloat16) for shape in shapes],
-        in_specs=[scalar_spec()] + [hbm_spec()] * 4,
+        in_specs=[scalar_spec()] + [vmem] * 3,
         out_specs=[vmem] * len(shapes),
-        scratch_shapes=[pltpu.VMEM(array.shape, array.dtype) for array in (ids, gates, hidden)]
-        + [pltpu.SemaphoreType.DMA((PARTS + 3,))],
         compiler_params=params(12),
         cost_estimate=pl.CostEstimate(flops=2 * rows * rows * wide, bytes_accessed=4 * rows * wide, transcendentals=0),
-        name="prepare_rows",
-    )(scalars, ids, gates, hidden, tokens)
+        name="send_rows",
+    )(scalars, ids, gates, hidden)
 
 
 def regroup(near_count, capacity, arrays):
@@ -351,10 +359,11 @@
 
     hidden_rows = hidden.reshape(row_total, hidden_width)
     scalars = jnp.stack([near, lax.axis_index("far"), lax.axis_index("dp")]).astype(jnp.int32)
-    prepared = prepare(far_count, near_count, capacity, scalars, expert_ids.T, gates.T, hidden_rows, grad_out)
-    prepared = list(prepared)
-    parts, sends, back_place = prepared[:PARTS], prepared[PARTS:-1], prepared[-1]
+    ids = expert_ids.T
+    parts = list(split_rows(ids, grad_out))
+    parts[0], ids = lax.optimization_barrier((parts[0], ids))
     blocks = line(parts[0])
+    *sends, back_place = send_rows(far_count, near_count, capacity, scalars, ids, gates.T, hidden_rows)
 
     rows, total = [], None
     for i in range(PARTS):
@@ -363,13 +372,12 @@
             picked, sends, parts = lax.optimization_barrier((picked, sends, parts))
         else:
             picked = pick_rows(pick, line(parts[i]))
-            picked, rows[-1] = lax.optimization_barrier((picked, rows[-1]))
+            crossed = [sends[0]] + [across(sends[apart], apart) for apart in range(1, far_count)]
+            picked, rows[-1], crossed = lax.optimization_barrier((picked, rows[-1], crossed))
         got = lax.all_to_all(
             picked.reshape(far_count, -1, part), "far", split_axis=0, concat_axis=0, tiled=True
         ).reshape(slot_total, part)
         rows.append(got)
-    crossed = [sends[0]] + [across(sends[apart], apart) for apart in range(1, far_count)]
-    rows[0], crossed = lax.optimization_barrier((rows[0], crossed))
     hids = list(regroup(near_count, capacity, crossed))
     hids = join_rows(hids[:1] + [along(hids[step], step) for step in range(1, near_count)])
     for i in range(PARTS):

time: 100 us -> 83.4 us (0.83)
  waiting for transfers between devices: 38.8 us -> 24 us
  starting transfers between devices: 35.1 us -> 32.8 us
    ppermute x3, waiting for transfers between devices: 12.3 us -> 3.01 us  [across(): lax.ppermute(array, 'far', [(i, i ^ apart) for i in range(far_count)])]
    ppermute x9, waiting for transfers between devices: 20 us -> 12.3 us  [along(): lax.ppermute(array, 'near', [(i, (i + steps) % near_count) for i in range...]
    all_to_all x2, waiting for transfers between devices: 0.01 us -> 2.17 us  [local(): lax.all_to_all(picked.reshape(far_count, -1, part), 'far', split_axis=0,...]
    ppermute x9, starting transfers between devices: 18.2 us -> 16.5 us  [along(): lax.ppermute(array, 'near', [(i, (i + steps) % near_count) for i in range...]
    unnamed x14 -> x16, local copies, waits for them, and re-layouts: 3.34 us -> 4.02 us
  transfers between devices with their start and end apart: 18 -> 18, of which waited for: 8 -> 7; matrix products, arithmetic and copies ran while one was open for 8% -> 9% of each run, Pallas kernels for 9% -> 12%
where the time goes in v12:
time: 83.4 us; the launch traced here: 82.9 us
  starting transfers between devices  32.8 us (39%)
  waiting for transfers between devices  24 us (29%)
  Pallas kernels  13.6 us (16%)
  matrix products  6.77 us (8%)
  local copies, waits for them, and re-layouts  4.02 us (5%)
  other arithmetic  0.9 us (1%)
    ppermute x9, starting transfers between devices, along(): lax.ppermute(array, 'near', [(i, (i + steps) % near_count) for i in range...  16.5 us
    ppermute x9, waiting for transfers between devices, along(): lax.ppermute(array, 'near', [(i, (i + steps) % near_count) for i in range...  12.3 us
    pallas_call x1, Pallas kernels, down_rows(): pl.pallas_call(functools.partial(down_kernel, near_count, capacity), grid...  7.24 us
    all_to_all x2, starting transfers between devices, local(): lax.all_to_all(picked.reshape(far_count, -1, part), 'far', split_axis=0,...  7.23 us
    dot_general x2, matrix products, local(): lax.dot_general(rows[i], weight[:, i * part:(i + 1) * part], (((1,), (1,)...  6.77 us
    all_to_all x1, waiting for transfers between devices, local(): lax.all_to_all(total.astype(jnp.bfloat16).reshape(experts, capacity, hidd...  4.96 us
    all_to_all x1, starting transfers between devices, local(): lax.all_to_all(total.astype(jnp.bfloat16).reshape(experts, capacity, hidd...  4.78 us
    ppermute x3, starting transfers between devices, across(): lax.ppermute(array, 'far', [(i, i ^ apart) for i in range(far_count)])  4.08 us
  transfers between devices with their start and end apart: 18, of which 7 were waited for; matrix products, arithmetic and copies ran while one was open for 9% of the time, Pallas kernels for 12%

profile of v12, /device:TPU:0, one launch (start us, length us, event | category | flops | bytes accessed | tf_op | source)
XLA Modules:
  0.0 82.9 jit_solution(382197511183315109)
XLA Ops:
  0.6 0.9 %copy-done.2 = bf16[32,4096]{1,0:T(8,128)(2,1)S(1)} copy-done((bf16[32,4096]{1,0:T(8,128)(2,1)S(1)}, bf16[32,4096]{1,0:T(8,128)(2,1)}, u32[]{:S(2)}) %copy-start.2) | copy-done | bytes 262168
  1.6 0.7 copy-done.3
  2.3 0.3 split_rows.1
  2.5 5.1 %collective-permute-start.2 = (bf16[32,2176]{1,0:T(8,128)(2,1)S(1)}, bf16[32,2176]{1,0:T(8,128)(2,1)S(1)}, u32[]{:S(2)}, u32[]{:S(2)}) collective-permute-start(bf16[32,2176]{1,0:T(8,128)(2,1)S(1)} %get-tuple-element.40.refs_0_), channel_id=1, source_target_pairs={{0,3},{1,0},{2,1},{3,2},{4,7},{5,4},{6,5},{7,6},{8,11},{9,8},{10,9... | collective-permute-start | bytes 417800 | tf_op jit(solution)/shard_map/ppermute | solution.py:349
  7.6 0.0 collective-permute-start.1
  7.7 1.0 %collective-permute-start = (bf16[32,2176]{1,0:T(8,128)(2,1)S(1)}, bf16[32,2176]{1,0:T(8,128)(2,1)S(1)}, u32[]{:S(2)}, u32[]{:S(2)}) collective-permute-start(bf16[32,2176]{1,0:T(8,128)(2,1)S(1)} %get-tuple-element.40.refs_0_), channel_id=1, source_target_pairs={{0,1},{1,2},{2,3},{3,0},{4,5},{5,6},{6,7},{7,4},{8,9},{9,10},{10,1... | collective-permute-start | bytes 417800 | tf_op jit(solution)/shard_map/ppermute | solution.py:349
  8.7 0.1 pad_add_fusion.scalars_ref
  8.7 1.0 %copy-done = bf16[32,8,768]{2,1,0:T(8,128)(2,1)S(1)} copy-done((bf16[32,8,768]{2,1,0:T(8,128)(2,1)S(1)}, bf16[32,8,768]{2,1,0:T(8,128)(2,1)}, u32[]{:S(2)}) %copy-start) | copy-done | bytes 393240
  9.7 0.7 copy-done.4
  10.4 0.7 copy-done.5
  11.1 1.1 %send_rows.1 = (bf16[64,768]{1,0:T(8,128)(2,1)S(1)}, bf16[64,768]{1,0:T(8,128)(2,1)S(1)}, bf16[64,768]{1,0:T(8,128)(2,1)S(1)}, bf16[64,768]{1,0:T(8,128)(2,1)S(1)}, bf16[256,256]{1,0:T(8,128)(2,1)S(1)}) custom-call(s32[3]{0:T(128)S(1)} %pad_add_fusion.scalars_ref, s32[8,32]{1,0:T(8,128)S(1)} %bitcast.28, f32[8,32]{1,0:T(8,128)S(1)} %bitcast.29, ...), custom_call_target="tpu_custom_call" | custom-call | flops 100663296 | bytes 786432 | tf_op jit(solution)/shard_map/send_rows/pallas_call | solution.py:226
  12.2 0.0 collective-permute-done.2.refs_3_
  12.2 7.2 %collective-permute-done.1.refs_2_ = bf16[32,2176]{1,0:T(8,128)(2,1)S(1)} collective-permute-done((bf16[32,2176]{1,0:T(8,128)(2,1)S(1)}, bf16[32,2176]{1,0:T(8,128)(2,1)S(1)}, u32[]{:S(2)}, u32[]{:S(2)}) %collective-permute-start.1) | collective-permute-done | bytes 139296 | tf_op jit(solution)/shard_map/ppermute | solution.py:349
  19.5 0.0 collective-permute-done.refs_1_
  19.5 1.8 %first_pick.1 = (bf16[256,2048]{1,0:T(8,128)(2,1)}, bf16[256,128]{1,0:T(8,128)(2,1)S(1)}) custom-call(s32[1]{0:T(128)} %bitcast.near_ref, bf16[32,2176]{1,0:T(8,128)(2,1)S(1)} %get-tuple-element.40.refs_0_, bf16[32,2176]{1,0:T(8,128)(2,1)S(1)} %collective-permute-done.refs_1_, bf16[32,2176]{1,0:T(8,128)(2,1)S(1)} %collective-permute-done.1.refs_2_, ...), custom_call_target="tpu_custom_call" | custom-call | tf_op jit(solution)/shard_map/first_pick/pallas_call | solution.py:274
  21.3 3.7 %all-to-all-start = ((bf16[4,64,2048]{2,1,0:T(8,128)(2,1)}), bf16[4,64,2048]{2,1,0:T(8,128)(2,1)S(1)}, u32[]{:S(2)}, u32[]{:S(2)}) async-start(bf16[4,64,2048]{2,1,0:T(8,128)(2,1)} %bitcast.6), calls=%async_computation | async-start | bytes 2097152 | tf_op jit(solution)/shard_map/all_to_all | solution.py:377
  25.0 1.5 %collective-permute-start.5 = (bf16[32,2048]{1,0:T(8,128)(2,1)S(1)}, bf16[32,2048]{1,0:T(8,128)(2,1)S(1)}, u32[]{:S(2)}, u32[]{:S(2)}) collective-permute-start(bf16[32,2048]{1,0:T(8,128)(2,1)S(1)} %get-tuple-element.48.refs_0_), channel_id=1, source_target_pairs={{0,3},{1,0},{2,1},{3,2},{4,7},{5,4},{6,5},{7,6},{8,11},{9,8},{10,9... | collective-permute-start | bytes 393224 | tf_op jit(solution)/shard_map/ppermute | solution.py:349
  26.5 1.2 %collective-permute-start.4 = (bf16[32,2048]{1,0:T(8,128)(2,1)S(1)}, bf16[32,2048]{1,0:T(8,128)(2,1)S(1)}, u32[]{:S(2)}, u32[]{:S(2)}) collective-permute-start(bf16[32,2048]{1,0:T(8,128)(2,1)S(1)} %get-tuple-element.48.refs_0_), channel_id=1, source_target_pairs={{0,2},{1,3},{2,0},{3,1},{4,6},{5,7},{6,4},{7,5},{8,10},{9,11},{10,... | collective-permute-start | bytes 393224 | tf_op jit(solution)/shard_map/ppermute | solution.py:349
  27.7 2.0 %collective-permute-start.3 = (bf16[32,2048]{1,0:T(8,128)(2,1)S(1)}, bf16[32,2048]{1,0:T(8,128)(2,1)S(1)}, u32[]{:S(2)}, u32[]{:S(2)}) collective-permute-start(bf16[32,2048]{1,0:T(8,128)(2,1)S(1)} %get-tuple-element.48.refs_0_), channel_id=1, source_target_pairs={{0,1},{1,2},{2,3},{3,0},{4,5},{5,6},{6,7},{7,4},{8,9},{9,10},{10,1... | collective-permute-start | bytes 393224 | tf_op jit(solution)/shard_map/ppermute | solution.py:349
  29.8 2.0 %collective-permute-start.6 = (bf16[64,768]{1,0:T(8,128)(2,1)S(1)}, bf16[64,768]{1,0:T(8,128)(2,1)S(1)}, u32[]{:S(2)}, u32[]{:S(2)}) collective-permute-start(bf16[64,768]{1,0:T(8,128)(2,1)S(1)} %get-tuple-element.51), channel_id=1, source_target_pairs={{0,4},{4,0},{8,12},{12,8},{1,5},{5,1},{9,13},{13,9},{2,6},{6,2},{1... | collective-permute-start | bytes 294920 | tf_op jit(solution)/shard_map/ppermute | solution.py:352
  31.8 1.5 %collective-permute-start.7 = (bf16[64,768]{1,0:T(8,128)(2,1)S(1)}, bf16[64,768]{1,0:T(8,128)(2,1)S(1)}, u32[]{:S(2)}, u32[]{:S(2)}) collective-permute-start(bf16[64,768]{1,0:T(8,128)(2,1)S(1)} %get-tuple-element.52), channel_id=1, source_target_pairs={{0,8},{4,12},{8,0},{12,4},{1,9},{5,13},{9,1},{13,5},{2,10},{6,14},... | collective-permute-start | bytes 294920 | tf_op jit(solution)/shard_map/ppermute | solution.py:352
  33.2 0.0 collective-permute-done.5.refs_3_
  33.2 0.6 collective-permute-start.8
  33.8 5.1 %collective-permute-done.4.refs_2_ = bf16[32,2048]{1,0:T(8,128)(2,1)S(1)} collective-permute-done((bf16[32,2048]{1,0:T(8,128)(2,1)S(1)}, bf16[32,2048]{1,0:T(8,128)(2,1)S(1)}, u32[]{:S(2)}, u32[]{:S(2)}) %collective-permute-start.4) | collective-permute-done | bytes 131104 | tf_op jit(solution)/shard_map/ppermute | solution.py:349
  38.9 0.0 collective-permute-done.3.refs_1_
  38.9 1.4 %pick_rows.1 = bf16[256,2048]{1,0:T(8,128)(2,1)} custom-call(bf16[256,128]{1,0:T(8,128)(2,1)S(1)} %get-tuple-element.41.pick_ref, bf16[32,2048]{1,0:T(8,128)(2,1)S(1)} %get-tuple-element.48.refs_0_, bf16[32,2048]{1,0:T(8,128)(2,1)S(1)} %collective-permute-done.3.refs_1_, bf16[32,2048]{1,0:T(8,128)(2,1)S(1)} %collective-permute-done.4.refs_2_, ...), custom_call_target="tpu_custom_call" | custom-call | tf_op jit(solution)/shard_map/pick_rows/pallas_call | solution.py:289
  40.3 1.1 %collective-permute-done.6.refs_1_ = bf16[64,768]{1,0:T(8,128)(2,1)S(1)} collective-permute-done((bf16[64,768]{1,0:T(8,128)(2,1)S(1)}, bf16[64,768]{1,0:T(8,128)(2,1)S(1)}, u32[]{:S(2)}, u32[]{:S(2)}) %collective-permute-start.6) | collective-permute-done | bytes 98336 | tf_op jit(solution)/shard_map/ppermute | solution.py:352
  41.4 0.0 collective-permute-done.7.refs_2_
  41.4 2.0 %collective-permute-done.8.refs_3_ = bf16[64,768]{1,0:T(8,128)(2,1)S(1)} collective-permute-done((bf16[64,768]{1,0:T(8,128)(2,1)S(1)}, bf16[64,768]{1,0:T(8,128)(2,1)S(1)}, u32[]{:S(2)}, u32[]{:S(2)}) %collective-permute-start.8) | collective-permute-done | bytes 98336 | tf_op jit(solution)/shard_map/ppermute | solution.py:352
  43.3 0.0 all-to-all-done
  43.3 3.5 %all-to-all-start.1 = ((bf16[4,64,2048]{2,1,0:T(8,128)(2,1)}), bf16[4,64,2048]{2,1,0:T(8,128)(2,1)S(1)}, u32[]{:S(2)}, u32[]{:S(2)}) async-start(bf16[4,64,2048]{2,1,0:T(8,128)(2,1)} %bitcast.8), calls=%async_computation.1 | async-start | bytes 2097152 | tf_op jit(solution)/shard_map/all_to_all | solution.py:377
  46.8 0.4 regroup_rows.1
  47.2 0.7 collective-permute-start.9
  48.0 2.0 %collective-permute-start.10 = (bf16[64,768]{1,0:T(8,128)(2,1)S(1)}, bf16[64,768]{1,0:T(8,128)(2,1)S(1)}, u32[]{:S(2)}, u32[]{:S(2)}) collective-permute-start(bf16[64,768]{1,0:T(8,128)(2,1)S(1)} %get-tuple-element.62), channel_id=1, source_target_pairs={{0,2},{1,3},{2,0},{3,1},{4,6},{5,7},{6,4},{7,5},{8,10},{9,11},{10,... | collective-permute-start | bytes 294920 | tf_op jit(solution)/shard_map/ppermute | solution.py:349
  50.0 2.8 %collective-permute-start.11 = (bf16[64,768]{1,0:T(8,128)(2,1)S(1)}, bf16[64,768]{1,0:T(8,128)(2,1)S(1)}, u32[]{:S(2)}, u32[]{:S(2)}) collective-permute-start(bf16[64,768]{1,0:T(8,128)(2,1)S(1)} %get-tuple-element.63), channel_id=1, source_target_pairs={{0,3},{1,0},{2,1},{3,2},{4,7},{5,4},{6,5},{7,6},{8,11},{9,8},{10,9... | collective-permute-start | bytes 294920 | tf_op jit(solution)/shard_map/ppermute | solution.py:349
  52.8 3.8 %fusion.2 = f32[256,768]{1,0:T(8,128)} fusion(bf16[256,2048]{1,0:T(8,128)(2,1)S(1)} %bitcast.19, bf16[768,4096]{1,0:T(8,128)(2,1)} %bitcast.33), kind=kOutput, calls=%fused_computation.2 | convolution fusion | flops 805306368 | bytes 4980736 | tf_op jit(solution)/shard_map/dot_general | solution.py:386
  56.7 2.2 %all-to-all-done.1 = bf16[4,64,2048]{2,1,0:T(8,128)(2,1)S(1)} async-done(((bf16[4,64,2048]{2,1,0:T(8,128)(2,1)}), bf16[4,64,2048]{2,1,0:T(8,128)(2,1)S(1)}, u32[]{:S(2)}, u32[]{:S(2)}) %all-to-all-start.1) | async-done | bytes 1048608 | tf_op jit(solution)/shard_map/all_to_all | solution.py:377
  58.9 3.0 %fusion = f32[256,768]{1,0:T(8,128)S(1)} fusion(bf16[256,2048]{1,0:T(8,128)(2,1)S(1)} %bitcast.22, bf16[768,4096]{1,0:T(8,128)(2,1)} %bitcast.34), kind=kOutput, calls=%fused_computation | convolution fusion | flops 805306368 | bytes 4980736 | tf_op jit(solution)/shard_map/dot_general | solution.py:386
  61.8 0.0 copy-start.1
  61.9 0.0 copy-start.6
  61.9 0.8 add_convert_fusion
  62.7 4.8 %all-to-all-start.2 = ((bf16[16,16,768]{2,1,0:T(8,128)(2,1)}), bf16[16,16,768]{2,1,0:T(8,128)(2,1)S(1)}, u32[]{:S(2)}, u32[]{:S(2)}) async-start(bf16[16,16,768]{2,1,0:T(8,128)(2,1)} %bitcast.32), calls=%async_computation.2 | async-start | bytes 786432 | tf_op jit(solution)/shard_map/all_to_all | solution.py:393
  67.5 0.2 collective-permute-start.14
  67.7 0.0 collective-permute-done.12.refs_2_
  67.7 1.6 %collective-permute-done.14.refs_5_ = bf16[64,3072]{1,0:T(8,128)(2,1)S(1)} collective-permute-done((bf16[64,3072]{1,0:T(8,128)(2,1)S(1)}, bf16[64,3072]{1,0:T(8,128)(2,1)S(1)}, u32[]{:S(2)}, u32[]{:S(2)}) %collective-permute-start.14) | collective-permute-done | bytes 393248 | tf_op jit(solution)/shard_map/ppermute | solution.py:355
  69.3 7.2 %down_rows.1 = bf16[384,4096]{1,0:T(8,128)(2,1)} custom-call(s32[3]{0:T(128)S(1)} %pad_add_fusion.scalars_ref, bf16[256,2048]{1,0:T(8,128)(2,1)S(1)} %bitcast.20, bf16[256,2048]{1,0:T(8,128)(2,1)S(1)} %bitcast.23, bf16[256,2048]{1,0:T(8,128)(2,1)} %collective-permute-done.12.refs_2_, bf16[256,2048]{1,0:T(8,128)(2,1)} %collective-permute-done.13.refs_3_, ...), custom_call_target="tpu_custom_call" | custom-call | flops 1610612736 | bytes 7340032 | tf_op jit(solution)/shard_map/down_rows/pallas_call | solution.py:318
  76.5 5.0 %all-to-all-done.2 = bf16[16,16,768]{2,1,0:T(8,128)(2,1)S(1)} async-done(((bf16[16,16,768]{2,1,0:T(8,128)(2,1)}), bf16[16,16,768]{2,1,0:T(8,128)(2,1)S(1)}, u32[]{:S(2)}, u32[]{:S(2)}) %all-to-all-start.2) | async-done | bytes 393248 | tf_op jit(solution)/shard_map/all_to_all | solution.py:393
  81.5 1.4 %close_rows.1 = (bf16[256,768]{1,0:T(8,128)(2,1)}, f32[8,32]{1,0:T(8,128)}) custom-call(bf16[256,256]{1,0:T(8,128)(2,1)S(1)} %get-tuple-element.39.back_ref, bf16[256,768]{1,0:T(8,128)(2,1)S(1)} %bitcast.26, f32[8,32]{1,0:T(8,128)S(1)} %bitcast.30, bf16[256,768]{1,0:T(8,128)(2,1)S(1)} %bitcast.25), custom_call_target="tpu_custom_call" | custom-call | tf_op jit(solution)/shard_map/close_rows/pallas_call | solution.py:252
  (16 shorter events, 0.1 us)
Async XLA Ops:
  0.6 1.0 %copy-start.2 = (bf16[32,4096]{1,0:T(8,128)(2,1)S(1)}, bf16[32,4096]{1,0:T(8,128)(2,1)}, u32[]{:S(2)}) copy-start(bf16[32,4096]{1,0:T(8,128)(2,1)} %tokens_hbm.1) | copy-start | bytes 786436
  1.6 0.7 copy-start.3
  2.5 9.7 %collective-permute-start.2 = (bf16[32,2176]{1,0:T(8,128)(2,1)S(1)}, bf16[32,2176]{1,0:T(8,128)(2,1)S(1)}, u32[]{:S(2)}, u32[]{:S(2)}) collective-permute-start(bf16[32,2176]{1,0:T(8,128)(2,1)S(1)} %get-tuple-element.40.refs_0_), channel_id=1, source_target_pairs={{0,3},{1,0},{2,1},{3,2},{4,7},{5,4},{6,5},{7,6},{8,11},{9,8},{10,9... | collective-permute-start | bytes 417800 | tf_op jit(solution)/shard_map/ppermute | solution.py:349
  7.6 11.8 %collective-permute-start.1 = (bf16[32,2176]{1,0:T(8,128)(2,1)S(1)}, bf16[32,2176]{1,0:T(8,128)(2,1)S(1)}, u32[]{:S(2)}, u32[]{:S(2)}) collective-permute-start(bf16[32,2176]{1,0:T(8,128)(2,1)S(1)} %get-tuple-element.40.refs_0_), channel_id=1, source_target_pairs={{0,2},{1,3},{2,0},{3,1},{4,6},{5,7},{6,4},{7,5},{8,10},{9,11},{10,... | collective-permute-start | bytes 417800 | tf_op jit(solution)/shard_map/ppermute | solution.py:349
  7.7 11.8 %collective-permute-start = (bf16[32,2176]{1,0:T(8,128)(2,1)S(1)}, bf16[32,2176]{1,0:T(8,128)(2,1)S(1)}, u32[]{:S(2)}, u32[]{:S(2)}) collective-permute-start(bf16[32,2176]{1,0:T(8,128)(2,1)S(1)} %get-tuple-element.40.refs_0_), channel_id=1, source_target_pairs={{0,1},{1,2},{2,3},{3,0},{4,5},{5,6},{6,7},{7,4},{8,9},{9,10},{10,1... | collective-permute-start | bytes 417800 | tf_op jit(solution)/shard_map/ppermute | solution.py:349
  8.7 1.0 %copy-start = (bf16[32,8,768]{2,1,0:T(8,128)(2,1)S(1)}, bf16[32,8,768]{2,1,0:T(8,128)(2,1)}, u32[]{:S(2)}) copy-start(bf16[32,8,768]{2,1,0:T(8,128)(2,1)} %param.6) | copy-start | bytes 1179652
  9.7 0.7 copy-start.4
  10.4 0.7 copy-start.5
  21.3 22.0 %all-to-all-start = ((bf16[4,64,2048]{2,1,0:T(8,128)(2,1)}), bf16[4,64,2048]{2,1,0:T(8,128)(2,1)S(1)}, u32[]{:S(2)}, u32[]{:S(2)}) async-start(bf16[4,64,2048]{2,1,0:T(8,128)(2,1)} %bitcast.6), calls=%async_computation | async-start | bytes 2097152 | tf_op jit(solution)/shard_map/all_to_all | solution.py:377
  25.0 8.3 %collective-permute-start.5 = (bf16[32,2048]{1,0:T(8,128)(2,1)S(1)}, bf16[32,2048]{1,0:T(8,128)(2,1)S(1)}, u32[]{:S(2)}, u32[]{:S(2)}) collective-permute-start(bf16[32,2048]{1,0:T(8,128)(2,1)S(1)} %get-tuple-element.48.refs_0_), channel_id=1, source_target_pairs={{0,3},{1,0},{2,1},{3,2},{4,7},{5,4},{6,5},{7,6},{8,11},{9,8},{10,9... | collective-permute-start | bytes 393224 | tf_op jit(solution)/shard_map/ppermute | solution.py:349
  26.5 12.4 %collective-permute-start.4 = (bf16[32,2048]{1,0:T(8,128)(2,1)S(1)}, bf16[32,2048]{1,0:T(8,128)(2,1)S(1)}, u32[]{:S(2)}, u32[]{:S(2)}) collective-permute-start(bf16[32,2048]{1,0:T(8,128)(2,1)S(1)} %get-tuple-element.48.refs_0_), channel_id=1, source_target_pairs={{0,2},{1,3},{2,0},{3,1},{4,6},{5,7},{6,4},{7,5},{8,10},{9,11},{10,... | collective-permute-start | bytes 393224 | tf_op jit(solution)/shard_map/ppermute | solution.py:349
  27.7 11.2 %collective-permute-start.3 = (bf16[32,2048]{1,0:T(8,128)(2,1)S(1)}, bf16[32,2048]{1,0:T(8,128)(2,1)S(1)}, u32[]{:S(2)}, u32[]{:S(2)}) collective-permute-start(bf16[32,2048]{1,0:T(8,128)(2,1)S(1)} %get-tuple-element.48.refs_0_), channel_id=1, source_target_pairs={{0,1},{1,2},{2,3},{3,0},{4,5},{5,6},{6,7},{7,4},{8,9},{9,10},{10,1... | collective-permute-start | bytes 393224 | tf_op jit(solution)/shard_map/ppermute | solution.py:349
  29.8 11.6 %collective-permute-start.6 = (bf16[64,768]{1,0:T(8,128)(2,1)S(1)}, bf16[64,768]{1,0:T(8,128)(2,1)S(1)}, u32[]{:S(2)}, u32[]{:S(2)}) collective-permute-start(bf16[64,768]{1,0:T(8,128)(2,1)S(1)} %get-tuple-element.51), channel_id=1, source_target_pairs={{0,4},{4,0},{8,12},{12,8},{1,5},{5,1},{9,13},{13,9},{2,6},{6,2},{1... | collective-permute-start | bytes 294920 | tf_op jit(solution)/shard_map/ppermute | solution.py:352
  31.8 9.6 %collective-permute-start.7 = (bf16[64,768]{1,0:T(8,128)(2,1)S(1)}, bf16[64,768]{1,0:T(8,128)(2,1)S(1)}, u32[]{:S(2)}, u32[]{:S(2)}) collective-permute-start(bf16[64,768]{1,0:T(8,128)(2,1)S(1)} %get-tuple-element.52), channel_id=1, source_target_pairs={{0,8},{4,12},{8,0},{12,4},{1,9},{5,13},{9,1},{13,5},{2,10},{6,14},... | collective-permute-start | bytes 294920 | tf_op jit(solution)/shard_map/ppermute | solution.py:352
  33.2 10.1 %collective-permute-start.8 = (bf16[64,768]{1,0:T(8,128)(2,1)S(1)}, bf16[64,768]{1,0:T(8,128)(2,1)S(1)}, u32[]{:S(2)}, u32[]{:S(2)}) collective-permute-start(bf16[64,768]{1,0:T(8,128)(2,1)S(1)} %get-tuple-element.53), channel_id=1, source_target_pairs={{0,12},{4,8},{8,4},{12,0},{1,13},{5,9},{9,5},{13,1},{2,14},{6,10},... | collective-permute-start | bytes 294920 | tf_op jit(solution)/shard_map/ppermute | solution.py:352
  43.3 15.5 %all-to-all-start.1 = ((bf16[4,64,2048]{2,1,0:T(8,128)(2,1)}), bf16[4,64,2048]{2,1,0:T(8,128)(2,1)S(1)}, u32[]{:S(2)}, u32[]{:S(2)}) async-start(bf16[4,64,2048]{2,1,0:T(8,128)(2,1)} %bitcast.8), calls=%async_computation.1 | async-start | bytes 2097152 | tf_op jit(solution)/shard_map/all_to_all | solution.py:377
  47.2 9.4 %collective-permute-start.9 = (bf16[64,768]{1,0:T(8,128)(2,1)S(1)}, bf16[64,768]{1,0:T(8,128)(2,1)S(1)}, u32[]{:S(2)}, u32[]{:S(2)}) collective-permute-start(bf16[64,768]{1,0:T(8,128)(2,1)S(1)} %get-tuple-element.61), channel_id=1, source_target_pairs={{0,1},{1,2},{2,3},{3,0},{4,5},{5,6},{6,7},{7,4},{8,9},{9,10},{10,1... | collective-permute-start | bytes 294920 | tf_op jit(solution)/shard_map/ppermute | solution.py:349
  48.0 8.6 %collective-permute-start.10 = (bf16[64,768]{1,0:T(8,128)(2,1)S(1)}, bf16[64,768]{1,0:T(8,128)(2,1)S(1)}, u32[]{:S(2)}, u32[]{:S(2)}) collective-permute-start(bf16[64,768]{1,0:T(8,128)(2,1)S(1)} %get-tuple-element.62), channel_id=1, source_target_pairs={{0,2},{1,3},{2,0},{3,1},{4,6},{5,7},{6,4},{7,5},{8,10},{9,11},{10,... | collective-permute-start | bytes 294920 | tf_op jit(solution)/shard_map/ppermute | solution.py:349
  50.0 6.7 %collective-permute-start.11 = (bf16[64,768]{1,0:T(8,128)(2,1)S(1)}, bf16[64,768]{1,0:T(8,128)(2,1)S(1)}, u32[]{:S(2)}, u32[]{:S(2)}) collective-permute-start(bf16[64,768]{1,0:T(8,128)(2,1)S(1)} %get-tuple-element.63), channel_id=1, source_target_pairs={{0,3},{1,0},{2,1},{3,2},{4,7},{5,4},{6,5},{7,6},{8,11},{9,8},{10,9... | collective-permute-start | bytes 294920 | tf_op jit(solution)/shard_map/ppermute | solution.py:349
  52.8 14.9 %collective-permute-start.12 = (bf16[256,2048]{1,0:T(8,128)(2,1)S(1)}, bf16[256,2048]{1,0:T(8,128)(2,1)}, u32[]{:S(2)}, u32[]{:S(2)}) collective-permute-start(bf16[256,2048]{1,0:T(8,128)(2,1)S(1)} %bitcast.18), channel_id=1, source_target_pairs={{0,16},{16,0},{1,17},{17,1},{2,18},{18,2},{3,19},{19,3},{4,20},{20... | collective-permute-start | bytes 3145736 | tf_op jit(solution)/shard_map/ppermute | solution.py:355
  58.8 3.0 %copy-start.7 = (f32[256,768]{1,0:T(8,128)S(1)}, f32[256,768]{1,0:T(8,128)}, u32[]{:S(2)}) copy-start(f32[256,768]{1,0:T(8,128)} %fusion.2) | copy-start | bytes 2359300
  58.8 10.4 %collective-permute-start.13 = (bf16[256,2048]{1,0:T(8,128)(2,1)S(1)}, bf16[256,2048]{1,0:T(8,128)(2,1)}, u32[]{:S(2)}, u32[]{:S(2)}) collective-permute-start(bf16[256,2048]{1,0:T(8,128)(2,1)S(1)} %bitcast.21), channel_id=1, source_target_pairs={{0,16},{16,0},{1,17},{17,1},{2,18},{18,2},{3,19},{19,3},{4,20},{20... | collective-permute-start | bytes 3145736 | tf_op jit(solution)/shard_map/ppermute | solution.py:355
  61.8 19.6 %copy-start.1 = (bf16[32,8,768]{2,1,0:T(8,128)(2,1)S(1)}, bf16[32,8,768]{2,1,0:T(8,128)(2,1)}, u32[]{:S(2)}) copy-start(bf16[32,8,768]{2,1,0:T(8,128)(2,1)} %param.6) | copy-start | bytes 1179652
  61.9 19.6 %copy-start.6 = (f32[32,8]{0,1:T(8,128)S(1)}, f32[32,8]{0,1:T(8,128)}, u32[]{:S(2)}) copy-start(f32[32,8]{0,1:T(8,128)} %param.7) | copy-start | bytes 3076
  62.7 18.8 %all-to-all-start.2 = ((bf16[16,16,768]{2,1,0:T(8,128)(2,1)}), bf16[16,16,768]{2,1,0:T(8,128)(2,1)S(1)}, u32[]{:S(2)}, u32[]{:S(2)}) async-start(bf16[16,16,768]{2,1,0:T(8,128)(2,1)} %bitcast.32), calls=%async_computation.2 | async-start | bytes 786432 | tf_op jit(solution)/shard_map/all_to_all | solution.py:393
  67.5 1.8 %collective-permute-start.14 = (bf16[64,3072]{1,0:T(8,128)(2,1)S(1)}, bf16[64,3072]{1,0:T(8,128)(2,1)S(1)}, u32[]{:S(2)}, u32[]{:S(2)}) collective-permute-start(bf16[64,3072]{1,0:T(8,128)(2,1)S(1)} %join_rows.1.refs_4_), channel_id=1, source_target_pairs={{0,16},{16,0},{1,17},{17,1},{2,18},{18,2},{3,19},{19,3},{4,20},{20... | collective-permute-start | bytes 1179656 | tf_op jit(solution)/shard_map/ppermute | solution.py:355

commit v13 on v12

--- a/solution.py
+++ b/solution.py
@@ -9,6 +9,7 @@
 
 ID_COLS = 128
 PARTS = 2
+TILE = 256
 MIB = 1024 * 1024
 
 
@@ -16,17 +17,21 @@
     return lax.broadcasted_iota(jnp.int32, shape, dim)
 
 
+def part_bounds(width):
+    first = width // TILE * 9 // 16 * TILE
+    return [(0, first), (first, width)]
+
+
 def exact_dot(one_hot, values):
     return jnp.dot(one_hot, values, preferred_element_type=jnp.float32)
 
 
 def split_kernel(ids_ref, tokens_hbm, *refs):
     outs, sem = refs[:-1], refs[-1]
-    part = outs[1].shape[1]
-    copies = [
-        pltpu.make_async_copy(tokens_hbm.at[:, i * part : (i + 1) * part], out.at[:, :part], sem.at[i])
-        for i, out in enumerate(outs)
-    ]
+    copies = []
+    for i, (start, stop) in enumerate(part_bounds(tokens_hbm.shape[1])):
+        target = outs[i].at[:, : stop - start]
+        copies.append(pltpu.make_async_copy(tokens_hbm.at[:, start:stop], target, sem.at[i]))
     for copy in copies:
         copy.start()
     top_count, tok_local = ids_ref.shape
@@ -34,7 +39,7 @@
     ids = ids_ref[...].astype(jnp.float32).astype(jnp.bfloat16)
     ids = lax.dot_general(ids, same, (((0,), (0,)), ((), ())), preferred_element_type=jnp.float32)
     ids = jnp.where(iota((tok_local, ID_COLS), 1) < top_count, ids, -1.0)
-    outs[0][:, part:] = ids.astype(jnp.bfloat16)
+    outs[0][:, outs[0].shape[1] - ID_COLS :] = ids.astype(jnp.bfloat16)
     for copy in copies:
         copy.wait()
 
@@ -108,7 +113,7 @@
 
 def picked_rows(pick, blocks, out_ref):
     width = out_ref.shape[1]
-    step = min(width, 512)
+    step = TILE
     for start in range(0, width, step):
         tokens = jnp.concatenate([block[:, start : start + step] for block in blocks], axis=0)
         out_ref[:, start : start + step] = exact_dot(pick, tokens).astype(jnp.bfloat16)
@@ -179,15 +184,18 @@
                 total = total + exact_dot(order, ref[:, pl.ds(start, share)])
             turned_ref[:, i * slots : (i + 1) * slots] = total.T.astype(jnp.bfloat16)
 
-    steps = rows[0].shape[1] // tile
+    done = 0
     for part in range(PARTS):
-
-        @pl.when(step // steps == part)
-        def _(part=part):
-            cols = pl.ds(pl.multiple_of(step % steps * tile, 128), tile)
+        steps = rows[part].shape[1] // tile
+
+        @pl.when((step >= done) & (step < done + steps))
+        def _(part=part, done=done):
+            cols = pl.ds(pl.multiple_of((step - done) * tile, 128), tile)
             tokens = jnp.concatenate([ref[:, cols] for ref in rows[part::PARTS]], axis=0)
             out_ref[...] = exact_dot(turned_ref[...], tokens).astype(jnp.bfloat16)
 
+        done += steps
+
 
 def scalar_spec():
     return pl.BlockSpec(memory_space=pltpu.SMEM)
@@ -203,13 +211,12 @@
 
 def split_rows(ids, tokens):
     tok_local, width = tokens.shape
-    part = width // PARTS
+    widths = [stop - start for start, stop in part_bounds(width)]
+    widths[0] += ID_COLS
     vmem = pl.BlockSpec(memory_space=pltpu.VMEM)
     return pl.pallas_call(
         split_kernel,
-        out_shape=[
-            jax.ShapeDtypeStruct((tok_local, part + (ID_COLS if i == 0 else 0)), jnp.bfloat16) for i in range(PARTS)
-        ],
+        out_shape=[jax.ShapeDtypeStruct((tok_local, part), jnp.bfloat16) for part in widths],
         in_specs=[vmem, hbm_spec()],
         out_specs=[vmem] * PARTS,
         scratch_shapes=[pltpu.SemaphoreType.DMA((PARTS,))],
@@ -310,10 +317,9 @@
 
 
 def down_rows(near_count, capacity, scalars, rows, hids, share):
-    part = rows[0].shape[1]
-    tile = min(part, 512)
+    tile = TILE
     lines = 2 * rows[0].shape[0]
-    width = part * PARTS
+    width = sum(array.shape[1] for array in rows[:PARTS])
     whole = lambda array: pl.BlockSpec(array.shape, lambda i: (0, 0))
     return pl.pallas_call(
         functools.partial(down_kernel, near_count, capacity),
@@ -342,7 +348,7 @@
     slot_total = experts * capacity
     near = lax.axis_index("near")
     near_ref = near.astype(jnp.int32).reshape(1)
-    part = width // PARTS
+    bounds = part_bounds(width)
     weight = w_down[0]
 
     def along(array, steps):
@@ -364,19 +370,19 @@
     parts[0], ids = lax.optimization_barrier((parts[0], ids))
     blocks = line(parts[0])
     *sends, back_place = send_rows(far_count, near_count, capacity, scalars, ids, gates.T, hidden_rows)
+    crossed = [sends[0]] + [across(sends[apart], apart) for apart in range(1, far_count)]
 
     rows, total = [], None
     for i in range(PARTS):
         if i == 0:
             picked, pick = first_pick(far_count, near_count, capacity, near_ref, blocks)
-            picked, sends, parts = lax.optimization_barrier((picked, sends, parts))
+            picked, crossed, parts = lax.optimization_barrier((picked, crossed, parts))
         else:
             picked = pick_rows(pick, line(parts[i]))
-            crossed = [sends[0]] + [across(sends[apart], apart) for apart in range(1, far_count)]
             picked, rows[-1], crossed = lax.optimization_barrier((picked, rows[-1], crossed))
         got = lax.all_to_all(
-            picked.reshape(far_count, -1, part), "far", split_axis=0, concat_axis=0, tiled=True
-        ).reshape(slot_total, part)
+            picked.reshape(far_count, -1, picked.shape[1]), "far", split_axis=0, concat_axis=0, tiled=True
+        ).reshape(picked.shape)
         rows.append(got)
     hids = list(regroup(near_count, capacity, crossed))
     hids = join_rows(hids[:1] + [along(hids[step], step) for step in range(1, near_count)])
@@ -385,7 +391,7 @@
             rows[i], total, hids = lax.optimization_barrier((rows[i], total, hids))
         product = lax.dot_general(
             rows[i],
-            weight[:, i * part : (i + 1) * part],
+            weight[:, bounds[i][0] : bounds[i][1]],
             (((1,), (1,)), ((), ())),
             preferred_element_type=jnp.float32,
         )

time: 83.4 us -> 81.9 us (0.982)
  waiting for transfers between devices: 24 us -> 18.8 us
  Pallas kernels: 13.6 us -> 16.7 us
    all_to_all x1, waiting for transfers between devices: 4.96 us -> 1.91 us  [local(): lax.all_to_all(total.astype(jnp.bfloat16).reshape(experts, capacity, hidd...]
    pallas_call x1, Pallas kernels: 7.24 us -> 10.3 us  [down_rows(): pl.pallas_call(functools.partial(down_kernel, near_count, capacity), grid...]
    ppermute x3, waiting for transfers between devices: 3.01 us -> 0.01 us  [across(): lax.ppermute(array, 'far', [(i, i ^ apart) for i in range(far_count)])]
    ppermute x9, waiting for transfers between devices: 12.3 us -> 13.4 us  [along(): lax.ppermute(array, 'near', [(i, (i + steps) % near_count) for i in range...]
    all_to_all x1, starting transfers between devices: 4.78 us -> 5.89 us  [local(): lax.all_to_all(total.astype(jnp.bfloat16).reshape(experts, capacity, hidd...]
  transfers between devices with their start and end apart: 18 -> 18, of which waited for: 7 -> 8; matrix products, arithmetic and copies ran while one was open for 9% -> 9% of each run, Pallas kernels for 12% -> 19%
where the time goes in v13:
time: 81.9 us; the launch traced here: 81.2 us
  starting transfers between devices  33.4 us (41%)
  waiting for transfers between devices  18.8 us (23%)
  Pallas kernels  16.7 us (20%)
  matrix products  6.67 us (8%)
  local copies, waits for them, and re-layouts  4.02 us (5%)
  other arithmetic  0.92 us (1%)
    ppermute x9, starting transfers between devices, along(): lax.ppermute(array, 'near', [(i, (i + steps) % near_count) for i in range...  16.5 us
    ppermute x9, waiting for transfers between devices, along(): lax.ppermute(array, 'near', [(i, (i + steps) % near_count) for i in range...  13.4 us
    pallas_call x1, Pallas kernels, down_rows(): pl.pallas_call(functools.partial(down_kernel, near_count, capacity), grid...  10.3 us
    all_to_all x2, starting transfers between devices, local(): lax.all_to_all(picked.reshape(far_count, -1, picked.shape[1]), 'far', spl...  7.23 us
    dot_general x2, matrix products, local(): lax.dot_general(rows[i], weight[:, bounds[i][0]:bounds[i][1]], (((1,), (1...  6.67 us
    all_to_all x1, starting transfers between devices, local(): lax.all_to_all(total.astype(jnp.bfloat16).reshape(experts, capacity, hidd...  5.89 us
    unnamed x16, local copies, waits for them, and re-layouts  4.02 us
    ppermute x3, starting transfers between devices, across(): lax.ppermute(array, 'far', [(i, i ^ apart) for i in range(far_count)])  3.55 us
  transfers between devices with their start and end apart: 18, of which 8 were waited for; matrix products, arithmetic and copies ran while one was open for 9% of the time, Pallas kernels for 19%

profile of v13, /device:TPU:0, one launch (start us, length us, event | category | flops | bytes accessed | tf_op | source)
XLA Modules:
  0.0 81.2 jit_solution(12948685662458381290)
XLA Ops:
  0.6 0.9 %copy-done.2 = bf16[32,4096]{1,0:T(8,128)(2,1)S(1)} copy-done((bf16[32,4096]{1,0:T(8,128)(2,1)S(1)}, bf16[32,4096]{1,0:T(8,128)(2,1)}, u32[]{:S(2)}) %copy-start.2) | copy-done | bytes 262168
  1.6 0.7 copy-done.3
  2.3 0.3 split_rows.1
  2.5 5.1 %collective-permute-start.2 = (bf16[32,2432]{1,0:T(8,128)(2,1)S(1)}, bf16[32,2432]{1,0:T(8,128)(2,1)S(1)}, u32[]{:S(2)}, u32[]{:S(2)}) collective-permute-start(bf16[32,2432]{1,0:T(8,128)(2,1)S(1)} %get-tuple-element.40.refs_0_), channel_id=1, source_target_pairs={{0,3},{1,0},{2,1},{3,2},{4,7},{5,4},{6,5},{7,6},{8,11},{9,8},{10,9... | collective-permute-start | bytes 466952 | tf_op jit(solution)/shard_map/ppermute | solution.py:355
  7.6 0.0 collective-permute-start.1
  7.7 1.0 %collective-permute-start = (bf16[32,2432]{1,0:T(8,128)(2,1)S(1)}, bf16[32,2432]{1,0:T(8,128)(2,1)S(1)}, u32[]{:S(2)}, u32[]{:S(2)}) collective-permute-start(bf16[32,2432]{1,0:T(8,128)(2,1)S(1)} %get-tuple-element.40.refs_0_), channel_id=1, source_target_pairs={{0,1},{1,2},{2,3},{3,0},{4,5},{5,6},{6,7},{7,4},{8,9},{9,10},{10,1... | collective-permute-start | bytes 466952 | tf_op jit(solution)/shard_map/ppermute | solution.py:355
  8.7 0.1 pad_add_fusion.scalars_ref
  8.7 1.0 %copy-done = bf16[32,8,768]{2,1,0:T(8,128)(2,1)S(1)} copy-done((bf16[32,8,768]{2,1,0:T(8,128)(2,1)S(1)}, bf16[32,8,768]{2,1,0:T(8,128)(2,1)}, u32[]{:S(2)}) %copy-start) | copy-done | bytes 393240
  9.7 0.7 copy-done.4
  10.4 0.7 copy-done.5
  11.1 1.1 %send_rows.1 = (bf16[64,768]{1,0:T(8,128)(2,1)S(1)}, bf16[64,768]{1,0:T(8,128)(2,1)S(1)}, bf16[64,768]{1,0:T(8,128)(2,1)S(1)}, bf16[64,768]{1,0:T(8,128)(2,1)S(1)}, bf16[256,256]{1,0:T(8,128)(2,1)S(1)}) custom-call(s32[3]{0:T(128)S(1)} %pad_add_fusion.scalars_ref, s32[8,32]{1,0:T(8,128)S(1)} %bitcast.28, f32[8,32]{1,0:T(8,128)S(1)} %bitcast.29, ...), custom_call_target="tpu_custom_call" | custom-call | flops 100663296 | bytes 786432 | tf_op jit(solution)/shard_map/send_rows/pallas_call | solution.py:233
  12.2 1.6 %collective-permute-start.3 = (bf16[64,768]{1,0:T(8,128)(2,1)S(1)}, bf16[64,768]{1,0:T(8,128)(2,1)S(1)}, u32[]{:S(2)}, u32[]{:S(2)}) collective-permute-start(bf16[64,768]{1,0:T(8,128)(2,1)S(1)} %get-tuple-element.44), channel_id=1, source_target_pairs={{0,4},{4,0},{8,12},{12,8},{1,5},{5,1},{9,13},{13,9},{2,6},{6,2},{1... | collective-permute-start | bytes 294920 | tf_op jit(solution)/shard_map/ppermute | solution.py:358
  13.8 1.5 %collective-permute-start.4 = (bf16[64,768]{1,0:T(8,128)(2,1)S(1)}, bf16[64,768]{1,0:T(8,128)(2,1)S(1)}, u32[]{:S(2)}, u32[]{:S(2)}) collective-permute-start(bf16[64,768]{1,0:T(8,128)(2,1)S(1)} %get-tuple-element.45), channel_id=1, source_target_pairs={{0,8},{4,12},{8,0},{12,4},{1,9},{5,13},{9,1},{13,5},{2,10},{6,14},... | collective-permute-start | bytes 294920 | tf_op jit(solution)/shard_map/ppermute | solution.py:358
  15.3 0.5 collective-permute-start.5
  15.8 5.0 %collective-permute-done.1.refs_2_ = bf16[32,2432]{1,0:T(8,128)(2,1)S(1)} collective-permute-done((bf16[32,2432]{1,0:T(8,128)(2,1)S(1)}, bf16[32,2432]{1,0:T(8,128)(2,1)S(1)}, u32[]{:S(2)}, u32[]{:S(2)}) %collective-permute-start.1) | collective-permute-done | bytes 155680 | tf_op jit(solution)/shard_map/ppermute | solution.py:355
  20.8 0.0 collective-permute-done.refs_1_
  20.8 2.0 %first_pick.1 = (bf16[256,2304]{1,0:T(8,128)(2,1)}, bf16[256,128]{1,0:T(8,128)(2,1)S(1)}) custom-call(s32[1]{0:T(128)} %bitcast.near_ref, bf16[32,2432]{1,0:T(8,128)(2,1)S(1)} %get-tuple-element.40.refs_0_, bf16[32,2432]{1,0:T(8,128)(2,1)S(1)} %collective-permute-done.refs_1_, bf16[32,2432]{1,0:T(8,128)(2,1)S(1)} %collective-permute-done.1.refs_2_, ...), custom_call_target="tpu_custom_call" | custom-call | tf_op jit(solution)/shard_map/first_pick/pallas_call | solution.py:281
  22.8 0.0 collective-permute-done.3.refs_1_
  22.8 0.0 collective-permute-done.4.refs_2_
  22.8 0.0 collective-permute-done.5.refs_3_
  22.8 3.7 %all-to-all-start = ((bf16[4,64,2304]{2,1,0:T(8,128)(2,1)}), bf16[4,64,2304]{2,1,0:T(8,128)(2,1)S(1)}, u32[]{:S(2)}, u32[]{:S(2)}) async-start(bf16[4,64,2304]{2,1,0:T(8,128)(2,1)} %bitcast.6), calls=%async_computation | async-start | bytes 2359296 | tf_op jit(solution)/shard_map/all_to_all | solution.py:383
  26.5 1.2 %collective-permute-start.8 = (bf16[32,1792]{1,0:T(8,128)(2,1)S(1)}, bf16[32,1792]{1,0:T(8,128)(2,1)S(1)}, u32[]{:S(2)}, u32[]{:S(2)}) collective-permute-start(bf16[32,1792]{1,0:T(8,128)(2,1)S(1)} %get-tuple-element.48.refs_0_), channel_id=1, source_target_pairs={{0,3},{1,0},{2,1},{3,2},{4,7},{5,4},{6,5},{7,6},{8,11},{9,8},{10,9... | collective-permute-start | bytes 344072 | tf_op jit(solution)/shard_map/ppermute | solution.py:355
  27.8 1.6 %collective-permute-start.7 = (bf16[32,1792]{1,0:T(8,128)(2,1)S(1)}, bf16[32,1792]{1,0:T(8,128)(2,1)S(1)}, u32[]{:S(2)}, u32[]{:S(2)}) collective-permute-start(bf16[32,1792]{1,0:T(8,128)(2,1)S(1)} %get-tuple-element.48.refs_0_), channel_id=1, source_target_pairs={{0,2},{1,3},{2,0},{3,1},{4,6},{5,7},{6,4},{7,5},{8,10},{9,11},{10,... | collective-permute-start | bytes 344072 | tf_op jit(solution)/shard_map/ppermute | solution.py:355
  29.3 2.0 %collective-permute-start.6 = (bf16[32,1792]{1,0:T(8,128)(2,1)S(1)}, bf16[32,1792]{1,0:T(8,128)(2,1)S(1)}, u32[]{:S(2)}, u32[]{:S(2)}) collective-permute-start(bf16[32,1792]{1,0:T(8,128)(2,1)S(1)} %get-tuple-element.48.refs_0_), channel_id=1, source_target_pairs={{0,1},{1,2},{2,3},{3,0},{4,5},{5,6},{6,7},{7,4},{8,9},{9,10},{10,1... | collective-permute-start | bytes 344072 | tf_op jit(solution)/shard_map/ppermute | solution.py:355
  31.4 0.8 %collective-permute-done.8.refs_3_ = bf16[32,1792]{1,0:T(8,128)(2,1)S(1)} collective-permute-done((bf16[32,1792]{1,0:T(8,128)(2,1)S(1)}, bf16[32,1792]{1,0:T(8,128)(2,1)S(1)}, u32[]{:S(2)}, u32[]{:S(2)}) %collective-permute-start.8) | collective-permute-done | bytes 114720 | tf_op jit(solution)/shard_map/ppermute | solution.py:355
  32.2 6.9 %collective-permute-done.7.refs_2_ = bf16[32,1792]{1,0:T(8,128)(2,1)S(1)} collective-permute-done((bf16[32,1792]{1,0:T(8,128)(2,1)S(1)}, bf16[32,1792]{1,0:T(8,128)(2,1)S(1)}, u32[]{:S(2)}, u32[]{:S(2)}) %collective-permute-start.7) | collective-permute-done | bytes 114720 | tf_op jit(solution)/shard_map/ppermute | solution.py:355
  39.1 0.0 collective-permute-done.6.refs_1_
  39.1 1.3 %pick_rows.1 = bf16[256,1792]{1,0:T(8,128)(2,1)} custom-call(bf16[256,128]{1,0:T(8,128)(2,1)S(1)} %get-tuple-element.41.pick_ref, bf16[32,1792]{1,0:T(8,128)(2,1)S(1)} %get-tuple-element.48.refs_0_, bf16[32,1792]{1,0:T(8,128)(2,1)S(1)} %collective-permute-done.6.refs_1_, bf16[32,1792]{1,0:T(8,128)(2,1)S(1)} %collective-permute-done.7.refs_2_, ...), custom_call_target="tpu_custom_call" | custom-call | tf_op jit(solution)/shard_map/pick_rows/pallas_call | solution.py:296
  40.4 0.8 %all-to-all-done = bf16[4,64,2304]{2,1,0:T(8,128)(2,1)S(1)} async-done(((bf16[4,64,2304]{2,1,0:T(8,128)(2,1)}), bf16[4,64,2304]{2,1,0:T(8,128)(2,1)S(1)}, u32[]{:S(2)}, u32[]{:S(2)}) %all-to-all-start) | async-done | bytes 1179680 | tf_op jit(solution)/shard_map/all_to_all | solution.py:383
  41.3 3.5 %all-to-all-start.1 = ((bf16[4,64,1792]{2,1,0:T(8,128)(2,1)}), bf16[4,64,1792]{2,1,0:T(8,128)(2,1)S(1)}, u32[]{:S(2)}, u32[]{:S(2)}) async-start(bf16[4,64,1792]{2,1,0:T(8,128)(2,1)} %bitcast.8), calls=%async_computation.1 | async-start | bytes 1835008 | tf_op jit(solution)/shard_map/all_to_all | solution.py:383
  44.8 0.4 regroup_rows.1
  45.2 0.7 collective-permute-start.9
  45.9 2.0 %collective-permute-start.10 = (bf16[64,768]{1,0:T(8,128)(2,1)S(1)}, bf16[64,768]{1,0:T(8,128)(2,1)S(1)}, u32[]{:S(2)}, u32[]{:S(2)}) collective-permute-start(bf16[64,768]{1,0:T(8,128)(2,1)S(1)} %get-tuple-element.62), channel_id=1, source_target_pairs={{0,2},{1,3},{2,0},{3,1},{4,6},{5,7},{6,4},{7,5},{8,10},{9,11},{10,... | collective-permute-start | bytes 294920 | tf_op jit(solution)/shard_map/ppermute | solution.py:355
  47.9 2.8 %collective-permute-start.11 = (bf16[64,768]{1,0:T(8,128)(2,1)S(1)}, bf16[64,768]{1,0:T(8,128)(2,1)S(1)}, u32[]{:S(2)}, u32[]{:S(2)}) collective-permute-start(bf16[64,768]{1,0:T(8,128)(2,1)S(1)} %get-tuple-element.63), channel_id=1, source_target_pairs={{0,3},{1,0},{2,1},{3,2},{4,7},{5,4},{6,5},{7,6},{8,11},{9,8},{10,9... | collective-permute-start | bytes 294920 | tf_op jit(solution)/shard_map/ppermute | solution.py:355
  50.7 4.0 %fusion = f32[256,768]{1,0:T(8,128)} fusion(bf16[256,2304]{1,0:T(8,128)(2,1)S(1)} %bitcast.19, bf16[768,4096]{1,0:T(8,128)(2,1)} %bitcast.32), kind=kOutput, calls=%fused_computation | convolution fusion | flops 905969664 | bytes 5505024 | tf_op jit(solution)/shard_map/dot_general | solution.py:392
  54.7 0.6 collective-permute-done.10.refs_2_
  55.4 0.0 copy-start.7
  55.4 1.1 %all-to-all-done.1 = bf16[4,64,1792]{2,1,0:T(8,128)(2,1)S(1)} async-done(((bf16[4,64,1792]{2,1,0:T(8,128)(2,1)}), bf16[4,64,1792]{2,1,0:T(8,128)(2,1)S(1)}, u32[]{:S(2)}, u32[]{:S(2)}) %all-to-all-start.1) | async-done | bytes 917536 | tf_op jit(solution)/shard_map/all_to_all | solution.py:383
  56.4 2.7 %fusion.2 = f32[256,768]{1,0:T(8,128)S(1)} fusion(bf16[256,1792]{1,0:T(8,128)(2,1)S(1)} %bitcast.22, bf16[768,4096]{1,0:T(8,128)(2,1)} %bitcast.33), kind=kOutput, calls=%fused_computation.2 | convolution fusion | flops 704643072 | bytes 4456448 | tf_op jit(solution)/shard_map/dot_general | solution.py:392
  59.1 0.8 %add_convert_fusion = bf16[256,768]{1,0:T(8,128)(2,1)} fusion(f32[256,768]{1,0:T(8,128)S(1)} %copy-done.7, f32[256,768]{1,0:T(8,128)S(1)} %fusion.2), kind=kLoop, calls=%fused_computation.4 | loop fusion | flops 393216 | bytes 1966080 | tf_op jit(solution)/shard_map/convert_element_type | solution.py:400
  60.0 5.9 %all-to-all-start.2 = ((bf16[16,16,768]{2,1,0:T(8,128)(2,1)}), bf16[16,16,768]{2,1,0:T(8,128)(2,1)S(1)}, u32[]{:S(2)}, u32[]{:S(2)}) async-start(bf16[16,16,768]{2,1,0:T(8,128)(2,1)} %bitcast.11), calls=%async_computation.2 | async-start | bytes 786432 | tf_op jit(solution)/shard_map/all_to_all | solution.py:399
  65.9 0.0 copy-start.1
  65.9 0.0 copy-start.6
  65.9 0.2 collective-permute-start.14
  66.1 1.6 %collective-permute-done.14.refs_5_ = bf16[64,3072]{1,0:T(8,128)(2,1)S(1)} collective-permute-done((bf16[64,3072]{1,0:T(8,128)(2,1)S(1)}, bf16[64,3072]{1,0:T(8,128)(2,1)S(1)}, u32[]{:S(2)}, u32[]{:S(2)}) %collective-permute-start.14) | collective-permute-done | bytes 393248 | tf_op jit(solution)/shard_map/ppermute | solution.py:361
  67.7 10.3 %down_rows.1 = bf16[384,4096]{1,0:T(8,128)(2,1)} custom-call(s32[3]{0:T(128)S(1)} %pad_add_fusion.scalars_ref, bf16[256,2304]{1,0:T(8,128)(2,1)S(1)} %bitcast.20, bf16[256,1792]{1,0:T(8,128)(2,1)S(1)} %bitcast.23, bf16[256,2304]{1,0:T(8,128)(2,1)} %collective-permute-done.12.refs_2_, bf16[256,1792]{1,0:T(8,128)(2,1)} %collective-permute-done.13.refs_3_, ...), custom_call_target="tpu_custom_call" | custom-call | flops 1610612736 | bytes 7340032 | tf_op jit(solution)/shard_map/down_rows/pallas_call | solution.py:324
  78.0 1.9 %all-to-all-done.2 = bf16[16,16,768]{2,1,0:T(8,128)(2,1)S(1)} async-done(((bf16[16,16,768]{2,1,0:T(8,128)(2,1)}), bf16[16,16,768]{2,1,0:T(8,128)(2,1)S(1)}, u32[]{:S(2)}, u32[]{:S(2)}) %all-to-all-start.2) | async-done | bytes 393248 | tf_op jit(solution)/shard_map/all_to_all | solution.py:399
  79.9 1.4 %close_rows.1 = (bf16[256,768]{1,0:T(8,128)(2,1)}, f32[8,32]{1,0:T(8,128)}) custom-call(bf16[256,256]{1,0:T(8,128)(2,1)S(1)} %get-tuple-element.39.back_ref, bf16[256,768]{1,0:T(8,128)(2,1)S(1)} %bitcast.26, f32[8,32]{1,0:T(8,128)S(1)} %bitcast.30, bf16[256,768]{1,0:T(8,128)(2,1)S(1)} %bitcast.25), custom_call_target="tpu_custom_call" | custom-call | tf_op jit(solution)/shard_map/close_rows/pallas_call | solution.py:259
  (16 shorter events, 0.1 us)
Async XLA Ops:
  0.6 1.0 %copy-start.2 = (bf16[32,4096]{1,0:T(8,128)(2,1)S(1)}, bf16[32,4096]{1,0:T(8,128)(2,1)}, u32[]{:S(2)}) copy-start(bf16[32,4096]{1,0:T(8,128)(2,1)} %tokens_hbm.1) | copy-start | bytes 786436
  1.6 0.7 copy-start.3
  2.5 12.8 %collective-permute-start.2 = (bf16[32,2432]{1,0:T(8,128)(2,1)S(1)}, bf16[32,2432]{1,0:T(8,128)(2,1)S(1)}, u32[]{:S(2)}, u32[]{:S(2)}) collective-permute-start(bf16[32,2432]{1,0:T(8,128)(2,1)S(1)} %get-tuple-element.40.refs_0_), channel_id=1, source_target_pairs={{0,3},{1,0},{2,1},{3,2},{4,7},{5,4},{6,5},{7,6},{8,11},{9,8},{10,9... | collective-permute-start | bytes 466952 | tf_op jit(solution)/shard_map/ppermute | solution.py:355
  7.6 13.2 %collective-permute-start.1 = (bf16[32,2432]{1,0:T(8,128)(2,1)S(1)}, bf16[32,2432]{1,0:T(8,128)(2,1)S(1)}, u32[]{:S(2)}, u32[]{:S(2)}) collective-permute-start(bf16[32,2432]{1,0:T(8,128)(2,1)S(1)} %get-tuple-element.40.refs_0_), channel_id=1, source_target_pairs={{0,2},{1,3},{2,0},{3,1},{4,6},{5,7},{6,4},{7,5},{8,10},{9,11},{10,... | collective-permute-start | bytes 466952 | tf_op jit(solution)/shard_map/ppermute | solution.py:355
  7.7 13.2 %collective-permute-start = (bf16[32,2432]{1,0:T(8,128)(2,1)S(1)}, bf16[32,2432]{1,0:T(8,128)(2,1)S(1)}, u32[]{:S(2)}, u32[]{:S(2)}) collective-permute-start(bf16[32,2432]{1,0:T(8,128)(2,1)S(1)} %get-tuple-element.40.refs_0_), channel_id=1, source_target_pairs={{0,1},{1,2},{2,3},{3,0},{4,5},{5,6},{6,7},{7,4},{8,9},{9,10},{10,1... | collective-permute-start | bytes 466952 | tf_op jit(solution)/shard_map/ppermute | solution.py:355
  8.7 1.0 %copy-start = (bf16[32,8,768]{2,1,0:T(8,128)(2,1)S(1)}, bf16[32,8,768]{2,1,0:T(8,128)(2,1)}, u32[]{:S(2)}) copy-start(bf16[32,8,768]{2,1,0:T(8,128)(2,1)} %param.6) | copy-start | bytes 1179652
  9.7 0.7 copy-start.4
  10.4 0.7 copy-start.5
  12.2 10.6 %collective-permute-start.3 = (bf16[64,768]{1,0:T(8,128)(2,1)S(1)}, bf16[64,768]{1,0:T(8,128)(2,1)S(1)}, u32[]{:S(2)}, u32[]{:S(2)}) collective-permute-start(bf16[64,768]{1,0:T(8,128)(2,1)S(1)} %get-tuple-element.44), channel_id=1, source_target_pairs={{0,4},{4,0},{8,12},{12,8},{1,5},{5,1},{9,13},{13,9},{2,6},{6,2},{1... | collective-permute-start | bytes 294920 | tf_op jit(solution)/shard_map/ppermute | solution.py:358
  13.8 9.0 %collective-permute-start.4 = (bf16[64,768]{1,0:T(8,128)(2,1)S(1)}, bf16[64,768]{1,0:T(8,128)(2,1)S(1)}, u32[]{:S(2)}, u32[]{:S(2)}) collective-permute-start(bf16[64,768]{1,0:T(8,128)(2,1)S(1)} %get-tuple-element.45), channel_id=1, source_target_pairs={{0,8},{4,12},{8,0},{12,4},{1,9},{5,13},{9,1},{13,5},{2,10},{6,14},... | collective-permute-start | bytes 294920 | tf_op jit(solution)/shard_map/ppermute | solution.py:358
  15.3 7.5 %collective-permute-start.5 = (bf16[64,768]{1,0:T(8,128)(2,1)S(1)}, bf16[64,768]{1,0:T(8,128)(2,1)S(1)}, u32[]{:S(2)}, u32[]{:S(2)}) collective-permute-start(bf16[64,768]{1,0:T(8,128)(2,1)S(1)} %get-tuple-element.46), channel_id=1, source_target_pairs={{0,12},{4,8},{8,4},{12,0},{1,13},{5,9},{9,5},{13,1},{2,14},{6,10},... | collective-permute-start | bytes 294920 | tf_op jit(solution)/shard_map/ppermute | solution.py:358
  22.8 18.5 %all-to-all-start = ((bf16[4,64,2304]{2,1,0:T(8,128)(2,1)}), bf16[4,64,2304]{2,1,0:T(8,128)(2,1)S(1)}, u32[]{:S(2)}, u32[]{:S(2)}) async-start(bf16[4,64,2304]{2,1,0:T(8,128)(2,1)} %bitcast.6), calls=%async_computation | async-start | bytes 2359296 | tf_op jit(solution)/shard_map/all_to_all | solution.py:383
  26.5 5.6 %collective-permute-start.8 = (bf16[32,1792]{1,0:T(8,128)(2,1)S(1)}, bf16[32,1792]{1,0:T(8,128)(2,1)S(1)}, u32[]{:S(2)}, u32[]{:S(2)}) collective-permute-start(bf16[32,1792]{1,0:T(8,128)(2,1)S(1)} %get-tuple-element.48.refs_0_), channel_id=1, source_target_pairs={{0,3},{1,0},{2,1},{3,2},{4,7},{5,4},{6,5},{7,6},{8,11},{9,8},{10,9... | collective-permute-start | bytes 344072 | tf_op jit(solution)/shard_map/ppermute | solution.py:355
  27.8 11.3 %collective-permute-start.7 = (bf16[32,1792]{1,0:T(8,128)(2,1)S(1)}, bf16[32,1792]{1,0:T(8,128)(2,1)S(1)}, u32[]{:S(2)}, u32[]{:S(2)}) collective-permute-start(bf16[32,1792]{1,0:T(8,128)(2,1)S(1)} %get-tuple-element.48.refs_0_), channel_id=1, source_target_pairs={{0,2},{1,3},{2,0},{3,1},{4,6},{5,7},{6,4},{7,5},{8,10},{9,11},{10,... | collective-permute-start | bytes 344072 | tf_op jit(solution)/shard_map/ppermute | solution.py:355
  29.3 9.8 %collective-permute-start.6 = (bf16[32,1792]{1,0:T(8,128)(2,1)S(1)}, bf16[32,1792]{1,0:T(8,128)(2,1)S(1)}, u32[]{:S(2)}, u32[]{:S(2)}) collective-permute-start(bf16[32,1792]{1,0:T(8,128)(2,1)S(1)} %get-tuple-element.48.refs_0_), channel_id=1, source_target_pairs={{0,1},{1,2},{2,3},{3,0},{4,5},{5,6},{6,7},{7,4},{8,9},{9,10},{10,1... | collective-permute-start | bytes 344072 | tf_op jit(solution)/shard_map/ppermute | solution.py:355
  41.3 15.2 %all-to-all-start.1 = ((bf16[4,64,1792]{2,1,0:T(8,128)(2,1)}), bf16[4,64,1792]{2,1,0:T(8,128)(2,1)S(1)}, u32[]{:S(2)}, u32[]{:S(2)}) async-start(bf16[4,64,1792]{2,1,0:T(8,128)(2,1)} %bitcast.8), calls=%async_computation.1 | async-start | bytes 1835008 | tf_op jit(solution)/shard_map/all_to_all | solution.py:383
  45.2 9.5 %collective-permute-start.9 = (bf16[64,768]{1,0:T(8,128)(2,1)S(1)}, bf16[64,768]{1,0:T(8,128)(2,1)S(1)}, u32[]{:S(2)}, u32[]{:S(2)}) collective-permute-start(bf16[64,768]{1,0:T(8,128)(2,1)S(1)} %get-tuple-element.61), channel_id=1, source_target_pairs={{0,1},{1,2},{2,3},{3,0},{4,5},{5,6},{6,7},{7,4},{8,9},{9,10},{10,1... | collective-permute-start | bytes 294920 | tf_op jit(solution)/shard_map/ppermute | solution.py:355
  45.9 9.5 %collective-permute-start.10 = (bf16[64,768]{1,0:T(8,128)(2,1)S(1)}, bf16[64,768]{1,0:T(8,128)(2,1)S(1)}, u32[]{:S(2)}, u32[]{:S(2)}) collective-permute-start(bf16[64,768]{1,0:T(8,128)(2,1)S(1)} %get-tuple-element.62), channel_id=1, source_target_pairs={{0,2},{1,3},{2,0},{3,1},{4,6},{5,7},{6,4},{7,5},{8,10},{9,11},{10,... | collective-permute-start | bytes 294920 | tf_op jit(solution)/shard_map/ppermute | solution.py:355
  47.9 7.5 %collective-permute-start.11 = (bf16[64,768]{1,0:T(8,128)(2,1)S(1)}, bf16[64,768]{1,0:T(8,128)(2,1)S(1)}, u32[]{:S(2)}, u32[]{:S(2)}) collective-permute-start(bf16[64,768]{1,0:T(8,128)(2,1)S(1)} %get-tuple-element.63), channel_id=1, source_target_pairs={{0,3},{1,0},{2,1},{3,2},{4,7},{5,4},{6,5},{7,6},{8,11},{9,8},{10,9... | collective-permute-start | bytes 294920 | tf_op jit(solution)/shard_map/ppermute | solution.py:355
  50.7 17.0 %collective-permute-start.12 = (bf16[256,2304]{1,0:T(8,128)(2,1)S(1)}, bf16[256,2304]{1,0:T(8,128)(2,1)}, u32[]{:S(2)}, u32[]{:S(2)}) collective-permute-start(bf16[256,2304]{1,0:T(8,128)(2,1)S(1)} %bitcast.18), channel_id=1, source_target_pairs={{0,16},{16,0},{1,17},{17,1},{2,18},{18,2},{3,19},{19,3},{4,20},{20... | collective-permute-start | bytes 3538952 | tf_op jit(solution)/shard_map/ppermute | solution.py:361
  55.4 3.8 %copy-start.7 = (f32[256,768]{1,0:T(8,128)S(1)}, f32[256,768]{1,0:T(8,128)}, u32[]{:S(2)}) copy-start(f32[256,768]{1,0:T(8,128)} %fusion) | copy-start | bytes 2359300
  56.4 11.3 %collective-permute-start.13 = (bf16[256,1792]{1,0:T(8,128)(2,1)S(1)}, bf16[256,1792]{1,0:T(8,128)(2,1)}, u32[]{:S(2)}, u32[]{:S(2)}) collective-permute-start(bf16[256,1792]{1,0:T(8,128)(2,1)S(1)} %bitcast.21), channel_id=1, source_target_pairs={{0,16},{16,0},{1,17},{17,1},{2,18},{18,2},{3,19},{19,3},{4,20},{20... | collective-permute-start | bytes 2752520 | tf_op jit(solution)/shard_map/ppermute | solution.py:361
  60.0 19.9 %all-to-all-start.2 = ((bf16[16,16,768]{2,1,0:T(8,128)(2,1)}), bf16[16,16,768]{2,1,0:T(8,128)(2,1)S(1)}, u32[]{:S(2)}, u32[]{:S(2)}) async-start(bf16[16,16,768]{2,1,0:T(8,128)(2,1)} %bitcast.11), calls=%async_computation.2 | async-start | bytes 786432 | tf_op jit(solution)/shard_map/all_to_all | solution.py:399
  65.9 14.0 %copy-start.1 = (bf16[32,8,768]{2,1,0:T(8,128)(2,1)S(1)}, bf16[32,8,768]{2,1,0:T(8,128)(2,1)}, u32[]{:S(2)}) copy-start(bf16[32,8,768]{2,1,0:T(8,128)(2,1)} %param.6) | copy-start | bytes 1179652
  65.9 14.0 %copy-start.6 = (f32[32,8]{0,1:T(8,128)S(1)}, f32[32,8]{0,1:T(8,128)}, u32[]{:S(2)}) copy-start(f32[32,8]{0,1:T(8,128)} %param.7) | copy-start | bytes 3076
  65.9 1.8 %collective-permute-start.14 = (bf16[64,3072]{1,0:T(8,128)(2,1)S(1)}, bf16[64,3072]{1,0:T(8,128)(2,1)S(1)}, u32[]{:S(2)}, u32[]{:S(2)}) collective-permute-start(bf16[64,3072]{1,0:T(8,128)(2,1)S(1)} %join_rows.1.refs_4_), channel_id=1, source_target_pairs={{0,16},{16,0},{1,17},{17,1},{2,18},{18,2},{3,19},{19,3},{4,20},{20... | collective-permute-start | bytes 1179656 | tf_op jit(solution)/shard_map/ppermute | solution.py:361

commit v14 on v13

--- a/solution.py
+++ b/solution.py
@@ -113,7 +113,7 @@
 
 def picked_rows(pick, blocks, out_ref):
     width = out_ref.shape[1]
-    step = TILE
+    step = max(lanes for lanes in range(128, 1025, 128) if width % lanes == 0)
     for start in range(0, width, step):
         tokens = jnp.concatenate([block[:, start : start + step] for block in blocks], axis=0)
         out_ref[:, start : start + step] = exact_dot(pick, tokens).astype(jnp.bfloat16)
@@ -184,17 +184,18 @@
                 total = total + exact_dot(order, ref[:, pl.ds(start, share)])
             turned_ref[:, i * slots : (i + 1) * slots] = total.T.astype(jnp.bfloat16)
 
-    done = 0
-    for part in range(PARTS):
-        steps = rows[part].shape[1] // tile
-
-        @pl.when((step >= done) & (step < done + steps))
-        def _(part=part, done=done):
-            cols = pl.ds(pl.multiple_of((step - done) * tile, 128), tile)
-            tokens = jnp.concatenate([ref[:, cols] for ref in rows[part::PARTS]], axis=0)
+    bounds = part_bounds(sum(ref.shape[1] for ref in rows[:PARTS]))
+    for i in range(bounds[-1][1] // tile):
+
+        @pl.when(step == i)
+        def _(i=i):
+            pieces = []
+            for part, (start, stop) in enumerate(bounds):
+                first, last = max(i * tile, start) - start, min((i + 1) * tile, stop) - start
+                if first < last:
+                    pieces.append(jnp.concatenate([ref[:, first:last] for ref in rows[part::PARTS]], axis=0))
+            tokens = pieces[0] if len(pieces) == 1 else jnp.concatenate(pieces, axis=1)
             out_ref[...] = exact_dot(turned_ref[...], tokens).astype(jnp.bfloat16)
-
-        done += steps
 
 
 def scalar_spec():
@@ -317,9 +318,9 @@
 
 
 def down_rows(near_count, capacity, scalars, rows, hids, share):
-    tile = TILE
     lines = 2 * rows[0].shape[0]
     width = sum(array.shape[1] for array in rows[:PARTS])
+    tile = 2 * TILE
     whole = lambda array: pl.BlockSpec(array.shape, lambda i: (0, 0))
     return pl.pallas_call(
         functools.partial(down_kernel, near_count, capacity),

time: 81.9 us -> 81.9 us (level)
  waiting for transfers between devices: 18.8 us -> 21.6 us
  Pallas kernels: 16.7 us -> 14 us
    all_to_all x1, waiting for transfers between devices: 1.91 us -> 4.66 us  [local(): lax.all_to_all(total.astype(jnp.bfloat16).reshape(experts, capacity, hidd...]
    pallas_call x1, Pallas kernels: 10.3 us -> 7.51 us  [down_rows(): pl.pallas_call(functools.partial(down_kernel, near_count, capacity), grid...]
  transfers between devices with their start and end apart: 18 -> 18, of which waited for: 8 -> 8; matrix products, arithmetic and copies ran while one was open for 9% -> 9% of each run, Pallas kernels for 19% -> 15%
where the time goes in v14:
time: 81.9 us; the launch traced here: 81.2 us
  starting transfers between devices  33.4 us (41%)
  waiting for transfers between devices  21.6 us (26%)
  Pallas kernels  14 us (17%)
  matrix products  6.67 us (8%)
  local copies, waits for them, and re-layouts  4.02 us (5%)
  other arithmetic  0.92 us (1%)
    ppermute x9, starting transfers between devices, along(): lax.ppermute(array, 'near', [(i, (i + steps) % near_count) for i in range...  16.5 us
    ppermute x9, waiting for transfers between devices, along(): lax.ppermute(array, 'near', [(i, (i + steps) % near_count) for i in range...  13.4 us
    pallas_call x1, Pallas kernels, down_rows(): pl.pallas_call(functools.partial(down_kernel, near_count, capacity), grid...  7.51 us
    all_to_all x2, starting transfers between devices, local(): lax.all_to_all(picked.reshape(far_count, -1, picked.shape[1]), 'far', spl...  7.23 us
    dot_general x2, matrix products, local(): lax.dot_general(rows[i], weight[:, bounds[i][0]:bounds[i][1]], (((1,), (1...  6.67 us
    all_to_all x1, starting transfers between devices, local(): lax.all_to_all(total.astype(jnp.bfloat16).reshape(experts, capacity, hidd...  5.89 us
    all_to_all x1, waiting for transfers between devices, local(): lax.all_to_all(total.astype(jnp.bfloat16).reshape(experts, capacity, hidd...  4.66 us
    unnamed x16, local copies, waits for them, and re-layouts  4.02 us
  transfers between devices with their start and end apart: 18, of which 8 were waited for; matrix products, arithmetic and copies ran while one was open for 9% of the time, Pallas kernels for 15%

profile of v14, /device:TPU:0, one launch (start us, length us, event | category | flops | bytes accessed | tf_op | source)
XLA Modules:
  0.0 81.2 jit_solution(10843836590048051091)
XLA Ops:
  0.6 0.9 %copy-done.2 = bf16[32,4096]{1,0:T(8,128)(2,1)S(1)} copy-done((bf16[32,4096]{1,0:T(8,128)(2,1)S(1)}, bf16[32,4096]{1,0:T(8,128)(2,1)}, u32[]{:S(2)}) %copy-start.2) | copy-done | bytes 262168
  1.6 0.7 copy-done.3
  2.3 0.3 split_rows.1
  2.5 5.1 %collective-permute-start.2 = (bf16[32,2432]{1,0:T(8,128)(2,1)S(1)}, bf16[32,2432]{1,0:T(8,128)(2,1)S(1)}, u32[]{:S(2)}, u32[]{:S(2)}) collective-permute-start(bf16[32,2432]{1,0:T(8,128)(2,1)S(1)} %get-tuple-element.40.refs_0_), channel_id=1, source_target_pairs={{0,3},{1,0},{2,1},{3,2},{4,7},{5,4},{6,5},{7,6},{8,11},{9,8},{10,9... | collective-permute-start | bytes 466952 | tf_op jit(solution)/shard_map/ppermute | solution.py:356
  7.6 0.0 collective-permute-start.1
  7.7 1.0 %collective-permute-start = (bf16[32,2432]{1,0:T(8,128)(2,1)S(1)}, bf16[32,2432]{1,0:T(8,128)(2,1)S(1)}, u32[]{:S(2)}, u32[]{:S(2)}) collective-permute-start(bf16[32,2432]{1,0:T(8,128)(2,1)S(1)} %get-tuple-element.40.refs_0_), channel_id=1, source_target_pairs={{0,1},{1,2},{2,3},{3,0},{4,5},{5,6},{6,7},{7,4},{8,9},{9,10},{10,1... | collective-permute-start | bytes 466952 | tf_op jit(solution)/shard_map/ppermute | solution.py:356
  8.7 0.1 pad_add_fusion.scalars_ref
  8.7 1.0 %copy-done = bf16[32,8,768]{2,1,0:T(8,128)(2,1)S(1)} copy-done((bf16[32,8,768]{2,1,0:T(8,128)(2,1)S(1)}, bf16[32,8,768]{2,1,0:T(8,128)(2,1)}, u32[]{:S(2)}) %copy-start) | copy-done | bytes 393240
  9.7 0.7 copy-done.4
  10.4 0.7 copy-done.5
  11.1 1.1 %send_rows.1 = (bf16[64,768]{1,0:T(8,128)(2,1)S(1)}, bf16[64,768]{1,0:T(8,128)(2,1)S(1)}, bf16[64,768]{1,0:T(8,128)(2,1)S(1)}, bf16[64,768]{1,0:T(8,128)(2,1)S(1)}, bf16[256,256]{1,0:T(8,128)(2,1)S(1)}) custom-call(s32[3]{0:T(128)S(1)} %pad_add_fusion.scalars_ref, s32[8,32]{1,0:T(8,128)S(1)} %bitcast.28, f32[8,32]{1,0:T(8,128)S(1)} %bitcast.29, ...), custom_call_target="tpu_custom_call" | custom-call | flops 100663296 | bytes 786432 | tf_op jit(solution)/shard_map/send_rows/pallas_call | solution.py:234
  12.2 1.6 %collective-permute-start.3 = (bf16[64,768]{1,0:T(8,128)(2,1)S(1)}, bf16[64,768]{1,0:T(8,128)(2,1)S(1)}, u32[]{:S(2)}, u32[]{:S(2)}) collective-permute-start(bf16[64,768]{1,0:T(8,128)(2,1)S(1)} %get-tuple-element.44), channel_id=1, source_target_pairs={{0,4},{4,0},{8,12},{12,8},{1,5},{5,1},{9,13},{13,9},{2,6},{6,2},{1... | collective-permute-start | bytes 294920 | tf_op jit(solution)/shard_map/ppermute | solution.py:359
  13.8 1.5 %collective-permute-start.4 = (bf16[64,768]{1,0:T(8,128)(2,1)S(1)}, bf16[64,768]{1,0:T(8,128)(2,1)S(1)}, u32[]{:S(2)}, u32[]{:S(2)}) collective-permute-start(bf16[64,768]{1,0:T(8,128)(2,1)S(1)} %get-tuple-element.45), channel_id=1, source_target_pairs={{0,8},{4,12},{8,0},{12,4},{1,9},{5,13},{9,1},{13,5},{2,10},{6,14},... | collective-permute-start | bytes 294920 | tf_op jit(solution)/shard_map/ppermute | solution.py:359
  15.3 0.0 collective-permute-done.2.refs_3_
  15.3 0.5 collective-permute-start.5
  15.8 5.0 %collective-permute-done.1.refs_2_ = bf16[32,2432]{1,0:T(8,128)(2,1)S(1)} collective-permute-done((bf16[32,2432]{1,0:T(8,128)(2,1)S(1)}, bf16[32,2432]{1,0:T(8,128)(2,1)S(1)}, u32[]{:S(2)}, u32[]{:S(2)}) %collective-permute-start.1) | collective-permute-done | bytes 155680 | tf_op jit(solution)/shard_map/ppermute | solution.py:356
  20.8 2.0 %first_pick.1 = (bf16[256,2304]{1,0:T(8,128)(2,1)}, bf16[256,128]{1,0:T(8,128)(2,1)S(1)}) custom-call(s32[1]{0:T(128)} %bitcast.near_ref, bf16[32,2432]{1,0:T(8,128)(2,1)S(1)} %get-tuple-element.40.refs_0_, bf16[32,2432]{1,0:T(8,128)(2,1)S(1)} %collective-permute-done.refs_1_, bf16[32,2432]{1,0:T(8,128)(2,1)S(1)} %collective-permute-done.1.refs_2_, ...), custom_call_target="tpu_custom_call" | custom-call | tf_op jit(solution)/shard_map/first_pick/pallas_call | solution.py:282
  22.8 0.0 collective-permute-done.3.refs_1_
  22.8 3.7 %all-to-all-start = ((bf16[4,64,2304]{2,1,0:T(8,128)(2,1)}), bf16[4,64,2304]{2,1,0:T(8,128)(2,1)S(1)}, u32[]{:S(2)}, u32[]{:S(2)}) async-start(bf16[4,64,2304]{2,1,0:T(8,128)(2,1)} %bitcast.6), calls=%async_computation | async-start | bytes 2359296 | tf_op jit(solution)/shard_map/all_to_all | solution.py:384
  26.5 1.2 %collective-permute-start.8 = (bf16[32,1792]{1,0:T(8,128)(2,1)S(1)}, bf16[32,1792]{1,0:T(8,128)(2,1)S(1)}, u32[]{:S(2)}, u32[]{:S(2)}) collective-permute-start(bf16[32,1792]{1,0:T(8,128)(2,1)S(1)} %get-tuple-element.48.refs_0_), channel_id=1, source_target_pairs={{0,3},{1,0},{2,1},{3,2},{4,7},{5,4},{6,5},{7,6},{8,11},{9,8},{10,9... | collective-permute-start | bytes 344072 | tf_op jit(solution)/shard_map/ppermute | solution.py:356
  27.8 1.6 %collective-permute-start.7 = (bf16[32,1792]{1,0:T(8,128)(2,1)S(1)}, bf16[32,1792]{1,0:T(8,128)(2,1)S(1)}, u32[]{:S(2)}, u32[]{:S(2)}) collective-permute-start(bf16[32,1792]{1,0:T(8,128)(2,1)S(1)} %get-tuple-element.48.refs_0_), channel_id=1, source_target_pairs={{0,2},{1,3},{2,0},{3,1},{4,6},{5,7},{6,4},{7,5},{8,10},{9,11},{10,... | collective-permute-start | bytes 344072 | tf_op jit(solution)/shard_map/ppermute | solution.py:356
  29.3 2.0 %collective-permute-start.6 = (bf16[32,1792]{1,0:T(8,128)(2,1)S(1)}, bf16[32,1792]{1,0:T(8,128)(2,1)S(1)}, u32[]{:S(2)}, u32[]{:S(2)}) collective-permute-start(bf16[32,1792]{1,0:T(8,128)(2,1)S(1)} %get-tuple-element.48.refs_0_), channel_id=1, source_target_pairs={{0,1},{1,2},{2,3},{3,0},{4,5},{5,6},{6,7},{7,4},{8,9},{9,10},{10,1... | collective-permute-start | bytes 344072 | tf_op jit(solution)/shard_map/ppermute | solution.py:356
  31.4 0.8 %collective-permute-done.8.refs_3_ = bf16[32,1792]{1,0:T(8,128)(2,1)S(1)} collective-permute-done((bf16[32,1792]{1,0:T(8,128)(2,1)S(1)}, bf16[32,1792]{1,0:T(8,128)(2,1)S(1)}, u32[]{:S(2)}, u32[]{:S(2)}) %collective-permute-start.8) | collective-permute-done | bytes 114720 | tf_op jit(solution)/shard_map/ppermute | solution.py:356
  32.2 6.9 %collective-permute-done.7.refs_2_ = bf16[32,1792]{1,0:T(8,128)(2,1)S(1)} collective-permute-done((bf16[32,1792]{1,0:T(8,128)(2,1)S(1)}, bf16[32,1792]{1,0:T(8,128)(2,1)S(1)}, u32[]{:S(2)}, u32[]{:S(2)}) %collective-permute-start.7) | collective-permute-done | bytes 114720 | tf_op jit(solution)/shard_map/ppermute | solution.py:356
  39.1 0.0 collective-permute-done.6.refs_1_
  39.1 1.3 %pick_rows.1 = bf16[256,1792]{1,0:T(8,128)(2,1)} custom-call(bf16[256,128]{1,0:T(8,128)(2,1)S(1)} %get-tuple-element.41.pick_ref, bf16[32,1792]{1,0:T(8,128)(2,1)S(1)} %get-tuple-element.48.refs_0_, bf16[32,1792]{1,0:T(8,128)(2,1)S(1)} %collective-permute-done.6.refs_1_, bf16[32,1792]{1,0:T(8,128)(2,1)S(1)} %collective-permute-done.7.refs_2_, ...), custom_call_target="tpu_custom_call" | custom-call | tf_op jit(solution)/shard_map/pick_rows/pallas_call | solution.py:297
  40.4 0.8 %all-to-all-done = bf16[4,64,2304]{2,1,0:T(8,128)(2,1)S(1)} async-done(((bf16[4,64,2304]{2,1,0:T(8,128)(2,1)}), bf16[4,64,2304]{2,1,0:T(8,128)(2,1)S(1)}, u32[]{:S(2)}, u32[]{:S(2)}) %all-to-all-start) | async-done | bytes 1179680 | tf_op jit(solution)/shard_map/all_to_all | solution.py:384
  41.3 3.5 %all-to-all-start.1 = ((bf16[4,64,1792]{2,1,0:T(8,128)(2,1)}), bf16[4,64,1792]{2,1,0:T(8,128)(2,1)S(1)}, u32[]{:S(2)}, u32[]{:S(2)}) async-start(bf16[4,64,1792]{2,1,0:T(8,128)(2,1)} %bitcast.8), calls=%async_computation.1 | async-start | bytes 1835008 | tf_op jit(solution)/shard_map/all_to_all | solution.py:384
  44.8 0.4 regroup_rows.1
  45.2 0.7 collective-permute-start.9
  45.9 2.0 %collective-permute-start.10 = (bf16[64,768]{1,0:T(8,128)(2,1)S(1)}, bf16[64,768]{1,0:T(8,128)(2,1)S(1)}, u32[]{:S(2)}, u32[]{:S(2)}) collective-permute-start(bf16[64,768]{1,0:T(8,128)(2,1)S(1)} %get-tuple-element.62), channel_id=1, source_target_pairs={{0,2},{1,3},{2,0},{3,1},{4,6},{5,7},{6,4},{7,5},{8,10},{9,11},{10,... | collective-permute-start | bytes 294920 | tf_op jit(solution)/shard_map/ppermute | solution.py:356
  47.9 2.8 %collective-permute-start.11 = (bf16[64,768]{1,0:T(8,128)(2,1)S(1)}, bf16[64,768]{1,0:T(8,128)(2,1)S(1)}, u32[]{:S(2)}, u32[]{:S(2)}) collective-permute-start(bf16[64,768]{1,0:T(8,128)(2,1)S(1)} %get-tuple-element.63), channel_id=1, source_target_pairs={{0,3},{1,0},{2,1},{3,2},{4,7},{5,4},{6,5},{7,6},{8,11},{9,8},{10,9... | collective-permute-start | bytes 294920 | tf_op jit(solution)/shard_map/ppermute | solution.py:356
  50.7 0.0 collective-permute-start.12
  50.7 4.0 %fusion = f32[256,768]{1,0:T(8,128)} fusion(bf16[256,2304]{1,0:T(8,128)(2,1)S(1)} %bitcast.19, bf16[768,4096]{1,0:T(8,128)(2,1)} %bitcast.32), kind=kOutput, calls=%fused_computation | convolution fusion | flops 905969664 | bytes 5505024 | tf_op jit(solution)/shard_map/dot_general | solution.py:393
  54.7 0.0 collective-permute-done.9.refs_1_
  54.7 0.6 collective-permute-done.10.refs_2_
  55.4 0.0 copy-start.7
  55.4 1.1 %all-to-all-done.1 = bf16[4,64,1792]{2,1,0:T(8,128)(2,1)S(1)} async-done(((bf16[4,64,1792]{2,1,0:T(8,128)(2,1)}), bf16[4,64,1792]{2,1,0:T(8,128)(2,1)S(1)}, u32[]{:S(2)}, u32[]{:S(2)}) %all-to-all-start.1) | async-done | bytes 917536 | tf_op jit(solution)/shard_map/all_to_all | solution.py:384
  56.4 2.7 %fusion.2 = f32[256,768]{1,0:T(8,128)S(1)} fusion(bf16[256,1792]{1,0:T(8,128)(2,1)S(1)} %bitcast.22, bf16[768,4096]{1,0:T(8,128)(2,1)} %bitcast.33), kind=kOutput, calls=%fused_computation.2 | convolution fusion | flops 704643072 | bytes 4456448 | tf_op jit(solution)/shard_map/dot_general | solution.py:393
  59.1 0.8 %add_convert_fusion = bf16[256,768]{1,0:T(8,128)(2,1)} fusion(f32[256,768]{1,0:T(8,128)S(1)} %copy-done.7, f32[256,768]{1,0:T(8,128)S(1)} %fusion.2), kind=kLoop, calls=%fused_computation.4 | loop fusion | flops 393216 | bytes 1966080 | tf_op jit(solution)/shard_map/convert_element_type | solution.py:401
  60.0 5.9 %all-to-all-start.2 = ((bf16[16,16,768]{2,1,0:T(8,128)(2,1)}), bf16[16,16,768]{2,1,0:T(8,128)(2,1)S(1)}, u32[]{:S(2)}, u32[]{:S(2)}) async-start(bf16[16,16,768]{2,1,0:T(8,128)(2,1)} %bitcast.11), calls=%async_computation.2 | async-start | bytes 786432 | tf_op jit(solution)/shard_map/all_to_all | solution.py:400
  65.9 0.0 copy-start.1
  65.9 0.0 copy-start.6
  65.9 0.2 collective-permute-start.14
  66.1 1.6 %collective-permute-done.14.refs_5_ = bf16[64,3072]{1,0:T(8,128)(2,1)S(1)} collective-permute-done((bf16[64,3072]{1,0:T(8,128)(2,1)S(1)}, bf16[64,3072]{1,0:T(8,128)(2,1)S(1)}, u32[]{:S(2)}, u32[]{:S(2)}) %collective-permute-start.14) | collective-permute-done | bytes 393248 | tf_op jit(solution)/shard_map/ppermute | solution.py:362
  67.7 7.5 %down_rows.1 = bf16[384,4096]{1,0:T(8,128)(2,1)} custom-call(s32[3]{0:T(128)S(1)} %pad_add_fusion.scalars_ref, bf16[256,2304]{1,0:T(8,128)(2,1)S(1)} %bitcast.20, bf16[256,1792]{1,0:T(8,128)(2,1)S(1)} %bitcast.23, bf16[256,2304]{1,0:T(8,128)(2,1)} %collective-permute-done.12.refs_2_, bf16[256,1792]{1,0:T(8,128)(2,1)} %collective-permute-done.13.refs_3_, ...), custom_call_target="tpu_custom_call" | custom-call | flops 1610612736 | bytes 7340032 | tf_op jit(solution)/shard_map/down_rows/pallas_call | solution.py:325
  75.2 4.7 %all-to-all-done.2 = bf16[16,16,768]{2,1,0:T(8,128)(2,1)S(1)} async-done(((bf16[16,16,768]{2,1,0:T(8,128)(2,1)}), bf16[16,16,768]{2,1,0:T(8,128)(2,1)S(1)}, u32[]{:S(2)}, u32[]{:S(2)}) %all-to-all-start.2) | async-done | bytes 393248 | tf_op jit(solution)/shard_map/all_to_all | solution.py:400
  79.9 1.4 %close_rows.1 = (bf16[256,768]{1,0:T(8,128)(2,1)}, f32[8,32]{1,0:T(8,128)}) custom-call(bf16[256,256]{1,0:T(8,128)(2,1)S(1)} %get-tuple-element.39.back_ref, bf16[256,768]{1,0:T(8,128)(2,1)S(1)} %bitcast.26, f32[8,32]{1,0:T(8,128)S(1)} %bitcast.30, bf16[256,768]{1,0:T(8,128)(2,1)S(1)} %bitcast.25), custom_call_target="tpu_custom_call" | custom-call | tf_op jit(solution)/shard_map/close_rows/pallas_call | solution.py:260
  (16 shorter events, 0.1 us)
Async XLA Ops:
  0.6 1.0 %copy-start.2 = (bf16[32,4096]{1,0:T(8,128)(2,1)S(1)}, bf16[32,4096]{1,0:T(8,128)(2,1)}, u32[]{:S(2)}) copy-start(bf16[32,4096]{1,0:T(8,128)(2,1)} %tokens_hbm.1) | copy-start | bytes 786436
  1.6 0.7 copy-start.3
  2.5 12.8 %collective-permute-start.2 = (bf16[32,2432]{1,0:T(8,128)(2,1)S(1)}, bf16[32,2432]{1,0:T(8,128)(2,1)S(1)}, u32[]{:S(2)}, u32[]{:S(2)}) collective-permute-start(bf16[32,2432]{1,0:T(8,128)(2,1)S(1)} %get-tuple-element.40.refs_0_), channel_id=1, source_target_pairs={{0,3},{1,0},{2,1},{3,2},{4,7},{5,4},{6,5},{7,6},{8,11},{9,8},{10,9... | collective-permute-start | bytes 466952 | tf_op jit(solution)/shard_map/ppermute | solution.py:356
  7.6 13.2 %collective-permute-start.1 = (bf16[32,2432]{1,0:T(8,128)(2,1)S(1)}, bf16[32,2432]{1,0:T(8,128)(2,1)S(1)}, u32[]{:S(2)}, u32[]{:S(2)}) collective-permute-start(bf16[32,2432]{1,0:T(8,128)(2,1)S(1)} %get-tuple-element.40.refs_0_), channel_id=1, source_target_pairs={{0,2},{1,3},{2,0},{3,1},{4,6},{5,7},{6,4},{7,5},{8,10},{9,11},{10,... | collective-permute-start | bytes 466952 | tf_op jit(solution)/shard_map/ppermute | solution.py:356
  7.7 13.2 %collective-permute-start = (bf16[32,2432]{1,0:T(8,128)(2,1)S(1)}, bf16[32,2432]{1,0:T(8,128)(2,1)S(1)}, u32[]{:S(2)}, u32[]{:S(2)}) collective-permute-start(bf16[32,2432]{1,0:T(8,128)(2,1)S(1)} %get-tuple-element.40.refs_0_), channel_id=1, source_target_pairs={{0,1},{1,2},{2,3},{3,0},{4,5},{5,6},{6,7},{7,4},{8,9},{9,10},{10,1... | collective-permute-start | bytes 466952 | tf_op jit(solution)/shard_map/ppermute | solution.py:356
  8.7 1.0 %copy-start = (bf16[32,8,768]{2,1,0:T(8,128)(2,1)S(1)}, bf16[32,8,768]{2,1,0:T(8,128)(2,1)}, u32[]{:S(2)}) copy-start(bf16[32,8,768]{2,1,0:T(8,128)(2,1)} %param.6) | copy-start | bytes 1179652
  9.7 0.7 copy-start.4
  10.4 0.7 copy-start.5
  12.2 10.6 %collective-permute-start.3 = (bf16[64,768]{1,0:T(8,128)(2,1)S(1)}, bf16[64,768]{1,0:T(8,128)(2,1)S(1)}, u32[]{:S(2)}, u32[]{:S(2)}) collective-permute-start(bf16[64,768]{1,0:T(8,128)(2,1)S(1)} %get-tuple-element.44), channel_id=1, source_target_pairs={{0,4},{4,0},{8,12},{12,8},{1,5},{5,1},{9,13},{13,9},{2,6},{6,2},{1... | collective-permute-start | bytes 294920 | tf_op jit(solution)/shard_map/ppermute | solution.py:359
  13.8 9.0 %collective-permute-start.4 = (bf16[64,768]{1,0:T(8,128)(2,1)S(1)}, bf16[64,768]{1,0:T(8,128)(2,1)S(1)}, u32[]{:S(2)}, u32[]{:S(2)}) collective-permute-start(bf16[64,768]{1,0:T(8,128)(2,1)S(1)} %get-tuple-element.45), channel_id=1, source_target_pairs={{0,8},{4,12},{8,0},{12,4},{1,9},{5,13},{9,1},{13,5},{2,10},{6,14},... | collective-permute-start | bytes 294920 | tf_op jit(solution)/shard_map/ppermute | solution.py:359
  15.3 7.5 %collective-permute-start.5 = (bf16[64,768]{1,0:T(8,128)(2,1)S(1)}, bf16[64,768]{1,0:T(8,128)(2,1)S(1)}, u32[]{:S(2)}, u32[]{:S(2)}) collective-permute-start(bf16[64,768]{1,0:T(8,128)(2,1)S(1)} %get-tuple-element.46), channel_id=1, source_target_pairs={{0,12},{4,8},{8,4},{12,0},{1,13},{5,9},{9,5},{13,1},{2,14},{6,10},... | collective-permute-start | bytes 294920 | tf_op jit(solution)/shard_map/ppermute | solution.py:359
  22.8 18.5 %all-to-all-start = ((bf16[4,64,2304]{2,1,0:T(8,128)(2,1)}), bf16[4,64,2304]{2,1,0:T(8,128)(2,1)S(1)}, u32[]{:S(2)}, u32[]{:S(2)}) async-start(bf16[4,64,2304]{2,1,0:T(8,128)(2,1)} %bitcast.6), calls=%async_computation | async-start | bytes 2359296 | tf_op jit(solution)/shard_map/all_to_all | solution.py:384
  26.5 5.6 %collective-permute-start.8 = (bf16[32,1792]{1,0:T(8,128)(2,1)S(1)}, bf16[32,1792]{1,0:T(8,128)(2,1)S(1)}, u32[]{:S(2)}, u32[]{:S(2)}) collective-permute-start(bf16[32,1792]{1,0:T(8,128)(2,1)S(1)} %get-tuple-element.48.refs_0_), channel_id=1, source_target_pairs={{0,3},{1,0},{2,1},{3,2},{4,7},{5,4},{6,5},{7,6},{8,11},{9,8},{10,9... | collective-permute-start | bytes 344072 | tf_op jit(solution)/shard_map/ppermute | solution.py:356
  27.8 11.3 %collective-permute-start.7 = (bf16[32,1792]{1,0:T(8,128)(2,1)S(1)}, bf16[32,1792]{1,0:T(8,128)(2,1)S(1)}, u32[]{:S(2)}, u32[]{:S(2)}) collective-permute-start(bf16[32,1792]{1,0:T(8,128)(2,1)S(1)} %get-tuple-element.48.refs_0_), channel_id=1, source_target_pairs={{0,2},{1,3},{2,0},{3,1},{4,6},{5,7},{6,4},{7,5},{8,10},{9,11},{10,... | collective-permute-start | bytes 344072 | tf_op jit(solution)/shard_map/ppermute | solution.py:356
  29.3 9.8 %collective-permute-start.6 = (bf16[32,1792]{1,0:T(8,128)(2,1)S(1)}, bf16[32,1792]{1,0:T(8,128)(2,1)S(1)}, u32[]{:S(2)}, u32[]{:S(2)}) collective-permute-start(bf16[32,1792]{1,0:T(8,128)(2,1)S(1)} %get-tuple-element.48.refs_0_), channel_id=1, source_target_pairs={{0,1},{1,2},{2,3},{3,0},{4,5},{5,6},{6,7},{7,4},{8,9},{9,10},{10,1... | collective-permute-start | bytes 344072 | tf_op jit(solution)/shard_map/ppermute | solution.py:356
  41.3 15.2 %all-to-all-start.1 = ((bf16[4,64,1792]{2,1,0:T(8,128)(2,1)}), bf16[4,64,1792]{2,1,0:T(8,128)(2,1)S(1)}, u32[]{:S(2)}, u32[]{:S(2)}) async-start(bf16[4,64,1792]{2,1,0:T(8,128)(2,1)} %bitcast.8), calls=%async_computation.1 | async-start | bytes 1835008 | tf_op jit(solution)/shard_map/all_to_all | solution.py:384
  45.2 9.5 %collective-permute-start.9 = (bf16[64,768]{1,0:T(8,128)(2,1)S(1)}, bf16[64,768]{1,0:T(8,128)(2,1)S(1)}, u32[]{:S(2)}, u32[]{:S(2)}) collective-permute-start(bf16[64,768]{1,0:T(8,128)(2,1)S(1)} %get-tuple-element.61), channel_id=1, source_target_pairs={{0,1},{1,2},{2,3},{3,0},{4,5},{5,6},{6,7},{7,4},{8,9},{9,10},{10,1... | collective-permute-start | bytes 294920 | tf_op jit(solution)/shard_map/ppermute | solution.py:356
  45.9 9.5 %collective-permute-start.10 = (bf16[64,768]{1,0:T(8,128)(2,1)S(1)}, bf16[64,768]{1,0:T(8,128)(2,1)S(1)}, u32[]{:S(2)}, u32[]{:S(2)}) collective-permute-start(bf16[64,768]{1,0:T(8,128)(2,1)S(1)} %get-tuple-element.62), channel_id=1, source_target_pairs={{0,2},{1,3},{2,0},{3,1},{4,6},{5,7},{6,4},{7,5},{8,10},{9,11},{10,... | collective-permute-start | bytes 294920 | tf_op jit(solution)/shard_map/ppermute | solution.py:356
  47.9 7.5 %collective-permute-start.11 = (bf16[64,768]{1,0:T(8,128)(2,1)S(1)}, bf16[64,768]{1,0:T(8,128)(2,1)S(1)}, u32[]{:S(2)}, u32[]{:S(2)}) collective-permute-start(bf16[64,768]{1,0:T(8,128)(2,1)S(1)} %get-tuple-element.63), channel_id=1, source_target_pairs={{0,3},{1,0},{2,1},{3,2},{4,7},{5,4},{6,5},{7,6},{8,11},{9,8},{10,9... | collective-permute-start | bytes 294920 | tf_op jit(solution)/shard_map/ppermute | solution.py:356
  50.7 17.0 %collective-permute-start.12 = (bf16[256,2304]{1,0:T(8,128)(2,1)S(1)}, bf16[256,2304]{1,0:T(8,128)(2,1)}, u32[]{:S(2)}, u32[]{:S(2)}) collective-permute-start(bf16[256,2304]{1,0:T(8,128)(2,1)S(1)} %bitcast.18), channel_id=1, source_target_pairs={{0,16},{16,0},{1,17},{17,1},{2,18},{18,2},{3,19},{19,3},{4,20},{20... | collective-permute-start | bytes 3538952 | tf_op jit(solution)/shard_map/ppermute | solution.py:362
  55.4 3.8 %copy-start.7 = (f32[256,768]{1,0:T(8,128)S(1)}, f32[256,768]{1,0:T(8,128)}, u32[]{:S(2)}) copy-start(f32[256,768]{1,0:T(8,128)} %fusion) | copy-start | bytes 2359300
  56.4 11.3 %collective-permute-start.13 = (bf16[256,1792]{1,0:T(8,128)(2,1)S(1)}, bf16[256,1792]{1,0:T(8,128)(2,1)}, u32[]{:S(2)}, u32[]{:S(2)}) collective-permute-start(bf16[256,1792]{1,0:T(8,128)(2,1)S(1)} %bitcast.21), channel_id=1, source_target_pairs={{0,16},{16,0},{1,17},{17,1},{2,18},{18,2},{3,19},{19,3},{4,20},{20... | collective-permute-start | bytes 2752520 | tf_op jit(solution)/shard_map/ppermute | solution.py:362
  60.0 19.9 %all-to-all-start.2 = ((bf16[16,16,768]{2,1,0:T(8,128)(2,1)}), bf16[16,16,768]{2,1,0:T(8,128)(2,1)S(1)}, u32[]{:S(2)}, u32[]{:S(2)}) async-start(bf16[16,16,768]{2,1,0:T(8,128)(2,1)} %bitcast.11), calls=%async_computation.2 | async-start | bytes 786432 | tf_op jit(solution)/shard_map/all_to_all | solution.py:400
  65.9 14.0 %copy-start.1 = (bf16[32,8,768]{2,1,0:T(8,128)(2,1)S(1)}, bf16[32,8,768]{2,1,0:T(8,128)(2,1)}, u32[]{:S(2)}) copy-start(bf16[32,8,768]{2,1,0:T(8,128)(2,1)} %param.6) | copy-start | bytes 1179652
  65.9 14.0 %copy-start.6 = (f32[32,8]{0,1:T(8,128)S(1)}, f32[32,8]{0,1:T(8,128)}, u32[]{:S(2)}) copy-start(f32[32,8]{0,1:T(8,128)} %param.7) | copy-start | bytes 3076
  65.9 1.8 %collective-permute-start.14 = (bf16[64,3072]{1,0:T(8,128)(2,1)S(1)}, bf16[64,3072]{1,0:T(8,128)(2,1)S(1)}, u32[]{:S(2)}, u32[]{:S(2)}) collective-permute-start(bf16[64,3072]{1,0:T(8,128)(2,1)S(1)} %join_rows.1.refs_4_), channel_id=1, source_target_pairs={{0,16},{16,0},{1,17},{17,1},{2,18},{18,2},{3,19},{19,3},{4,20},{20... | collective-permute-start | bytes 1179656 | tf_op jit(solution)/shard_map/ppermute | solution.py:362

commit v15 on v14

--- a/solution.py
+++ b/solution.py
@@ -362,7 +362,10 @@
         return lax.ppermute(array, "dp", [(i, i ^ 1) for i in range(lax.axis_size("dp"))])
 
     def line(array):
-        return [array] + [along(array, step) for step in range(1, near_count)]
+        blocks = {0: array}
+        for step in sorted(range(1, near_count), key=lambda step: min(step, near_count - step)):
+            blocks[step] = along(array, step)
+        return [blocks[step] for step in range(near_count)]
 
     hidden_rows = hidden.reshape(row_total, hidden_width)
     scalars = jnp.stack([near, lax.axis_index("far"), lax.axis_index("dp")]).astype(jnp.int32)

time: 81.9 us -> 81.9 us (level)
  no operation moved by 1% of the time
where the time goes in v15:
time: 81.9 us; the launch traced here: 81.2 us
  starting transfers between devices  33.4 us (41%)
  waiting for transfers between devices  21.6 us (26%)
  Pallas kernels  14 us (17%)
  matrix products  6.67 us (8%)
  local copies, waits for them, and re-layouts  4.02 us (5%)
  other arithmetic  0.92 us (1%)
    ppermute x9, starting transfers between devices, along(): lax.ppermute(array, 'near', [(i, (i + steps) % near_count) for i in range...  16.5 us
    ppermute x9, waiting for transfers between devices, along(): lax.ppermute(array, 'near', [(i, (i + steps) % near_count) for i in range...  13.4 us
    pallas_call x1, Pallas kernels, down_rows(): pl.pallas_call(functools.partial(down_kernel, near_count, capacity), grid...  7.51 us
    all_to_all x2, starting transfers between devices, local(): lax.all_to_all(picked.reshape(far_count, -1, picked.shape[1]), 'far', spl...  7.23 us
    dot_general x2, matrix products, local(): lax.dot_general(rows[i], weight[:, bounds[i][0]:bounds[i][1]], (((1,), (1...  6.67 us
    all_to_all x1, starting transfers between devices, local(): lax.all_to_all(total.astype(jnp.bfloat16).reshape(experts, capacity, hidd...  5.89 us
    all_to_all x1, waiting for transfers between devices, local(): lax.all_to_all(total.astype(jnp.bfloat16).reshape(experts, capacity, hidd...  4.66 us
    unnamed x16, local copies, waits for them, and re-layouts  4.02 us
  transfers between devices with their start and end apart: 18, of which 8 were waited for; matrix products, arithmetic and copies ran while one was open for 9% of the time, Pallas kernels for 15%

profile of v15, /device:TPU:0, one launch (start us, length us, event | category | flops | bytes accessed | tf_op | source)
XLA Modules:
  0.0 81.2 jit_solution(10843836590048051091)
XLA Ops:
  0.6 0.9 %copy-done.2 = bf16[32,4096]{1,0:T(8,128)(2,1)S(1)} copy-done((bf16[32,4096]{1,0:T(8,128)(2,1)S(1)}, bf16[32,4096]{1,0:T(8,128)(2,1)}, u32[]{:S(2)}) %copy-start.2) | copy-done | bytes 262168
  1.6 0.7 copy-done.3
  2.3 0.3 split_rows.1
  2.5 5.1 %collective-permute-start.2 = (bf16[32,2432]{1,0:T(8,128)(2,1)S(1)}, bf16[32,2432]{1,0:T(8,128)(2,1)S(1)}, u32[]{:S(2)}, u32[]{:S(2)}) collective-permute-start(bf16[32,2432]{1,0:T(8,128)(2,1)S(1)} %get-tuple-element.40.refs_0_), channel_id=1, source_target_pairs={{0,3},{1,0},{2,1},{3,2},{4,7},{5,4},{6,5},{7,6},{8,11},{9,8},{10,9... | collective-permute-start | bytes 466952 | tf_op jit(solution)/shard_map/ppermute | solution.py:356
  7.6 0.0 collective-permute-start.1
  7.7 1.0 %collective-permute-start = (bf16[32,2432]{1,0:T(8,128)(2,1)S(1)}, bf16[32,2432]{1,0:T(8,128)(2,1)S(1)}, u32[]{:S(2)}, u32[]{:S(2)}) collective-permute-start(bf16[32,2432]{1,0:T(8,128)(2,1)S(1)} %get-tuple-element.40.refs_0_), channel_id=1, source_target_pairs={{0,1},{1,2},{2,3},{3,0},{4,5},{5,6},{6,7},{7,4},{8,9},{9,10},{10,1... | collective-permute-start | bytes 466952 | tf_op jit(solution)/shard_map/ppermute | solution.py:356
  8.7 0.1 pad_add_fusion.scalars_ref
  8.7 1.0 %copy-done = bf16[32,8,768]{2,1,0:T(8,128)(2,1)S(1)} copy-done((bf16[32,8,768]{2,1,0:T(8,128)(2,1)S(1)}, bf16[32,8,768]{2,1,0:T(8,128)(2,1)}, u32[]{:S(2)}) %copy-start) | copy-done | bytes 393240
  9.7 0.7 copy-done.4
  10.4 0.7 copy-done.5
  11.1 1.1 %send_rows.1 = (bf16[64,768]{1,0:T(8,128)(2,1)S(1)}, bf16[64,768]{1,0:T(8,128)(2,1)S(1)}, bf16[64,768]{1,0:T(8,128)(2,1)S(1)}, bf16[64,768]{1,0:T(8,128)(2,1)S(1)}, bf16[256,256]{1,0:T(8,128)(2,1)S(1)}) custom-call(s32[3]{0:T(128)S(1)} %pad_add_fusion.scalars_ref, s32[8,32]{1,0:T(8,128)S(1)} %bitcast.28, f32[8,32]{1,0:T(8,128)S(1)} %bitcast.29, ...), custom_call_target="tpu_custom_call" | custom-call | flops 100663296 | bytes 786432 | tf_op jit(solution)/shard_map/send_rows/pallas_call | solution.py:234
  12.2 1.6 %collective-permute-start.3 = (bf16[64,768]{1,0:T(8,128)(2,1)S(1)}, bf16[64,768]{1,0:T(8,128)(2,1)S(1)}, u32[]{:S(2)}, u32[]{:S(2)}) collective-permute-start(bf16[64,768]{1,0:T(8,128)(2,1)S(1)} %get-tuple-element.44), channel_id=1, source_target_pairs={{0,4},{4,0},{8,12},{12,8},{1,5},{5,1},{9,13},{13,9},{2,6},{6,2},{1... | collective-permute-start | bytes 294920 | tf_op jit(solution)/shard_map/ppermute | solution.py:359
  13.8 1.5 %collective-permute-start.4 = (bf16[64,768]{1,0:T(8,128)(2,1)S(1)}, bf16[64,768]{1,0:T(8,128)(2,1)S(1)}, u32[]{:S(2)}, u32[]{:S(2)}) collective-permute-start(bf16[64,768]{1,0:T(8,128)(2,1)S(1)} %get-tuple-element.45), channel_id=1, source_target_pairs={{0,8},{4,12},{8,0},{12,4},{1,9},{5,13},{9,1},{13,5},{2,10},{6,14},... | collective-permute-start | bytes 294920 | tf_op jit(solution)/shard_map/ppermute | solution.py:359
  15.3 0.0 collective-permute-done.2.refs_3_
  15.3 0.5 collective-permute-start.5
  15.8 5.0 %collective-permute-done.1.refs_2_ = bf16[32,2432]{1,0:T(8,128)(2,1)S(1)} collective-permute-done((bf16[32,2432]{1,0:T(8,128)(2,1)S(1)}, bf16[32,2432]{1,0:T(8,128)(2,1)S(1)}, u32[]{:S(2)}, u32[]{:S(2)}) %collective-permute-start.1) | collective-permute-done | bytes 155680 | tf_op jit(solution)/shard_map/ppermute | solution.py:356
  20.8 2.0 %first_pick.1 = (bf16[256,2304]{1,0:T(8,128)(2,1)}, bf16[256,128]{1,0:T(8,128)(2,1)S(1)}) custom-call(s32[1]{0:T(128)} %bitcast.near_ref, bf16[32,2432]{1,0:T(8,128)(2,1)S(1)} %get-tuple-element.40.refs_0_, bf16[32,2432]{1,0:T(8,128)(2,1)S(1)} %collective-permute-done.refs_1_, bf16[32,2432]{1,0:T(8,128)(2,1)S(1)} %collective-permute-done.1.refs_2_, ...), custom_call_target="tpu_custom_call" | custom-call | tf_op jit(solution)/shard_map/first_pick/pallas_call | solution.py:282
  22.8 0.0 collective-permute-done.3.refs_1_
  22.8 3.7 %all-to-all-start = ((bf16[4,64,2304]{2,1,0:T(8,128)(2,1)}), bf16[4,64,2304]{2,1,0:T(8,128)(2,1)S(1)}, u32[]{:S(2)}, u32[]{:S(2)}) async-start(bf16[4,64,2304]{2,1,0:T(8,128)(2,1)} %bitcast.6), calls=%async_computation | async-start | bytes 2359296 | tf_op jit(solution)/shard_map/all_to_all | solution.py:387
  26.5 1.2 %collective-permute-start.8 = (bf16[32,1792]{1,0:T(8,128)(2,1)S(1)}, bf16[32,1792]{1,0:T(8,128)(2,1)S(1)}, u32[]{:S(2)}, u32[]{:S(2)}) collective-permute-start(bf16[32,1792]{1,0:T(8,128)(2,1)S(1)} %get-tuple-element.48.refs_0_), channel_id=1, source_target_pairs={{0,3},{1,0},{2,1},{3,2},{4,7},{5,4},{6,5},{7,6},{8,11},{9,8},{10,9... | collective-permute-start | bytes 344072 | tf_op jit(solution)/shard_map/ppermute | solution.py:356
  27.8 1.6 %collective-permute-start.7 = (bf16[32,1792]{1,0:T(8,128)(2,1)S(1)}, bf16[32,1792]{1,0:T(8,128)(2,1)S(1)}, u32[]{:S(2)}, u32[]{:S(2)}) collective-permute-start(bf16[32,1792]{1,0:T(8,128)(2,1)S(1)} %get-tuple-element.48.refs_0_), channel_id=1, source_target_pairs={{0,2},{1,3},{2,0},{3,1},{4,6},{5,7},{6,4},{7,5},{8,10},{9,11},{10,... | collective-permute-start | bytes 344072 | tf_op jit(solution)/shard_map/ppermute | solution.py:356
  29.3 2.0 %collective-permute-start.6 = (bf16[32,1792]{1,0:T(8,128)(2,1)S(1)}, bf16[32,1792]{1,0:T(8,128)(2,1)S(1)}, u32[]{:S(2)}, u32[]{:S(2)}) collective-permute-start(bf16[32,1792]{1,0:T(8,128)(2,1)S(1)} %get-tuple-element.48.refs_0_), channel_id=1, source_target_pairs={{0,1},{1,2},{2,3},{3,0},{4,5},{5,6},{6,7},{7,4},{8,9},{9,10},{10,1... | collective-permute-start | bytes 344072 | tf_op jit(solution)/shard_map/ppermute | solution.py:356
  31.4 0.8 %collective-permute-done.8.refs_3_ = bf16[32,1792]{1,0:T(8,128)(2,1)S(1)} collective-permute-done((bf16[32,1792]{1,0:T(8,128)(2,1)S(1)}, bf16[32,1792]{1,0:T(8,128)(2,1)S(1)}, u32[]{:S(2)}, u32[]{:S(2)}) %collective-permute-start.8) | collective-permute-done | bytes 114720 | tf_op jit(solution)/shard_map/ppermute | solution.py:356
  32.2 6.9 %collective-permute-done.7.refs_2_ = bf16[32,1792]{1,0:T(8,128)(2,1)S(1)} collective-permute-done((bf16[32,1792]{1,0:T(8,128)(2,1)S(1)}, bf16[32,1792]{1,0:T(8,128)(2,1)S(1)}, u32[]{:S(2)}, u32[]{:S(2)}) %collective-permute-start.7) | collective-permute-done | bytes 114720 | tf_op jit(solution)/shard_map/ppermute | solution.py:356
  39.1 0.0 collective-permute-done.6.refs_1_
  39.1 1.3 %pick_rows.1 = bf16[256,1792]{1,0:T(8,128)(2,1)} custom-call(bf16[256,128]{1,0:T(8,128)(2,1)S(1)} %get-tuple-element.41.pick_ref, bf16[32,1792]{1,0:T(8,128)(2,1)S(1)} %get-tuple-element.48.refs_0_, bf16[32,1792]{1,0:T(8,128)(2,1)S(1)} %collective-permute-done.6.refs_1_, bf16[32,1792]{1,0:T(8,128)(2,1)S(1)} %collective-permute-done.7.refs_2_, ...), custom_call_target="tpu_custom_call" | custom-call | tf_op jit(solution)/shard_map/pick_rows/pallas_call | solution.py:297
  40.4 0.8 %all-to-all-done = bf16[4,64,2304]{2,1,0:T(8,128)(2,1)S(1)} async-done(((bf16[4,64,2304]{2,1,0:T(8,128)(2,1)}), bf16[4,64,2304]{2,1,0:T(8,128)(2,1)S(1)}, u32[]{:S(2)}, u32[]{:S(2)}) %all-to-all-start) | async-done | bytes 1179680 | tf_op jit(solution)/shard_map/all_to_all | solution.py:387
  41.3 3.5 %all-to-all-start.1 = ((bf16[4,64,1792]{2,1,0:T(8,128)(2,1)}), bf16[4,64,1792]{2,1,0:T(8,128)(2,1)S(1)}, u32[]{:S(2)}, u32[]{:S(2)}) async-start(bf16[4,64,1792]{2,1,0:T(8,128)(2,1)} %bitcast.8), calls=%async_computation.1 | async-start | bytes 1835008 | tf_op jit(solution)/shard_map/all_to_all | solution.py:387
  44.8 0.4 regroup_rows.1
  45.2 0.7 collective-permute-start.9
  45.9 2.0 %collective-permute-start.10 = (bf16[64,768]{1,0:T(8,128)(2,1)S(1)}, bf16[64,768]{1,0:T(8,128)(2,1)S(1)}, u32[]{:S(2)}, u32[]{:S(2)}) collective-permute-start(bf16[64,768]{1,0:T(8,128)(2,1)S(1)} %get-tuple-element.62), channel_id=1, source_target_pairs={{0,2},{1,3},{2,0},{3,1},{4,6},{5,7},{6,4},{7,5},{8,10},{9,11},{10,... | collective-permute-start | bytes 294920 | tf_op jit(solution)/shard_map/ppermute | solution.py:356
  47.9 2.8 %collective-permute-start.11 = (bf16[64,768]{1,0:T(8,128)(2,1)S(1)}, bf16[64,768]{1,0:T(8,128)(2,1)S(1)}, u32[]{:S(2)}, u32[]{:S(2)}) collective-permute-start(bf16[64,768]{1,0:T(8,128)(2,1)S(1)} %get-tuple-element.63), channel_id=1, source_target_pairs={{0,3},{1,0},{2,1},{3,2},{4,7},{5,4},{6,5},{7,6},{8,11},{9,8},{10,9... | collective-permute-start | bytes 294920 | tf_op jit(solution)/shard_map/ppermute | solution.py:356
  50.7 0.0 collective-permute-start.12
  50.7 4.0 %fusion = f32[256,768]{1,0:T(8,128)} fusion(bf16[256,2304]{1,0:T(8,128)(2,1)S(1)} %bitcast.19, bf16[768,4096]{1,0:T(8,128)(2,1)} %bitcast.32), kind=kOutput, calls=%fused_computation | convolution fusion | flops 905969664 | bytes 5505024 | tf_op jit(solution)/shard_map/dot_general | solution.py:396
  54.7 0.0 collective-permute-done.9.refs_1_
  54.7 0.6 collective-permute-done.10.refs_2_
  55.4 0.0 copy-start.7
  55.4 1.1 %all-to-all-done.1 = bf16[4,64,1792]{2,1,0:T(8,128)(2,1)S(1)} async-done(((bf16[4,64,1792]{2,1,0:T(8,128)(2,1)}), bf16[4,64,1792]{2,1,0:T(8,128)(2,1)S(1)}, u32[]{:S(2)}, u32[]{:S(2)}) %all-to-all-start.1) | async-done | bytes 917536 | tf_op jit(solution)/shard_map/all_to_all | solution.py:387
  56.4 2.7 %fusion.2 = f32[256,768]{1,0:T(8,128)S(1)} fusion(bf16[256,1792]{1,0:T(8,128)(2,1)S(1)} %bitcast.22, bf16[768,4096]{1,0:T(8,128)(2,1)} %bitcast.33), kind=kOutput, calls=%fused_computation.2 | convolution fusion | flops 704643072 | bytes 4456448 | tf_op jit(solution)/shard_map/dot_general | solution.py:396
  59.1 0.8 %add_convert_fusion = bf16[256,768]{1,0:T(8,128)(2,1)} fusion(f32[256,768]{1,0:T(8,128)S(1)} %copy-done.7, f32[256,768]{1,0:T(8,128)S(1)} %fusion.2), kind=kLoop, calls=%fused_computation.4 | loop fusion | flops 393216 | bytes 1966080 | tf_op jit(solution)/shard_map/convert_element_type | solution.py:404
  60.0 5.9 %all-to-all-start.2 = ((bf16[16,16,768]{2,1,0:T(8,128)(2,1)}), bf16[16,16,768]{2,1,0:T(8,128)(2,1)S(1)}, u32[]{:S(2)}, u32[]{:S(2)}) async-start(bf16[16,16,768]{2,1,0:T(8,128)(2,1)} %bitcast.11), calls=%async_computation.2 | async-start | bytes 786432 | tf_op jit(solution)/shard_map/all_to_all | solution.py:403
  65.9 0.0 copy-start.1
  65.9 0.0 copy-start.6
  65.9 0.2 collective-permute-start.14
  66.1 1.6 %collective-permute-done.14.refs_5_ = bf16[64,3072]{1,0:T(8,128)(2,1)S(1)} collective-permute-done((bf16[64,3072]{1,0:T(8,128)(2,1)S(1)}, bf16[64,3072]{1,0:T(8,128)(2,1)S(1)}, u32[]{:S(2)}, u32[]{:S(2)}) %collective-permute-start.14) | collective-permute-done | bytes 393248 | tf_op jit(solution)/shard_map/ppermute | solution.py:362
  67.7 7.5 %down_rows.1 = bf16[384,4096]{1,0:T(8,128)(2,1)} custom-call(s32[3]{0:T(128)S(1)} %pad_add_fusion.scalars_ref, bf16[256,2304]{1,0:T(8,128)(2,1)S(1)} %bitcast.20, bf16[256,1792]{1,0:T(8,128)(2,1)S(1)} %bitcast.23, bf16[256,2304]{1,0:T(8,128)(2,1)} %collective-permute-done.12.refs_2_, bf16[256,1792]{1,0:T(8,128)(2,1)} %collective-permute-done.13.refs_3_, ...), custom_call_target="tpu_custom_call" | custom-call | flops 1610612736 | bytes 7340032 | tf_op jit(solution)/shard_map/down_rows/pallas_call | solution.py:325
  75.2 4.7 %all-to-all-done.2 = bf16[16,16,768]{2,1,0:T(8,128)(2,1)S(1)} async-done(((bf16[16,16,768]{2,1,0:T(8,128)(2,1)}), bf16[16,16,768]{2,1,0:T(8,128)(2,1)S(1)}, u32[]{:S(2)}, u32[]{:S(2)}) %all-to-all-start.2) | async-done | bytes 393248 | tf_op jit(solution)/shard_map/all_to_all | solution.py:403
  79.9 1.4 %close_rows.1 = (bf16[256,768]{1,0:T(8,128)(2,1)}, f32[8,32]{1,0:T(8,128)}) custom-call(bf16[256,256]{1,0:T(8,128)(2,1)S(1)} %get-tuple-element.39.back_ref, bf16[256,768]{1,0:T(8,128)(2,1)S(1)} %bitcast.26, f32[8,32]{1,0:T(8,128)S(1)} %bitcast.30, bf16[256,768]{1,0:T(8,128)(2,1)S(1)} %bitcast.25), custom_call_target="tpu_custom_call" | custom-call | tf_op jit(solution)/shard_map/close_rows/pallas_call | solution.py:260
  (16 shorter events, 0.1 us)
Async XLA Ops:
  0.6 1.0 %copy-start.2 = (bf16[32,4096]{1,0:T(8,128)(2,1)S(1)}, bf16[32,4096]{1,0:T(8,128)(2,1)}, u32[]{:S(2)}) copy-start(bf16[32,4096]{1,0:T(8,128)(2,1)} %tokens_hbm.1) | copy-start | bytes 786436
  1.6 0.7 copy-start.3
  2.5 12.8 %collective-permute-start.2 = (bf16[32,2432]{1,0:T(8,128)(2,1)S(1)}, bf16[32,2432]{1,0:T(8,128)(2,1)S(1)}, u32[]{:S(2)}, u32[]{:S(2)}) collective-permute-start(bf16[32,2432]{1,0:T(8,128)(2,1)S(1)} %get-tuple-element.40.refs_0_), channel_id=1, source_target_pairs={{0,3},{1,0},{2,1},{3,2},{4,7},{5,4},{6,5},{7,6},{8,11},{9,8},{10,9... | collective-permute-start | bytes 466952 | tf_op jit(solution)/shard_map/ppermute | solution.py:356
  7.6 13.2 %collective-permute-start.1 = (bf16[32,2432]{1,0:T(8,128)(2,1)S(1)}, bf16[32,2432]{1,0:T(8,128)(2,1)S(1)}, u32[]{:S(2)}, u32[]{:S(2)}) collective-permute-start(bf16[32,2432]{1,0:T(8,128)(2,1)S(1)} %get-tuple-element.40.refs_0_), channel_id=1, source_target_pairs={{0,2},{1,3},{2,0},{3,1},{4,6},{5,7},{6,4},{7,5},{8,10},{9,11},{10,... | collective-permute-start | bytes 466952 | tf_op jit(solution)/shard_map/ppermute | solution.py:356
  7.7 13.2 %collective-permute-start = (bf16[32,2432]{1,0:T(8,128)(2,1)S(1)}, bf16[32,2432]{1,0:T(8,128)(2,1)S(1)}, u32[]{:S(2)}, u32[]{:S(2)}) collective-permute-start(bf16[32,2432]{1,0:T(8,128)(2,1)S(1)} %get-tuple-element.40.refs_0_), channel_id=1, source_target_pairs={{0,1},{1,2},{2,3},{3,0},{4,5},{5,6},{6,7},{7,4},{8,9},{9,10},{10,1... | collective-permute-start | bytes 466952 | tf_op jit(solution)/shard_map/ppermute | solution.py:356
  8.7 1.0 %copy-start = (bf16[32,8,768]{2,1,0:T(8,128)(2,1)S(1)}, bf16[32,8,768]{2,1,0:T(8,128)(2,1)}, u32[]{:S(2)}) copy-start(bf16[32,8,768]{2,1,0:T(8,128)(2,1)} %param.6) | copy-start | bytes 1179652
  9.7 0.7 copy-start.4
  10.4 0.7 copy-start.5
  12.2 10.6 %collective-permute-start.3 = (bf16[64,768]{1,0:T(8,128)(2,1)S(1)}, bf16[64,768]{1,0:T(8,128)(2,1)S(1)}, u32[]{:S(2)}, u32[]{:S(2)}) collective-permute-start(bf16[64,768]{1,0:T(8,128)(2,1)S(1)} %get-tuple-element.44), channel_id=1, source_target_pairs={{0,4},{4,0},{8,12},{12,8},{1,5},{5,1},{9,13},{13,9},{2,6},{6,2},{1... | collective-permute-start | bytes 294920 | tf_op jit(solution)/shard_map/ppermute | solution.py:359
  13.8 9.0 %collective-permute-start.4 = (bf16[64,768]{1,0:T(8,128)(2,1)S(1)}, bf16[64,768]{1,0:T(8,128)(2,1)S(1)}, u32[]{:S(2)}, u32[]{:S(2)}) collective-permute-start(bf16[64,768]{1,0:T(8,128)(2,1)S(1)} %get-tuple-element.45), channel_id=1, source_target_pairs={{0,8},{4,12},{8,0},{12,4},{1,9},{5,13},{9,1},{13,5},{2,10},{6,14},... | collective-permute-start | bytes 294920 | tf_op jit(solution)/shard_map/ppermute | solution.py:359
  15.3 7.5 %collective-permute-start.5 = (bf16[64,768]{1,0:T(8,128)(2,1)S(1)}, bf16[64,768]{1,0:T(8,128)(2,1)S(1)}, u32[]{:S(2)}, u32[]{:S(2)}) collective-permute-start(bf16[64,768]{1,0:T(8,128)(2,1)S(1)} %get-tuple-element.46), channel_id=1, source_target_pairs={{0,12},{4,8},{8,4},{12,0},{1,13},{5,9},{9,5},{13,1},{2,14},{6,10},... | collective-permute-start | bytes 294920 | tf_op jit(solution)/shard_map/ppermute | solution.py:359
  22.8 18.5 %all-to-all-start = ((bf16[4,64,2304]{2,1,0:T(8,128)(2,1)}), bf16[4,64,2304]{2,1,0:T(8,128)(2,1)S(1)}, u32[]{:S(2)}, u32[]{:S(2)}) async-start(bf16[4,64,2304]{2,1,0:T(8,128)(2,1)} %bitcast.6), calls=%async_computation | async-start | bytes 2359296 | tf_op jit(solution)/shard_map/all_to_all | solution.py:387
  26.5 5.6 %collective-permute-start.8 = (bf16[32,1792]{1,0:T(8,128)(2,1)S(1)}, bf16[32,1792]{1,0:T(8,128)(2,1)S(1)}, u32[]{:S(2)}, u32[]{:S(2)}) collective-permute-start(bf16[32,1792]{1,0:T(8,128)(2,1)S(1)} %get-tuple-element.48.refs_0_), channel_id=1, source_target_pairs={{0,3},{1,0},{2,1},{3,2},{4,7},{5,4},{6,5},{7,6},{8,11},{9,8},{10,9... | collective-permute-start | bytes 344072 | tf_op jit(solution)/shard_map/ppermute | solution.py:356
  27.8 11.3 %collective-permute-start.7 = (bf16[32,1792]{1,0:T(8,128)(2,1)S(1)}, bf16[32,1792]{1,0:T(8,128)(2,1)S(1)}, u32[]{:S(2)}, u32[]{:S(2)}) collective-permute-start(bf16[32,1792]{1,0:T(8,128)(2,1)S(1)} %get-tuple-element.48.refs_0_), channel_id=1, source_target_pairs={{0,2},{1,3},{2,0},{3,1},{4,6},{5,7},{6,4},{7,5},{8,10},{9,11},{10,... | collective-permute-start | bytes 344072 | tf_op jit(solution)/shard_map/ppermute | solution.py:356
  29.3 9.8 %collective-permute-start.6 = (bf16[32,1792]{1,0:T(8,128)(2,1)S(1)}, bf16[32,1792]{1,0:T(8,128)(2,1)S(1)}, u32[]{:S(2)}, u32[]{:S(2)}) collective-permute-start(bf16[32,1792]{1,0:T(8,128)(2,1)S(1)} %get-tuple-element.48.refs_0_), channel_id=1, source_target_pairs={{0,1},{1,2},{2,3},{3,0},{4,5},{5,6},{6,7},{7,4},{8,9},{9,10},{10,1... | collective-permute-start | bytes 344072 | tf_op jit(solution)/shard_map/ppermute | solution.py:356
  41.3 15.2 %all-to-all-start.1 = ((bf16[4,64,1792]{2,1,0:T(8,128)(2,1)}), bf16[4,64,1792]{2,1,0:T(8,128)(2,1)S(1)}, u32[]{:S(2)}, u32[]{:S(2)}) async-start(bf16[4,64,1792]{2,1,0:T(8,128)(2,1)} %bitcast.8), calls=%async_computation.1 | async-start | bytes 1835008 | tf_op jit(solution)/shard_map/all_to_all | solution.py:387
  45.2 9.5 %collective-permute-start.9 = (bf16[64,768]{1,0:T(8,128)(2,1)S(1)}, bf16[64,768]{1,0:T(8,128)(2,1)S(1)}, u32[]{:S(2)}, u32[]{:S(2)}) collective-permute-start(bf16[64,768]{1,0:T(8,128)(2,1)S(1)} %get-tuple-element.61), channel_id=1, source_target_pairs={{0,1},{1,2},{2,3},{3,0},{4,5},{5,6},{6,7},{7,4},{8,9},{9,10},{10,1... | collective-permute-start | bytes 294920 | tf_op jit(solution)/shard_map/ppermute | solution.py:356
  45.9 9.5 %collective-permute-start.10 = (bf16[64,768]{1,0:T(8,128)(2,1)S(1)}, bf16[64,768]{1,0:T(8,128)(2,1)S(1)}, u32[]{:S(2)}, u32[]{:S(2)}) collective-permute-start(bf16[64,768]{1,0:T(8,128)(2,1)S(1)} %get-tuple-element.62), channel_id=1, source_target_pairs={{0,2},{1,3},{2,0},{3,1},{4,6},{5,7},{6,4},{7,5},{8,10},{9,11},{10,... | collective-permute-start | bytes 294920 | tf_op jit(solution)/shard_map/ppermute | solution.py:356
  47.9 7.5 %collective-permute-start.11 = (bf16[64,768]{1,0:T(8,128)(2,1)S(1)}, bf16[64,768]{1,0:T(8,128)(2,1)S(1)}, u32[]{:S(2)}, u32[]{:S(2)}) collective-permute-start(bf16[64,768]{1,0:T(8,128)(2,1)S(1)} %get-tuple-element.63), channel_id=1, source_target_pairs={{0,3},{1,0},{2,1},{3,2},{4,7},{5,4},{6,5},{7,6},{8,11},{9,8},{10,9... | collective-permute-start | bytes 294920 | tf_op jit(solution)/shard_map/ppermute | solution.py:356
  50.7 17.0 %collective-permute-start.12 = (bf16[256,2304]{1,0:T(8,128)(2,1)S(1)}, bf16[256,2304]{1,0:T(8,128)(2,1)}, u32[]{:S(2)}, u32[]{:S(2)}) collective-permute-start(bf16[256,2304]{1,0:T(8,128)(2,1)S(1)} %bitcast.18), channel_id=1, source_target_pairs={{0,16},{16,0},{1,17},{17,1},{2,18},{18,2},{3,19},{19,3},{4,20},{20... | collective-permute-start | bytes 3538952 | tf_op jit(solution)/shard_map/ppermute | solution.py:362
  55.4 3.8 %copy-start.7 = (f32[256,768]{1,0:T(8,128)S(1)}, f32[256,768]{1,0:T(8,128)}, u32[]{:S(2)}) copy-start(f32[256,768]{1,0:T(8,128)} %fusion) | copy-start | bytes 2359300
  56.4 11.3 %collective-permute-start.13 = (bf16[256,1792]{1,0:T(8,128)(2,1)S(1)}, bf16[256,1792]{1,0:T(8,128)(2,1)}, u32[]{:S(2)}, u32[]{:S(2)}) collective-permute-start(bf16[256,1792]{1,0:T(8,128)(2,1)S(1)} %bitcast.21), channel_id=1, source_target_pairs={{0,16},{16,0},{1,17},{17,1},{2,18},{18,2},{3,19},{19,3},{4,20},{20... | collective-permute-start | bytes 2752520 | tf_op jit(solution)/shard_map/ppermute | solution.py:362
  60.0 19.9 %all-to-all-start.2 = ((bf16[16,16,768]{2,1,0:T(8,128)(2,1)}), bf16[16,16,768]{2,1,0:T(8,128)(2,1)S(1)}, u32[]{:S(2)}, u32[]{:S(2)}) async-start(bf16[16,16,768]{2,1,0:T(8,128)(2,1)} %bitcast.11), calls=%async_computation.2 | async-start | bytes 786432 | tf_op jit(solution)/shard_map/all_to_all | solution.py:403
  65.9 14.0 %copy-start.1 = (bf16[32,8,768]{2,1,0:T(8,128)(2,1)S(1)}, bf16[32,8,768]{2,1,0:T(8,128)(2,1)}, u32[]{:S(2)}) copy-start(bf16[32,8,768]{2,1,0:T(8,128)(2,1)} %param.6) | copy-start | bytes 1179652
  65.9 14.0 %copy-start.6 = (f32[32,8]{0,1:T(8,128)S(1)}, f32[32,8]{0,1:T(8,128)}, u32[]{:S(2)}) copy-start(f32[32,8]{0,1:T(8,128)} %param.7) | copy-start | bytes 3076
  65.9 1.8 %collective-permute-start.14 = (bf16[64,3072]{1,0:T(8,128)(2,1)S(1)}, bf16[64,3072]{1,0:T(8,128)(2,1)S(1)}, u32[]{:S(2)}, u32[]{:S(2)}) collective-permute-start(bf16[64,3072]{1,0:T(8,128)(2,1)S(1)} %join_rows.1.refs_4_), channel_id=1, source_target_pairs={{0,16},{16,0},{1,17},{17,1},{2,18},{18,2},{3,19},{19,3},{4,20},{20... | collective-permute-start | bytes 1179656 | tf_op jit(solution)/shard_map/ppermute | solution.py:362

commit v16 on v14

--- a/solution.py
+++ b/solution.py
@@ -389,7 +389,7 @@
     hids = join_rows(hids[:1] + [along(hids[step], step) for step in range(1, near_count)])
     for i in range(PARTS):
         if i:
-            rows[i], total, hids = lax.optimization_barrier((rows[i], total, hids))
+            rows[i], total = lax.optimization_barrier((rows[i], total))
         product = lax.dot_general(
             rows[i],
             weight[:, bounds[i][0] : bounds[i][1]],
@@ -397,6 +397,7 @@
             preferred_element_type=jnp.float32,
         )
         total = product if total is None else total + product
+    total, hids = lax.optimization_barrier((total, hids))
     came_back = lax.all_to_all(
         total.astype(jnp.bfloat16).reshape(experts, capacity, hidden_width),
         ("far", "near"),

time: 81.9 us -> 81.9 us (level)
  matrix products: 6.67 us -> 7.61 us
  other arithmetic: 0.92 us -> 0.08 us
    dot_general x2, matrix products: 6.67 us -> 7.61 us  [local(): lax.dot_general(rows[i], weight[:, bounds[i][0]:bounds[i][1]], (((1,), (1...]
    convert_element_type x1 -> x0, other arithmetic: 0.84 us -> none  [local(): total.astype(jnp.bfloat16).reshape(experts, capacity, hidden_width)]
    unnamed x16 -> x14, local copies, waits for them, and re-layouts: 4.02 us -> 4.01 us
where the time goes in v16:
time: 81.9 us; the launch traced here: 81.3 us
  starting transfers between devices  33.4 us (41%)
  waiting for transfers between devices  21.6 us (26%)
  Pallas kernels  14 us (17%)
  matrix products  7.61 us (9%)
  local copies, waits for them, and re-layouts  4.01 us (5%)
    ppermute x9, starting transfers between devices, along(): lax.ppermute(array, 'near', [(i, (i + steps) % near_count) for i in range...  16.5 us
    ppermute x9, waiting for transfers between devices, along(): lax.ppermute(array, 'near', [(i, (i + steps) % near_count) for i in range...  13.4 us
    dot_general x2, matrix products, local(): lax.dot_general(rows[i], weight[:, bounds[i][0]:bounds[i][1]], (((1,), (1...  7.61 us
    pallas_call x1, Pallas kernels, down_rows(): pl.pallas_call(functools.partial(down_kernel, near_count, capacity), grid...  7.5 us
    all_to_all x2, starting transfers between devices, local(): lax.all_to_all(picked.reshape(far_count, -1, picked.shape[1]), 'far', spl...  7.23 us
    all_to_all x1, starting transfers between devices, local(): lax.all_to_all(total.astype(jnp.bfloat16).reshape(experts, capacity, hidd...  5.82 us
    all_to_all x1, waiting for transfers between devices, local(): lax.all_to_all(total.astype(jnp.bfloat16).reshape(experts, capacity, hidd...  4.72 us
    unnamed x14, local copies, waits for them, and re-layouts  4.01 us
  transfers between devices with their start and end apart: 18, of which 8 were waited for; matrix products, arithmetic and copies ran while one was open for 9% of the time, Pallas kernels for 15%

profile of v16, /device:TPU:0, one launch (start us, length us, event | category | flops | bytes accessed | tf_op | source)
XLA Modules:
  0.0 81.3 jit_solution(16948128705005405895)
XLA Ops:
  0.6 0.9 %copy-done.2 = bf16[32,4096]{1,0:T(8,128)(2,1)S(1)} copy-done((bf16[32,4096]{1,0:T(8,128)(2,1)S(1)}, bf16[32,4096]{1,0:T(8,128)(2,1)}, u32[]{:S(2)}) %copy-start.2) | copy-done | bytes 262168
  1.6 0.7 copy-done.3
  2.3 0.3 split_rows.1
  2.5 5.1 %collective-permute-start.2 = (bf16[32,2432]{1,0:T(8,128)(2,1)S(1)}, bf16[32,2432]{1,0:T(8,128)(2,1)S(1)}, u32[]{:S(2)}, u32[]{:S(2)}) collective-permute-start(bf16[32,2432]{1,0:T(8,128)(2,1)S(1)} %get-tuple-element.41.refs_0_), channel_id=1, source_target_pairs={{0,3},{1,0},{2,1},{3,2},{4,7},{5,4},{6,5},{7,6},{8,11},{9,8},{10,9... | collective-permute-start | bytes 466952 | tf_op jit(solution)/shard_map/ppermute | solution.py:356
  7.6 0.0 collective-permute-start.1
  7.7 1.0 %collective-permute-start = (bf16[32,2432]{1,0:T(8,128)(2,1)S(1)}, bf16[32,2432]{1,0:T(8,128)(2,1)S(1)}, u32[]{:S(2)}, u32[]{:S(2)}) collective-permute-start(bf16[32,2432]{1,0:T(8,128)(2,1)S(1)} %get-tuple-element.41.refs_0_), channel_id=1, source_target_pairs={{0,1},{1,2},{2,3},{3,0},{4,5},{5,6},{6,7},{7,4},{8,9},{9,10},{10,1... | collective-permute-start | bytes 466952 | tf_op jit(solution)/shard_map/ppermute | solution.py:356
  8.7 0.1 pad_add_fusion.scalars_ref
  8.7 1.0 %copy-done = bf16[32,8,768]{2,1,0:T(8,128)(2,1)S(1)} copy-done((bf16[32,8,768]{2,1,0:T(8,128)(2,1)S(1)}, bf16[32,8,768]{2,1,0:T(8,128)(2,1)}, u32[]{:S(2)}) %copy-start) | copy-done | bytes 393240
  9.7 0.7 copy-done.4
  10.4 0.7 copy-done.5
  11.1 1.1 %send_rows.1 = (bf16[64,768]{1,0:T(8,128)(2,1)S(1)}, bf16[64,768]{1,0:T(8,128)(2,1)S(1)}, bf16[64,768]{1,0:T(8,128)(2,1)S(1)}, bf16[64,768]{1,0:T(8,128)(2,1)S(1)}, bf16[256,256]{1,0:T(8,128)(2,1)S(1)}) custom-call(s32[3]{0:T(128)S(1)} %pad_add_fusion.scalars_ref, s32[8,32]{1,0:T(8,128)S(1)} %bitcast.28, f32[8,32]{1,0:T(8,128)S(1)} %bitcast.29, ...), custom_call_target="tpu_custom_call" | custom-call | flops 100663296 | bytes 786432 | tf_op jit(solution)/shard_map/send_rows/pallas_call | solution.py:234
  12.2 1.6 %collective-permute-start.3 = (bf16[64,768]{1,0:T(8,128)(2,1)S(1)}, bf16[64,768]{1,0:T(8,128)(2,1)S(1)}, u32[]{:S(2)}, u32[]{:S(2)}) collective-permute-start(bf16[64,768]{1,0:T(8,128)(2,1)S(1)} %get-tuple-element.45), channel_id=1, source_target_pairs={{0,4},{4,0},{8,12},{12,8},{1,5},{5,1},{9,13},{13,9},{2,6},{6,2},{1... | collective-permute-start | bytes 294920 | tf_op jit(solution)/shard_map/ppermute | solution.py:359
  13.8 1.5 %collective-permute-start.4 = (bf16[64,768]{1,0:T(8,128)(2,1)S(1)}, bf16[64,768]{1,0:T(8,128)(2,1)S(1)}, u32[]{:S(2)}, u32[]{:S(2)}) collective-permute-start(bf16[64,768]{1,0:T(8,128)(2,1)S(1)} %get-tuple-element.46), channel_id=1, source_target_pairs={{0,8},{4,12},{8,0},{12,4},{1,9},{5,13},{9,1},{13,5},{2,10},{6,14},... | collective-permute-start | bytes 294920 | tf_op jit(solution)/shard_map/ppermute | solution.py:359
  15.3 0.0 collective-permute-done.2.refs_3_
  15.3 0.5 collective-permute-start.5
  15.8 5.0 %collective-permute-done.1.refs_2_ = bf16[32,2432]{1,0:T(8,128)(2,1)S(1)} collective-permute-done((bf16[32,2432]{1,0:T(8,128)(2,1)S(1)}, bf16[32,2432]{1,0:T(8,128)(2,1)S(1)}, u32[]{:S(2)}, u32[]{:S(2)}) %collective-permute-start.1) | collective-permute-done | bytes 155680 | tf_op jit(solution)/shard_map/ppermute | solution.py:356
  20.8 2.0 %first_pick.1 = (bf16[256,2304]{1,0:T(8,128)(2,1)}, bf16[256,128]{1,0:T(8,128)(2,1)S(1)}) custom-call(s32[1]{0:T(128)} %bitcast.near_ref, bf16[32,2432]{1,0:T(8,128)(2,1)S(1)} %get-tuple-element.41.refs_0_, bf16[32,2432]{1,0:T(8,128)(2,1)S(1)} %collective-permute-done.refs_1_, bf16[32,2432]{1,0:T(8,128)(2,1)S(1)} %collective-permute-done.1.refs_2_, ...), custom_call_target="tpu_custom_call" | custom-call | tf_op jit(solution)/shard_map/first_pick/pallas_call | solution.py:282
  22.8 0.0 collective-permute-done.3.refs_1_
  22.8 3.7 %all-to-all-start = ((bf16[4,64,2304]{2,1,0:T(8,128)(2,1)}), bf16[4,64,2304]{2,1,0:T(8,128)(2,1)S(1)}, u32[]{:S(2)}, u32[]{:S(2)}) async-start(bf16[4,64,2304]{2,1,0:T(8,128)(2,1)} %bitcast.6), calls=%async_computation | async-start | bytes 2359296 | tf_op jit(solution)/shard_map/all_to_all | solution.py:384
  26.5 1.2 %collective-permute-start.8 = (bf16[32,1792]{1,0:T(8,128)(2,1)S(1)}, bf16[32,1792]{1,0:T(8,128)(2,1)S(1)}, u32[]{:S(2)}, u32[]{:S(2)}) collective-permute-start(bf16[32,1792]{1,0:T(8,128)(2,1)S(1)} %get-tuple-element.49.refs_0_), channel_id=1, source_target_pairs={{0,3},{1,0},{2,1},{3,2},{4,7},{5,4},{6,5},{7,6},{8,11},{9,8},{10,9... | collective-permute-start | bytes 344072 | tf_op jit(solution)/shard_map/ppermute | solution.py:356
  27.8 1.6 %collective-permute-start.7 = (bf16[32,1792]{1,0:T(8,128)(2,1)S(1)}, bf16[32,1792]{1,0:T(8,128)(2,1)S(1)}, u32[]{:S(2)}, u32[]{:S(2)}) collective-permute-start(bf16[32,1792]{1,0:T(8,128)(2,1)S(1)} %get-tuple-element.49.refs_0_), channel_id=1, source_target_pairs={{0,2},{1,3},{2,0},{3,1},{4,6},{5,7},{6,4},{7,5},{8,10},{9,11},{10,... | collective-permute-start | bytes 344072 | tf_op jit(solution)/shard_map/ppermute | solution.py:356
  29.3 2.0 %collective-permute-start.6 = (bf16[32,1792]{1,0:T(8,128)(2,1)S(1)}, bf16[32,1792]{1,0:T(8,128)(2,1)S(1)}, u32[]{:S(2)}, u32[]{:S(2)}) collective-permute-start(bf16[32,1792]{1,0:T(8,128)(2,1)S(1)} %get-tuple-element.49.refs_0_), channel_id=1, source_target_pairs={{0,1},{1,2},{2,3},{3,0},{4,5},{5,6},{6,7},{7,4},{8,9},{9,10},{10,1... | collective-permute-start | bytes 344072 | tf_op jit(solution)/shard_map/ppermute | solution.py:356
  31.4 0.8 %collective-permute-done.8.refs_3_ = bf16[32,1792]{1,0:T(8,128)(2,1)S(1)} collective-permute-done((bf16[32,1792]{1,0:T(8,128)(2,1)S(1)}, bf16[32,1792]{1,0:T(8,128)(2,1)S(1)}, u32[]{:S(2)}, u32[]{:S(2)}) %collective-permute-start.8) | collective-permute-done | bytes 114720 | tf_op jit(solution)/shard_map/ppermute | solution.py:356
  32.2 6.9 %collective-permute-done.7.refs_2_ = bf16[32,1792]{1,0:T(8,128)(2,1)S(1)} collective-permute-done((bf16[32,1792]{1,0:T(8,128)(2,1)S(1)}, bf16[32,1792]{1,0:T(8,128)(2,1)S(1)}, u32[]{:S(2)}, u32[]{:S(2)}) %collective-permute-start.7) | collective-permute-done | bytes 114720 | tf_op jit(solution)/shard_map/ppermute | solution.py:356
  39.1 0.0 collective-permute-done.6.refs_1_
  39.1 1.3 %pick_rows.1 = bf16[256,1792]{1,0:T(8,128)(2,1)} custom-call(bf16[256,128]{1,0:T(8,128)(2,1)S(1)} %get-tuple-element.42.pick_ref, bf16[32,1792]{1,0:T(8,128)(2,1)S(1)} %get-tuple-element.49.refs_0_, bf16[32,1792]{1,0:T(8,128)(2,1)S(1)} %collective-permute-done.6.refs_1_, bf16[32,1792]{1,0:T(8,128)(2,1)S(1)} %collective-permute-done.7.refs_2_, ...), custom_call_target="tpu_custom_call" | custom-call | tf_op jit(solution)/shard_map/pick_rows/pallas_call | solution.py:297
  40.4 0.8 %all-to-all-done = bf16[4,64,2304]{2,1,0:T(8,128)(2,1)S(1)} async-done(((bf16[4,64,2304]{2,1,0:T(8,128)(2,1)}), bf16[4,64,2304]{2,1,0:T(8,128)(2,1)S(1)}, u32[]{:S(2)}, u32[]{:S(2)}) %all-to-all-start) | async-done | bytes 1179680 | tf_op jit(solution)/shard_map/all_to_all | solution.py:384
  41.3 3.5 %all-to-all-start.1 = ((bf16[4,64,1792]{2,1,0:T(8,128)(2,1)}), bf16[4,64,1792]{2,1,0:T(8,128)(2,1)S(1)}, u32[]{:S(2)}, u32[]{:S(2)}) async-start(bf16[4,64,1792]{2,1,0:T(8,128)(2,1)} %bitcast.8), calls=%async_computation.1 | async-start | bytes 1835008 | tf_op jit(solution)/shard_map/all_to_all | solution.py:384
  44.8 0.4 regroup_rows.1
  45.2 0.7 collective-permute-start.9
  45.9 2.0 %collective-permute-start.10 = (bf16[64,768]{1,0:T(8,128)(2,1)S(1)}, bf16[64,768]{1,0:T(8,128)(2,1)S(1)}, u32[]{:S(2)}, u32[]{:S(2)}) collective-permute-start(bf16[64,768]{1,0:T(8,128)(2,1)S(1)} %get-tuple-element.65), channel_id=1, source_target_pairs={{0,2},{1,3},{2,0},{3,1},{4,6},{5,7},{6,4},{7,5},{8,10},{9,11},{10,... | collective-permute-start | bytes 294920 | tf_op jit(solution)/shard_map/ppermute | solution.py:356
  47.9 2.8 %collective-permute-start.11 = (bf16[64,768]{1,0:T(8,128)(2,1)S(1)}, bf16[64,768]{1,0:T(8,128)(2,1)S(1)}, u32[]{:S(2)}, u32[]{:S(2)}) collective-permute-start(bf16[64,768]{1,0:T(8,128)(2,1)S(1)} %get-tuple-element.66), channel_id=1, source_target_pairs={{0,3},{1,0},{2,1},{3,2},{4,7},{5,4},{6,5},{7,6},{8,11},{9,8},{10,9... | collective-permute-start | bytes 294920 | tf_op jit(solution)/shard_map/ppermute | solution.py:356
  50.7 0.0 collective-permute-start.12
  50.7 4.0 %fusion = f32[256,768]{1,0:T(8,128)} fusion(bf16[256,2304]{1,0:T(8,128)(2,1)S(1)} %bitcast.19, bf16[768,4096]{1,0:T(8,128)(2,1)} %bitcast.32), kind=kOutput, calls=%fused_computation | convolution fusion | flops 905969664 | bytes 5505024 | tf_op jit(solution)/shard_map/dot_general | solution.py:393
  54.7 0.0 collective-permute-done.9.refs_1_
  54.7 0.6 collective-permute-done.10.refs_2_
  55.3 0.0 collective-permute-done.11.refs_3_
  55.4 1.1 %all-to-all-done.1 = bf16[4,64,1792]{2,1,0:T(8,128)(2,1)S(1)} async-done(((bf16[4,64,1792]{2,1,0:T(8,128)(2,1)}), bf16[4,64,1792]{2,1,0:T(8,128)(2,1)S(1)}, u32[]{:S(2)}, u32[]{:S(2)}) %all-to-all-start.1) | async-done | bytes 917536 | tf_op jit(solution)/shard_map/all_to_all | solution.py:384
  56.4 0.0 collective-permute-start.13
  56.4 3.6 %fusion.4 = bf16[256,768]{1,0:T(8,128)(2,1)} fusion(f32[256,768]{1,0:T(8,128)} %fusion, bf16[256,1792]{1,0:T(8,128)(2,1)S(1)} %bitcast.22, bf16[768,4096]{1,0:T(8,128)(2,1)} %bitcast.33), kind=kOutput, calls=%fused_computation.4 | convolution fusion | flops 705036288 | bytes 4849664 | tf_op jit(solution)/shard_map/dot_general | solution.py:393
  60.1 5.8 %all-to-all-start.2 = ((bf16[16,16,768]{2,1,0:T(8,128)(2,1)}), bf16[16,16,768]{2,1,0:T(8,128)(2,1)S(1)}, u32[]{:S(2)}, u32[]{:S(2)}) async-start(bf16[16,16,768]{2,1,0:T(8,128)(2,1)} %bitcast.11), calls=%async_computation.2 | async-start | bytes 786432 | tf_op jit(solution)/shard_map/all_to_all | solution.py:401
  65.9 0.0 copy-start.1
  65.9 0.0 copy-start.6
  65.9 0.3 collective-permute-start.14
  66.2 1.5 %collective-permute-done.14.refs_5_ = bf16[64,3072]{1,0:T(8,128)(2,1)S(1)} collective-permute-done((bf16[64,3072]{1,0:T(8,128)(2,1)S(1)}, bf16[64,3072]{1,0:T(8,128)(2,1)S(1)}, u32[]{:S(2)}, u32[]{:S(2)}) %collective-permute-start.14) | collective-permute-done | bytes 393248 | tf_op jit(solution)/shard_map/ppermute | solution.py:362
  67.7 7.5 %down_rows.1 = bf16[384,4096]{1,0:T(8,128)(2,1)} custom-call(s32[3]{0:T(128)S(1)} %pad_add_fusion.scalars_ref, bf16[256,2304]{1,0:T(8,128)(2,1)S(1)} %bitcast.20, bf16[256,1792]{1,0:T(8,128)(2,1)S(1)} %bitcast.23, bf16[256,2304]{1,0:T(8,128)(2,1)} %collective-permute-done.12.refs_2_, bf16[256,1792]{1,0:T(8,128)(2,1)} %collective-permute-done.13.refs_3_, ...), custom_call_target="tpu_custom_call" | custom-call | flops 1610612736 | bytes 7340032 | tf_op jit(solution)/shard_map/down_rows/pallas_call | solution.py:325
  75.2 4.7 %all-to-all-done.2 = bf16[16,16,768]{2,1,0:T(8,128)(2,1)S(1)} async-done(((bf16[16,16,768]{2,1,0:T(8,128)(2,1)}), bf16[16,16,768]{2,1,0:T(8,128)(2,1)S(1)}, u32[]{:S(2)}, u32[]{:S(2)}) %all-to-all-start.2) | async-done | bytes 393248 | tf_op jit(solution)/shard_map/all_to_all | solution.py:401
  79.9 1.4 %close_rows.1 = (bf16[256,768]{1,0:T(8,128)(2,1)}, f32[8,32]{1,0:T(8,128)}) custom-call(bf16[256,256]{1,0:T(8,128)(2,1)S(1)} %get-tuple-element.40.back_ref, bf16[256,768]{1,0:T(8,128)(2,1)S(1)} %bitcast.26, f32[8,32]{1,0:T(8,128)S(1)} %bitcast.30, bf16[256,768]{1,0:T(8,128)(2,1)S(1)} %bitcast.25), custom_call_target="tpu_custom_call" | custom-call | tf_op jit(solution)/shard_map/close_rows/pallas_call | solution.py:260
  (13 shorter events, 0.1 us)
Async XLA Ops:
  0.6 1.0 %copy-start.2 = (bf16[32,4096]{1,0:T(8,128)(2,1)S(1)}, bf16[32,4096]{1,0:T(8,128)(2,1)}, u32[]{:S(2)}) copy-start(bf16[32,4096]{1,0:T(8,128)(2,1)} %tokens_hbm.1) | copy-start | bytes 786436
  1.6 0.7 copy-start.3
  2.5 12.8 %collective-permute-start.2 = (bf16[32,2432]{1,0:T(8,128)(2,1)S(1)}, bf16[32,2432]{1,0:T(8,128)(2,1)S(1)}, u32[]{:S(2)}, u32[]{:S(2)}) collective-permute-start(bf16[32,2432]{1,0:T(8,128)(2,1)S(1)} %get-tuple-element.41.refs_0_), channel_id=1, source_target_pairs={{0,3},{1,0},{2,1},{3,2},{4,7},{5,4},{6,5},{7,6},{8,11},{9,8},{10,9... | collective-permute-start | bytes 466952 | tf_op jit(solution)/shard_map/ppermute | solution.py:356
  7.6 13.2 %collective-permute-start.1 = (bf16[32,2432]{1,0:T(8,128)(2,1)S(1)}, bf16[32,2432]{1,0:T(8,128)(2,1)S(1)}, u32[]{:S(2)}, u32[]{:S(2)}) collective-permute-start(bf16[32,2432]{1,0:T(8,128)(2,1)S(1)} %get-tuple-element.41.refs_0_), channel_id=1, source_target_pairs={{0,2},{1,3},{2,0},{3,1},{4,6},{5,7},{6,4},{7,5},{8,10},{9,11},{10,... | collective-permute-start | bytes 466952 | tf_op jit(solution)/shard_map/ppermute | solution.py:356
  7.7 13.2 %collective-permute-start = (bf16[32,2432]{1,0:T(8,128)(2,1)S(1)}, bf16[32,2432]{1,0:T(8,128)(2,1)S(1)}, u32[]{:S(2)}, u32[]{:S(2)}) collective-permute-start(bf16[32,2432]{1,0:T(8,128)(2,1)S(1)} %get-tuple-element.41.refs_0_), channel_id=1, source_target_pairs={{0,1},{1,2},{2,3},{3,0},{4,5},{5,6},{6,7},{7,4},{8,9},{9,10},{10,1... | collective-permute-start | bytes 466952 | tf_op jit(solution)/shard_map/ppermute | solution.py:356
  8.7 1.0 %copy-start = (bf16[32,8,768]{2,1,0:T(8,128)(2,1)S(1)}, bf16[32,8,768]{2,1,0:T(8,128)(2,1)}, u32[]{:S(2)}) copy-start(bf16[32,8,768]{2,1,0:T(8,128)(2,1)} %param.6) | copy-start | bytes 1179652
  9.7 0.7 copy-start.4
  10.4 0.7 copy-start.5
  12.2 10.6 %collective-permute-start.3 = (bf16[64,768]{1,0:T(8,128)(2,1)S(1)}, bf16[64,768]{1,0:T(8,128)(2,1)S(1)}, u32[]{:S(2)}, u32[]{:S(2)}) collective-permute-start(bf16[64,768]{1,0:T(8,128)(2,1)S(1)} %get-tuple-element.45), channel_id=1, source_target_pairs={{0,4},{4,0},{8,12},{12,8},{1,5},{5,1},{9,13},{13,9},{2,6},{6,2},{1... | collective-permute-start | bytes 294920 | tf_op jit(solution)/shard_map/ppermute | solution.py:359
  13.8 9.0 %collective-permute-start.4 = (bf16[64,768]{1,0:T(8,128)(2,1)S(1)}, bf16[64,768]{1,0:T(8,128)(2,1)S(1)}, u32[]{:S(2)}, u32[]{:S(2)}) collective-permute-start(bf16[64,768]{1,0:T(8,128)(2,1)S(1)} %get-tuple-element.46), channel_id=1, source_target_pairs={{0,8},{4,12},{8,0},{12,4},{1,9},{5,13},{9,1},{13,5},{2,10},{6,14},... | collective-permute-start | bytes 294920 | tf_op jit(solution)/shard_map/ppermute | solution.py:359
  15.3 7.5 %collective-permute-start.5 = (bf16[64,768]{1,0:T(8,128)(2,1)S(1)}, bf16[64,768]{1,0:T(8,128)(2,1)S(1)}, u32[]{:S(2)}, u32[]{:S(2)}) collective-permute-start(bf16[64,768]{1,0:T(8,128)(2,1)S(1)} %get-tuple-element.47), channel_id=1, source_target_pairs={{0,12},{4,8},{8,4},{12,0},{1,13},{5,9},{9,5},{13,1},{2,14},{6,10},... | collective-permute-start | bytes 294920 | tf_op jit(solution)/shard_map/ppermute | solution.py:359
  22.8 18.5 %all-to-all-start = ((bf16[4,64,2304]{2,1,0:T(8,128)(2,1)}), bf16[4,64,2304]{2,1,0:T(8,128)(2,1)S(1)}, u32[]{:S(2)}, u32[]{:S(2)}) async-start(bf16[4,64,2304]{2,1,0:T(8,128)(2,1)} %bitcast.6), calls=%async_computation | async-start | bytes 2359296 | tf_op jit(solution)/shard_map/all_to_all | solution.py:384
  26.5 5.6 %collective-permute-start.8 = (bf16[32,1792]{1,0:T(8,128)(2,1)S(1)}, bf16[32,1792]{1,0:T(8,128)(2,1)S(1)}, u32[]{:S(2)}, u32[]{:S(2)}) collective-permute-start(bf16[32,1792]{1,0:T(8,128)(2,1)S(1)} %get-tuple-element.49.refs_0_), channel_id=1, source_target_pairs={{0,3},{1,0},{2,1},{3,2},{4,7},{5,4},{6,5},{7,6},{8,11},{9,8},{10,9... | collective-permute-start | bytes 344072 | tf_op jit(solution)/shard_map/ppermute | solution.py:356
  27.8 11.3 %collective-permute-start.7 = (bf16[32,1792]{1,0:T(8,128)(2,1)S(1)}, bf16[32,1792]{1,0:T(8,128)(2,1)S(1)}, u32[]{:S(2)}, u32[]{:S(2)}) collective-permute-start(bf16[32,1792]{1,0:T(8,128)(2,1)S(1)} %get-tuple-element.49.refs_0_), channel_id=1, source_target_pairs={{0,2},{1,3},{2,0},{3,1},{4,6},{5,7},{6,4},{7,5},{8,10},{9,11},{10,... | collective-permute-start | bytes 344072 | tf_op jit(solution)/shard_map/ppermute | solution.py:356
  29.3 9.8 %collective-permute-start.6 = (bf16[32,1792]{1,0:T(8,128)(2,1)S(1)}, bf16[32,1792]{1,0:T(8,128)(2,1)S(1)}, u32[]{:S(2)}, u32[]{:S(2)}) collective-permute-start(bf16[32,1792]{1,0:T(8,128)(2,1)S(1)} %get-tuple-element.49.refs_0_), channel_id=1, source_target_pairs={{0,1},{1,2},{2,3},{3,0},{4,5},{5,6},{6,7},{7,4},{8,9},{9,10},{10,1... | collective-permute-start | bytes 344072 | tf_op jit(solution)/shard_map/ppermute | solution.py:356
  41.3 15.2 %all-to-all-start.1 = ((bf16[4,64,1792]{2,1,0:T(8,128)(2,1)}), bf16[4,64,1792]{2,1,0:T(8,128)(2,1)S(1)}, u32[]{:S(2)}, u32[]{:S(2)}) async-start(bf16[4,64,1792]{2,1,0:T(8,128)(2,1)} %bitcast.8), calls=%async_computation.1 | async-start | bytes 1835008 | tf_op jit(solution)/shard_map/all_to_all | solution.py:384
  45.2 9.5 %collective-permute-start.9 = (bf16[64,768]{1,0:T(8,128)(2,1)S(1)}, bf16[64,768]{1,0:T(8,128)(2,1)S(1)}, u32[]{:S(2)}, u32[]{:S(2)}) collective-permute-start(bf16[64,768]{1,0:T(8,128)(2,1)S(1)} %get-tuple-element.64), channel_id=1, source_target_pairs={{0,1},{1,2},{2,3},{3,0},{4,5},{5,6},{6,7},{7,4},{8,9},{9,10},{10,1... | collective-permute-start | bytes 294920 | tf_op jit(solution)/shard_map/ppermute | solution.py:356
  45.9 9.5 %collective-permute-start.10 = (bf16[64,768]{1,0:T(8,128)(2,1)S(1)}, bf16[64,768]{1,0:T(8,128)(2,1)S(1)}, u32[]{:S(2)}, u32[]{:S(2)}) collective-permute-start(bf16[64,768]{1,0:T(8,128)(2,1)S(1)} %get-tuple-element.65), channel_id=1, source_target_pairs={{0,2},{1,3},{2,0},{3,1},{4,6},{5,7},{6,4},{7,5},{8,10},{9,11},{10,... | collective-permute-start | bytes 294920 | tf_op jit(solution)/shard_map/ppermute | solution.py:356
  47.9 7.5 %collective-permute-start.11 = (bf16[64,768]{1,0:T(8,128)(2,1)S(1)}, bf16[64,768]{1,0:T(8,128)(2,1)S(1)}, u32[]{:S(2)}, u32[]{:S(2)}) collective-permute-start(bf16[64,768]{1,0:T(8,128)(2,1)S(1)} %get-tuple-element.66), channel_id=1, source_target_pairs={{0,3},{1,0},{2,1},{3,2},{4,7},{5,4},{6,5},{7,6},{8,11},{9,8},{10,9... | collective-permute-start | bytes 294920 | tf_op jit(solution)/shard_map/ppermute | solution.py:356
  50.7 17.0 %collective-permute-start.12 = (bf16[256,2304]{1,0:T(8,128)(2,1)S(1)}, bf16[256,2304]{1,0:T(8,128)(2,1)}, u32[]{:S(2)}, u32[]{:S(2)}) collective-permute-start(bf16[256,2304]{1,0:T(8,128)(2,1)S(1)} %bitcast.18), channel_id=1, source_target_pairs={{0,16},{16,0},{1,17},{17,1},{2,18},{18,2},{3,19},{19,3},{4,20},{20... | collective-permute-start | bytes 3538952 | tf_op jit(solution)/shard_map/ppermute | solution.py:362
  56.4 11.3 %collective-permute-start.13 = (bf16[256,1792]{1,0:T(8,128)(2,1)S(1)}, bf16[256,1792]{1,0:T(8,128)(2,1)}, u32[]{:S(2)}, u32[]{:S(2)}) collective-permute-start(bf16[256,1792]{1,0:T(8,128)(2,1)S(1)} %bitcast.21), channel_id=1, source_target_pairs={{0,16},{16,0},{1,17},{17,1},{2,18},{18,2},{3,19},{19,3},{4,20},{20... | collective-permute-start | bytes 2752520 | tf_op jit(solution)/shard_map/ppermute | solution.py:362
  60.1 19.9 %all-to-all-start.2 = ((bf16[16,16,768]{2,1,0:T(8,128)(2,1)}), bf16[16,16,768]{2,1,0:T(8,128)(2,1)S(1)}, u32[]{:S(2)}, u32[]{:S(2)}) async-start(bf16[16,16,768]{2,1,0:T(8,128)(2,1)} %bitcast.11), calls=%async_computation.2 | async-start | bytes 786432 | tf_op jit(solution)/shard_map/all_to_all | solution.py:401
  65.9 14.0 %copy-start.1 = (bf16[32,8,768]{2,1,0:T(8,128)(2,1)S(1)}, bf16[32,8,768]{2,1,0:T(8,128)(2,1)}, u32[]{:S(2)}) copy-start(bf16[32,8,768]{2,1,0:T(8,128)(2,1)} %param.6) | copy-start | bytes 1179652
  65.9 14.0 %copy-start.6 = (f32[32,8]{0,1:T(8,128)S(1)}, f32[32,8]{0,1:T(8,128)}, u32[]{:S(2)}) copy-start(f32[32,8]{0,1:T(8,128)} %param.7) | copy-start | bytes 3076
  65.9 1.8 %collective-permute-start.14 = (bf16[64,3072]{1,0:T(8,128)(2,1)S(1)}, bf16[64,3072]{1,0:T(8,128)(2,1)S(1)}, u32[]{:S(2)}, u32[]{:S(2)}) collective-permute-start(bf16[64,3072]{1,0:T(8,128)(2,1)S(1)} %join_rows.1.refs_4_), channel_id=1, source_target_pairs={{0,16},{16,0},{1,17},{17,1},{2,18},{18,2},{3,19},{19,3},{4,20},{20... | collective-permute-start | bytes 1179656 | tf_op jit(solution)/shard_map/ppermute | solution.py:362
